TPU v7x, 256 devices: a whole 4x4x8 slice. The times are simulated.
256 devices in a mesh: gx: 8 (over z), gy: 8 (over y, x_hi), col: 4 (over x_lo, core).
Axes of the slice: x: 4 (x_hi: 2, x_lo: 2; x = x_hi * 2 + x_lo), y: 4, z: 8, core: 2. Of those that a mesh axis runs over, the one named last changes fastest.
Arguments:
- pre_bottom: bfloat16 [8, 16, 16, 1024], P(None, None, 'col', 'gy'), may hold values from -6 to 6
- bottom_input: bfloat16 [8, 16, 16, 1024], P(None, None, 'col', 'gx'), may hold values from -6 to 6
- bottom_weight: bfloat16 [1024, 27, 1024], P('gx', None, 'gy'), may hold values from -0.0390625 to 0.0390625
- up_weight: bfloat16 [1024, 512], P('gy'), may hold values from -0.09375 to 0.09375
- level_input: bfloat16 [16, 32, 32, 512], P('gx', 'gy', None, 'col'), may hold values from -6 to 6
- pre_level: bfloat16 [16, 32, 32, 512], P('gx', 'gy', None, 'col'), may hold values from -6 to 6
- level_cotangent: bfloat16 [16, 32, 32, 512], P('gx', 'gy', None, 'col'), may hold values from -6 to 6
- labels: int32 [16, 32, 32], P('gx', 'gy'), may hold values from 0 to 13
- level_weight: bfloat16 [512, 13824], P('col'), may hold values from -0.0546875 to 0.0546875
- aux_weight: bfloat16 [512, 14], P('col'), may hold values from -2 to 2
Outputs:
- level_input_grad: bfloat16 [16, 32, 32, 512], P('gx', 'gy', None, 'col')
- bottom_input_grad: bfloat16 [8, 16, 16, 1024], P('gy', None, 'col', 'gx')
- level_weight_grad: float32 [512, 13824], P('col', ('gx', 'gy'))
- bottom_weight_grad: float32 [1024, 27, 1024], P(('gx', 'col'), None, 'gy')
- up_weight_grad: float32 [1024, 512], P('gy', 'col')
- aux_weight_grad: float32 [512, 14], P('col')
All inputs are finite; a program needn't handle non-finite values.
Results may differ from a plain program's by a relative error of at most 0.011.
Values may be sent and summed in bfloat16 or wider, within the bound.
No kernel may reach another device: no remote copies, remote signals or barrier semaphores. Data moves between devices by JAX's collectives and lax.ppermute only.
A program may use at most 64 MiB of HBM per device.

v0:
```python
import jax
import jax.numpy as jnp
from jax import lax
from jax.sharding import PartitionSpec as P

CLASSES = 14
TAPS = 27


def extended_2(x, sides, width):
    for axis, dim in sides:
        size, length = (lax.axis_size(axis), x.shape[dim])
        up = [(i, (i + 1) % size) for i in range(size - 1)]
        down = [(j, i) for i, j in up]
        last = lax.slice_in_dim(x, length - width, length, axis=dim)
        leading = lax.slice_in_dim(x, 0, width, axis=dim)
        before = lax.ppermute(last, axis, up)
        after = lax.ppermute(leading, axis, down)
        x = jnp.concatenate([before, x, after], axis=dim)
    return x


def tap_offsets():
    return [
        (depth_step, height_step, width_step)
        for depth_step in (-1, 0, 1)
        for height_step in (-1, 0, 1)
        for width_step in (-1, 0, 1)
    ]


def taps_back(source, padded, weight):
    depth_size, height_size, width_size, inner_width = source.shape
    outer_width = padded.shape[3]
    row_count = depth_size * height_size * width_size
    flat_source = source.reshape(row_count, inner_width)
    input_grad = jnp.zeros((row_count, inner_width), jnp.float32)
    pieces = []
    for tap_index, (depth_step, height_step, width_step) in enumerate(tap_offsets()):
        shifted = lax.slice(
            padded,
            (1 - depth_step, 1 - height_step, 1 - width_step, 0),
            (
                1 - depth_step + depth_size,
                1 - height_step + height_size,
                1 - width_step + width_size,
                outer_width,
            ),
        ).reshape(row_count, outer_width)
        tap_weight = weight[:, tap_index * outer_width : (tap_index + 1) * outer_width]
        input_grad = input_grad + lax.dot_general(
            shifted, tap_weight, (((1,), (1,)), ((), ())), preferred_element_type=jnp.float32
        )
        pieces.append(
            lax.dot_general(
                flat_source, shifted, (((0,), (0,)), ((), ())), preferred_element_type=jnp.float32
            )
        )
    return (
        input_grad.reshape(depth_size, height_size, width_size, inner_width),
        jnp.concatenate(pieces, axis=1),
    )


def per_device(
    pre_bottom,
    bottom_input,
    bottom_weight,
    up_weight,
    level_input,
    pre_level,
    level_cotangent,
    labels,
    level_weight,
    aux_weight,
):
    inner_width = level_input.shape[3]
    full_width = level_weight.shape[1] // TAPS
    active_rows = jnp.maximum(pre_level, 0).reshape(-1, inner_width)
    part_logits = jnp.dot(active_rows, aux_weight, preferred_element_type=jnp.float32)
    logits = lax.psum(part_logits, "col")
    probabilities = jax.nn.softmax(logits, axis=-1)
    onehot = (labels.reshape(-1)[:, None] == jnp.arange(CLASSES, dtype=jnp.int32)[None, :]).astype(
        jnp.float32
    )
    logit_grad = (probabilities - onehot).astype(jnp.bfloat16)
    aux_part = lax.dot_general(
        active_rows, logit_grad, (((0,), (0,)), ((), ())), preferred_element_type=jnp.float32
    )
    aux_weight_grad = lax.psum(aux_part, ("gx", "gy"))
    aux_back = lax.dot_general(
        logit_grad, aux_weight, (((1,), (1,)), ((), ())), preferred_element_type=jnp.float32
    )
    total_grad = level_cotangent.reshape(-1, inner_width).astype(jnp.float32) + aux_back
    level_pre_grad = (
        jnp.where(pre_level.reshape(-1, inner_width) > 0, total_grad, jnp.zeros_like(total_grad))
        .astype(jnp.bfloat16)
        .reshape(pre_level.shape)
    )
    gathered = lax.all_gather(level_pre_grad, "col", axis=3, tiled=True)
    extended = extended_2(gathered, (("gx", 0), ("gy", 1)), 1)
    extended = jnp.pad(extended, ((0, 0), (0, 0), (1, 1), (0, 0)))
    skip_grad, level_part = taps_back(level_input, extended, level_weight)
    level_input_grad = skip_grad.astype(jnp.bfloat16)
    level_weight_grad = lax.psum_scatter(level_part, ("gx", "gy"), scatter_dimension=1, tiled=True)
    sub_depth, sub_height, full_cells, _ = skip_grad.shape
    down_local = (
        skip_grad.reshape(sub_depth // 2, 2, sub_height // 2, 2, full_cells // 2, 2, inner_width)
        .sum(axis=(1, 3, 5))
        .astype(jnp.bfloat16)
    )
    relayed = lax.all_to_all(down_local, "col", split_axis=2, concat_axis=3, tiled=True)
    relayed = lax.all_gather(relayed, "gx", axis=0, tiled=True)
    down_grad = lax.all_gather(relayed, "gy", axis=1, tiled=True)
    flat_down = down_grad.reshape(-1, full_width)
    filter_width = pre_bottom.shape[3]
    bottom_active = jnp.maximum(pre_bottom, 0).reshape(-1, filter_width)
    up_part = lax.dot_general(
        bottom_active, flat_down, (((0,), (0,)), ((), ())), preferred_element_type=jnp.float32
    )
    up_weight_grad = lax.psum_scatter(
        up_part.astype(jnp.bfloat16), "col", scatter_dimension=1, tiled=True
    ).astype(jnp.float32)
    bottom_back = lax.dot_general(
        flat_down, up_weight, (((1,), (1,)), ((), ())), preferred_element_type=jnp.float32
    ).reshape(pre_bottom.shape)
    bottom_pre_grad = jnp.where(pre_bottom > 0, bottom_back, jnp.zeros_like(bottom_back)).astype(
        jnp.bfloat16
    )
    bottom_padded = extended_2(bottom_pre_grad, (("col", 2),), 1)
    bottom_padded = jnp.pad(bottom_padded, ((1, 1), (1, 1), (0, 0), (0, 0)))
    channel_width = bottom_weight.shape[0]
    flat_weight = bottom_weight.reshape(channel_width, -1)
    bottom_part, bottom_weight_part = taps_back(bottom_input, bottom_padded, flat_weight)
    bottom_input_grad = lax.psum_scatter(bottom_part, "gy", scatter_dimension=0, tiled=True).astype(
        jnp.bfloat16
    )
    bottom_weight_grad = lax.psum_scatter(
        bottom_weight_part.reshape(bottom_weight.shape), "col", scatter_dimension=0, tiled=True
    )
    return (
        level_input_grad,
        bottom_input_grad,
        level_weight_grad,
        bottom_weight_grad,
        up_weight_grad,
        aux_weight_grad,
    )


def solution(mesh):
    return jax.shard_map(
        per_device,
        mesh=mesh,
        in_specs=(
            P(None, None, "col", "gy"),
            P(None, None, "col", "gx"),
            P("gx", None, "gy"),
            P("gy", None),
            P("gx", "gy", None, "col"),
            P("gx", "gy", None, "col"),
            P("gx", "gy", None, "col"),
            P("gx", "gy", None),
            P("col", None),
            P("col", None),
        ),
        out_specs=(
            P("gx", "gy", None, "col"),
            P("gy", None, "col", "gx"),
            P("col", ("gx", "gy")),
            P(("gx", "col"), None, "gy"),
            P("gy", "col"),
            P("col", None),
        ),
        check_vma=False,
    )
```

profile of v0, /device:TPU:1, one launch (start us, length us, event | category | flops | bytes accessed | tf_op | source)
XLA Modules:
  0.0 1120.1 jit_solution(11027660149962761967)
XLA Ops:
  10.6 11.0 psum.14
  21.7 1.1 fusion.40
  22.8 8.0 all_gather.9
  30.8 2.9 collective-permute-start
  33.7 1.3 collective-permute-start.1
  35.0 1.4 collective-permute-done
  36.5 4.1 collective-permute-done.1
  41.3 4.3 collective-permute-start.2
  45.7 1.3 collective-permute-start.3
  47.0 1.3 copy.175
  48.3 1.0 slice.505
  49.3 3.8 collective-permute-done.3
  54.3 1.2 copy-done.1
  62.6 1.0 reduce_sum.19
  64.2 5.7 all-to-all-start
  69.9 1.0 fusion.27
  70.9 1.0 fusion.8
  71.9 1.0 fusion.26
  72.8 1.0 fusion.25
  73.8 1.0 fusion.7
  75.7 1.0 fusion.23
  76.7 1.0 fusion.6
  77.7 1.0 fusion.22
  78.7 1.0 fusion.21
  79.6 1.0 fusion.5
  80.6 1.0 fusion.20
  81.6 20.7 %all_gather.10 = bf16[8,2,4,512]{3,2,1,0:T(4,128)(2,1)S(1)} all-gather(bf16[1,2,4,512]{3,2,1,0:T(4,128)(2,1)S(1)} %bitcast.697), channel_id=1, replica_groups=mesh['gx'=8,'gy'=8,'col'=4] {'gx'}, dimensions={0}, use_global_device_ids=true | all-gather | bytes 73728 | tf_op jit(solution)/shard_map/all_gather | solution.py:113
  102.4 30.9 %all_gather.11 = bf16[8,16,4,512]{3,0,2,1:T(8,128)(2,1)S(1)} all-gather(bf16[8,2,4,512]{3,0,2,1:T(8,128)(2,1)S(1)} %copy.172), channel_id=1, replica_groups=mesh['gx'=8,'gy'=8,'col'=4] {'gy'}, dimensions={1}, use_global_device_ids=true | all-gather | bytes 589824 | tf_op jit(solution)/shard_map/all_gather | solution.py:114
  133.9 15.3 %collective-permute-start.4 = (bf16[8,16,1,128]{3,1,2,0:T(8,128)(2,1)S(1)}, bf16[8,16,1,128]{3,1,2,0:T(8,128)(2,1)S(1)}, u32[]{:S(2)}, u32[]{:S(2)}) collective-permute-start(bf16[8,16,1,128]{3,1,2,0:T(8,128)(2,1)S(1)} %get-tuple-element.78), channel_id=1, source_target_pairs={{0,1},{1,2},{2,3},{4,5},{5,6},{6,7},{8,9},{9,10},{10,11},{12,13},{... | collective-permute-start | bytes 98312 | tf_op jit(solution)/shard_map/ppermute | solution.py:17
  149.2 1.9 collective-permute-start.5
  167.6 1.6 fusion.42
  187.8 2.8 copy.230
  190.7 1.0 fusion.19
  191.6 1.0 fusion.18
  193.6 1.0 fusion.16
  194.5 1.0 fusion.4
  195.5 1.0 fusion.15
  196.5 1.0 fusion.14
  197.5 1.0 fusion.3
  198.5 1.0 fusion.13
  199.4 1.0 fusion.12
  200.4 1.0 fusion.2
  201.4 1.0 fusion.11
  202.3 1.0 fusion.10
  203.3 1.0 fusion.1
  204.3 1.0 fusion.9
  206.2 155.7 %psum.15 = f32[128,14]{0,1:T(8,128)} all-reduce(f32[128,14]{0,1:T(8,128)S(1)} %fusion.166), channel_id=1, replica_groups=mesh['gx'=8,'gy'=8,'col'=4] {'gx','gy'}, use_global_device_ids=true, to_apply=%region_8.9 | all-reduce | flops 1792 | bytes 14336 | tf_op jit(solution)/shard_map/psum | solution.py:90
  364.8 748.7 %reduce-scatter.15.cloned.1.call-done = f32[128,216]{0,1:T(8,128)} async-done(((f32[128,13824]{0,1:T(8,128)}), f32[128,216]{0,1:T(8,128)}) %reduce-scatter.15.cloned.1.call-update) | async-done | bytes 110608
  (191 shorter events, 54.0 us)
Async XLA Ops:
  7.2 150.3 %copy-start = (bf16[8,16,4,128]{3,2,1,0:T(4,128)(2,1)S(1)}, bf16[8,16,4,128]{3,2,1,0:T(4,128)(2,1)}, u32[]{:S(2)}) copy-start(bf16[8,16,4,128]{3,2,1,0:T(4,128)(2,1)} %param.11) | copy-start | bytes 393220
  7.2 39.8 %copy-start.2 = (bf16[128,27,128]{2,0,1:T(8,128)(2,1)S(1)}, bf16[128,27,128]{2,0,1:T(8,128)(2,1)}, u32[]{:S(2)}) copy-start(bf16[128,27,128]{2,0,1:T(8,128)(2,1)} %param.12) | copy-start | bytes 2654212
  9.0 26.0 %copy-start.6 = (bf16[2,4,32,128]{3,2,1,0:T(8,128)(2,1)}, bf16[2,4,32,128]{3,2,1,0:T(8,128)(2,1)S(1)}, u32[]{:S(2)}) copy-start(bf16[2,4,32,128]{3,2,1,0:T(8,128)(2,1)S(1)} %broadcast_maximum_fusion) | copy-start | bytes 196612
  21.6 13.4 %copy-start.8 = (f32[256,14]{0,1:T(8,128)}, f32[256,14]{0,1:T(8,128)S(1)}, u32[]{:S(2)}) copy-start(f32[256,14]{0,1:T(8,128)S(1)} %psum.14) | copy-start | bytes 43012
  21.7 12.0 %copy-start.12 = (f32[256]{0:T(256)}, f32[256]{0:T(256)S(1)}, u32[]{:S(2)}) copy-start(f32[256]{0:T(256)S(1)} %fusion.156) | copy-start | bytes 3076
  30.8 5.6 collective-permute-start
  33.7 6.9 collective-permute-start.1
  36.5 9.2 copy-start.4
  41.3 8.0 collective-permute-start.2
  45.7 7.4 collective-permute-start.3
  53.6 2.0 copy-start.1
  59.7 10.3 copy-start.16
  64.2 17.4 %all-to-all-start = ((bf16[1,2,16,128]{3,1,0,2:T(2,128)(2,1)}), bf16[1,2,16,128]{3,1,0,2:T(2,128)(2,1)S(1)}, u32[]{:S(2)}, u32[]{:S(2)}) async-start(bf16[1,2,16,128]{3,1,0,2:T(2,128)(2,1)} %copy.170), calls=%async_computation | async-start | bytes 16384 | tf_op jit(solution)/shard_map/all_to_all | solution.py:112
  69.9 292.0 %reduce-scatter.13.cloned.1.call-start = ((), (), s32[]{:S(2)}) async-start(), calls=%async_computation.7 | async-start | bytes 163840
  76.7 56.5 %copy-start.14 = (bf16[128,512]{1,0:T(8,128)(2,1)S(1)}, bf16[128,512]{1,0:T(8,128)(2,1)}, u32[]{:S(2)}) copy-start(bf16[128,512]{1,0:T(8,128)(2,1)} %param.13) | copy-start | bytes 393220
  76.7 56.5 %copy-start.15 = (bf16[8,16,4,128]{3,2,1,0:T(4,128)(2,1)S(1)}, bf16[8,16,4,128]{3,2,1,0:T(4,128)(2,1)}, u32[]{:S(2)}) copy-start(bf16[8,16,4,128]{3,2,1,0:T(4,128)(2,1)} %param.10) | copy-start | bytes 393220
  133.9 19.7 %collective-permute-start.4 = (bf16[8,16,1,128]{3,1,2,0:T(8,128)(2,1)S(1)}, bf16[8,16,1,128]{3,1,2,0:T(8,128)(2,1)S(1)}, u32[]{:S(2)}, u32[]{:S(2)}) collective-permute-start(bf16[8,16,1,128]{3,1,2,0:T(8,128)(2,1)S(1)} %get-tuple-element.78), channel_id=1, source_target_pairs={{0,1},{1,2},{2,3},{4,5},{5,6},{6,7},{8,9},{9,10},{10,11},{12,13},{... | collective-permute-start | bytes 98312 | tf_op jit(solution)/shard_map/ppermute | solution.py:17
  149.2 5.3 collective-permute-start.5
  153.4 210.1 %reduce-scatter.9.cloned.1.call-start = ((), (), s32[]{:S(2)}) async-start(), calls=%async_computation.5 | async-start | bytes 294912 | tf_op jit(solution)/shard_map/reduce_scatter | solution.py:135
  153.6 0.6 copy-start.10
  154.6 1.6 copy-start.11
  178.5 1.8 copy-start.3
  185.2 179.6 %reduce-scatter.11.cloned.1.call-start = ((), (), s32[]{:S(2)}) async-start(), calls=%async_computation.6 | async-start | bytes 2211840 | tf_op jit(solution)/shard_map/reduce_scatter | solution.py:138
  186.1 4.5 copy-start.17
  190.6 922.9 %reduce-scatter.15.cloned.1.call-start = ((), (), s32[]{:S(2)}) async-start(), calls=%async_computation.8 | async-start | bytes 7188480
  194.5 5.9 copy-start.5
  205.3 0.8 copy-start.7
  205.3 0.8 copy-start.9
  205.3 0.8 copy-start.13
Sparse Core Ops, SparseCore 0:
  153.5 16.8 reduce-scatter.12
  185.4 69.6 reduce-scatter.8
  258.4 30.5 reduce-scatter.10
  295.2 818.2 reduce-scatter.14
where the time goes:
time: 1120 us
  waiting for transfers between devices  758 us (68%)
  blocking collectives  226 us (20%)
  matrix products  64.5 us (6%)
  starting transfers between devices  33.1 us (3%)
  local copies, waits for them, and re-layouts  16.5 us (1%)
  between operations  14.7 us (1%)
    unnamed x6, waiting for transfers between devices  749 us
    psum x1, blocking collectives, per_device(): aux_weight_grad = lax.psum(aux_part, ('gx', 'gy'))  156 us
    dot_general x54, matrix products, taps_back(): lax.dot_general(flat_source, shifted, (((0,), (0,)), ((), ())), preferred...  49.8 us
    all_gather x1, blocking collectives, per_device(): down_grad = lax.all_gather(relayed, 'gy', axis=1, tiled=True)  30.9 us
    ppermute x3, starting transfers between devices, extended_2(): before = lax.ppermute(last, axis, up)  22.5 us
  transfers between devices with their start and end apart: 11, of which 5 were waited for; matrix products, arithmetic and copies ran while one was open for 6% of the time, Pallas kernels for 0%

commit v1 on v0

v1 whole, which is shorter than its diff:
```python
import jax
import jax.numpy as jnp
from jax import lax
from jax.sharding import PartitionSpec as P

CLASSES = 14
TAPS = 27


def tap_offsets():
    return [
        (depth_step, height_step, width_step)
        for depth_step in (-1, 0, 1)
        for height_step in (-1, 0, 1)
        for width_step in (-1, 0, 1)
    ]


def shifted(padded, step, dims):
    starts = tuple(1 - s for s in step)
    return lax.slice(
        padded,
        starts + (0,),
        tuple(a + n for a, n in zip(starts, dims)) + (padded.shape[3],),
    ).reshape(-1, padded.shape[3])


def exchange(x, axis):
    return lax.all_to_all(x, axis, split_axis=0, concat_axis=0, tiled=False)


def spread(x, axis):
    size = lax.axis_size(axis)
    return exchange(jnp.broadcast_to(x[None], (size,) + x.shape), axis)


def neighbour(x, depth, height):
    nx, ny = lax.axis_size("gx"), lax.axis_size("gy")
    pairs = [
        (i * ny + j, (i + depth) * ny + j + height)
        for i in range(nx)
        for j in range(ny)
        if 0 <= i + depth < nx and 0 <= j + height < ny
    ]
    return lax.ppermute(x, ("gx", "gy"), pairs)


def with_halo(x):
    lines = []
    for depth in (1, 0, -1):
        part = {1: x[-1:], 0: x, -1: x[:1]}[depth]
        cells = []
        for height in (1, 0, -1):
            piece = {1: part[:, -1:], 0: part, -1: part[:, :1]}[height]
            cells.append(piece if depth == 0 and height == 0 else neighbour(piece, depth, height))
        lines.append(jnp.concatenate(cells, axis=1))
    return jnp.concatenate(lines, axis=0)


def dot_rows(a, b):
    return lax.dot_general(a, b, (((0,), (0,)), ((), ())), preferred_element_type=jnp.float32)


def dot_lanes(a, b):
    return lax.dot_general(a, b, (((1,), (1,)), ((), ())), preferred_element_type=jnp.float32)


def per_device(
    pre_bottom,
    bottom_input,
    bottom_weight,
    up_weight,
    level_input,
    pre_level,
    level_cotangent,
    labels,
    level_weight,
    aux_weight,
):
    nx, ny, nc = (lax.axis_size(a) for a in ("gx", "gy", "col"))
    depth, height, width, inner = level_input.shape
    full = inner * nc
    rows = depth * height * width
    bf16, f32 = jnp.bfloat16, jnp.float32

    ups = [(i, i + 1) for i in range(nc - 1)]
    downs = [(j, i) for i, j in ups]
    pre_before = lax.ppermute(pre_bottom[:, :, -1:], "col", ups)
    pre_after = lax.ppermute(pre_bottom[:, :, :1], "col", downs)
    pre_wide = lax.optimization_barrier(
        jnp.concatenate([pre_before, pre_bottom, pre_after], axis=2)
    )

    own_pre = pre_level.reshape(rows, inner)
    payload = jnp.concatenate(
        [own_pre, level_cotangent.reshape(rows, inner), jnp.pad(aux_weight.T, ((0, 2), (0, 0)))]
    )
    gathered = lax.all_gather(payload, "col")

    def channels(x):
        return x.transpose(1, 0, 2).reshape(x.shape[1], full)

    pre = channels(gathered[:, :rows])
    cotangent = channels(gathered[:, rows : 2 * rows])
    aux = channels(gathered[:, 2 * rows : 2 * rows + CLASSES])
    logits = dot_lanes(jnp.maximum(pre, 0), aux)
    probabilities = jax.nn.softmax(logits, axis=-1)
    onehot = (labels.reshape(-1)[:, None] == jnp.arange(CLASSES, dtype=jnp.int32)[None, :]).astype(f32)
    logit_grad = (probabilities - onehot).astype(bf16)
    aux_back = lax.dot_general(
        logit_grad, aux, (((1,), (0,)), ((), ())), preferred_element_type=f32
    )
    total_grad = cotangent.astype(f32) + aux_back
    level_pre_grad = (
        jnp.where(pre > 0, total_grad, 0.0).astype(bf16).reshape(depth, height, width, full)
    )
    aux_part = dot_rows(logit_grad, jnp.maximum(own_pre, 0)).astype(bf16)

    extended = jnp.pad(with_halo(level_pre_grad), ((0, 0), (0, 0), (1, 1), (0, 0)))
    skip_grad = jnp.zeros((rows, inner), f32)
    for tap, step in enumerate(tap_offsets()):
        piece = shifted(extended, step, (depth, height, width))
        skip_grad = skip_grad + dot_lanes(piece, level_weight[:, tap * full : (tap + 1) * full])
    level_input_grad = skip_grad.astype(bf16).reshape(level_input.shape)

    half_d, half_h, half_w = depth // 2, height // 2, width // 2
    down_local = (
        skip_grad.reshape(half_d, 2, half_h, 2, half_w, 2, inner).sum(axis=(1, 3, 5)).astype(bf16)
    )
    block = half_w // nc
    wide = block + 2
    down_padded = jnp.pad(down_local, ((0, 0), (0, 0), (1, 1), (0, 0)))
    cells = half_d * half_h * wide
    parts = jnp.stack(
        [down_padded[:, :, c * block : c * block + wide].reshape(cells, inner) for c in range(nc)]
    )
    relayed = exchange(parts, "col").reshape(nc * cells, inner)

    flat_input = level_input.reshape(rows, inner)
    pieces = [
        dot_rows(shifted(extended, step, (depth, height, width)), flat_input).astype(bf16)
        for step in tap_offsets()
    ]
    chunk = TAPS * full // (nx * ny)
    level_part = jnp.concatenate(pieces).reshape(nx, ny, chunk, inner).transpose(1, 0, 2, 3)
    level_part = exchange(level_part, "gy").astype(f32).sum(axis=0).astype(bf16)

    tail = jnp.pad(aux_part, ((0, 2), (0, 0)))
    by_depth = spread(jnp.concatenate([relayed, tail]), "gx")
    aux_sum = by_depth[:, nc * cells :].astype(f32).sum(axis=0).astype(bf16)
    line = jnp.concatenate([by_depth[:, : nc * cells].reshape(-1, inner), aux_sum])
    by_height = spread(line, "gy")
    split = nx * nc * cells
    aux_weight_grad = by_height[:, split : split + CLASSES].astype(f32).sum(axis=0).T
    down_wide = (
        by_height[:, :split]
        .reshape(ny, nx, nc, half_d, half_h, wide, inner)
        .transpose(1, 3, 0, 4, 5, 2, 6)
        .reshape(nx * half_d, ny * half_h, wide, full)
    )

    level_part = exchange(level_part, "gx").astype(f32).sum(axis=0)
    level_weight_grad = level_part.T

    bottom_d, bottom_h = pre_bottom.shape[:2]
    filters = pre_bottom.shape[3]
    bottom_back = dot_lanes(down_wide.reshape(-1, full), up_weight).reshape(pre_wide.shape)
    bottom_pre_grad = jnp.where(pre_wide > 0, bottom_back, 0.0).astype(bf16)
    flat_down = down_wide[:, :, 1:-1].reshape(-1, full)
    up_part = dot_rows(jnp.maximum(pre_bottom, 0).reshape(-1, filters), flat_down).astype(bf16)
    padded = jnp.pad(bottom_pre_grad, ((1, 1), (1, 1), (0, 0), (0, 0)))
    bottom_rows = bottom_d * bottom_h * block
    channel_width = bottom_weight.shape[0]
    source = bottom_input.reshape(bottom_rows, channel_width)
    bottom_part = jnp.zeros((bottom_rows, channel_width), f32)
    weight_parts = []
    for tap, step in enumerate(tap_offsets()):
        piece = shifted(padded, step, (bottom_d, bottom_h, block))
        bottom_part = bottom_part + dot_lanes(piece, bottom_weight[:, tap])
        weight_parts.append(dot_rows(source, piece).astype(bf16))

    share = bottom_d // ny
    bottom_part = exchange(
        bottom_part.astype(bf16).reshape(ny, share * bottom_h * block, channel_width), "gy"
    )
    bottom_input_grad = (
        bottom_part.astype(f32).sum(axis=0).astype(bf16).reshape(share, bottom_h, block, channel_width)
    )
    thin = channel_width // nc
    weight_parts = (
        jnp.stack(weight_parts)
        .reshape(TAPS, nc, thin, filters)
        .transpose(1, 0, 2, 3)
        .reshape(nc, TAPS * thin, filters)
    )
    up_parts = up_part.reshape(filters, nc, inner).transpose(1, 0, 2)
    both = exchange(jnp.concatenate([weight_parts, up_parts], axis=1), "col").astype(f32).sum(axis=0)
    bottom_weight_grad = both[: TAPS * thin].reshape(TAPS, thin, filters).transpose(1, 0, 2)
    up_weight_grad = both[TAPS * thin :]
    return (
        level_input_grad,
        bottom_input_grad,
        level_weight_grad,
        bottom_weight_grad,
        up_weight_grad,
        aux_weight_grad,
    )


def solution(mesh):
    return jax.shard_map(
        per_device,
        mesh=mesh,
        in_specs=(
            P(None, None, "col", "gy"),
            P(None, None, "col", "gx"),
            P("gx", None, "gy"),
            P("gy", None),
            P("gx", "gy", None, "col"),
            P("gx", "gy", None, "col"),
            P("gx", "gy", None, "col"),
            P("gx", "gy", None),
            P("col", None),
            P("col", None),
        ),
        out_specs=(
            P("gx", "gy", None, "col"),
            P("gy", None, "col", "gx"),
            P("col", ("gx", "gy")),
            P(("gx", "col"), None, "gy"),
            P("gy", "col"),
            P("col", None),
        ),
        check_vma=False,
    )
```

time: 1120 us -> 247 us (0.22)
  waiting for transfers between devices: 758 us -> 91.6 us
  blocking collectives: 226 us -> 9.63 us
  starting transfers between devices: 33.1 us -> 67.9 us
  matrix products: 64.5 us -> 51.7 us
  between operations: 14.7 us -> 2.21 us
    unnamed x6 -> x0, waiting for transfers between devices: 749 us -> none
    psum x2 -> x0, blocking collectives: 167 us -> none  [the longest x1 156 us: per_device(): aux_weight_grad = lax.psum(aux_part, ('gx', 'gy'))]
    all_to_all x1 -> x7, waiting for transfers between devices: 0.01 us -> 78.6 us  [exchange(): return lax.all_to_all(x, axis, split_axis=0, concat_axis=0, tiled=False)]
    all_gather x3 -> x1, blocking collectives: 59.6 us -> 9.63 us  [per_device(): gathered = lax.all_gather(payload, 'col')]
    all_to_all x1 -> x7, starting transfers between devices: 5.73 us -> 43.3 us  [exchange(): return lax.all_to_all(x, axis, split_axis=0, concat_axis=0, tiled=False)]
    dot_general x113, matrix products: 64.5 us -> 51.7 us  [the longest x56 38.5 us: dot_rows(): lax.dot_general(a, b, (((0,), (0,)), ((), ())), preferred_element_type=jn...]
    ppermute x6 -> x10, starting transfers between devices: 27.1 us -> 24.5 us  [the longest x8 19.9 us: neighbour(): return lax.ppermute(x, ('gx', 'gy'), pairs)]
  transfers between devices with their start and end apart: 11 -> 17, of which waited for: 5 -> 10; matrix products, arithmetic and copies ran while one was open for 6% -> 16% of each run, Pallas kernels for 0% -> 0%
where the time goes in v1:
time: 247 us; the launch traced here: 246 us
  waiting for transfers between devices  91.6 us (37%)
  starting transfers between devices  67.9 us (27%)
  matrix products  51.7 us (21%)
  local copies, waits for them, and re-layouts  14.3 us (6%)
  blocking collectives  9.63 us (4%)
  other arithmetic  9.14 us (4%)
    all_to_all x7, waiting for transfers between devices, exchange(): return lax.all_to_all(x, axis, split_axis=0, concat_axis=0, tiled=False)  78.6 us
    all_to_all x7, starting transfers between devices, exchange(): return lax.all_to_all(x, axis, split_axis=0, concat_axis=0, tiled=False)  43.3 us
    dot_general x56, matrix products, dot_rows(): lax.dot_general(a, b, (((0,), (0,)), ((), ())), preferred_element_type=jn...  38.5 us
    ppermute x8, starting transfers between devices, neighbour(): return lax.ppermute(x, ('gx', 'gy'), pairs)  19.9 us
    dot_general x56, matrix products, dot_lanes(): lax.dot_general(a, b, (((1,), (1,)), ((), ())), preferred_element_type=jn...  12.9 us
    ppermute x8, waiting for transfers between devices, neighbour(): return lax.ppermute(x, ('gx', 'gy'), pairs)  10.6 us
    all_gather x1, blocking collectives, per_device(): gathered = lax.all_gather(payload, 'col')  9.63 us
  transfers between devices with their start and end apart: 17, of which 10 were waited for; matrix products, arithmetic and copies ran while one was open for 16% of the time, Pallas kernels for 0%

profile of v1, /device:TPU:1, one launch (start us, length us, event | category | flops | bytes accessed | tf_op | source)
XLA Modules:
  0.0 246.4 jit_solution(2848981495623724626)
XLA Ops:
  0.7 0.9 fusion.105
  1.6 9.6 %all-gather = bf16[2112,128]{1,0:T(8,128)(2,1)S(1)} all-gather(bf16[528,128]{1,0:T(8,128)(2,1)S(1)} %fusion.105), channel_id=2, replica_groups=mesh['gx'=8,'gy'=8,'col'=4] {'col'}, dimensions={0}, use_global_device_ids=true | all-gather | bytes 675840 | tf_op jit(solution)/shard_map/all_gather | solution.py:98
  12.9 2.5 %collective-permute-start.1 = (bf16[1,4,32,512]{3,2,1,0:T(8,128)(2,1)S(1)}, bf16[1,4,32,512]{3,2,1,0:T(8,128)(2,1)S(1)}, u32[]{:S(2)}, u32[]{:S(2)}) collective-permute-start(bf16[1,4,32,512]{3,2,1,0:T(8,128)(2,1)S(1)} %bitcast.889), channel_id=1, source_target_pairs={{0,32},{4,36},{8,40},{12,44},{16,48},{20,52},{24,56},{28,60},{32,6... | collective-permute-start | bytes 393224 | tf_op jit(solution)/shard_map/ppermute | solution.py:45
  15.4 5.7 %collective-permute-start = (bf16[1,1,32,512]{3,2,1,0:T(8,128)(2,1)S(1)}, bf16[1,1,32,512]{3,2,1,0:T(8,128)(2,1)S(1)}, u32[]{:S(2)}, u32[]{:S(2)}) collective-permute-start(bf16[1,1,32,512]{3,2,1,0:T(8,128)(2,1)S(1)} %get-tuple-element.68), channel_id=1, source_target_pairs={{0,36},{4,40},{8,44},{12,48},{16,52},{20,56},{24,60},{32,68},{36,7... | collective-permute-start | bytes 98312 | tf_op jit(solution)/shard_map/ppermute | solution.py:45
  21.2 1.3 collective-permute-start.6
  22.5 2.7 %collective-permute-start.8 = (bf16[8,16,1,128]{3,1,2,0:T(8,128)(2,1)S(1)}, bf16[8,16,1,128]{3,1,2,0:T(8,128)(2,1)S(1)}, u32[]{:S(2)}, u32[]{:S(2)}) collective-permute-start(bf16[8,16,1,128]{3,1,2,0:T(8,128)(2,1)S(1)} %get-tuple-element.65), channel_id=1, source_target_pairs={{0,1},{1,2},{2,3},{4,5},{5,6},{6,7},{8,9},{9,10},{10,11},{12,13},{... | collective-permute-start | bytes 98312 | tf_op jit(solution)/shard_map/ppermute | solution.py:88
  25.3 1.9 collective-permute-start.9
  28.1 2.4 collective-permute-done.9
  31.2 6.5 %collective-permute-start.3 = (bf16[2,1,32,512]{3,2,1,0:T(8,128)(2,1)S(1)}, bf16[2,1,32,512]{3,2,1,0:T(8,128)(2,1)S(1)}, u32[]{:S(2)}, u32[]{:S(2)}) collective-permute-start(bf16[2,1,32,512]{3,2,1,0:T(8,128)(2,1)S(1)} %get-tuple-element.34), channel_id=1, source_target_pairs={{0,4},{4,8},{8,12},{12,16},{16,20},{20,24},{24,28},{32,36},{36,40}... | collective-permute-start | bytes 196616 | tf_op jit(solution)/shard_map/ppermute | solution.py:45
  37.7 1.3 collective-permute-start.4
  39.5 1.3 collective-permute-start.7
  40.8 4.8 %collective-permute-done.4 = bf16[2,1,32,512]{3,2,1,0:T(8,128)(2,1)S(1)} collective-permute-done((bf16[2,1,32,512]{3,2,1,0:T(8,128)(2,1)S(1)}, bf16[2,1,32,512]{3,2,1,0:T(8,128)(2,1)S(1)}, u32[]{:S(2)}, u32[]{:S(2)}) %collective-permute-start.4) | collective-permute-done | bytes 65568 | tf_op jit(solution)/shard_map/ppermute | solution.py:45
  45.7 5.2 %collective-permute-done.7 = bf16[1,1,32,512]{3,2,1,0:T(8,128)(2,1)S(1)} collective-permute-done((bf16[1,1,32,512]{3,2,1,0:T(8,128)(2,1)S(1)}, bf16[1,1,32,512]{3,2,1,0:T(8,128)(2,1)S(1)}, u32[]{:S(2)}, u32[]{:S(2)}) %collective-permute-start.7) | collective-permute-done | bytes 32800 | tf_op jit(solution)/shard_map/ppermute | solution.py:45
  52.2 1.3 copy-done.1
  61.4 4.9 %all-to-all-start = ((bf16[4,12,128]{2,1,0:T(8,128)(2,1)}), bf16[4,12,128]{2,1,0:T(8,128)(2,1)S(1)}, u32[]{:S(2)}, u32[]{:S(2)}) async-start(bf16[4,12,128]{2,1,0:T(8,128)(2,1)} %pad_maximum_fusion.6), calls=%async_computation | async-start | bytes 32768 | tf_op jit(solution)/shard_map/all_to_all | solution.py:29
  66.4 0.9 fusion.41
  69.2 0.9 fusion.39
  70.1 0.9 fusion.50
  71.0 0.9 fusion.38
  72.0 0.9 fusion.37
  72.9 0.9 fusion.52
  74.8 0.9 fusion.35
  75.7 0.9 fusion.43
  76.6 0.9 fusion.34
  77.6 1.0 fusion.33
  78.5 0.9 fusion.32
  79.4 0.9 fusion.31
  80.4 0.9 fusion.30
  81.3 0.9 fusion.45
  83.2 0.9 fusion.28
  86.6 8.9 %all-to-all-start.1 = ((bf16[8,64,128]{2,1,0:T(8,128)(2,1)}), bf16[8,64,128]{2,1,0:T(8,128)(2,1)S(1)}, u32[]{:S(2)}, u32[]{:S(2)}) async-start(bf16[8,64,128]{2,1,0:T(8,128)(2,1)} %broadcast_in_dim.12), calls=%async_computation.1 | async-start | bytes 262144 | tf_op jit(solution)/shard_map/all_to_all | solution.py:29
  95.5 0.9 fusion.26
  97.4 6.7 %all-to-all-done.1 = bf16[8,64,128]{2,1,0:T(8,128)(2,1)S(1)} async-done(((bf16[8,64,128]{2,1,0:T(8,128)(2,1)}), bf16[8,64,128]{2,1,0:T(8,128)(2,1)S(1)}, u32[]{:S(2)}, u32[]{:S(2)}) %all-to-all-start.1) | async-done | bytes 131104 | tf_op jit(solution)/shard_map/all_to_all | solution.py:29
  104.1 1.0 broadcast_in_dim.13
  105.1 9.7 %all-to-all-start.2 = ((bf16[8,400,128]{2,1,0:T(8,128)(2,1)}), bf16[8,400,128]{2,1,0:T(8,128)(2,1)S(1)}, u32[]{:S(2)}, u32[]{:S(2)}) async-start(bf16[8,400,128]{2,1,0:T(8,128)(2,1)} %broadcast_in_dim.13), calls=%async_computation.2 | async-start | bytes 1638400 | tf_op jit(solution)/shard_map/all_to_all | solution.py:29
  115.8 0.9 fusion.24
  118.5 4.1 %copy.445 = bf16[8,8,216,128]{3,2,0,1:T(8,128)(2,1)} copy(bf16[8,8,216,128]{3,2,1,0:T(8,128)(2,1)} %bitcast.158) | data formatting | bytes 7077888 | tf_op jit(solution)/shard_map/reshape | solution.py:145
  122.6 5.2 %all-to-all-done.2 = bf16[8,400,128]{2,1,0:T(8,128)(2,1)S(1)} async-done(((bf16[8,400,128]{2,1,0:T(8,128)(2,1)}), bf16[8,400,128]{2,1,0:T(8,128)(2,1)S(1)}, u32[]{:S(2)}, u32[]{:S(2)}) %all-to-all-start.2) | async-done | bytes 819232 | tf_op jit(solution)/shard_map/all_to_all | solution.py:29
  149.5 3.4 %all-to-all-start.3 = ((bf16[8,64,128]{2,1,0:T(8,128)(2,1)}), bf16[8,64,128]{2,1,0:T(8,128)(2,1)S(1)}, u32[]{:S(2)}, u32[]{:S(2)}) async-start(bf16[8,64,128]{2,1,0:T(8,128)(2,1)} %bitcast.102), calls=%async_computation.3 | async-start | bytes 262144 | tf_op jit(solution)/shard_map/all_to_all | solution.py:29
  153.2 6.7 %all-to-all-done.3 = bf16[8,64,128]{2,1,0:T(8,128)(2,1)S(1)} async-done(((bf16[8,64,128]{2,1,0:T(8,128)(2,1)}), bf16[8,64,128]{2,1,0:T(8,128)(2,1)S(1)}, u32[]{:S(2)}, u32[]{:S(2)}) %all-to-all-start.3) | async-done | bytes 131104 | tf_op jit(solution)/shard_map/all_to_all | solution.py:29
  159.8 4.6 %all-to-all-start.4 = ((bf16[8,8,216,128]{3,2,1,0:T(8,128)(2,1)}), bf16[8,8,216,128]{3,2,1,0:T(8,128)(2,1)}, u32[]{:S(2)}, u32[]{:S(2)}) async-start(bf16[8,8,216,128]{3,2,1,0:T(8,128)(2,1)} %bitcast.808), calls=%async_computation.4 | async-start | bytes 7077888 | tf_op jit(solution)/shard_map/all_to_all | solution.py:29
  166.6 1.1 pad_maximum_fusion
  167.6 36.9 %all-to-all-done.4 = bf16[8,8,216,128]{3,2,1,0:T(8,128)(2,1)} async-done(((bf16[8,8,216,128]{3,2,1,0:T(8,128)(2,1)}), bf16[8,8,216,128]{3,2,1,0:T(8,128)(2,1)}, u32[]{:S(2)}, u32[]{:S(2)}) %all-to-all-start.4) | async-done | bytes 3538976 | tf_op jit(solution)/shard_map/all_to_all | solution.py:29
  204.5 8.3 %all-to-all-start.6 = ((bf16[4,992,128]{2,1,0:T(8,128)(2,1)}), bf16[4,992,128]{2,1,0:T(8,128)(2,1)S(1)}, u32[]{:S(2)}, u32[]{:S(2)}) async-start(bf16[4,992,128]{2,1,0:T(8,128)(2,1)} %pad_maximum_fusion), calls=%async_computation.6 | async-start | bytes 2031616 | tf_op jit(solution)/shard_map/all_to_all | solution.py:29
  212.9 3.4 %reduce_sum.85 = bf16[8,216,128]{2,1,0:T(8,128)(2,1)} reduce(bf16[8,8,216,128]{3,2,1,0:T(8,128)(2,1)} %all-to-all-done.4, bf16[]{:T(256)} %constant.4.clone.1), dimensions={0}, to_apply=%region_5.6 | reduce | flops 1548288 | bytes 3981314 | tf_op jit(solution)/shard_map/reduce_sum | solution.py:146
  216.2 9.9 %all-to-all-done.6 = bf16[4,992,128]{2,1,0:T(8,128)(2,1)S(1)} async-done(((bf16[4,992,128]{2,1,0:T(8,128)(2,1)}), bf16[4,992,128]{2,1,0:T(8,128)(2,1)S(1)}, u32[]{:S(2)}, u32[]{:S(2)}) %all-to-all-start.6) | async-done | bytes 1015840 | tf_op jit(solution)/shard_map/all_to_all | solution.py:29
  226.1 3.5 %all-to-all-start.5 = ((bf16[8,216,128]{2,1,0:T(8,128)(2,1)}), bf16[8,216,128]{2,1,0:T(8,128)(2,1)S(1)}, u32[]{:S(2)}, u32[]{:S(2)}) async-start(bf16[8,216,128]{2,1,0:T(8,128)(2,1)} %reduce_sum.85), calls=%async_computation.5 | async-start | bytes 884736 | tf_op jit(solution)/shard_map/all_to_all | solution.py:29
  232.4 13.3 %all-to-all-done.5 = bf16[8,216,128]{2,1,0:T(8,128)(2,1)S(1)} async-done(((bf16[8,216,128]{2,1,0:T(8,128)(2,1)}), bf16[8,216,128]{2,1,0:T(8,128)(2,1)S(1)}, u32[]{:S(2)}, u32[]{:S(2)}) %all-to-all-start.5) | async-done | bytes 442400 | tf_op jit(solution)/shard_map/all_to_all | solution.py:29
  (255 shorter events, 49.3 us)
Async XLA Ops:
  0.6 129.0 %copy-start = (bf16[8,16,4,128]{3,2,1,0:T(4,128)(2,1)S(1)}, bf16[8,16,4,128]{3,2,1,0:T(4,128)(2,1)}, u32[]{:S(2)}) copy-start(bf16[8,16,4,128]{3,2,1,0:T(4,128)(2,1)} %param.11) | copy-start | bytes 393220
  0.6 11.8 %copy-start.17 = (s32[2,4,32]{2,1,0:T(4,128)S(1)}, s32[2,4,32]{2,1,0:T(4,128)}, u32[]{:S(2)}) copy-start(s32[2,4,32]{2,1,0:T(4,128)} %param.17) | copy-start | bytes 3076
  0.7 21.8 %copy-start.3 = (bf16[8,16,4,128]{3,2,1,0:T(4,128)(2,1)S(1)}, bf16[8,16,4,128]{3,2,1,0:T(4,128)(2,1)}, u32[]{:S(2)}) copy-start(bf16[8,16,4,128]{3,2,1,0:T(4,128)(2,1)} %param.10) | copy-start | bytes 393220
  11.3 16.0 %copy-start.5 = (bf16[2,4,32,128]{3,2,1,0:T(8,128)(2,1)S(1)}, bf16[2,4,32,128]{3,2,1,0:T(8,128)(2,1)}, u32[]{:S(2)}) copy-start(bf16[2,4,32,128]{3,2,1,0:T(8,128)(2,1)} %param.15) | copy-start | bytes 196612
  12.9 32.7 %collective-permute-start.1 = (bf16[1,4,32,512]{3,2,1,0:T(8,128)(2,1)S(1)}, bf16[1,4,32,512]{3,2,1,0:T(8,128)(2,1)S(1)}, u32[]{:S(2)}, u32[]{:S(2)}) collective-permute-start(bf16[1,4,32,512]{3,2,1,0:T(8,128)(2,1)S(1)} %bitcast.889), channel_id=1, source_target_pairs={{0,32},{4,36},{8,40},{12,44},{16,48},{20,52},{24,56},{28,60},{32,6... | collective-permute-start | bytes 393224 | tf_op jit(solution)/shard_map/ppermute | solution.py:45
  15.4 15.7 %collective-permute-start = (bf16[1,1,32,512]{3,2,1,0:T(8,128)(2,1)S(1)}, bf16[1,1,32,512]{3,2,1,0:T(8,128)(2,1)S(1)}, u32[]{:S(2)}, u32[]{:S(2)}) collective-permute-start(bf16[1,1,32,512]{3,2,1,0:T(8,128)(2,1)S(1)} %get-tuple-element.68), channel_id=1, source_target_pairs={{0,36},{4,40},{8,44},{12,48},{16,52},{20,56},{24,60},{32,68},{36,7... | collective-permute-start | bytes 98312 | tf_op jit(solution)/shard_map/ppermute | solution.py:45
  21.2 24.5 %collective-permute-start.6 = (bf16[1,4,32,512]{3,2,1,0:T(8,128)(2,1)S(1)}, bf16[1,4,32,512]{3,2,1,0:T(8,128)(2,1)S(1)}, u32[]{:S(2)}, u32[]{:S(2)}) collective-permute-start(bf16[1,4,32,512]{3,2,1,0:T(8,128)(2,1)S(1)} %bitcast.887), channel_id=1, source_target_pairs={{32,0},{36,4},{40,8},{44,12},{48,16},{52,20},{56,24},{60,28},{64,3... | collective-permute-start | bytes 393224 | tf_op jit(solution)/shard_map/ppermute | solution.py:45
  22.5 4.9 %collective-permute-start.8 = (bf16[8,16,1,128]{3,1,2,0:T(8,128)(2,1)S(1)}, bf16[8,16,1,128]{3,1,2,0:T(8,128)(2,1)S(1)}, u32[]{:S(2)}, u32[]{:S(2)}) collective-permute-start(bf16[8,16,1,128]{3,1,2,0:T(8,128)(2,1)S(1)} %get-tuple-element.65), channel_id=1, source_target_pairs={{0,1},{1,2},{2,3},{4,5},{5,6},{6,7},{8,9},{9,10},{10,11},{12,13},{... | collective-permute-start | bytes 98312 | tf_op jit(solution)/shard_map/ppermute | solution.py:88
  25.3 5.2 %collective-permute-start.9 = (bf16[8,16,1,128]{3,1,2,0:T(8,128)(2,1)S(1)}, bf16[8,16,1,128]{3,1,2,0:T(8,128)(2,1)S(1)}, u32[]{:S(2)}, u32[]{:S(2)}) collective-permute-start(bf16[8,16,1,128]{3,1,2,0:T(8,128)(2,1)S(1)} %get-tuple-element.66), channel_id=1, source_target_pairs={{1,0},{2,1},{3,2},{5,4},{6,5},{7,6},{9,8},{10,9},{11,10},{13,12},{... | collective-permute-start | bytes 98312 | tf_op jit(solution)/shard_map/ppermute | solution.py:89
  27.4 18.3 %collective-permute-start.2 = (bf16[1,1,32,512]{3,2,1,0:T(8,128)(2,1)S(1)}, bf16[1,1,32,512]{3,2,1,0:T(8,128)(2,1)S(1)}, u32[]{:S(2)}, u32[]{:S(2)}) collective-permute-start(bf16[1,1,32,512]{3,2,1,0:T(8,128)(2,1)S(1)} %get-tuple-element.67), channel_id=1, source_target_pairs={{4,32},{8,36},{12,40},{16,44},{20,48},{24,52},{28,56},{36,64},{40,... | collective-permute-start | bytes 98312 | tf_op jit(solution)/shard_map/ppermute | solution.py:45
  30.5 7.2 %collective-permute-start.5 = (bf16[1,1,32,512]{3,2,1,0:T(8,128)(2,1)S(1)}, bf16[1,1,32,512]{3,2,1,0:T(8,128)(2,1)S(1)}, u32[]{:S(2)}, u32[]{:S(2)}) collective-permute-start(bf16[1,1,32,512]{3,2,1,0:T(8,128)(2,1)S(1)} %get-tuple-element.70), channel_id=1, source_target_pairs={{32,4},{36,8},{40,12},{44,16},{48,20},{52,24},{56,28},{64,36},{68,... | collective-permute-start | bytes 98312 | tf_op jit(solution)/shard_map/ppermute | solution.py:45
  31.2 8.4 %collective-permute-start.3 = (bf16[2,1,32,512]{3,2,1,0:T(8,128)(2,1)S(1)}, bf16[2,1,32,512]{3,2,1,0:T(8,128)(2,1)S(1)}, u32[]{:S(2)}, u32[]{:S(2)}) collective-permute-start(bf16[2,1,32,512]{3,2,1,0:T(8,128)(2,1)S(1)} %get-tuple-element.34), channel_id=1, source_target_pairs={{0,4},{4,8},{8,12},{12,16},{16,20},{20,24},{24,28},{32,36},{36,40}... | collective-permute-start | bytes 196616 | tf_op jit(solution)/shard_map/ppermute | solution.py:45
  37.7 7.9 %collective-permute-start.4 = (bf16[2,1,32,512]{3,2,1,0:T(8,128)(2,1)S(1)}, bf16[2,1,32,512]{3,2,1,0:T(8,128)(2,1)S(1)}, u32[]{:S(2)}, u32[]{:S(2)}) collective-permute-start(bf16[2,1,32,512]{3,2,1,0:T(8,128)(2,1)S(1)} %get-tuple-element.35), channel_id=1, source_target_pairs={{4,0},{8,4},{12,8},{16,12},{20,16},{24,20},{28,24},{36,32},{40,36}... | collective-permute-start | bytes 196616 | tf_op jit(solution)/shard_map/ppermute | solution.py:45
  39.5 11.4 %collective-permute-start.7 = (bf16[1,1,32,512]{3,2,1,0:T(8,128)(2,1)S(1)}, bf16[1,1,32,512]{3,2,1,0:T(8,128)(2,1)S(1)}, u32[]{:S(2)}, u32[]{:S(2)}) collective-permute-start(bf16[1,1,32,512]{3,2,1,0:T(8,128)(2,1)S(1)} %get-tuple-element.69), channel_id=1, source_target_pairs={{36,0},{40,4},{44,8},{48,12},{52,16},{56,20},{60,24},{68,32},{72,3... | collective-permute-start | bytes 98312 | tf_op jit(solution)/shard_map/ppermute | solution.py:45
  51.4 2.0 copy-start.1
  57.8 8.6 %copy-start.18 = (bf16[2,4,32,128]{3,2,1,0:T(8,128)(2,1)S(1)}, bf16[2,4,32,128]{3,2,1,0:T(8,128)(2,1)}, u32[]{:S(2)}) copy-start(bf16[2,4,32,128]{3,2,1,0:T(8,128)(2,1)} %param.14) | copy-start | bytes 196612
  61.4 24.5 %all-to-all-start = ((bf16[4,12,128]{2,1,0:T(8,128)(2,1)}), bf16[4,12,128]{2,1,0:T(8,128)(2,1)S(1)}, u32[]{:S(2)}, u32[]{:S(2)}) async-start(bf16[4,12,128]{2,1,0:T(8,128)(2,1)} %pad_maximum_fusion.6), calls=%async_computation | async-start | bytes 32768 | tf_op jit(solution)/shard_map/all_to_all | solution.py:29
  86.6 17.4 %all-to-all-start.1 = ((bf16[8,64,128]{2,1,0:T(8,128)(2,1)}), bf16[8,64,128]{2,1,0:T(8,128)(2,1)S(1)}, u32[]{:S(2)}, u32[]{:S(2)}) async-start(bf16[8,64,128]{2,1,0:T(8,128)(2,1)} %broadcast_in_dim.12), calls=%async_computation.1 | async-start | bytes 262144 | tf_op jit(solution)/shard_map/all_to_all | solution.py:29
  105.1 22.7 %all-to-all-start.2 = ((bf16[8,400,128]{2,1,0:T(8,128)(2,1)}), bf16[8,400,128]{2,1,0:T(8,128)(2,1)S(1)}, u32[]{:S(2)}, u32[]{:S(2)}) async-start(bf16[8,400,128]{2,1,0:T(8,128)(2,1)} %broadcast_in_dim.13), calls=%async_computation.2 | async-start | bytes 1638400 | tf_op jit(solution)/shard_map/all_to_all | solution.py:29
  122.6 6.5 %copy-start.4 = (bf16[128,512]{1,0:T(8,128)(2,1)S(1)}, bf16[128,512]{1,0:T(8,128)(2,1)}, u32[]{:S(2)}) copy-start(bf16[128,512]{1,0:T(8,128)(2,1)} %param.13) | copy-start | bytes 393220
  141.9 1.6 copy-start.2
  146.8 6.1 %copy-start.16 = (bf16[128,128]{0,1:T(8,128)(2,1)S(1)}, bf16[128,128]{0,1:T(8,128)(2,1)}, u32[]{:S(2)}) copy-start(bf16[128,128]{0,1:T(8,128)(2,1)} %fusion.67) | copy-start | bytes 98308
  146.8 6.1 %copy-start.15 = (bf16[128,128]{0,1:T(8,128)(2,1)S(1)}, bf16[128,128]{0,1:T(8,128)(2,1)}, u32[]{:S(2)}) copy-start(bf16[128,128]{0,1:T(8,128)(2,1)} %fusion.68) | copy-start | bytes 98308
  147.0 5.9 %copy-start.14 = (bf16[128,128]{0,1:T(8,128)(2,1)S(1)}, bf16[128,128]{0,1:T(8,128)(2,1)}, u32[]{:S(2)}) copy-start(bf16[128,128]{0,1:T(8,128)(2,1)} %fusion.69) | copy-start | bytes 98308
  147.0 6.0 %copy-start.13 = (bf16[128,128]{0,1:T(8,128)(2,1)S(1)}, bf16[128,128]{0,1:T(8,128)(2,1)}, u32[]{:S(2)}) copy-start(bf16[128,128]{0,1:T(8,128)(2,1)} %fusion.70) | copy-start | bytes 98308
  147.1 6.0 %copy-start.12 = (bf16[128,128]{0,1:T(8,128)(2,1)S(1)}, bf16[128,128]{0,1:T(8,128)(2,1)}, u32[]{:S(2)}) copy-start(bf16[128,128]{0,1:T(8,128)(2,1)} %fusion.71) | copy-start | bytes 98308
  147.1 6.0 %copy-start.11 = (bf16[128,128]{0,1:T(8,128)(2,1)S(1)}, bf16[128,128]{0,1:T(8,128)(2,1)}, u32[]{:S(2)}) copy-start(bf16[128,128]{0,1:T(8,128)(2,1)} %fusion.72) | copy-start | bytes 98308
  147.1 6.0 %copy-start.10 = (bf16[128,128]{0,1:T(8,128)(2,1)S(1)}, bf16[128,128]{0,1:T(8,128)(2,1)}, u32[]{:S(2)}) copy-start(bf16[128,128]{0,1:T(8,128)(2,1)} %fusion.73) | copy-start | bytes 98308
  147.1 6.1 %copy-start.9 = (bf16[128,128]{0,1:T(8,128)(2,1)S(1)}, bf16[128,128]{0,1:T(8,128)(2,1)}, u32[]{:S(2)}) copy-start(bf16[128,128]{0,1:T(8,128)(2,1)} %fusion.74) | copy-start | bytes 98308
  149.5 10.4 %all-to-all-start.3 = ((bf16[8,64,128]{2,1,0:T(8,128)(2,1)}), bf16[8,64,128]{2,1,0:T(8,128)(2,1)S(1)}, u32[]{:S(2)}, u32[]{:S(2)}) async-start(bf16[8,64,128]{2,1,0:T(8,128)(2,1)} %bitcast.102), calls=%async_computation.3 | async-start | bytes 262144 | tf_op jit(solution)/shard_map/all_to_all | solution.py:29
  159.8 4.6 %copy-start.8 = (bf16[128,128]{0,1:T(8,128)(2,1)S(1)}, bf16[128,128]{0,1:T(8,128)(2,1)}, u32[]{:S(2)}) copy-start(bf16[128,128]{0,1:T(8,128)(2,1)} %fusion.75) | copy-start | bytes 98308
  159.8 4.7 %copy-start.7 = (bf16[128,128]{0,1:T(8,128)(2,1)S(1)}, bf16[128,128]{0,1:T(8,128)(2,1)}, u32[]{:S(2)}) copy-start(bf16[128,128]{0,1:T(8,128)(2,1)} %fusion.76) | copy-start | bytes 98308
  159.8 4.7 %copy-start.6 = (bf16[128,128]{0,1:T(8,128)(2,1)S(1)}, bf16[128,128]{0,1:T(8,128)(2,1)}, u32[]{:S(2)}) copy-start(bf16[128,128]{0,1:T(8,128)(2,1)} %fusion.77) | copy-start | bytes 98308
  159.8 44.7 %all-to-all-start.4 = ((bf16[8,8,216,128]{3,2,1,0:T(8,128)(2,1)}), bf16[8,8,216,128]{3,2,1,0:T(8,128)(2,1)}, u32[]{:S(2)}, u32[]{:S(2)}) async-start(bf16[8,8,216,128]{3,2,1,0:T(8,128)(2,1)} %bitcast.808), calls=%async_computation.4 | async-start | bytes 7077888 | tf_op jit(solution)/shard_map/all_to_all | solution.py:29
  204.5 21.6 %all-to-all-start.6 = ((bf16[4,992,128]{2,1,0:T(8,128)(2,1)}), bf16[4,992,128]{2,1,0:T(8,128)(2,1)S(1)}, u32[]{:S(2)}, u32[]{:S(2)}) async-start(bf16[4,992,128]{2,1,0:T(8,128)(2,1)} %pad_maximum_fusion), calls=%async_computation.6 | async-start | bytes 2031616 | tf_op jit(solution)/shard_map/all_to_all | solution.py:29
  226.1 19.6 %all-to-all-start.5 = ((bf16[8,216,128]{2,1,0:T(8,128)(2,1)}), bf16[8,216,128]{2,1,0:T(8,128)(2,1)S(1)}, u32[]{:S(2)}, u32[]{:S(2)}) async-start(bf16[8,216,128]{2,1,0:T(8,128)(2,1)} %reduce_sum.85), calls=%async_computation.5 | async-start | bytes 884736 | tf_op jit(solution)/shard_map/all_to_all | solution.py:29

commit v2 on v1

v2 whole, which is shorter than its diff:
```python
import functools

import jax
import jax.numpy as jnp
from jax import lax
from jax.experimental import pallas as pl
from jax.experimental.pallas import tpu as pltpu
from jax.sharding import PartitionSpec as P

CLASSES = 14
CLASS_ROWS = 16
TAPS = 27
VMEM_LIMIT = 48 * 1024 * 1024
STEPS = (-1, 0, 1)


def exchange(x, axis):
    return lax.all_to_all(x, axis, split_axis=0, concat_axis=0, tiled=False)


def spread(x, axis):
    size = lax.axis_size(axis)
    return exchange(jnp.broadcast_to(x[None], (size,) + x.shape), axis)


def neighbour(x, depth, height):
    nx, ny = lax.axis_size("gx"), lax.axis_size("gy")
    pairs = [
        (i * ny + j, (i + depth) * ny + j + height)
        for i in range(nx)
        for j in range(ny)
        if 0 <= i + depth < nx and 0 <= j + height < ny
    ]
    return lax.ppermute(x, ("gx", "gy"), pairs)


def dot_nn(a, b):
    return lax.dot_general(a, b, (((1,), (0,)), ((), ())), preferred_element_type=jnp.float32)


def dot_tn(a, b):
    return lax.dot_general(a, b, (((0,), (0,)), ((), ())), preferred_element_type=jnp.float32)


def dot_nt(a, b):
    return lax.dot_general(a, b, (((1,), (1,)), ((), ())), preferred_element_type=jnp.float32)


def moved(x, step, period):
    if step == 0:
        return x
    rows = x.shape[0]
    place = lax.rem(lax.broadcasted_iota(jnp.int32, x.shape, 0), period)
    edge = 0 if step == 1 else period - 1
    return jnp.where(place == edge, 0.0, pltpu.roll(x, step % rows, 0))


def local_call(body, out_shapes, scratch, flops, moved_bytes, *args):
    return pl.pallas_call(
        body,
        out_shape=out_shapes,
        in_specs=[pl.BlockSpec(memory_space=pltpu.VMEM)] * len(args),
        out_specs=jax.tree.map(lambda _: pl.BlockSpec(memory_space=pltpu.VMEM), out_shapes),
        scratch_shapes=scratch,
        cost_estimate=pl.CostEstimate(flops=flops, bytes_accessed=moved_bytes, transcendentals=0),
        compiler_params=pltpu.CompilerParams(vmem_limit_bytes=VMEM_LIMIT),
    )(*args)


def class_kernel(gathered_ref, own_ref, label_ref, grad_ref, aux_ref):
    groups, rows, inner = gathered_ref.shape[0], own_ref.shape[0], own_ref.shape[1]
    logits = jnp.zeros((CLASS_ROWS, rows), jnp.float32)
    for c in range(groups):
        weight = gathered_ref[c, 2 * rows : 2 * rows + CLASS_ROWS]
        logits += dot_nt(weight, jnp.maximum(gathered_ref[c, :rows], 0))
    place = lax.broadcasted_iota(jnp.int32, logits.shape, 0)
    real = place < CLASSES
    logits = jnp.where(real, logits, -jnp.inf)
    powers = jnp.exp(logits - jnp.max(logits, axis=0, keepdims=True))
    probabilities = powers / jnp.sum(powers, axis=0, keepdims=True)
    onehot = jnp.where(place == label_ref[...], 1.0, 0.0)
    logit_grad = jnp.where(real, probabilities - onehot, 0.0).astype(jnp.bfloat16)
    for c in range(groups):
        weight = gathered_ref[c, 2 * rows : 2 * rows + CLASS_ROWS]
        total = gathered_ref[c, rows : 2 * rows].astype(jnp.float32) + dot_tn(logit_grad, weight)
        active = gathered_ref[c, :rows].astype(jnp.float32) > 0
        grad_ref[:, c * inner : (c + 1) * inner] = jnp.where(active, total, 0.0).astype(jnp.bfloat16)
    aux_ref[...] = dot_nn(logit_grad, jnp.maximum(own_ref[...], 0)).astype(jnp.bfloat16)


def conv_kernel(grad_ref, weight_ref, low_ref, mid_ref, high_ref, acc_ref):
    _, far_d, far_h, width, inner = acc_ref.shape
    depth, height = far_d - 2, far_h - 2
    full = grad_ref.shape[1]
    acc_ref[...] = jnp.zeros_like(acc_ref)
    for a in STEPS:
        for b in STEPS:
            for c in STEPS:
                tap = 9 * (a + 1) + 3 * (b + 1) + c + 1
                term = dot_nt(grad_ref[...], weight_ref[:, tap * full : (tap + 1) * full])
                acc_ref[c + 1, 1 + a : 1 + a + depth, 1 + b : 1 + b + height] += term.reshape(
                    depth, height, width, inner
                )
    for d in range(far_d):
        lines = sum(
            moved(acc_ref[c + 1, d].reshape(far_h * width, inner), c, width) for c in STEPS
        ).reshape(far_h, width, inner)
        if d == 0:
            low_ref[...] = lines.astype(jnp.bfloat16)
        elif d == far_d - 1:
            high_ref[...] = lines.astype(jnp.bfloat16)
        else:
            mid_ref[d - 1] = lines


def kernel_grad_kernel(chunk, grad_ref, input_ref, out_ref, shift_ref):
    far_d, far_h, width, inner = input_ref.shape
    depth, height = far_d - 2, far_h - 2
    rows, full = grad_ref.shape
    by_height, by_depth, window, _ = out_ref.shape
    flat = input_ref[...].astype(jnp.float32).reshape(far_d * far_h * width, inner)
    for c in STEPS:
        shift_ref[c + 1] = moved(flat, -c, width).astype(jnp.bfloat16).reshape(input_ref.shape)
    turned = grad_ref[...].T
    for a in STEPS:
        for b in STEPS:
            piece = jnp.concatenate(
                [
                    shift_ref[c, 1 + a : 1 + a + depth, 1 + b : 1 + b + height].reshape(rows, inner)
                    for c in range(3)
                ],
                axis=1,
            )
            terms = dot_nn(turned, piece).astype(jnp.bfloat16)
            for c in range(3):
                first = (9 * (a + 1) + 3 * (b + 1) + c) * full
                for owner in range(by_depth * by_height):
                    start = owner * chunk // 16 * 16
                    low, high = max(start, first), min(start + window, first + full)
                    if low < high:
                        out_ref[owner % by_height, owner // by_height, low - start : high - start] = terms[
                            low - first : high - first, c * inner : (c + 1) * inner
                        ]


def bottom_kernel(
    down_ref, up_ref, pre_ref, source_ref, weight_ref, part_ref, both_ref, shift_ref
):
    _, far_d, far_w, height, filters = shift_ref.shape
    depth, width = far_d - 2, far_w - 2
    rows = depth * width * height
    channels = source_ref.shape[1]
    groups = both_ref.shape[0]
    thin = channels // groups
    full = down_ref.shape[1]
    inner = full // groups
    back = dot_nt(down_ref[...], up_ref[...])
    saved = pre_ref[...]
    grad = jnp.where(saved.astype(jnp.float32) > 0, back, 0.0)
    shift_ref[:, :1] = jnp.zeros((3, 1) + shift_ref.shape[2:], jnp.bfloat16)
    shift_ref[:, far_d - 1 :] = jnp.zeros((3, 1) + shift_ref.shape[2:], jnp.bfloat16)
    for b in STEPS:
        shift_ref[b + 1, 1 : 1 + depth] = (
            moved(grad, b, height).astype(jnp.bfloat16).reshape(depth, far_w, height, filters)
        )
    own_down = down_ref[...].reshape(depth, far_w, height, full)[:, 1 : 1 + width].reshape(rows, full)
    own_saved = saved.reshape(depth, far_w, height, filters)[:, 1 : 1 + width].reshape(rows, filters)
    up_part = dot_tn(jnp.maximum(own_saved, 0), own_down).astype(jnp.bfloat16)
    for cc in range(groups):
        both_ref[cc, TAPS * thin :] = up_part[:, cc * inner : (cc + 1) * inner]
    turned = source_ref[...].T
    total = jnp.zeros((rows, channels), jnp.float32)
    for a in STEPS:
        for b in STEPS:
            tap = 9 * (a + 1) + 3 * (b + 1)
            piece = jnp.concatenate(
                [
                    shift_ref[b + 1, 1 - a : 1 - a + depth, 1 - c : 1 - c + width].reshape(rows, filters)
                    for c in STEPS
                ],
                axis=1,
            )
            weight = jnp.concatenate([weight_ref[tap + c] for c in range(3)], axis=1)
            total += dot_nt(piece, weight)
            terms = dot_nn(turned, piece).astype(jnp.bfloat16)
            for c in range(3):
                for cc in range(groups):
                    both_ref[cc, (tap + c) * thin : (tap + c + 1) * thin] = terms[
                        cc * thin : (cc + 1) * thin, c * filters : (c + 1) * filters
                    ]
    part_ref[...] = total.astype(jnp.bfloat16)


def per_device(
    pre_bottom,
    bottom_input,
    bottom_weight,
    up_weight,
    level_input,
    pre_level,
    level_cotangent,
    labels,
    level_weight,
    aux_weight,
):
    nx, ny, nc = (lax.axis_size(a) for a in ("gx", "gy", "col"))
    depth, height, width, inner = level_input.shape
    full = inner * nc
    rows = depth * height * width
    far_d, far_h = depth + 2, height + 2
    bf16, f32 = jnp.bfloat16, jnp.float32
    struct = jax.ShapeDtypeStruct

    own_pre = pre_level.reshape(rows, inner)
    payload = jnp.concatenate(
        [
            own_pre,
            level_cotangent.reshape(rows, inner),
            jnp.pad(aux_weight.T, ((0, CLASS_ROWS - CLASSES), (0, 0))),
        ]
    )
    gathered = spread(payload, "col")

    lines = jnp.concatenate(
        [neighbour(level_input[-1:], 1, 0), level_input, neighbour(level_input[:1], -1, 0)], axis=0
    )
    input_far = jnp.concatenate(
        [neighbour(lines[:, -1:], 0, 1), lines, neighbour(lines[:, :1], 0, -1)], axis=1
    )

    turned_pre = pre_bottom.transpose(0, 2, 1, 3)
    ups = [(i, i + 1) for i in range(nc - 1)]
    downs = [(j, i) for i, j in ups]
    pre_wide = jnp.concatenate(
        [
            lax.ppermute(turned_pre[:, -1:], "col", ups),
            turned_pre,
            lax.ppermute(turned_pre[:, :1], "col", downs),
        ],
        axis=1,
    )

    level_pre_grad, aux_part = local_call(
        class_kernel,
        (struct((rows, full), bf16), struct((CLASS_ROWS, inner), bf16)),
        [],
        6 * rows * full * CLASS_ROWS,
        2 * gathered.size,
        gathered,
        own_pre,
        labels.reshape(1, rows),
    )

    low, mid, high = local_call(
        conv_kernel,
        (
            struct((far_h, width, inner), bf16),
            struct((depth, far_h, width, inner), f32),
            struct((far_h, width, inner), bf16),
        ),
        [pltpu.VMEM((3, far_d, far_h, width, inner), f32)],
        2 * rows * full * TAPS * inner,
        2 * level_weight.size,
        level_pre_grad,
        level_weight,
    )
    from_low = neighbour(high, 1, 0)
    from_high = neighbour(low, -1, 0)
    mid = jnp.concatenate([(mid[0] + from_low)[None], mid[1:-1], (mid[-1] + from_high)[None]], axis=0)
    before = neighbour(mid[:, -1].astype(bf16), 0, 1)
    after = neighbour(mid[:, 0].astype(bf16), 0, -1)

    chunk = TAPS * full // (nx * ny)
    window = chunk + 8 if chunk % 16 else chunk
    level_part = local_call(
        functools.partial(kernel_grad_kernel, chunk),
        struct((ny, nx, window, inner), bf16),
        [pltpu.VMEM((3, far_d, far_h, width, inner), bf16)],
        2 * rows * full * TAPS * inner,
        2 * nx * ny * window * inner,
        level_pre_grad,
        input_far,
    )
    level_part = exchange(level_part, "gy").astype(f32).sum(axis=0).astype(bf16)
    level_part = exchange(level_part, "gx").astype(f32).sum(axis=0)
    if window != chunk:
        odd = lax.rem(lax.axis_index("gy") + lax.axis_index("gx") * ny, 2)
        level_part = jnp.where(odd == 1, level_part[window - chunk :], level_part[:chunk])
    level_weight_grad = level_part.T

    skip_grad = jnp.concatenate(
        [
            (mid[:, 1] + before)[:, None],
            mid[:, 2 : far_h - 2],
            (mid[:, far_h - 2] + after)[:, None],
        ],
        axis=1,
    )
    level_input_grad = skip_grad.astype(bf16)

    half_d, half_h, half_w = depth // 2, height // 2, width // 2
    down_local = (
        skip_grad.reshape(half_d, 2, half_h, 2, half_w, 2, inner).sum(axis=(1, 3, 5)).astype(bf16)
    )
    block = half_w // nc
    wide = block + 2
    down_padded = jnp.pad(down_local, ((0, 0), (0, 0), (1, 1), (0, 0)))
    cells = half_d * half_h * wide
    parts = jnp.stack(
        [down_padded[:, :, c * block : c * block + wide].reshape(cells, inner) for c in range(nc)]
    )
    relayed = exchange(parts, "col").reshape(nc * cells, inner)

    by_depth = spread(jnp.concatenate([relayed, aux_part]), "gx")
    aux_sum = by_depth[:, nc * cells :].astype(f32).sum(axis=0).astype(bf16)
    line = jnp.concatenate([by_depth[:, : nc * cells].reshape(-1, inner), aux_sum])
    by_height = spread(line, "gy")
    split = nx * nc * cells
    aux_weight_grad = by_height[:, split : split + CLASSES].astype(f32).sum(axis=0).T
    bottom_d, bottom_h, _, filters = pre_bottom.shape
    down_wide = (
        by_height[:, :split]
        .reshape(ny, nx, nc, half_d, half_h, wide, inner)
        .transpose(1, 3, 5, 0, 4, 2, 6)
        .reshape(bottom_d * wide * bottom_h, full)
    )

    bottom_rows = bottom_d * block * bottom_h
    channel_width = bottom_weight.shape[0]
    thin = channel_width // nc
    part, both = local_call(
        bottom_kernel,
        (
            struct((bottom_rows, channel_width), bf16),
            struct((nc, TAPS * thin + filters, inner), bf16),
        ),
        [pltpu.VMEM((3, bottom_d + 2, wide, bottom_h, filters), bf16)],
        4 * bottom_rows * channel_width * TAPS * filters,
        2 * bottom_weight.size,
        down_wide,
        up_weight,
        pre_wide.reshape(-1, filters),
        bottom_input.transpose(0, 2, 1, 3).reshape(bottom_rows, channel_width),
        bottom_weight.transpose(1, 0, 2),
    )
    share = bottom_d // ny
    bottom_input_grad = (
        exchange(part.reshape(ny, bottom_rows // ny, channel_width), "gy")
        .astype(f32)
        .sum(axis=0)
        .astype(bf16)
        .reshape(share, block, bottom_h, channel_width)
        .transpose(0, 2, 1, 3)
    )
    both = exchange(both, "col").astype(f32).sum(axis=0)
    bottom_weight_grad = both[: TAPS * thin].reshape(TAPS, thin, filters).transpose(1, 0, 2)
    up_weight_grad = both[TAPS * thin :]
    return (
        level_input_grad,
        bottom_input_grad,
        level_weight_grad,
        bottom_weight_grad,
        up_weight_grad,
        aux_weight_grad,
    )


def solution(mesh):
    return jax.shard_map(
        per_device,
        mesh=mesh,
        in_specs=(
            P(None, None, "col", "gy"),
            P(None, None, "col", "gx"),
            P("gx", None, "gy"),
            P("gy", None),
            P("gx", "gy", None, "col"),
            P("gx", "gy", None, "col"),
            P("gx", "gy", None, "col"),
            P("gx", "gy", None),
            P("col", None),
            P("col", None),
        ),
        out_specs=(
            P("gx", "gy", None, "col"),
            P("gy", None, "col", "gx"),
            P("col", ("gx", "gy")),
            P(("gx", "col"), None, "gy"),
            P("gy", "col"),
            P("col", None),
        ),
        check_vma=False,
    )
```

time: 247 us -> 194 us (0.79)
  matrix products: 51.7 us -> 0 us
  blocking collectives: 9.63 us -> 57.8 us
  waiting for transfers between devices: 91.6 us -> 44.2 us
  Pallas kernels: 0 us -> 7.5 us
  starting transfers between devices: 67.9 us -> 64 us
  local copies, waits for them, and re-layouts: 14.3 us -> 11.4 us
    all_to_all x0 -> x2, blocking collectives: none -> 57.8 us  [exchange(): return lax.all_to_all(x, axis, split_axis=0, concat_axis=0, tiled=False)]
    dot_general x113 -> x0, matrix products: 51.7 us -> none  [the longest x56 38.5 us: dot_rows(): lax.dot_general(a, b, (((0,), (0,)), ((), ())), preferred_element_type=jn...]
    all_to_all x7 -> x6, waiting for transfers between devices: 78.6 us -> 35.8 us  [exchange(): return lax.all_to_all(x, axis, split_axis=0, concat_axis=0, tiled=False)]
    all_gather x1 -> x0, blocking collectives: 9.63 us -> none  [per_device(): gathered = lax.all_gather(payload, 'col')]
    pallas_call x0 -> x4, Pallas kernels: none -> 7.5 us  [local_call(): pl.pallas_call(body, out_shape=out_shapes, in_specs=[pl.BlockSpec(memory_...]
    all_to_all x7 -> x6, starting transfers between devices: 43.3 us -> 36.9 us  [exchange(): return lax.all_to_all(x, axis, split_axis=0, concat_axis=0, tiled=False)]
    unnamed x72 -> x21, local copies, waits for them, and re-layouts: 2.21 us -> 5.98 us
    reshape x2 -> x1, local copies, waits for them, and re-layouts: 4.08 us -> 0.77 us  [per_device(): labels.reshape(1, rows)]
  transfers between devices with their start and end apart: 17 -> 16, of which waited for: 10 -> 7; matrix products, arithmetic and copies ran while one was open for 16% -> 5% of each run, Pallas kernels for 0% -> 3%
where the time goes in v2:
time: 194 us; the launch traced here: 193 us
  starting transfers between devices  64 us (33%)
  blocking collectives  57.8 us (30%)
  waiting for transfers between devices  44.2 us (23%)
  local copies, waits for them, and re-layouts  11.4 us (6%)
  Pallas kernels  7.5 us (4%)
  other arithmetic  6.89 us (4%)
    all_to_all x2, blocking collectives, exchange(): return lax.all_to_all(x, axis, split_axis=0, concat_axis=0, tiled=False)  57.8 us
    all_to_all x6, starting transfers between devices, exchange(): return lax.all_to_all(x, axis, split_axis=0, concat_axis=0, tiled=False)  36.9 us
    all_to_all x6, waiting for transfers between devices, exchange(): return lax.all_to_all(x, axis, split_axis=0, concat_axis=0, tiled=False)  35.8 us
    ppermute x8, starting transfers between devices, neighbour(): return lax.ppermute(x, ('gx', 'gy'), pairs)  21.3 us
    ppermute x8, waiting for transfers between devices, neighbour(): return lax.ppermute(x, ('gx', 'gy'), pairs)  8.39 us
    pallas_call x4, Pallas kernels, local_call(): pl.pallas_call(body, out_shape=out_shapes, in_specs=[pl.BlockSpec(memory_...  7.5 us
    unnamed x21, local copies, waits for them, and re-layouts  5.98 us
  transfers between devices with their start and end apart: 16, of which 7 were waited for; matrix products, arithmetic and copies ran while one was open for 5% of the time, Pallas kernels for 3%

profile of v2, /device:TPU:1, one launch (start us, length us, event | category | flops | bytes accessed | tf_op | source)
XLA Modules:
  0.0 193.0 jit_solution(6183314531825295868)
XLA Ops:
  0.6 0.9 fusion.1
  1.5 0.9 broadcast_in_dim.14
  2.4 6.8 %all-to-all-start = ((bf16[4,528,128]{2,1,0:T(8,128)(2,1)}), bf16[4,528,128]{2,1,0:T(8,128)(2,1)S(1)}, u32[]{:S(2)}, u32[]{:S(2)}) async-start(bf16[4,528,128]{2,1,0:T(8,128)(2,1)} %broadcast_in_dim.14), calls=%async_computation | async-start | bytes 1081344 | tf_op jit(solution)/shard_map/all_to_all | solution.py:18
  9.2 0.8 reshape.67.label_ref
  10.0 7.4 %all-to-all-done.gathered_ref = bf16[4,528,128]{2,1,0:T(8,128)(2,1)S(1)} async-done(((bf16[4,528,128]{2,1,0:T(8,128)(2,1)}), bf16[4,528,128]{2,1,0:T(8,128)(2,1)S(1)}, u32[]{:S(2)}, u32[]{:S(2)}) %all-to-all-start) | async-done | bytes 540704 | tf_op jit(solution)/shard_map/all_to_all | solution.py:18
  17.4 0.8 copy-done.2
  18.2 0.6 shard_map.145
  18.8 2.0 %copy-done.1 = bf16[128,13824]{1,0:T(8,128)(2,1)S(1)} copy-done((bf16[128,13824]{1,0:T(8,128)(2,1)S(1)}, bf16[128,13824]{1,0:T(8,128)(2,1)}, u32[]{:S(2)}) %copy-start.1) | copy-done | bytes 3538968
  20.8 2.0 %shard_map.146 = (bf16[6,32,128]{2,1,0:T(8,128)(2,1)S(1)}, f32[2,6,32,128]{3,2,1,0:T(8,128)S(1)}, bf16[6,32,128]{2,1,0:T(8,128)(2,1)S(1)}) custom-call(bf16[256,512]{1,0:T(8,128)(2,1)S(1)} %get-tuple-element.13.grad_ref, bf16[128,13824]{1,0:T(8,128)(2,1)S(1)} %copy-done.1), custom_call_target="tpu_custom_call" | custom-call | flops 905969664 | bytes 3538944 | tf_op jit(solution)/shard_map/pallas_call | solution.py:59
  22.9 1.9 %collective-permute-start = (bf16[6,32,128]{2,1,0:T(8,128)(2,1)S(1)}, bf16[6,32,128]{2,1,0:T(8,128)(2,1)S(1)}, u32[]{:S(2)}, u32[]{:S(2)}) collective-permute-start(bf16[6,32,128]{2,1,0:T(8,128)(2,1)S(1)} %get-tuple-element.15), channel_id=1, source_target_pairs={{0,32},{4,36},{8,40},{12,44},{16,48},{20,52},{24,56},{28,60},{32,6... | collective-permute-start | bytes 147464 | tf_op jit(solution)/shard_map/ppermute | solution.py:34
  24.8 1.3 collective-permute-start.1
  26.1 3.7 %collective-permute-done.1 = bf16[6,32,128]{2,1,0:T(8,128)(2,1)S(1)} collective-permute-done((bf16[6,32,128]{2,1,0:T(8,128)(2,1)S(1)}, bf16[6,32,128]{2,1,0:T(8,128)(2,1)S(1)}, u32[]{:S(2)}, u32[]{:S(2)}) %collective-permute-start.1) | collective-permute-done | bytes 49184 | tf_op jit(solution)/shard_map/ppermute | solution.py:34
  29.9 4.7 %collective-permute-start.2 = (bf16[2,32,128]{2,1,0:T(8,128)(2,1)S(1)}, bf16[2,32,128]{2,1,0:T(8,128)(2,1)S(1)}, u32[]{:S(2)}, u32[]{:S(2)}) collective-permute-start(bf16[2,32,128]{2,1,0:T(8,128)(2,1)S(1)} %get-tuple-element.50), channel_id=1, source_target_pairs={{0,4},{4,8},{8,12},{12,16},{16,20},{20,24},{24,28},{32,36},{36,40}... | collective-permute-start | bytes 49160 | tf_op jit(solution)/shard_map/ppermute | solution.py:34
  34.5 1.3 collective-permute-start.3
  35.9 4.7 %collective-permute-done.3 = bf16[2,32,128]{2,1,0:T(8,128)(2,1)S(1)} collective-permute-done((bf16[2,32,128]{2,1,0:T(8,128)(2,1)S(1)}, bf16[2,32,128]{2,1,0:T(8,128)(2,1)S(1)}, u32[]{:S(2)}, u32[]{:S(2)}) %collective-permute-start.3) | collective-permute-done | bytes 16416 | tf_op jit(solution)/shard_map/ppermute | solution.py:34
  40.7 9.0 %all_to_all.40 = bf16[4,12,128]{2,1,0:T(8,128)(2,1)S(1)} all-to-all(bf16[4,12,128]{2,1,0:T(8,128)(2,1)S(1)} %pad_maximum_fusion.5), channel_id=1, replica_groups=mesh['gx'=8,'gy'=8,'col'=4] {'col'}, dimensions={0} | all-to-all | bytes 24576 | tf_op jit(solution)/shard_map/all_to_all | solution.py:18
  49.7 0.7 broadcast_in_dim.35
  50.4 8.0 %all-to-all-start.2 = ((bf16[8,64,128]{2,1,0:T(8,128)(2,1)}), bf16[8,64,128]{2,1,0:T(8,128)(2,1)S(1)}, u32[]{:S(2)}, u32[]{:S(2)}) async-start(bf16[8,64,128]{2,1,0:T(8,128)(2,1)} %broadcast_in_dim.35), calls=%async_computation.2 | async-start | bytes 262144 | tf_op jit(solution)/shard_map/all_to_all | solution.py:18
  58.5 1.3 collective-permute-start.7
  59.8 4.0 %collective-permute-start.6 = (bf16[1,4,32,128]{3,2,1,0:T(8,128)(2,1)S(1)}, bf16[1,4,32,128]{3,2,1,0:T(8,128)(2,1)S(1)}, u32[]{:S(2)}, u32[]{:S(2)}) collective-permute-start(bf16[1,4,32,128]{3,2,1,0:T(8,128)(2,1)S(1)} %get-tuple-element.53), channel_id=1, source_target_pairs={{0,32},{4,36},{8,40},{12,44},{16,48},{20,52},{24,56},{28,60},{32,6... | collective-permute-start | bytes 98312 | tf_op jit(solution)/shard_map/ppermute | solution.py:34
  63.8 2.5 %all-to-all-done.2 = bf16[8,64,128]{2,1,0:T(8,128)(2,1)S(1)} async-done(((bf16[8,64,128]{2,1,0:T(8,128)(2,1)}), bf16[8,64,128]{2,1,0:T(8,128)(2,1)S(1)}, u32[]{:S(2)}, u32[]{:S(2)}) %all-to-all-start.2) | async-done | bytes 131104 | tf_op jit(solution)/shard_map/all_to_all | solution.py:18
  66.3 1.0 broadcast_in_dim.36
  67.3 5.8 %all-to-all-start.3 = ((bf16[8,400,128]{2,1,0:T(8,128)(2,1)}), bf16[8,400,128]{2,1,0:T(8,128)(2,1)S(1)}, u32[]{:S(2)}, u32[]{:S(2)}) async-start(bf16[8,400,128]{2,1,0:T(8,128)(2,1)} %broadcast_in_dim.36), calls=%async_computation.3 | async-start | bytes 1638400 | tf_op jit(solution)/shard_map/all_to_all | solution.py:18
  73.1 3.6 %collective-permute-start.4 = (bf16[8,1,16,128]{3,1,2,0:T(2,128)(2,1)S(1)}, bf16[8,1,16,128]{3,1,2,0:T(2,128)(2,1)S(1)}, u32[]{:S(2)}, u32[]{:S(2)}) collective-permute-start(bf16[8,1,16,128]{3,1,2,0:T(2,128)(2,1)S(1)} %get-tuple-element.48), channel_id=1, source_target_pairs={{0,1},{1,2},{2,3},{4,5},{5,6},{6,7},{8,9},{9,10},{10,11},{12,13},{... | collective-permute-start | bytes 98312 | tf_op jit(solution)/shard_map/ppermute | solution.py:236
  76.7 2.2 %collective-permute-start.5 = (bf16[8,1,16,128]{3,1,2,0:T(2,128)(2,1)S(1)}, bf16[8,1,16,128]{3,1,2,0:T(2,128)(2,1)S(1)}, u32[]{:S(2)}, u32[]{:S(2)}) collective-permute-start(bf16[8,1,16,128]{3,1,2,0:T(2,128)(2,1)S(1)} %get-tuple-element.49), channel_id=1, source_target_pairs={{1,0},{2,1},{3,2},{5,4},{6,5},{7,6},{9,8},{10,9},{11,10},{13,12},{... | collective-permute-start | bytes 98312 | tf_op jit(solution)/shard_map/ppermute | solution.py:238
  79.1 5.6 %collective-permute-start.8 = (bf16[4,1,32,128]{3,2,1,0:T(8,128)(2,1)S(1)}, bf16[4,1,32,128]{3,2,1,0:T(8,128)(2,1)S(1)}, u32[]{:S(2)}, u32[]{:S(2)}) collective-permute-start(bf16[4,1,32,128]{3,2,1,0:T(8,128)(2,1)S(1)} %get-tuple-element.46), channel_id=1, source_target_pairs={{0,4},{4,8},{8,12},{12,16},{16,20},{20,24},{24,28},{32,36},{36,40}... | collective-permute-start | bytes 98312 | tf_op jit(solution)/shard_map/ppermute | solution.py:34
  84.7 1.3 collective-permute-start.9
  86.0 0.2 pad_maximum_fusion.1
  86.4 0.5 copy.59
  86.9 0.4 copy.54
  87.4 3.4 %shard_map.147 = (bf16[512,128]{1,0:T(8,128)(2,1)}, bf16[4,992,128]{2,1,0:T(8,128)(2,1)}) custom-call(bf16[768,512]{1,0:T(8,128)(2,1)S(1)} %bitcast.68, bf16[128,512]{1,0:T(8,128)(2,1)S(1)} %copy-done.4, bf16[768,128]{1,0:T(8,128)(2,1)S(1)} %bitcast.71, bf16[512,128]{1,0:T(8,128)(2,1)S(1)} %bitcast.72, bf16[27,128,128]{2,1,0:T(8,128)(2,1)S(1)} %bitcast.73), custom_call_target="tpu_custom_call" | custom-call | flops 905969664 | bytes 884736 | tf_op jit(solution)/shard_map/pallas_call | solution.py:59
  90.8 7.3 %all-to-all-start.4 = ((bf16[8,64,128]{2,1,0:T(8,128)(2,1)}), bf16[8,64,128]{2,1,0:T(8,128)(2,1)S(1)}, u32[]{:S(2)}, u32[]{:S(2)}) async-start(bf16[8,64,128]{2,1,0:T(8,128)(2,1)} %bitcast.25), calls=%async_computation.4 | async-start | bytes 262144 | tf_op jit(solution)/shard_map/all_to_all | solution.py:18
  98.2 1.5 shard_map.148
  99.7 1.8 copy-done
  101.5 4.2 %all-to-all-done.4 = bf16[8,64,128]{2,1,0:T(8,128)(2,1)S(1)} async-done(((bf16[8,64,128]{2,1,0:T(8,128)(2,1)}), bf16[8,64,128]{2,1,0:T(8,128)(2,1)S(1)}, u32[]{:S(2)}, u32[]{:S(2)}) %all-to-all-start.4) | async-done | bytes 131104 | tf_op jit(solution)/shard_map/all_to_all | solution.py:18
  105.8 48.8 %all_to_all.41 = bf16[8,8,224,128]{3,2,1,0:T(8,128)(2,1)} all-to-all(bf16[8,8,224,128]{3,2,1,0:T(8,128)(2,1)} %copy-done), channel_id=1, replica_groups=mesh['gx'=8,'gy'=8,'col'=4] {'gy'}, dimensions={0} | all-to-all | bytes 7340032 | tf_op jit(solution)/shard_map/all_to_all | solution.py:18
  154.5 5.4 %all-to-all-start.7 = ((bf16[4,992,128]{2,1,0:T(8,128)(2,1)}), bf16[4,992,128]{2,1,0:T(8,128)(2,1)S(1)}, u32[]{:S(2)}, u32[]{:S(2)}) async-start(bf16[4,992,128]{2,1,0:T(8,128)(2,1)} %get-tuple-element.19), calls=%async_computation.7 | async-start | bytes 2031616 | tf_op jit(solution)/shard_map/all_to_all | solution.py:18
  159.9 3.4 %reduce_sum.84 = bf16[8,224,128]{2,1,0:T(8,128)(2,1)} reduce(bf16[8,8,224,128]{3,2,1,0:T(8,128)(2,1)} %all_to_all.41, bf16[]{:T(256)} %constant.18.clone.1), dimensions={0}, to_apply=%region_4.5 | reduce | flops 1605632 | bytes 4128770 | tf_op jit(solution)/shard_map/reduce_sum | solution.py:284
  163.4 9.8 %all-to-all-done.7 = bf16[4,992,128]{2,1,0:T(8,128)(2,1)S(1)} async-done(((bf16[4,992,128]{2,1,0:T(8,128)(2,1)}), bf16[4,992,128]{2,1,0:T(8,128)(2,1)S(1)}, u32[]{:S(2)}, u32[]{:S(2)}) %all-to-all-start.7) | async-done | bytes 1015840 | tf_op jit(solution)/shard_map/all_to_all | solution.py:18
  173.2 3.6 %all-to-all-start.6 = ((bf16[8,224,128]{2,1,0:T(8,128)(2,1)}), bf16[8,224,128]{2,1,0:T(8,128)(2,1)S(1)}, u32[]{:S(2)}, u32[]{:S(2)}) async-start(bf16[8,224,128]{2,1,0:T(8,128)(2,1)} %reduce_sum.84), calls=%async_computation.6 | async-start | bytes 917504 | tf_op jit(solution)/shard_map/all_to_all | solution.py:18
  176.8 0.6 fusion.6
  177.4 0.6 convert_reduce_fusion.2
  178.1 0.6 copy.57
  178.7 0.1 convert_reduce_fusion
  178.8 0.6 slice.123
  179.5 0.8 slice.122
  180.3 12.0 %all-to-all-done.6 = bf16[8,224,128]{2,1,0:T(8,128)(2,1)S(1)} async-done(((bf16[8,224,128]{2,1,0:T(8,128)(2,1)}), bf16[8,224,128]{2,1,0:T(8,128)(2,1)S(1)}, u32[]{:S(2)}, u32[]{:S(2)}) %all-to-all-start.6) | async-done | bytes 458784 | tf_op jit(solution)/shard_map/all_to_all | solution.py:18
  192.3 0.7 fusion.2
  (53 shorter events, 0.8 us)
Async XLA Ops:
  2.4 56.0 %copy-start.6 = (bf16[2,4,32,128]{3,2,1,0:T(8,128)(2,1)S(1)}, bf16[2,4,32,128]{3,2,1,0:T(8,128)(2,1)}, u32[]{:S(2)}) copy-start(bf16[2,4,32,128]{3,2,1,0:T(8,128)(2,1)} %param.14) | copy-start | bytes 196612
  2.4 15.0 %all-to-all-start = ((bf16[4,528,128]{2,1,0:T(8,128)(2,1)}), bf16[4,528,128]{2,1,0:T(8,128)(2,1)S(1)}, u32[]{:S(2)}, u32[]{:S(2)}) async-start(bf16[4,528,128]{2,1,0:T(8,128)(2,1)} %broadcast_in_dim.14), calls=%async_computation | async-start | bytes 1081344 | tf_op jit(solution)/shard_map/all_to_all | solution.py:18
  17.4 0.8 copy-start.2
  18.8 2.0 %copy-start.1 = (bf16[128,13824]{1,0:T(8,128)(2,1)S(1)}, bf16[128,13824]{1,0:T(8,128)(2,1)}, u32[]{:S(2)}) copy-start(bf16[128,13824]{1,0:T(8,128)(2,1)} %weight_ref.1) | copy-start | bytes 10616836
  22.8 50.2 %copy-start.5 = (bf16[8,16,4,128]{3,2,1,0:T(4,128)(2,1)S(1)}, bf16[8,16,4,128]{3,2,1,0:T(4,128)(2,1)}, u32[]{:S(2)}) copy-start(bf16[8,16,4,128]{3,2,1,0:T(4,128)(2,1)} %param.10) | copy-start | bytes 393220
  22.8 56.1 %copy-start.7 = (bf16[8,16,4,128]{3,2,1,0:T(4,128)(2,1)S(1)}, bf16[8,16,4,128]{3,2,1,0:T(4,128)(2,1)}, u32[]{:S(2)}) copy-start(bf16[8,16,4,128]{3,2,1,0:T(4,128)(2,1)} %param.11) | copy-start | bytes 393220
  22.9 3.2 %collective-permute-start = (bf16[6,32,128]{2,1,0:T(8,128)(2,1)S(1)}, bf16[6,32,128]{2,1,0:T(8,128)(2,1)S(1)}, u32[]{:S(2)}, u32[]{:S(2)}) collective-permute-start(bf16[6,32,128]{2,1,0:T(8,128)(2,1)S(1)} %get-tuple-element.15), channel_id=1, source_target_pairs={{0,32},{4,36},{8,40},{12,44},{16,48},{20,52},{24,56},{28,60},{32,6... | collective-permute-start | bytes 147464 | tf_op jit(solution)/shard_map/ppermute | solution.py:34
  24.8 5.0 %collective-permute-start.1 = (bf16[6,32,128]{2,1,0:T(8,128)(2,1)S(1)}, bf16[6,32,128]{2,1,0:T(8,128)(2,1)S(1)}, u32[]{:S(2)}, u32[]{:S(2)}) collective-permute-start(bf16[6,32,128]{2,1,0:T(8,128)(2,1)S(1)} %get-tuple-element.16), channel_id=1, source_target_pairs={{32,0},{36,4},{40,8},{44,12},{48,16},{52,20},{56,24},{60,28},{64,3... | collective-permute-start | bytes 147464 | tf_op jit(solution)/shard_map/ppermute | solution.py:34
  29.9 6.0 %collective-permute-start.2 = (bf16[2,32,128]{2,1,0:T(8,128)(2,1)S(1)}, bf16[2,32,128]{2,1,0:T(8,128)(2,1)S(1)}, u32[]{:S(2)}, u32[]{:S(2)}) collective-permute-start(bf16[2,32,128]{2,1,0:T(8,128)(2,1)S(1)} %get-tuple-element.50), channel_id=1, source_target_pairs={{0,4},{4,8},{8,12},{12,16},{16,20},{20,24},{24,28},{32,36},{36,40}... | collective-permute-start | bytes 49160 | tf_op jit(solution)/shard_map/ppermute | solution.py:34
  34.5 6.0 %collective-permute-start.3 = (bf16[2,32,128]{2,1,0:T(8,128)(2,1)S(1)}, bf16[2,32,128]{2,1,0:T(8,128)(2,1)S(1)}, u32[]{:S(2)}, u32[]{:S(2)}) collective-permute-start(bf16[2,32,128]{2,1,0:T(8,128)(2,1)S(1)} %get-tuple-element.51), channel_id=1, source_target_pairs={{4,0},{8,4},{12,8},{16,12},{20,16},{24,20},{28,24},{36,32},{40,36}... | collective-permute-start | bytes 49160 | tf_op jit(solution)/shard_map/ppermute | solution.py:34
  50.4 15.8 %all-to-all-start.2 = ((bf16[8,64,128]{2,1,0:T(8,128)(2,1)}), bf16[8,64,128]{2,1,0:T(8,128)(2,1)S(1)}, u32[]{:S(2)}, u32[]{:S(2)}) async-start(bf16[8,64,128]{2,1,0:T(8,128)(2,1)} %broadcast_in_dim.35), calls=%async_computation.2 | async-start | bytes 262144 | tf_op jit(solution)/shard_map/all_to_all | solution.py:18
  58.5 20.6 %collective-permute-start.7 = (bf16[1,4,32,128]{3,2,1,0:T(8,128)(2,1)S(1)}, bf16[1,4,32,128]{3,2,1,0:T(8,128)(2,1)S(1)}, u32[]{:S(2)}, u32[]{:S(2)}) collective-permute-start(bf16[1,4,32,128]{3,2,1,0:T(8,128)(2,1)S(1)} %get-tuple-element.52), channel_id=1, source_target_pairs={{32,0},{36,4},{40,8},{44,12},{48,16},{52,20},{56,24},{60,28},{64,3... | collective-permute-start | bytes 98312 | tf_op jit(solution)/shard_map/ppermute | solution.py:34
  59.8 19.2 %collective-permute-start.6 = (bf16[1,4,32,128]{3,2,1,0:T(8,128)(2,1)S(1)}, bf16[1,4,32,128]{3,2,1,0:T(8,128)(2,1)S(1)}, u32[]{:S(2)}, u32[]{:S(2)}) collective-permute-start(bf16[1,4,32,128]{3,2,1,0:T(8,128)(2,1)S(1)} %get-tuple-element.53), channel_id=1, source_target_pairs={{0,32},{4,36},{8,40},{12,44},{16,48},{20,52},{24,56},{28,60},{32,6... | collective-permute-start | bytes 98312 | tf_op jit(solution)/shard_map/ppermute | solution.py:34
  67.3 19.0 %all-to-all-start.3 = ((bf16[8,400,128]{2,1,0:T(8,128)(2,1)}), bf16[8,400,128]{2,1,0:T(8,128)(2,1)S(1)}, u32[]{:S(2)}, u32[]{:S(2)}) async-start(bf16[8,400,128]{2,1,0:T(8,128)(2,1)} %broadcast_in_dim.36), calls=%async_computation.3 | async-start | bytes 1638400 | tf_op jit(solution)/shard_map/all_to_all | solution.py:18
  73.1 12.9 %collective-permute-start.4 = (bf16[8,1,16,128]{3,1,2,0:T(2,128)(2,1)S(1)}, bf16[8,1,16,128]{3,1,2,0:T(2,128)(2,1)S(1)}, u32[]{:S(2)}, u32[]{:S(2)}) collective-permute-start(bf16[8,1,16,128]{3,1,2,0:T(2,128)(2,1)S(1)} %get-tuple-element.48), channel_id=1, source_target_pairs={{0,1},{1,2},{2,3},{4,5},{5,6},{6,7},{8,9},{9,10},{10,11},{12,13},{... | collective-permute-start | bytes 98312 | tf_op jit(solution)/shard_map/ppermute | solution.py:236
  76.7 9.3 %collective-permute-start.5 = (bf16[8,1,16,128]{3,1,2,0:T(2,128)(2,1)S(1)}, bf16[8,1,16,128]{3,1,2,0:T(2,128)(2,1)S(1)}, u32[]{:S(2)}, u32[]{:S(2)}) collective-permute-start(bf16[8,1,16,128]{3,1,2,0:T(2,128)(2,1)S(1)} %get-tuple-element.49), channel_id=1, source_target_pairs={{1,0},{2,1},{3,2},{5,4},{6,5},{7,6},{9,8},{10,9},{11,10},{13,12},{... | collective-permute-start | bytes 98312 | tf_op jit(solution)/shard_map/ppermute | solution.py:238
  79.1 8.3 %copy-start.3 = (bf16[128,27,128]{2,0,1:T(8,128)(2,1)S(1)}, bf16[128,27,128]{2,0,1:T(8,128)(2,1)}, u32[]{:S(2)}) copy-start(bf16[128,27,128]{2,0,1:T(8,128)(2,1)} %param.12) | copy-start | bytes 2654212
  79.1 8.3 %copy-start.4 = (bf16[128,512]{1,0:T(8,128)(2,1)S(1)}, bf16[128,512]{1,0:T(8,128)(2,1)}, u32[]{:S(2)}) copy-start(bf16[128,512]{1,0:T(8,128)(2,1)} %up_ref.1) | copy-start | bytes 393220
  79.1 19.0 %collective-permute-start.8 = (bf16[4,1,32,128]{3,2,1,0:T(8,128)(2,1)S(1)}, bf16[4,1,32,128]{3,2,1,0:T(8,128)(2,1)S(1)}, u32[]{:S(2)}, u32[]{:S(2)}) collective-permute-start(bf16[4,1,32,128]{3,2,1,0:T(8,128)(2,1)S(1)} %get-tuple-element.46), channel_id=1, source_target_pairs={{0,4},{4,8},{8,12},{12,16},{16,20},{20,24},{24,28},{32,36},{36,40}... | collective-permute-start | bytes 98312 | tf_op jit(solution)/shard_map/ppermute | solution.py:34
  84.7 13.4 %collective-permute-start.9 = (bf16[4,1,32,128]{3,2,1,0:T(8,128)(2,1)S(1)}, bf16[4,1,32,128]{3,2,1,0:T(8,128)(2,1)S(1)}, u32[]{:S(2)}, u32[]{:S(2)}) collective-permute-start(bf16[4,1,32,128]{3,2,1,0:T(8,128)(2,1)S(1)} %get-tuple-element.47), channel_id=1, source_target_pairs={{4,0},{8,4},{12,8},{16,12},{20,16},{24,20},{28,24},{36,32},{40,36}... | collective-permute-start | bytes 98312 | tf_op jit(solution)/shard_map/ppermute | solution.py:34
  90.8 14.9 %all-to-all-start.4 = ((bf16[8,64,128]{2,1,0:T(8,128)(2,1)}), bf16[8,64,128]{2,1,0:T(8,128)(2,1)S(1)}, u32[]{:S(2)}, u32[]{:S(2)}) async-start(bf16[8,64,128]{2,1,0:T(8,128)(2,1)} %bitcast.25), calls=%async_computation.4 | async-start | bytes 262144 | tf_op jit(solution)/shard_map/all_to_all | solution.py:18
  99.7 1.8 copy-start
  154.5 18.6 %all-to-all-start.7 = ((bf16[4,992,128]{2,1,0:T(8,128)(2,1)}), bf16[4,992,128]{2,1,0:T(8,128)(2,1)S(1)}, u32[]{:S(2)}, u32[]{:S(2)}) async-start(bf16[4,992,128]{2,1,0:T(8,128)(2,1)} %get-tuple-element.19), calls=%async_computation.7 | async-start | bytes 2031616 | tf_op jit(solution)/shard_map/all_to_all | solution.py:18
  173.2 19.1 %all-to-all-start.6 = ((bf16[8,224,128]{2,1,0:T(8,128)(2,1)}), bf16[8,224,128]{2,1,0:T(8,128)(2,1)S(1)}, u32[]{:S(2)}, u32[]{:S(2)}) async-start(bf16[8,224,128]{2,1,0:T(8,128)(2,1)} %reduce_sum.84), calls=%async_computation.6 | async-start | bytes 917504 | tf_op jit(solution)/shard_map/all_to_all | solution.py:18

commit v3 on v2

v3 whole, which is shorter than its diff:
```python
import functools

import jax
import jax.numpy as jnp
from jax import lax
from jax.experimental import pallas as pl
from jax.experimental.pallas import tpu as pltpu
from jax.sharding import PartitionSpec as P

CLASSES = 14
CLASS_ROWS = 16
TAPS = 27
VMEM_LIMIT = 48 * 1024 * 1024
STEPS = (-1, 0, 1)


def exchange(x, axis):
    return lax.all_to_all(x, axis, split_axis=0, concat_axis=0, tiled=False)


def spread(x, axis):
    size = lax.axis_size(axis)
    return exchange(jnp.broadcast_to(x[None], (size,) + x.shape), axis)


def behind(x, *others):
    return lax.optimization_barrier((x,) + others)[0]


def neighbour(x, depth, height):
    nx, ny = lax.axis_size("gx"), lax.axis_size("gy")
    pairs = [
        (i * ny + j, (i + depth) * ny + j + height)
        for i in range(nx)
        for j in range(ny)
        if 0 <= i + depth < nx and 0 <= j + height < ny
    ]
    return lax.ppermute(x, ("gx", "gy"), pairs)


def bits_of(axis):
    return [1 << k for k in reversed(range(lax.axis_size(axis).bit_length() - 1))]


def swap(x, axis, bit):
    return lax.ppermute(x, axis, [(i, i ^ bit) for i in range(lax.axis_size(axis))])


def mine_and_other(x, axis, bit, dim):
    own = lax.axis_index(axis) // bit % 2
    take = functools.partial(lax.dynamic_index_in_dim, x, axis=dim, keepdims=False)
    return take(own), take(1 - own)


def in_order(own, other, axis, bit, dim):
    flag = lax.axis_index(axis) // bit % 2 == 1
    first = jnp.where(flag, other, own)
    second = jnp.where(flag, own, other)
    return jnp.stack([first, second], axis=dim)


def gathered_by_pairs(x, axis):
    steps = [x]
    for k, bit in enumerate(bits_of(axis)):
        x = in_order(x, swap(x, axis, bit), axis, bit, k)
        steps.append(x)
    size = lax.axis_size(axis)
    return x.reshape((size,) + x.shape[len(steps) - 1 :]), steps


def exchanged_by_pairs(x, axis):
    shape = x.shape
    bits = bits_of(axis)
    x = x.reshape((2,) * len(bits) + shape[1:])
    steps = []
    for k, bit in reversed(list(enumerate(bits))):
        own, other = mine_and_other(x, axis, bit, k)
        x = in_order(own, swap(other, axis, bit), axis, bit, k)
        steps.append(x)
    return x.reshape(shape), steps


def summed_by_pairs(x, axis, bits):
    names = bits_of(axis)
    x = x.reshape((2,) * len(names) + x.shape[1:])
    left = list(names)
    steps = []
    for bit in bits:
        own, other = mine_and_other(x, axis, bit, left.index(bit))
        left.remove(bit)
        x = own.astype(jnp.float32) + swap(other.astype(jnp.bfloat16), axis, bit).astype(jnp.float32)
        steps.append(x)
    return x, steps


def dot_nn(a, b):
    return lax.dot_general(a, b, (((1,), (0,)), ((), ())), preferred_element_type=jnp.float32)


def dot_tn(a, b):
    return lax.dot_general(a, b, (((0,), (0,)), ((), ())), preferred_element_type=jnp.float32)


def dot_nt(a, b):
    return lax.dot_general(a, b, (((1,), (1,)), ((), ())), preferred_element_type=jnp.float32)


def moved(x, step, period):
    if step == 0:
        return x
    rows = x.shape[0]
    place = lax.rem(lax.broadcasted_iota(jnp.int32, x.shape, 0), period)
    edge = 0 if step == 1 else period - 1
    return jnp.where(place == edge, 0.0, pltpu.roll(x, step % rows, 0))


def local_call(body, out_shapes, scratch, flops, moved_bytes, *args):
    return pl.pallas_call(
        body,
        out_shape=out_shapes,
        in_specs=[
            pl.BlockSpec(memory_space=pltpu.SMEM if a.ndim == 1 else pltpu.VMEM) for a in args
        ],
        out_specs=jax.tree.map(lambda _: pl.BlockSpec(memory_space=pltpu.VMEM), out_shapes),
        scratch_shapes=scratch,
        cost_estimate=pl.CostEstimate(flops=flops, bytes_accessed=moved_bytes, transcendentals=0),
        compiler_params=pltpu.CompilerParams(vmem_limit_bytes=VMEM_LIMIT),
    )(*args)


def class_kernel(gathered_ref, own_ref, label_ref, grad_ref, turned_ref, aux_ref):
    groups, rows, inner = gathered_ref.shape[0], own_ref.shape[0], own_ref.shape[1]
    owners, piece_rows, lanes = turned_ref.shape
    logits = jnp.zeros((CLASS_ROWS, rows), jnp.float32)
    for c in range(groups):
        weight = gathered_ref[c, 2 * rows : 2 * rows + CLASS_ROWS]
        logits += dot_nt(weight, jnp.maximum(gathered_ref[c, :rows], 0))
    place = lax.broadcasted_iota(jnp.int32, logits.shape, 0)
    real = place < CLASSES
    logits = jnp.where(real, logits, -jnp.inf)
    powers = jnp.exp(logits - jnp.max(logits, axis=0, keepdims=True))
    probabilities = powers / jnp.sum(powers, axis=0, keepdims=True)
    onehot = jnp.where(place == label_ref[...], 1.0, 0.0)
    logit_grad = jnp.where(real, probabilities - onehot, 0.0).astype(jnp.bfloat16)
    granules = []
    for c in range(groups):
        weight = gathered_ref[c, 2 * rows : 2 * rows + CLASS_ROWS]
        total = gathered_ref[c, rows : 2 * rows].astype(jnp.float32) + dot_tn(logit_grad, weight)
        active = gathered_ref[c, :rows].astype(jnp.float32) > 0
        grad = jnp.where(active, total, 0.0)
        grad_ref[:, c * inner : (c + 1) * inner] = grad.astype(jnp.bfloat16)
        turned = grad.T
        granules += [turned[8 * q : 8 * q + 8] for q in range(inner // 8)]
    for i in range(owners):
        mine = jnp.concatenate(granules[i::owners], axis=0).astype(jnp.bfloat16)
        size = mine.shape[0]
        for k in range(rows // lanes):
            turned_ref[i, k * size : (k + 1) * size] = mine[:, k * lanes : (k + 1) * lanes]
    aux_ref[...] = dot_nn(logit_grad, jnp.maximum(own_ref[...], 0)).astype(jnp.bfloat16)


def conv_kernel(place_ref, grad_ref, weight_ref, edge_ref, mid_ref, part_ref, acc_ref, sum_ref, pool_ref):
    _, far_d, far_h, width, inner = acc_ref.shape
    depth, height = far_d - 2, far_h - 2
    full = grad_ref.shape[1]
    ny, nc = part_ref.shape[:2]
    at_y = place_ref[0]
    acc_ref[...] = jnp.zeros_like(acc_ref)
    for a in STEPS:
        for b in STEPS:
            for c in STEPS:
                tap = 9 * (a + 1) + 3 * (b + 1) + c + 1
                term = dot_nt(grad_ref[...], weight_ref[:, tap * full : (tap + 1) * full])
                acc_ref[c + 1, 1 + a : 1 + a + depth, 1 + b : 1 + b + height] += term.reshape(
                    depth, height, width, inner
                )
    planes = []
    for d in range(far_d):
        planes.append(
            sum(
                moved(acc_ref[c + 1, d].reshape(far_h * width, inner), c, width) for c in STEPS
            ).reshape(far_h, width, inner)
        )
    edge_ref[0] = planes[0].astype(jnp.bfloat16)
    edge_ref[1] = planes[-1].astype(jnp.bfloat16)
    for d in range(depth):
        mid_ref[d] = planes[d + 1]
    half_h, half_w = height // 2, width // 2
    block = half_w // nc
    blocks = [planes[0], sum(planes[1 : 1 + depth]), planes[-1]]
    pool_ref[...] = jnp.zeros_like(pool_ref)
    for k, lines in enumerate(blocks):
        rows = [lines[0]]
        rows += [lines[1 + 2 * h] + lines[2 + 2 * h] for h in range(half_h)]
        rows += [lines[far_h - 1]]
        for h, row in enumerate(rows):
            sum_ref[k, h] = row
            pool_ref[k, h, 8 : 8 + half_w] = (
                sum_ref[k, h, pl.ds(0, half_w, stride=2)] + sum_ref[k, h, pl.ds(1, half_w, stride=2)]
            )
    part_ref[...] = jnp.zeros_like(part_ref)
    window = part_ref.shape[2] // (3 * half_h)
    empty = jnp.zeros((window, inner), jnp.float32)

    def put(to, first):
        for c in range(nc):
            for k in range(3):
                cells = []
                for h in range(half_h):
                    line = first + h
                    if 0 <= line < half_h + 2:
                        start = 7 + c * block
                        cells.append(pool_ref[k, line, start : start + window])
                    else:
                        cells.append(empty)
                size = half_h * window
                part_ref[to, c, k * size : (k + 1) * size] = jnp.concatenate(cells, axis=0).astype(
                    jnp.bfloat16
                )

    put(at_y, 1)

    @pl.when(at_y > 0)
    def _():
        put(at_y - 1, 1 - half_h)

    @pl.when(at_y < ny - 1)
    def _():
        put(at_y + 1, 1 + half_h)


def kernel_grad_kernel(granules, turned_ref, input_ref, out_ref, shift_ref, all_ref):
    blocks, piece_rows, lanes = turned_ref.shape
    all_d, far_h, width, inner = input_ref.shape
    height = far_h - 2
    per_block = all_d // blocks
    size = piece_rows // per_block
    cells = all_d * height * width
    owners, window, _ = out_ref.shape
    empty = jnp.zeros((3, 1) + shift_ref.shape[2:], jnp.bfloat16)
    shift_ref[:, :1] = empty
    shift_ref[:, all_d + 1 :] = empty
    flat = input_ref[...].astype(jnp.float32).reshape(all_d * far_h * width, inner)
    for c in STEPS:
        shift_ref[c + 1, 1 : 1 + all_d] = (
            moved(flat, -c, width).astype(jnp.bfloat16).reshape(input_ref.shape)
        )
    turned = jnp.concatenate(
        [
            turned_ref[k, d * size : (d + 1) * size]
            for k in range(blocks)
            for d in range(per_block)
        ],
        axis=1,
    )
    for a in STEPS:
        for b in STEPS:
            piece = jnp.concatenate(
                [
                    shift_ref[c, 1 + a : 1 + a + all_d, 1 + b : 1 + b + height].reshape(cells, inner)
                    for c in range(3)
                ],
                axis=1,
            )
            terms = dot_nn(turned, piece)
            for c in range(3):
                tap = 9 * (a + 1) + 3 * (b + 1) + c
                all_ref[tap * size : (tap + 1) * size] = terms[:, c * inner : (c + 1) * inner]
    all_ref[TAPS * size :] = jnp.zeros((window, inner), jnp.float32)
    for owner in range(owners):
        start = owner * granules // blocks * 8
        out_ref[owner] = all_ref[start : start + window].astype(jnp.bfloat16)


def bottom_kernel(
    down_ref, up_ref, pre_ref, source_ref, weight_ref, part_ref, both_ref, shift_ref
):
    _, far_d, far_w, height, filters = shift_ref.shape
    depth, width = far_d - 2, far_w - 2
    rows = depth * width * height
    channels = source_ref.shape[1]
    groups = both_ref.shape[0]
    thin = channels // groups
    full = down_ref.shape[1]
    inner = full // groups
    back = dot_nt(down_ref[...], up_ref[...])
    saved = pre_ref[...]
    grad = jnp.where(saved.astype(jnp.float32) > 0, back, 0.0)
    shift_ref[:, :1] = jnp.zeros((3, 1) + shift_ref.shape[2:], jnp.bfloat16)
    shift_ref[:, far_d - 1 :] = jnp.zeros((3, 1) + shift_ref.shape[2:], jnp.bfloat16)
    for b in STEPS:
        shift_ref[b + 1, 1 : 1 + depth] = (
            moved(grad, b, height).astype(jnp.bfloat16).reshape(depth, far_w, height, filters)
        )
    own_down = down_ref[...].reshape(depth, far_w, height, full)[:, 1 : 1 + width].reshape(rows, full)
    own_saved = saved.reshape(depth, far_w, height, filters)[:, 1 : 1 + width].reshape(rows, filters)
    up_part = dot_tn(jnp.maximum(own_saved, 0), own_down).astype(jnp.bfloat16)
    for cc in range(groups):
        both_ref[cc, TAPS * thin :] = up_part[:, cc * inner : (cc + 1) * inner]
    turned = source_ref[...].T
    total = jnp.zeros((rows, channels), jnp.float32)
    for a in STEPS:
        for b in STEPS:
            tap = 9 * (a + 1) + 3 * (b + 1)
            piece = jnp.concatenate(
                [
                    shift_ref[b + 1, 1 - a : 1 - a + depth, 1 - c : 1 - c + width].reshape(rows, filters)
                    for c in STEPS
                ],
                axis=1,
            )
            weight = jnp.concatenate([weight_ref[tap + c] for c in range(3)], axis=1)
            total += dot_nt(piece, weight)
            terms = dot_nn(turned, piece).astype(jnp.bfloat16)
            for c in range(3):
                for cc in range(groups):
                    both_ref[cc, (tap + c) * thin : (tap + c + 1) * thin] = terms[
                        cc * thin : (cc + 1) * thin, c * filters : (c + 1) * filters
                    ]
    part_ref[...] = total.astype(jnp.bfloat16)


def per_device(
    pre_bottom,
    bottom_input,
    bottom_weight,
    up_weight,
    level_input,
    pre_level,
    level_cotangent,
    labels,
    level_weight,
    aux_weight,
):
    nx, ny, nc = (lax.axis_size(a) for a in ("gx", "gy", "col"))
    at_x, at_y, at_c = (lax.axis_index(a) for a in ("gx", "gy", "col"))
    depth, height, width, inner = level_input.shape
    full = inner * nc
    rows = depth * height * width
    far_d, far_h = depth + 2, height + 2
    half_d, half_h, half_w = depth // 2, height // 2, width // 2
    block = half_w // nc
    wide = block + 2
    bottom_d, bottom_h, _, filters = pre_bottom.shape
    bf16, f32 = jnp.bfloat16, jnp.float32
    struct = jax.ShapeDtypeStruct

    own_pre = pre_level.reshape(rows, inner)
    turned_pre = pre_bottom.transpose(0, 2, 1, 3)
    payload = jnp.concatenate(
        [
            own_pre,
            level_cotangent.reshape(rows, inner),
            jnp.pad(aux_weight.T, ((0, CLASS_ROWS - CLASSES), (0, 0))),
        ]
    )
    first_edge = turned_pre[:, 0].reshape(-1, filters)
    last_edge = turned_pre[:, -1].reshape(-1, filters)
    payload = jnp.stack(
        [
            jnp.concatenate([payload, jnp.where(at_c < c, last_edge, first_edge)], axis=0)
            for c in range(nc)
        ]
    )
    gathered = exchange(payload, "col")
    edges = gathered[:, 2 * rows + CLASS_ROWS :].reshape(nc, bottom_d, 1, bottom_h, filters)

    def edge_of(c):
        found = lax.dynamic_index_in_dim(edges, jnp.clip(c, 0, nc - 1), 0, keepdims=False)
        return jnp.where((c >= 0) & (c < nc), found, jnp.zeros_like(found))

    pre_wide = jnp.concatenate([edge_of(at_c - 1), turned_pre, edge_of(at_c + 1)], axis=1)

    size = full // nx
    lanes = height * width
    level_pre_grad, turned_grad, aux_part = local_call(
        class_kernel,
        (
            struct((rows, full), bf16),
            struct((nx, depth * size, lanes), bf16),
            struct((CLASS_ROWS, inner), bf16),
        ),
        [],
        6 * rows * full * CLASS_ROWS,
        2 * gathered.size,
        gathered,
        own_pre,
        labels.reshape(1, rows),
    )

    window = (wide + 7) // 8 * 8
    edge, mid, parts = local_call(
        conv_kernel,
        (
            struct((2, far_h, width, inner), bf16),
            struct((depth, far_h, width, inner), f32),
            struct((ny, nc, 3 * half_h * window, inner), bf16),
        ),
        [
            pltpu.VMEM((3, far_d, far_h, width, inner), f32),
            pltpu.VMEM((3, half_h + 2, width, inner), f32),
            pltpu.VMEM((3, half_h + 2, half_w + 24, inner), f32),
        ],
        2 * rows * full * TAPS * inner,
        2 * level_weight.size,
        jnp.full((1,), at_y, jnp.int32),
        level_pre_grad,
        level_weight,
    )

    near = behind(level_input, parts)
    input_far = jnp.concatenate(
        [neighbour(near[:, -1:], 0, 1), near, neighbour(near[:, :1], 0, -1)], axis=1
    )
    moved_grad, moved_steps = exchanged_by_pairs(behind(turned_grad, parts), "gx")

    relayed = exchange(parts.reshape(ny * nc, 3 * half_h * window, inner), ("gy", "col"))
    relayed = (
        relayed.reshape(ny, nc, 3 * half_h, window, inner)[:, :, :, :wide]
        .astype(f32)
        .sum(axis=0)
        .astype(bf16)
        .reshape(nc * 3 * half_h * wide, inner)
    )

    relayed = behind(relayed, input_far, moved_steps[1])
    input_all, input_steps = gathered_by_pairs(input_far, "gx")
    input_all = input_all.reshape(nx * depth, far_h, width, inner)

    by_depth = spread(jnp.concatenate([relayed, aux_part]), "gx")
    split = nc * 3 * half_h * wide
    aux_sum = by_depth[:, split:].astype(f32).sum(axis=0).astype(bf16)
    down = by_depth[:, :split].reshape(nx, nc, 3, half_h, wide, inner).astype(f32)
    line = (
        down[:, :, 1]
        + jnp.pad(down[1:, :, 0], ((0, 1), (0, 0), (0, 0), (0, 0), (0, 0)))
        + jnp.pad(down[:-1, :, 2], ((1, 0), (0, 0), (0, 0), (0, 0), (0, 0)))
    ).astype(bf16)

    line = behind(line, input_steps[2], moved_grad)
    split = nx * nc * half_h * wide
    by_height = spread(jnp.concatenate([line.reshape(split, inner), aux_sum]), "gy")
    aux_weight_grad = by_height[:, split : split + CLASSES].astype(f32).sum(axis=0).T
    down_wide = (
        by_height[:, :split]
        .reshape(ny, nx, nc, half_h, wide, inner)
        .transpose(1, 4, 0, 3, 2, 5)
        .reshape(bottom_d * wide * bottom_h, full)
    )

    chunk = TAPS * full // (nx * ny)
    granules = chunk // 8
    slots = max((granules * o % nx + granules - 1) // nx + 1 for o in range(nx * ny))
    slots += slots % 2
    level_part = local_call(
        functools.partial(kernel_grad_kernel, granules),
        struct((nx * ny, 8 * slots, inner), bf16),
        [
            pltpu.VMEM((3, nx * depth + 2, far_h, width, inner), bf16),
            pltpu.VMEM((TAPS * size + 8 * slots, inner), f32),
        ],
        2 * rows * full * TAPS * inner,
        2 * nx * ny * slots * 8 * inner,
        moved_grad,
        input_all,
    )
    level_part = level_part.reshape(nx, ny, slots * 8, inner).transpose(1, 0, 2, 3)
    summed, sum_steps = summed_by_pairs(level_part, "gy", (2, 4, 1) if ny == 8 else bits_of("gy"))
    down_wide = behind(down_wide, sum_steps[0])
    level_part, _ = exchanged_by_pairs(summed.astype(bf16), "gx")
    level_part = (
        level_part.reshape(nx, slots, 8, inner).transpose(1, 0, 2, 3).reshape(-1, inner).astype(f32)
    )
    begin = lax.rem((at_x * ny + at_y) * granules, nx) * 8
    level_weight_grad = lax.dynamic_slice_in_dim(level_part, begin, chunk, axis=0).T

    bottom_rows = bottom_d * block * bottom_h
    channel_width = bottom_weight.shape[0]
    thin = channel_width // nc
    part, both = local_call(
        bottom_kernel,
        (
            struct((bottom_rows, channel_width), bf16),
            struct((nc, TAPS * thin + filters, inner), bf16),
        ),
        [pltpu.VMEM((3, bottom_d + 2, wide, bottom_h, filters), bf16)],
        4 * bottom_rows * channel_width * TAPS * filters,
        2 * bottom_weight.size,
        down_wide,
        up_weight,
        pre_wide.reshape(-1, filters),
        bottom_input.transpose(0, 2, 1, 3).reshape(bottom_rows, channel_width),
        bottom_weight.transpose(1, 0, 2),
    )
    edge = behind(edge, down_wide)
    mid = jnp.concatenate(
        [
            (mid[0] + neighbour(edge[1], 1, 0))[None],
            mid[1:-1],
            (mid[-1] + neighbour(edge[0], -1, 0))[None],
        ],
        axis=0,
    )
    before = neighbour(mid[:, -1].astype(bf16), 0, 1)
    after = neighbour(mid[:, 0].astype(bf16), 0, -1)
    level_input_grad = jnp.concatenate(
        [
            (mid[:, 1] + before)[:, None],
            mid[:, 2 : far_h - 2],
            (mid[:, far_h - 2] + after)[:, None],
        ],
        axis=1,
    ).astype(bf16)
    share = bottom_d // ny
    bottom_input_grad = (
        exchange(part.reshape(ny, bottom_rows // ny, channel_width), "gy")
        .astype(f32)
        .sum(axis=0)
        .astype(bf16)
        .reshape(share, block, bottom_h, channel_width)
        .transpose(0, 2, 1, 3)
    )
    both, _ = summed_by_pairs(both, "col", bits_of("col")[::-1])
    bottom_weight_grad = both[: TAPS * thin].reshape(TAPS, thin, filters).transpose(1, 0, 2)
    up_weight_grad = both[TAPS * thin :]
    return (
        level_input_grad,
        bottom_input_grad,
        level_weight_grad,
        bottom_weight_grad,
        up_weight_grad,
        aux_weight_grad,
    )


def solution(mesh):
    return jax.shard_map(
        per_device,
        mesh=mesh,
        in_specs=(
            P(None, None, "col", "gy"),
            P(None, None, "col", "gx"),
            P("gx", None, "gy"),
            P("gy", None),
            P("gx", "gy", None, "col"),
            P("gx", "gy", None, "col"),
            P("gx", "gy", None, "col"),
            P("gx", "gy", None),
            P("col", None),
            P("col", None),
        ),
        out_specs=(
            P("gx", "gy", None, "col"),
            P("gy", None, "col", "gx"),
            P("col", ("gx", "gy")),
            P(("gx", "col"), None, "gy"),
            P("gy", "col"),
            P("col", None),
        ),
        check_vma=False,
    )
```

time: 194 us -> 179 us (0.923); the launches traced: 193 us -> 175 us
  blocking collectives: 57.8 us -> 0 us
  starting transfers between devices: 64 us -> 82.4 us
  waiting for transfers between devices: 44.2 us -> 61.1 us
  local copies, waits for them, and re-layouts: 11.4 us -> 15.6 us
  Pallas kernels: 7.5 us -> 9.51 us
    all_to_all x2 -> x0, blocking collectives: 57.8 us -> none  [exchange(): return lax.all_to_all(x, axis, split_axis=0, concat_axis=0, tiled=False)]
    ppermute x2 -> x14, waiting for transfers between devices: 0.01 us -> 46.5 us  [swap(): lax.ppermute(x, axis, [(i, i ^ bit) for i in range(lax.axis_size(axis))])]
    ppermute x2 -> x14, starting transfers between devices: 5.8 us -> 37.2 us  [swap(): lax.ppermute(x, axis, [(i, i ^ bit) for i in range(lax.axis_size(axis))])]
    all_to_all x6 -> x5, waiting for transfers between devices: 35.8 us -> 12.1 us  [exchange(): return lax.all_to_all(x, axis, split_axis=0, concat_axis=0, tiled=False)]
    all_to_all x6 -> x5, starting transfers between devices: 36.9 us -> 26.9 us  [exchange(): return lax.all_to_all(x, axis, split_axis=0, concat_axis=0, tiled=False)]
    ppermute x8 -> x6, waiting for transfers between devices: 8.39 us -> 2.47 us  [neighbour(): return lax.ppermute(x, ('gx', 'gy'), pairs)]
    reduce_sum x6 -> x2, other arithmetic: 3.73 us -> 0.09 us  [the longest x1 0.08 us: per_device(): relayed = relayed.reshape(ny, nc, 3 * half_h, window, inner)[:, :, :, :wi...]
    another operation x1 -> x17, other arithmetic: 0.01 us -> 3.24 us  [the longest x2 1.91 us: per_device(): jnp.stack([jnp.concatenate([payload, jnp.where(at_c < c, last_edge, first...]
  transfers between devices with their start and end apart: 16 -> 25, of which waited for: 7 -> 13; matrix products, arithmetic and copies ran while one was open for 5% -> 6% of each run, Pallas kernels for 3% -> 3%
where the time goes in v3:
time: 179 us; the launch traced here: 175 us
  starting transfers between devices  82.4 us (46%)
  waiting for transfers between devices  61.1 us (34%)
  local copies, waits for them, and re-layouts  15.6 us (9%)
  Pallas kernels  9.51 us (5%)
  other arithmetic  5.41 us (3%)
    ppermute x14, waiting for transfers between devices, swap(): lax.ppermute(x, axis, [(i, i ^ bit) for i in range(lax.axis_size(axis))])  46.5 us
    ppermute x14, starting transfers between devices, swap(): lax.ppermute(x, axis, [(i, i ^ bit) for i in range(lax.axis_size(axis))])  37.2 us
    all_to_all x5, starting transfers between devices, exchange(): return lax.all_to_all(x, axis, split_axis=0, concat_axis=0, tiled=False)  26.9 us
    ppermute x6, starting transfers between devices, neighbour(): return lax.ppermute(x, ('gx', 'gy'), pairs)  18.2 us
    all_to_all x5, waiting for transfers between devices, exchange(): return lax.all_to_all(x, axis, split_axis=0, concat_axis=0, tiled=False)  12.1 us
    pallas_call x4, Pallas kernels, local_call(): pl.pallas_call(body, out_shape=out_shapes, in_specs=[pl.BlockSpec(memory_...  9.51 us
    unnamed x37, local copies, waits for them, and re-layouts  8.17 us
  transfers between devices with their start and end apart: 25, of which 13 were waited for; matrix products, arithmetic and copies ran while one was open for 6% of the time, Pallas kernels for 3%

profile of v3, /device:TPU:1, one launch (start us, length us, event | category | flops | bytes accessed | tf_op | source)
XLA Modules:
  0.0 175.4 jit_solution(10964738809552381532)
XLA Ops:
  0.7 1.1 copy.123
  2.4 1.0 maximum_bitcast_fusion
  3.4 0.9 pad_maximum_fusion.1
  4.3 7.4 %all-to-all-start = ((bf16[4,656,128]{2,1,0:T(8,128)(2,1)}), bf16[4,656,128]{2,1,0:T(8,128)(2,1)}, u32[]{:S(2)}, u32[]{:S(2)}) async-start(bf16[4,656,128]{2,1,0:T(8,128)(2,1)} %pad_maximum_fusion.1), calls=%async_computation | async-start | bytes 1343488 | tf_op jit(solution)/shard_map/all_to_all | solution.py:18
  11.8 9.6 %all-to-all-done.gathered_ref = bf16[4,656,128]{2,1,0:T(8,128)(2,1)} async-done(((bf16[4,656,128]{2,1,0:T(8,128)(2,1)}), bf16[4,656,128]{2,1,0:T(8,128)(2,1)}, u32[]{:S(2)}, u32[]{:S(2)}) %all-to-all-start) | async-done | bytes 671776 | tf_op jit(solution)/shard_map/all_to_all | solution.py:18
  21.4 0.8 copy-done.2
  22.2 1.8 %shard_map.145 = (bf16[256,512]{1,0:T(8,128)(2,1)S(1)}, bf16[8,128,128]{2,1,0:T(8,128)(2,1)S(1)}, bf16[16,128]{1,0:T(8,128)(2,1)S(1)}) custom-call(bf16[4,656,128]{2,1,0:T(8,128)(2,1)} %all-to-all-done.gathered_ref, bf16[256,128]{1,0:T(8,128)(2,1)S(1)} %bitcast.252, s32[1,256]{1,0:T(1,128)S(1)} %reshape.134.label_ref), custom_call_target="tpu_custom_call" | custom-call | flops 12582912 | bytes 671744 | tf_op jit(solution)/shard_map/pallas_call | solution.py:118
  24.7 2.1 %shard_map.146 = (bf16[2,6,32,128]{3,2,1,0:T(8,128)(2,1)S(1)}, f32[2,6,32,128]{3,2,1,0:T(8,128)S(1)}, bf16[8,4,48,128]{3,2,1,0:T(8,128)(2,1)S(1)}) custom-call(s32[1]{0:T(128)} %bitcast.place_ref, bf16[256,512]{1,0:T(8,128)(2,1)S(1)} %get-tuple-element.20.grad_ref, bf16[128,13824]{1,0:T(8,128)(2,1)S(1)} %copy-done), custom_call_target="tpu_custom_call" | custom-call | flops 905969664 | bytes 3538944 | tf_op jit(solution)/shard_map/pallas_call | solution.py:118
  28.9 6.2 %all-to-all-start.1 = ((bf16[32,48,128]{2,1,0:T(8,128)(2,1)}), bf16[32,48,128]{2,1,0:T(8,128)(2,1)S(1)}, u32[]{:S(2)}, u32[]{:S(2)}) async-start(bf16[32,48,128]{2,1,0:T(8,128)(2,1)} %bitcast.250), calls=%async_computation.1 | async-start | bytes 786432 | tf_op jit(solution)/shard_map/all_to_all | solution.py:18
  35.8 1.3 collective-permute-start.1
  37.1 5.5 %collective-permute-start = (bf16[2,1,32,128]{3,2,1,0:T(8,128)(2,1)S(1)}, bf16[2,1,32,128]{3,2,1,0:T(8,128)(2,1)S(1)}, u32[]{:S(2)}, u32[]{:S(2)}) collective-permute-start(bf16[2,1,32,128]{3,2,1,0:T(8,128)(2,1)S(1)} %get-tuple-element.99), channel_id=1, source_target_pairs={{0,4},{4,8},{8,12},{12,16},{16,20},{20,24},{24,28},{32,36},{36,40}... | collective-permute-start | bytes 49160 | tf_op jit(solution)/shard_map/ppermute | solution.py:38
  42.6 0.9 dynamic-slice_bitcast_fusion.2
  43.5 1.7 collective-permute-start.2
  45.3 0.9 constant_dynamic-update-slice_fusion.1
  46.1 6.1 %collective-permute-start.4 = (bf16[2,6,32,128]{3,2,1,0:T(8,128)(2,1)S(1)}, bf16[2,6,32,128]{3,2,1,0:T(8,128)(2,1)S(1)}, u32[]{:S(2)}, u32[]{:S(2)}) collective-permute-start(bf16[2,6,32,128]{3,2,1,0:T(8,128)(2,1)S(1)} %constant_dynamic-update-slice_fusion), channel_id=1, source_target_pairs={{0,128},{32,160},{64,192},{96,224},{128,0},{160,32},{192,64},{224,... | collective-permute-start | bytes 294920 | tf_op jit(solution)/shard_map/ppermute | solution.py:46
  52.2 0.9 fusion.18
  53.2 1.3 collective-permute-start.3
  54.5 1.3 collective-permute-done.4
  55.9 4.3 %collective-permute-start.5 = (bf16[2,2,6,32,128]{4,3,2,1,0:T(8,128)(2,1)S(1)}, bf16[2,2,6,32,128]{4,3,2,1,0:T(8,128)(2,1)S(1)}, u32[]{:S(2)}, u32[]{:S(2)}) collective-permute-start(bf16[2,2,6,32,128]{4,3,2,1,0:T(8,128)(2,1)S(1)} %pad_maximum_fusion.6), channel_id=1, source_target_pairs={{0,64},{32,96},{64,0},{96,32},{128,192},{160,224},{192,128},{224,1... | collective-permute-start | bytes 589832 | tf_op jit(solution)/shard_map/ppermute | solution.py:46
  60.2 8.6 %collective-permute-done.3 = bf16[2,2,128,128]{3,2,1,0:T(8,128)(2,1)S(1)} collective-permute-done((bf16[2,2,128,128]{3,2,1,0:T(8,128)(2,1)S(1)}, bf16[2,2,128,128]{3,2,1,0:T(8,128)(2,1)S(1)}, u32[]{:S(2)}, u32[]{:S(2)}) %collective-permute-start.3) | collective-permute-done | bytes 131104 | tf_op jit(solution)/shard_map/ppermute | solution.py:46
  68.8 1.9 %collective-permute-start.6 = (bf16[2,2,128,128]{3,2,1,0:T(8,128)(2,1)S(1)}, bf16[2,2,128,128]{3,2,1,0:T(8,128)(2,1)S(1)}, u32[]{:S(2)}, u32[]{:S(2)}) collective-permute-start(bf16[2,2,128,128]{3,2,1,0:T(8,128)(2,1)S(1)} %fusion.12), channel_id=1, source_target_pairs={{0,128},{32,160},{64,192},{96,224},{128,0},{160,32},{192,64},{224,... | collective-permute-start | bytes 393224 | tf_op jit(solution)/shard_map/ppermute | solution.py:46
  70.8 2.3 %collective-permute-done.5 = bf16[2,2,6,32,128]{4,3,2,1,0:T(8,128)(2,1)S(1)} collective-permute-done((bf16[2,2,6,32,128]{4,3,2,1,0:T(8,128)(2,1)S(1)}, bf16[2,2,6,32,128]{4,3,2,1,0:T(8,128)(2,1)S(1)}, u32[]{:S(2)}, u32[]{:S(2)}) %collective-permute-start.5) | collective-permute-done | bytes 196640 | tf_op jit(solution)/shard_map/ppermute | solution.py:46
  74.1 3.5 %all-to-all-start.2 = ((bf16[8,160,128]{2,1,0:T(8,128)(2,1)}), bf16[8,160,128]{2,1,0:T(8,128)(2,1)S(1)}, u32[]{:S(2)}, u32[]{:S(2)}) async-start(bf16[8,160,128]{2,1,0:T(8,128)(2,1)} %broadcast_in_dim.30), calls=%async_computation.2 | async-start | bytes 655360 | tf_op jit(solution)/shard_map/all_to_all | solution.py:18
  77.7 11.1 %collective-permute-done.7 = bf16[2,2,2,6,32,128]{5,4,3,2,0,1:T(8,128)(2,1)S(1)} collective-permute-done((bf16[2,2,2,6,32,128]{5,4,3,2,0,1:T(8,128)(2,1)S(1)}, bf16[2,2,2,6,32,128]{5,4,3,2,0,1:T(8,128)(2,1)S(1)}, u32[]{:S(2)}, u32[]{:S(2)}) %collective-permute-start.7) | collective-permute-done | bytes 393248 | tf_op jit(solution)/shard_map/ppermute | solution.py:46
  89.0 2.7 %shard_map.147 = bf16[64,48,128]{2,1,0:T(8,128)(2,1)S(1)} custom-call(bf16[8,128,128]{2,1,0:T(8,128)(2,1)S(1)} %bitcast.253, bf16[16,6,32,128]{3,2,1,0:T(8,128)(2,1)S(1)} %bitcast.247), custom_call_target="tpu_custom_call" | custom-call | flops 905969664 | bytes 786432 | tf_op jit(solution)/shard_map/pallas_call | solution.py:118
  91.7 4.6 %collective-permute-start.8 = (bf16[2,2,8,48,128]{4,3,1,0,2:T(8,128)(2,1)S(1)}, bf16[2,2,8,48,128]{4,3,1,0,2:T(8,128)(2,1)S(1)}, u32[]{:S(2)}, u32[]{:S(2)}) collective-permute-start(bf16[2,2,8,48,128]{4,3,1,0,2:T(8,128)(2,1)S(1)} %dynamic-slice_bitcast_fusion.1), channel_id=1, source_target_pairs={{0,8},{4,12},{8,0},{12,4},{16,24},{20,28},{24,16},{28,20},{1,9},{5... | collective-permute-start | bytes 1179656 | tf_op jit(solution)/shard_map/ppermute | solution.py:46
  96.4 0.9 slice.114
  97.6 3.9 %collective-permute-done.8 = bf16[2,2,8,48,128]{4,3,1,0,2:T(8,128)(2,1)S(1)} collective-permute-done((bf16[2,2,8,48,128]{4,3,1,0,2:T(8,128)(2,1)S(1)}, bf16[2,2,8,48,128]{4,3,1,0,2:T(8,128)(2,1)S(1)}, u32[]{:S(2)}, u32[]{:S(2)}) %collective-permute-start.8) | collective-permute-done | bytes 393248 | tf_op jit(solution)/shard_map/ppermute | solution.py:46
  101.7 3.1 %collective-permute-start.13 = (bf16[2,8,48,128]{3,2,0,1:T(8,128)(2,1)S(1)}, bf16[2,8,48,128]{3,2,0,1:T(8,128)(2,1)S(1)}, u32[]{:S(2)}, u32[]{:S(2)}) collective-permute-start(bf16[2,8,48,128]{3,2,0,1:T(8,128)(2,1)S(1)} %fusion.3), channel_id=1, source_target_pairs={{0,16},{4,20},{8,24},{12,28},{16,0},{20,4},{24,8},{28,12},{1,17},{... | collective-permute-start | bytes 589832 | tf_op jit(solution)/shard_map/ppermute | solution.py:46
  104.7 5.1 %collective-permute-done.13 = bf16[2,8,48,128]{3,2,0,1:T(8,128)(2,1)S(1)} collective-permute-done((bf16[2,8,48,128]{3,2,0,1:T(8,128)(2,1)S(1)}, bf16[2,8,48,128]{3,2,0,1:T(8,128)(2,1)S(1)}, u32[]{:S(2)}, u32[]{:S(2)}) %collective-permute-start.13) | collective-permute-done | bytes 196640 | tf_op jit(solution)/shard_map/ppermute | solution.py:46
  110.0 2.8 %collective-permute-start.14 = (bf16[8,48,128]{2,1,0:T(8,128)(2,1)S(1)}, bf16[8,48,128]{2,1,0:T(8,128)(2,1)S(1)}, u32[]{:S(2)}, u32[]{:S(2)}) collective-permute-start(bf16[8,48,128]{2,1,0:T(8,128)(2,1)S(1)} %fusion.19), channel_id=1, source_target_pairs={{0,4},{4,0},{8,12},{12,8},{16,20},{20,16},{24,28},{28,24},{1,5},{5... | collective-permute-start | bytes 294920 | tf_op jit(solution)/shard_map/ppermute | solution.py:46
  112.8 2.4 %collective-permute-done.14 = bf16[8,48,128]{2,1,0:T(8,128)(2,1)S(1)} collective-permute-done((bf16[8,48,128]{2,1,0:T(8,128)(2,1)S(1)}, bf16[8,48,128]{2,1,0:T(8,128)(2,1)S(1)}, u32[]{:S(2)}, u32[]{:S(2)}) %collective-permute-start.14) | collective-permute-done | bytes 98336 | tf_op jit(solution)/shard_map/ppermute | solution.py:46
  115.5 2.8 %collective-permute-done.15 = bf16[2,2,48,128]{3,2,0,1:T(8,128)(2,1)S(1)} collective-permute-done((bf16[2,2,48,128]{3,2,0,1:T(8,128)(2,1)S(1)}, bf16[2,2,48,128]{3,2,0,1:T(8,128)(2,1)S(1)}, u32[]{:S(2)}, u32[]{:S(2)}) %collective-permute-start.15) | collective-permute-done | bytes 49184 | tf_op jit(solution)/shard_map/ppermute | solution.py:46
  118.3 0.9 collective-permute-start.16
  119.2 1.0 broadcast_in_dim.31
  120.3 5.9 %all-to-all-start.3 = ((bf16[8,400,128]{2,1,0:T(8,128)(2,1)}), bf16[8,400,128]{2,1,0:T(8,128)(2,1)S(1)}, u32[]{:S(2)}, u32[]{:S(2)}) async-start(bf16[8,400,128]{2,1,0:T(8,128)(2,1)} %broadcast_in_dim.31), calls=%async_computation.3 | async-start | bytes 1638400 | tf_op jit(solution)/shard_map/all_to_all | solution.py:18
  127.0 6.4 %collective-permute-done.17 = bf16[2,2,48,128]{3,2,1,0:T(8,128)(2,1)S(1)} collective-permute-done((bf16[2,2,48,128]{3,2,1,0:T(8,128)(2,1)S(1)}, bf16[2,2,48,128]{3,2,1,0:T(8,128)(2,1)S(1)}, u32[]{:S(2)}, u32[]{:S(2)}) %collective-permute-start.17) | collective-permute-done | bytes 49184 | tf_op jit(solution)/shard_map/ppermute | solution.py:46
  134.3 2.5 %all-to-all-done.3 = bf16[8,400,128]{2,1,0:T(8,128)(2,1)S(1)} async-done(((bf16[8,400,128]{2,1,0:T(8,128)(2,1)}), bf16[8,400,128]{2,1,0:T(8,128)(2,1)S(1)}, u32[]{:S(2)}, u32[]{:S(2)}) %all-to-all-start.3) | async-done | bytes 819232 | tf_op jit(solution)/shard_map/all_to_all | solution.py:18
  137.9 3.7 %collective-permute-start.9 = (bf16[6,32,128]{2,1,0:T(8,128)(2,1)S(1)}, bf16[6,32,128]{2,1,0:T(8,128)(2,1)S(1)}, u32[]{:S(2)}, u32[]{:S(2)}) collective-permute-start(bf16[6,32,128]{2,1,0:T(8,128)(2,1)S(1)} %get-tuple-element.96), channel_id=1, source_target_pairs={{0,32},{4,36},{8,40},{12,44},{16,48},{20,52},{24,56},{28,60},{32,6... | collective-permute-start | bytes 147464 | tf_op jit(solution)/shard_map/ppermute | solution.py:38
  141.7 1.3 collective-permute-start.10
  143.0 3.0 %shard_map.148 = (bf16[512,128]{1,0:T(8,128)(2,1)}, bf16[4,992,128]{2,1,0:T(8,128)(2,1)S(1)}) custom-call(bf16[768,512]{1,0:T(8,128)(2,1)S(1)} %bitcast.246, bf16[128,512]{1,0:T(8,128)(2,1)S(1)} %copy-done.9, bf16[768,128]{1,0:T(8,128)(2,1)S(1)} %bitcast.256, bf16[512,128]{1,0:T(8,128)(2,1)S(1)} %bitcast.257, bf16[27,128,128]{2,1,0:T(8,128)(2,1)S(1)} %bitcast.258), custom_call_target="tpu_custom_call" | custom-call | flops 905969664 | bytes 884736 | tf_op jit(solution)/shard_map/pallas_call | solution.py:118
  145.9 4.0 %all-to-all-start.4 = ((bf16[8,64,128]{2,1,0:T(8,128)(2,1)}), bf16[8,64,128]{2,1,0:T(8,128)(2,1)S(1)}, u32[]{:S(2)}, u32[]{:S(2)}) async-start(bf16[8,64,128]{2,1,0:T(8,128)(2,1)} %bitcast.72), calls=%async_computation.4 | async-start | bytes 262144 | tf_op jit(solution)/shard_map/all_to_all | solution.py:18
  150.0 7.6 %collective-permute-start.18 = (bf16[2,992,128]{2,1,0:T(8,128)(2,1)S(1)}, bf16[2,992,128]{2,1,0:T(8,128)(2,1)S(1)}, u32[]{:S(2)}, u32[]{:S(2)}) collective-permute-start(bf16[2,992,128]{2,1,0:T(8,128)(2,1)S(1)} %dynamic-slice_bitcast_fusion), channel_id=1, source_target_pairs={{0,1},{1,0},{2,3},{3,2},{4,5},{5,4},{6,7},{7,6},{8,9},{9,8},{10,11... | collective-permute-start | bytes 1523720 | tf_op jit(solution)/shard_map/ppermute | solution.py:46
  159.0 5.2 %collective-permute-start.11 = (bf16[2,32,128]{2,1,0:T(8,128)(2,1)S(1)}, bf16[2,32,128]{2,1,0:T(8,128)(2,1)S(1)}, u32[]{:S(2)}, u32[]{:S(2)}) collective-permute-start(bf16[2,32,128]{2,1,0:T(8,128)(2,1)S(1)} %get-tuple-element.94), channel_id=1, source_target_pairs={{0,4},{4,8},{8,12},{12,16},{16,20},{20,24},{24,28},{32,36},{36,40}... | collective-permute-start | bytes 49160 | tf_op jit(solution)/shard_map/ppermute | solution.py:38
  164.2 1.3 collective-permute-start.12
  165.7 2.0 %collective-permute-start.19 = (bf16[992,128]{1,0:T(8,128)(2,1)S(1)}, bf16[992,128]{1,0:T(8,128)(2,1)S(1)}, u32[]{:S(2)}, u32[]{:S(2)}) collective-permute-start(bf16[992,128]{1,0:T(8,128)(2,1)S(1)} %fusion.2), channel_id=1, source_target_pairs={{0,2},{1,3},{2,0},{3,1},{4,6},{5,7},{6,4},{7,5},{8,10},{9,11},{10,... | collective-permute-start | bytes 761864 | tf_op jit(solution)/shard_map/ppermute | solution.py:46
  167.7 2.5 %collective-permute-done.12 = bf16[2,32,128]{2,1,0:T(8,128)(2,1)S(1)} collective-permute-done((bf16[2,32,128]{2,1,0:T(8,128)(2,1)S(1)}, bf16[2,32,128]{2,1,0:T(8,128)(2,1)S(1)}, u32[]{:S(2)}, u32[]{:S(2)}) %collective-permute-start.12) | collective-permute-done | bytes 16416 | tf_op jit(solution)/shard_map/ppermute | solution.py:38
  171.5 2.5 %collective-permute-done.19 = bf16[992,128]{1,0:T(8,128)(2,1)S(1)} collective-permute-done((bf16[992,128]{1,0:T(8,128)(2,1)S(1)}, bf16[992,128]{1,0:T(8,128)(2,1)S(1)}, u32[]{:S(2)}, u32[]{:S(2)}) %collective-permute-start.19) | collective-permute-done | bytes 253984 | tf_op jit(solution)/shard_map/ppermute | solution.py:46
  (117 shorter events, 13.6 us)
Async XLA Ops:
  0.6 11.1 %copy-start.13 = (s32[2,4,32]{2,1,0:T(4,128)S(1)}, s32[2,4,32]{2,1,0:T(4,128)}, u32[]{:S(2)}) copy-start(s32[2,4,32]{2,1,0:T(4,128)} %param.17) | copy-start | bytes 3076
  0.6 24.0 %copy-start = (bf16[128,13824]{1,0:T(8,128)(2,1)S(1)}, bf16[128,13824]{1,0:T(8,128)(2,1)}, u32[]{:S(2)}) copy-start(bf16[128,13824]{1,0:T(8,128)(2,1)} %weight_ref.1) | copy-start | bytes 10616836
  1.7 0.7 copy-start.10
  4.3 17.0 %all-to-all-start = ((bf16[4,656,128]{2,1,0:T(8,128)(2,1)}), bf16[4,656,128]{2,1,0:T(8,128)(2,1)}, u32[]{:S(2)}, u32[]{:S(2)}) async-start(bf16[4,656,128]{2,1,0:T(8,128)(2,1)} %pad_maximum_fusion.1), calls=%async_computation | async-start | bytes 1343488 | tf_op jit(solution)/shard_map/all_to_all | solution.py:18
  21.4 0.8 copy-start.2
  24.0 0.7 copy-start.3
  26.8 0.7 copy-start.1
  27.5 0.7 copy-start.4
  28.2 0.6 copy-start.6
  28.9 44.4 %all-to-all-start.1 = ((bf16[32,48,128]{2,1,0:T(8,128)(2,1)}), bf16[32,48,128]{2,1,0:T(8,128)(2,1)S(1)}, u32[]{:S(2)}, u32[]{:S(2)}) async-start(bf16[32,48,128]{2,1,0:T(8,128)(2,1)} %bitcast.250), calls=%async_computation.1 | async-start | bytes 786432 | tf_op jit(solution)/shard_map/all_to_all | solution.py:18
  35.8 10.3 %collective-permute-start.1 = (bf16[2,1,32,128]{3,2,1,0:T(8,128)(2,1)S(1)}, bf16[2,1,32,128]{3,2,1,0:T(8,128)(2,1)S(1)}, u32[]{:S(2)}, u32[]{:S(2)}) collective-permute-start(bf16[2,1,32,128]{3,2,1,0:T(8,128)(2,1)S(1)} %get-tuple-element.98), channel_id=1, source_target_pairs={{4,0},{8,4},{12,8},{16,12},{20,16},{24,20},{28,24},{36,32},{40,36}... | collective-permute-start | bytes 49160 | tf_op jit(solution)/shard_map/ppermute | solution.py:38
  37.1 8.2 %collective-permute-start = (bf16[2,1,32,128]{3,2,1,0:T(8,128)(2,1)S(1)}, bf16[2,1,32,128]{3,2,1,0:T(8,128)(2,1)S(1)}, u32[]{:S(2)}, u32[]{:S(2)}) collective-permute-start(bf16[2,1,32,128]{3,2,1,0:T(8,128)(2,1)S(1)} %get-tuple-element.99), channel_id=1, source_target_pairs={{0,4},{4,8},{8,12},{12,16},{16,20},{20,24},{24,28},{32,36},{36,40}... | collective-permute-start | bytes 49160 | tf_op jit(solution)/shard_map/ppermute | solution.py:38
  43.5 8.7 %collective-permute-start.2 = (bf16[2,2,128,128]{3,2,1,0:T(8,128)(2,1)S(1)}, bf16[2,2,128,128]{3,2,1,0:T(8,128)(2,1)S(1)}, u32[]{:S(2)}, u32[]{:S(2)}) collective-permute-start(bf16[2,2,128,128]{3,2,1,0:T(8,128)(2,1)S(1)} %dynamic-slice_bitcast_fusion.2), channel_id=1, source_target_pairs={{0,32},{32,0},{64,96},{96,64},{128,160},{160,128},{192,224},{224,1... | collective-permute-start | bytes 393224 | tf_op jit(solution)/shard_map/ppermute | solution.py:46
  46.1 9.7 %collective-permute-start.4 = (bf16[2,6,32,128]{3,2,1,0:T(8,128)(2,1)S(1)}, bf16[2,6,32,128]{3,2,1,0:T(8,128)(2,1)S(1)}, u32[]{:S(2)}, u32[]{:S(2)}) collective-permute-start(bf16[2,6,32,128]{3,2,1,0:T(8,128)(2,1)S(1)} %constant_dynamic-update-slice_fusion), channel_id=1, source_target_pairs={{0,128},{32,160},{64,192},{96,224},{128,0},{160,32},{192,64},{224,... | collective-permute-start | bytes 294920 | tf_op jit(solution)/shard_map/ppermute | solution.py:46
  53.2 15.5 %collective-permute-start.3 = (bf16[2,2,128,128]{3,2,1,0:T(8,128)(2,1)S(1)}, bf16[2,2,128,128]{3,2,1,0:T(8,128)(2,1)S(1)}, u32[]{:S(2)}, u32[]{:S(2)}) collective-permute-start(bf16[2,2,128,128]{3,2,1,0:T(8,128)(2,1)S(1)} %bitcast.275), channel_id=1, source_target_pairs={{0,64},{32,96},{64,0},{96,32},{128,192},{160,224},{192,128},{224,1... | collective-permute-start | bytes 393224 | tf_op jit(solution)/shard_map/ppermute | solution.py:46
  55.9 17.1 %collective-permute-start.5 = (bf16[2,2,6,32,128]{4,3,2,1,0:T(8,128)(2,1)S(1)}, bf16[2,2,6,32,128]{4,3,2,1,0:T(8,128)(2,1)S(1)}, u32[]{:S(2)}, u32[]{:S(2)}) collective-permute-start(bf16[2,2,6,32,128]{4,3,2,1,0:T(8,128)(2,1)S(1)} %pad_maximum_fusion.6), channel_id=1, source_target_pairs={{0,64},{32,96},{64,0},{96,32},{128,192},{160,224},{192,128},{224,1... | collective-permute-start | bytes 589832 | tf_op jit(solution)/shard_map/ppermute | solution.py:46
  68.8 8.8 %collective-permute-start.6 = (bf16[2,2,128,128]{3,2,1,0:T(8,128)(2,1)S(1)}, bf16[2,2,128,128]{3,2,1,0:T(8,128)(2,1)S(1)}, u32[]{:S(2)}, u32[]{:S(2)}) collective-permute-start(bf16[2,2,128,128]{3,2,1,0:T(8,128)(2,1)S(1)} %fusion.12), channel_id=1, source_target_pairs={{0,128},{32,160},{64,192},{96,224},{128,0},{160,32},{192,64},{224,... | collective-permute-start | bytes 393224 | tf_op jit(solution)/shard_map/ppermute | solution.py:46
  73.1 15.7 %collective-permute-start.7 = (bf16[2,2,2,6,32,128]{5,4,3,2,0,1:T(8,128)(2,1)S(1)}, bf16[2,2,2,6,32,128]{5,4,3,2,0,1:T(8,128)(2,1)S(1)}, u32[]{:S(2)}, u32[]{:S(2)}) collective-permute-start(bf16[2,2,2,6,32,128]{5,4,3,2,0,1:T(8,128)(2,1)S(1)} %pad_maximum_fusion.2), channel_id=1, source_target_pairs={{0,32},{32,0},{64,96},{96,64},{128,160},{160,128},{192,224},{224,1... | collective-permute-start | bytes 1179656 | tf_op jit(solution)/shard_map/ppermute | solution.py:46
  74.1 23.2 %all-to-all-start.2 = ((bf16[8,160,128]{2,1,0:T(8,128)(2,1)}), bf16[8,160,128]{2,1,0:T(8,128)(2,1)S(1)}, u32[]{:S(2)}, u32[]{:S(2)}) async-start(bf16[8,160,128]{2,1,0:T(8,128)(2,1)} %broadcast_in_dim.30), calls=%async_computation.2 | async-start | bytes 655360 | tf_op jit(solution)/shard_map/all_to_all | solution.py:18
  88.9 7.5 %copy-start.12 = (bf16[8,16,4,128]{3,2,1,0:T(4,128)(2,1)S(1)}, bf16[8,16,4,128]{3,2,1,0:T(4,128)(2,1)}, u32[]{:S(2)}) copy-start(bf16[8,16,4,128]{3,2,1,0:T(4,128)(2,1)} %param.11) | copy-start | bytes 393220
  91.7 9.8 %collective-permute-start.8 = (bf16[2,2,8,48,128]{4,3,1,0,2:T(8,128)(2,1)S(1)}, bf16[2,2,8,48,128]{4,3,1,0,2:T(8,128)(2,1)S(1)}, u32[]{:S(2)}, u32[]{:S(2)}) collective-permute-start(bf16[2,2,8,48,128]{4,3,1,0,2:T(8,128)(2,1)S(1)} %dynamic-slice_bitcast_fusion.1), channel_id=1, source_target_pairs={{0,8},{4,12},{8,0},{12,4},{16,24},{20,28},{24,16},{28,20},{1,9},{5... | collective-permute-start | bytes 1179656 | tf_op jit(solution)/shard_map/ppermute | solution.py:46
  101.6 25.4 %copy-start.11 = (bf16[8,16,4,128]{3,1,0,2:T(8,128)(2,1)S(1)}, bf16[8,16,4,128]{3,1,0,2:T(8,128)(2,1)}, u32[]{:S(2)}) copy-start(bf16[8,16,4,128]{3,1,0,2:T(8,128)(2,1)} %copy-done.10) | copy-start | bytes 393220
  101.7 8.2 %collective-permute-start.13 = (bf16[2,8,48,128]{3,2,0,1:T(8,128)(2,1)S(1)}, bf16[2,8,48,128]{3,2,0,1:T(8,128)(2,1)S(1)}, u32[]{:S(2)}, u32[]{:S(2)}) collective-permute-start(bf16[2,8,48,128]{3,2,0,1:T(8,128)(2,1)S(1)} %fusion.3), channel_id=1, source_target_pairs={{0,16},{4,20},{8,24},{12,28},{16,0},{20,4},{24,8},{28,12},{1,17},{... | collective-permute-start | bytes 589832 | tf_op jit(solution)/shard_map/ppermute | solution.py:46
  110.0 5.2 %collective-permute-start.14 = (bf16[8,48,128]{2,1,0:T(8,128)(2,1)S(1)}, bf16[8,48,128]{2,1,0:T(8,128)(2,1)S(1)}, u32[]{:S(2)}, u32[]{:S(2)}) collective-permute-start(bf16[8,48,128]{2,1,0:T(8,128)(2,1)S(1)} %fusion.19), channel_id=1, source_target_pairs={{0,4},{4,0},{8,12},{12,8},{16,20},{20,16},{24,28},{28,24},{1,5},{5... | collective-permute-start | bytes 294920 | tf_op jit(solution)/shard_map/ppermute | solution.py:46
  115.3 3.0 %collective-permute-start.15 = (bf16[2,2,48,128]{3,2,0,1:T(8,128)(2,1)S(1)}, bf16[2,2,48,128]{3,2,0,1:T(8,128)(2,1)S(1)}, u32[]{:S(2)}, u32[]{:S(2)}) collective-permute-start(bf16[2,2,48,128]{3,2,0,1:T(8,128)(2,1)S(1)} %bitcast.278), channel_id=1, source_target_pairs={{0,32},{32,0},{64,96},{96,64},{128,160},{160,128},{192,224},{224,1... | collective-permute-start | bytes 147464 | tf_op jit(solution)/shard_map/ppermute | solution.py:46
  118.3 7.8 %collective-permute-start.16 = (bf16[2,2,48,128]{3,2,1,0:T(8,128)(2,1)S(1)}, bf16[2,2,48,128]{3,2,1,0:T(8,128)(2,1)S(1)}, u32[]{:S(2)}, u32[]{:S(2)}) collective-permute-start(bf16[2,2,48,128]{3,2,1,0:T(8,128)(2,1)S(1)} %fusion.29), channel_id=1, source_target_pairs={{0,64},{32,96},{64,0},{96,32},{128,192},{160,224},{192,128},{224,1... | collective-permute-start | bytes 147464 | tf_op jit(solution)/shard_map/ppermute | solution.py:46
  120.3 16.5 %all-to-all-start.3 = ((bf16[8,400,128]{2,1,0:T(8,128)(2,1)}), bf16[8,400,128]{2,1,0:T(8,128)(2,1)S(1)}, u32[]{:S(2)}, u32[]{:S(2)}) async-start(bf16[8,400,128]{2,1,0:T(8,128)(2,1)} %broadcast_in_dim.31), calls=%async_computation.3 | async-start | bytes 1638400 | tf_op jit(solution)/shard_map/all_to_all | solution.py:18
  126.2 7.3 %collective-permute-start.17 = (bf16[2,2,48,128]{3,2,1,0:T(8,128)(2,1)S(1)}, bf16[2,2,48,128]{3,2,1,0:T(8,128)(2,1)S(1)}, u32[]{:S(2)}, u32[]{:S(2)}) collective-permute-start(bf16[2,2,48,128]{3,2,1,0:T(8,128)(2,1)S(1)} %fusion.25), channel_id=1, source_target_pairs={{0,128},{32,160},{64,192},{96,224},{128,0},{160,32},{192,64},{224,... | collective-permute-start | bytes 147464 | tf_op jit(solution)/shard_map/ppermute | solution.py:46
  133.5 4.4 %copy-start.7 = (bf16[2,6,32,128]{3,2,1,0:T(8,128)(2,1)S(1)}, bf16[2,6,32,128]{3,2,1,0:T(8,128)(2,1)}, u32[]{:S(2)}) copy-start(bf16[2,6,32,128]{3,2,1,0:T(8,128)(2,1)} %copy-done.6) | copy-start | bytes 294916
  133.5 9.4 %copy-start.8 = (bf16[128,27,128]{2,0,1:T(8,128)(2,1)S(1)}, bf16[128,27,128]{2,0,1:T(8,128)(2,1)}, u32[]{:S(2)}) copy-start(bf16[128,27,128]{2,0,1:T(8,128)(2,1)} %param.12) | copy-start | bytes 2654212
  133.6 9.4 %copy-start.9 = (bf16[128,512]{1,0:T(8,128)(2,1)S(1)}, bf16[128,512]{1,0:T(8,128)(2,1)}, u32[]{:S(2)}) copy-start(bf16[128,512]{1,0:T(8,128)(2,1)} %up_ref.1) | copy-start | bytes 393220
  137.8 20.4 %copy-start.5 = (f32[2,6,32,128]{3,2,1,0:T(8,128)S(1)}, f32[2,6,32,128]{3,2,1,0:T(8,128)}, u32[]{:S(2)}) copy-start(f32[2,6,32,128]{3,2,1,0:T(8,128)} %copy-done.4) | copy-start | bytes 589828
  137.9 20.2 %collective-permute-start.9 = (bf16[6,32,128]{2,1,0:T(8,128)(2,1)S(1)}, bf16[6,32,128]{2,1,0:T(8,128)(2,1)S(1)}, u32[]{:S(2)}, u32[]{:S(2)}) collective-permute-start(bf16[6,32,128]{2,1,0:T(8,128)(2,1)S(1)} %get-tuple-element.96), channel_id=1, source_target_pairs={{0,32},{4,36},{8,40},{12,44},{16,48},{20,52},{24,56},{28,60},{32,6... | collective-permute-start | bytes 147464 | tf_op jit(solution)/shard_map/ppermute | solution.py:38
  141.7 16.5 %collective-permute-start.10 = (bf16[6,32,128]{2,1,0:T(8,128)(2,1)S(1)}, bf16[6,32,128]{2,1,0:T(8,128)(2,1)}, u32[]{:S(2)}, u32[]{:S(2)}) collective-permute-start(bf16[6,32,128]{2,1,0:T(8,128)(2,1)S(1)} %get-tuple-element.97), channel_id=1, source_target_pairs={{32,0},{36,4},{40,8},{44,12},{48,16},{52,20},{56,24},{60,28},{64,3... | collective-permute-start | bytes 147464 | tf_op jit(solution)/shard_map/ppermute | solution.py:38
  145.9 24.9 %all-to-all-start.4 = ((bf16[8,64,128]{2,1,0:T(8,128)(2,1)}), bf16[8,64,128]{2,1,0:T(8,128)(2,1)S(1)}, u32[]{:S(2)}, u32[]{:S(2)}) async-start(bf16[8,64,128]{2,1,0:T(8,128)(2,1)} %bitcast.72), calls=%async_computation.4 | async-start | bytes 262144 | tf_op jit(solution)/shard_map/all_to_all | solution.py:18
  150.0 15.6 %collective-permute-start.18 = (bf16[2,992,128]{2,1,0:T(8,128)(2,1)S(1)}, bf16[2,992,128]{2,1,0:T(8,128)(2,1)S(1)}, u32[]{:S(2)}, u32[]{:S(2)}) collective-permute-start(bf16[2,992,128]{2,1,0:T(8,128)(2,1)S(1)} %dynamic-slice_bitcast_fusion), channel_id=1, source_target_pairs={{0,1},{1,0},{2,3},{3,2},{4,5},{5,4},{6,7},{7,6},{8,9},{9,8},{10,11... | collective-permute-start | bytes 1523720 | tf_op jit(solution)/shard_map/ppermute | solution.py:46
  159.0 6.5 %collective-permute-start.11 = (bf16[2,32,128]{2,1,0:T(8,128)(2,1)S(1)}, bf16[2,32,128]{2,1,0:T(8,128)(2,1)S(1)}, u32[]{:S(2)}, u32[]{:S(2)}) collective-permute-start(bf16[2,32,128]{2,1,0:T(8,128)(2,1)S(1)} %get-tuple-element.94), channel_id=1, source_target_pairs={{0,4},{4,8},{8,12},{12,16},{16,20},{20,24},{24,28},{32,36},{36,40}... | collective-permute-start | bytes 49160 | tf_op jit(solution)/shard_map/ppermute | solution.py:38
  164.2 6.0 %collective-permute-start.12 = (bf16[2,32,128]{2,1,0:T(8,128)(2,1)S(1)}, bf16[2,32,128]{2,1,0:T(8,128)(2,1)S(1)}, u32[]{:S(2)}, u32[]{:S(2)}) collective-permute-start(bf16[2,32,128]{2,1,0:T(8,128)(2,1)S(1)} %get-tuple-element.95), channel_id=1, source_target_pairs={{4,0},{8,4},{12,8},{16,12},{20,16},{24,20},{28,24},{36,32},{40,36}... | collective-permute-start | bytes 49160 | tf_op jit(solution)/shard_map/ppermute | solution.py:38
  165.7 8.2 %collective-permute-start.19 = (bf16[992,128]{1,0:T(8,128)(2,1)S(1)}, bf16[992,128]{1,0:T(8,128)(2,1)S(1)}, u32[]{:S(2)}, u32[]{:S(2)}) collective-permute-start(bf16[992,128]{1,0:T(8,128)(2,1)S(1)} %fusion.2), channel_id=1, source_target_pairs={{0,2},{1,3},{2,0},{3,1},{4,6},{5,7},{6,4},{7,5},{8,10},{9,11},{10,... | collective-permute-start | bytes 761864 | tf_op jit(solution)/shard_map/ppermute | solution.py:46

commit v4 on v2

v4 whole, which is shorter than its diff:
```python
import functools

import jax
import jax.numpy as jnp
from jax import lax
from jax.experimental import pallas as pl
from jax.experimental.pallas import tpu as pltpu
from jax.sharding import PartitionSpec as P

CLASSES = 14
CLASS_ROWS = 16
TAPS = 27
VMEM_LIMIT = 48 * 1024 * 1024
STEPS = (-1, 0, 1)


def exchange(x, axis):
    return lax.all_to_all(x, axis, split_axis=0, concat_axis=0, tiled=False)


def spread(x, axis):
    size = lax.axis_size(axis)
    return exchange(jnp.broadcast_to(x[None], (size,) + x.shape), axis)


def behind(x, *others):
    return lax.optimization_barrier((x,) + others)[0]


def neighbour(x, depth, height):
    nx, ny = lax.axis_size("gx"), lax.axis_size("gy")
    pairs = [
        (i * ny + j, (i + depth) * ny + j + height)
        for i in range(nx)
        for j in range(ny)
        if 0 <= i + depth < nx and 0 <= j + height < ny
    ]
    return lax.ppermute(x, ("gx", "gy"), pairs)


def bits_of(axis):
    return [1 << k for k in reversed(range(lax.axis_size(axis).bit_length() - 1))]


def swap(x, axis, bit):
    return lax.ppermute(x, axis, [(i, i ^ bit) for i in range(lax.axis_size(axis))])


def mine_and_other(x, axis, bit, dim):
    own = lax.axis_index(axis) // bit % 2
    take = functools.partial(lax.dynamic_index_in_dim, x, axis=dim, keepdims=False)
    return take(own), take(1 - own)


def summed_by_pairs(x, axis, bits):
    names = bits_of(axis)
    x = x.reshape((2,) * len(names) + x.shape[1:])
    left = list(names)
    steps = []
    for bit in bits:
        own, other = mine_and_other(x, axis, bit, left.index(bit))
        left.remove(bit)
        x = own.astype(jnp.float32) + swap(other.astype(jnp.bfloat16), axis, bit).astype(jnp.float32)
        steps.append(x)
    return x, steps


def dot_nn(a, b):
    return lax.dot_general(a, b, (((1,), (0,)), ((), ())), preferred_element_type=jnp.float32)


def dot_tn(a, b):
    return lax.dot_general(a, b, (((0,), (0,)), ((), ())), preferred_element_type=jnp.float32)


def dot_nt(a, b):
    return lax.dot_general(a, b, (((1,), (1,)), ((), ())), preferred_element_type=jnp.float32)


def moved(x, step, period):
    if step == 0:
        return x
    rows = x.shape[0]
    place = lax.rem(lax.broadcasted_iota(jnp.int32, x.shape, 0), period)
    edge = 0 if step == 1 else period - 1
    return jnp.where(place == edge, 0.0, pltpu.roll(x, step % rows, 0))


def local_call(body, out_shapes, scratch, flops, moved_bytes, *args):
    return pl.pallas_call(
        body,
        out_shape=list(out_shapes),
        in_specs=[
            pl.BlockSpec(memory_space=pltpu.SMEM if a.ndim == 1 else pltpu.VMEM) for a in args
        ],
        out_specs=[pl.BlockSpec(memory_space=pltpu.VMEM)] * len(out_shapes),
        scratch_shapes=scratch,
        cost_estimate=pl.CostEstimate(flops=flops, bytes_accessed=moved_bytes, transcendentals=0),
        compiler_params=pltpu.CompilerParams(vmem_limit_bytes=VMEM_LIMIT),
    )(*args)


def class_kernel(gathered_ref, own_ref, label_ref, *out_refs):
    plane_refs, aux_ref = out_refs[:-1], out_refs[-1]
    groups, rows, inner = gathered_ref.shape[0], own_ref.shape[0], own_ref.shape[1]
    logits = jnp.zeros((CLASS_ROWS, rows), jnp.float32)
    for c in range(groups):
        weight = gathered_ref[c, 2 * rows : 2 * rows + CLASS_ROWS]
        logits += dot_nt(weight, jnp.maximum(gathered_ref[c, :rows], 0))
    place = lax.broadcasted_iota(jnp.int32, logits.shape, 0)
    real = place < CLASSES
    logits = jnp.where(real, logits, -jnp.inf)
    powers = jnp.exp(logits - jnp.max(logits, axis=0, keepdims=True))
    probabilities = powers / jnp.sum(powers, axis=0, keepdims=True)
    onehot = jnp.where(place == label_ref[...], 1.0, 0.0)
    logit_grad = jnp.where(real, probabilities - onehot, 0.0).astype(jnp.bfloat16)
    for c in range(groups):
        weight = gathered_ref[c, 2 * rows : 2 * rows + CLASS_ROWS]
        total = gathered_ref[c, rows : 2 * rows].astype(jnp.float32) + dot_tn(logit_grad, weight)
        active = gathered_ref[c, :rows].astype(jnp.float32) > 0
        grad = jnp.where(active, total, 0.0).astype(jnp.bfloat16)
        size = rows // len(plane_refs)
        for d, plane_ref in enumerate(plane_refs):
            plane_ref[:, c * inner : (c + 1) * inner] = grad[d * size : (d + 1) * size]
    aux_ref[...] = dot_nn(logit_grad, jnp.maximum(own_ref[...], 0)).astype(jnp.bfloat16)


def conv_kernel(*refs):
    planes, (low_ref, high_ref, weight_ref) = refs[:-8], refs[-8:-5]
    far_ref, out_ref, part_ref, acc_ref, pool_ref = refs[-5:]
    far_d, far_h, width, full = far_ref.shape
    depth, height = far_d - 2, far_h - 2
    inner = out_ref.shape[1]
    rows = depth * height * width
    for d, plane_ref in enumerate(planes):
        far_ref[d, 1 : 1 + height] = plane_ref[...].reshape(height, width, full)
    far_ref[:, 0] = low_ref[...]
    far_ref[:, far_h - 1] = high_ref[...]
    total = jnp.zeros((rows, inner), jnp.float32)
    terms = [total] * 3
    for a in STEPS:
        for b in STEPS:
            piece = far_ref[1 - a : 1 - a + depth, 1 - b : 1 - b + height].reshape(rows, full)
            for c in STEPS:
                tap = 9 * (a + 1) + 3 * (b + 1) + c + 1
                terms[c + 1] += dot_nt(piece, weight_ref[:, tap * full : (tap + 1) * full])
    for c in STEPS:
        total += moved(terms[c + 1], c, width)
    out_ref[...] = total.astype(jnp.bfloat16)

    half_d, half_h, half_w = depth // 2, height // 2, width // 2
    nc = part_ref.shape[0]
    block = half_w // nc
    window = part_ref.shape[1] // (half_d * half_h)
    pool_ref[...] = jnp.zeros_like(pool_ref)
    lines = total.reshape(depth, height, width, inner)
    for d in range(half_d):
        for h in range(half_h):
            acc_ref[...] = (
                lines[2 * d, 2 * h]
                + lines[2 * d, 2 * h + 1]
                + lines[2 * d + 1, 2 * h]
                + lines[2 * d + 1, 2 * h + 1]
            )
            pool_ref[d, h, 8 : 8 + half_w] = (
                acc_ref[pl.ds(0, half_w, stride=2)] + acc_ref[pl.ds(1, half_w, stride=2)]
            )
    for c in range(nc):
        start = 7 + c * block
        part_ref[c] = jnp.concatenate(
            [pool_ref[d, h, start : start + window] for d in range(half_d) for h in range(half_h)],
            axis=0,
        ).astype(jnp.bfloat16)


def kernel_grad_kernel(chunk, place_ref, far_ref, input_ref, *refs):
    out_refs, all_ref, turn_ref = refs[:-2], refs[-2], refs[-1]
    far_d, far_h, width, full = far_ref.shape
    depth, height = far_d - 2, far_h - 2
    rows, inner = input_ref.shape
    by_height, by_depth, window, _ = all_ref.shape
    lanes = height * width
    flat = input_ref[...].astype(jnp.float32)
    wide = jnp.concatenate([moved(flat, -c, width).astype(jnp.bfloat16) for c in STEPS], axis=1)
    for d in range(far_d):
        for b in range(3):
            turn_ref[d, b] = far_ref[d, b : b + height].reshape(lanes, full).T
    for a in STEPS:
        for b in STEPS:
            turned = jnp.concatenate([turn_ref[1 - a + d, 1 - b] for d in range(depth)], axis=1)
            terms = dot_nn(turned, wide).astype(jnp.bfloat16)
            for c in range(3):
                first = (9 * (a + 1) + 3 * (b + 1) + c) * full
                for owner in range(by_depth * by_height):
                    start = owner * chunk // 16 * 16
                    low, high = max(start, first), min(start + window, first + full)
                    if low < high:
                        all_ref[owner % by_height, owner // by_height, low - start : high - start] = terms[
                            low - first : high - first, c * inner : (c + 1) * inner
                        ]
    for k, out_ref in enumerate(out_refs):
        out_ref[...] = all_ref[place_ref[0] ^ k]


def bottom_kernel(
    down_ref,
    up_ref,
    before_ref,
    pre_ref,
    after_ref,
    source_ref,
    weight_ref,
    part_ref,
    both_ref,
    shift_ref,
):
    _, far_d, far_w, height, filters = shift_ref.shape
    depth, width = far_d - 2, far_w - 2
    rows = depth * width * height
    channels = source_ref.shape[1]
    groups = both_ref.shape[0]
    thin = channels // groups
    full = down_ref.shape[1]
    inner = full // groups
    back = dot_nt(down_ref[...], up_ref[...])
    own_saved = pre_ref[...].reshape(rows, filters)
    saved = jnp.concatenate([before_ref[...], pre_ref[...], after_ref[...]], axis=1)
    saved = saved.reshape(depth * far_w * height, filters)
    grad = jnp.where(saved.astype(jnp.float32) > 0, back, 0.0)
    shift_ref[:, :1] = jnp.zeros((3, 1) + shift_ref.shape[2:], jnp.bfloat16)
    shift_ref[:, far_d - 1 :] = jnp.zeros((3, 1) + shift_ref.shape[2:], jnp.bfloat16)
    for b in STEPS:
        shift_ref[b + 1, 1 : 1 + depth] = (
            moved(grad, b, height).astype(jnp.bfloat16).reshape(depth, far_w, height, filters)
        )
    own_down = down_ref[...].reshape(depth, far_w, height, full)[:, 1 : 1 + width].reshape(rows, full)
    up_part = dot_tn(jnp.maximum(own_saved, 0), own_down).astype(jnp.bfloat16)
    for cc in range(groups):
        both_ref[cc, TAPS * thin :] = up_part[:, cc * inner : (cc + 1) * inner]
    turned = source_ref[...].T
    total = jnp.zeros((rows, channels), jnp.float32)
    for a in STEPS:
        for b in STEPS:
            tap = 9 * (a + 1) + 3 * (b + 1)
            piece = jnp.concatenate(
                [
                    shift_ref[b + 1, 1 - a : 1 - a + depth, 1 - c : 1 - c + width].reshape(rows, filters)
                    for c in STEPS
                ],
                axis=1,
            )
            weight = jnp.concatenate([weight_ref[tap + c] for c in range(3)], axis=1)
            total += dot_nt(piece, weight)
            terms = dot_nn(turned, piece).astype(jnp.bfloat16)
            for c in range(3):
                for cc in range(groups):
                    both_ref[cc, (tap + c) * thin : (tap + c + 1) * thin] = terms[
                        cc * thin : (cc + 1) * thin, c * filters : (c + 1) * filters
                    ]
    part_ref[...] = total.astype(jnp.bfloat16)


def per_device(
    pre_bottom,
    bottom_input,
    bottom_weight,
    up_weight,
    level_input,
    pre_level,
    level_cotangent,
    labels,
    level_weight,
    aux_weight,
):
    nx, ny, nc = (lax.axis_size(a) for a in ("gx", "gy", "col"))
    at_x, at_y = lax.axis_index("gx"), lax.axis_index("gy")
    depth, height, width, inner = level_input.shape
    full = inner * nc
    rows = depth * height * width
    far_d, far_h = depth + 2, height + 2
    half_d, half_h, half_w = depth // 2, height // 2, width // 2
    block = half_w // nc
    wide = block + 2
    bottom_d, bottom_h, _, filters = pre_bottom.shape
    bf16, f32 = jnp.bfloat16, jnp.float32
    struct = jax.ShapeDtypeStruct

    own_pre = pre_level.reshape(rows, inner)
    payload = jnp.concatenate(
        [
            own_pre,
            level_cotangent.reshape(rows, inner),
            jnp.pad(aux_weight.T, ((0, CLASS_ROWS - CLASSES), (0, 0))),
        ]
    )
    gathered = lax.all_gather(payload, "col")
    lanes = height * width
    *planes, aux_part = local_call(
        class_kernel,
        [struct((lanes, full), bf16)] * depth + [struct((CLASS_ROWS, inner), bf16)],
        [],
        6 * rows * full * CLASS_ROWS,
        2 * gathered.size,
        gathered,
        own_pre,
        labels.reshape(1, rows),
    )

    planes = [neighbour(planes[-1], 1, 0)] + planes + [neighbour(planes[0], -1, 0)]
    low = neighbour(jnp.stack([p[lanes - width :] for p in planes]), 0, 1)
    high = neighbour(jnp.stack([p[:width] for p in planes]), 0, -1)

    window = (wide + 7) // 8 * 8
    cells = half_d * half_h * window
    far, level_input_grad, parts = local_call(
        conv_kernel,
        (
            struct((far_d, far_h, width, full), bf16),
            struct((rows, inner), bf16),
            struct((nc, cells, inner), bf16),
        ),
        [
            pltpu.VMEM((width, inner), f32),
            pltpu.VMEM((half_d, half_h, half_w + 24, inner), f32),
        ],
        2 * rows * full * TAPS * inner,
        2 * level_weight.size,
        *planes,
        low,
        high,
        level_weight,
    )
    level_input_grad = level_input_grad.reshape(level_input.shape)

    relayed = exchange(parts, "col").reshape(nc * cells, inner)

    chunk = TAPS * full // (nx * ny)
    span = chunk + 8 if chunk % 16 else chunk
    level_parts = local_call(
        functools.partial(kernel_grad_kernel, chunk),
        [struct((nx, span, inner), bf16)] * ny,
        [
            pltpu.VMEM((ny, nx, span, inner), bf16),
            pltpu.VMEM((far_d, 3, full, lanes), bf16),
        ],
        2 * rows * full * TAPS * inner,
        2 * nx * ny * span * inner,
        jnp.full((1,), at_y, jnp.int32),
        far,
        level_input.reshape(rows, inner),
    )
    relayed = behind(relayed, level_parts[0])

    turned_pre = pre_bottom.transpose(0, 2, 1, 3)
    edges = behind(turned_pre, parts)
    ups = [(i, i + 1) for i in range(nc - 1)]
    downs = [(j, i) for i, j in ups]
    pre_before = lax.ppermute(edges[:, -1:], "col", ups)
    pre_after = lax.ppermute(edges[:, :1], "col", downs)

    by_depth = spread(jnp.concatenate([relayed, aux_part]), "gx")
    aux_sum = by_depth[:, nc * cells :].astype(f32).sum(axis=0).astype(bf16)
    line = by_depth[:, : nc * cells].reshape(nx, nc, half_d * half_h, window, inner)[:, :, :, :wide]
    split = nx * nc * half_d * half_h * wide
    by_height = spread(jnp.concatenate([line.reshape(split, inner), aux_sum]), "gy")
    aux_weight_grad = by_height[:, split : split + CLASSES].astype(f32).sum(axis=0).T
    down_wide = (
        by_height[:, :split]
        .reshape(ny, nx, nc, half_d, half_h, wide, inner)
        .transpose(1, 3, 5, 0, 4, 2, 6)
        .reshape(bottom_d * wide * bottom_h, full)
    )

    level_part = level_parts[0].astype(f32)
    for k in range(1, ny):
        level_part += swap(level_parts[k], "gy", k).astype(f32)
    level_part = exchange(level_part.astype(bf16), "gx").astype(f32).sum(axis=0)
    if span != chunk:
        odd = lax.rem(at_y + at_x * ny, 2)
        level_part = jnp.where(odd == 1, level_part[span - chunk :], level_part[:chunk])
    level_weight_grad = level_part.T

    bottom_rows = bottom_d * block * bottom_h
    channel_width = bottom_weight.shape[0]
    thin = channel_width // nc
    part, both = local_call(
        bottom_kernel,
        (
            struct((bottom_rows, channel_width), bf16),
            struct((nc, TAPS * thin + filters, inner), bf16),
        ),
        [pltpu.VMEM((3, bottom_d + 2, wide, bottom_h, filters), bf16)],
        4 * bottom_rows * channel_width * TAPS * filters,
        2 * bottom_weight.size,
        down_wide,
        up_weight,
        pre_before,
        turned_pre,
        pre_after,
        bottom_input.transpose(0, 2, 1, 3).reshape(bottom_rows, channel_width),
        bottom_weight.transpose(1, 0, 2),
    )
    share = bottom_d // ny
    bottom_input_grad = (
        exchange(part.reshape(ny, bottom_rows // ny, channel_width), "gy")
        .astype(f32)
        .sum(axis=0)
        .astype(bf16)
        .reshape(share, block, bottom_h, channel_width)
        .transpose(0, 2, 1, 3)
    )
    both, _ = summed_by_pairs(both, "col", bits_of("col")[::-1])
    bottom_weight_grad = both[: TAPS * thin].reshape(TAPS, thin, filters).transpose(1, 0, 2)
    up_weight_grad = both[TAPS * thin :]
    return (
        level_input_grad,
        bottom_input_grad,
        level_weight_grad,
        bottom_weight_grad,
        up_weight_grad,
        aux_weight_grad,
    )


def solution(mesh):
    return jax.shard_map(
        per_device,
        mesh=mesh,
        in_specs=(
            P(None, None, "col", "gy"),
            P(None, None, "col", "gx"),
            P("gx", None, "gy"),
            P("gy", None),
            P("gx", "gy", None, "col"),
            P("gx", "gy", None, "col"),
            P("gx", "gy", None, "col"),
            P("gx", "gy", None),
            P("col", None),
            P("col", None),
        ),
        out_specs=(
            P("gx", "gy", None, "col"),
            P("gy", None, "col", "gx"),
            P("col", ("gx", "gy")),
            P(("gx", "col"), None, "gy"),
            P("gy", "col"),
            P("col", None),
        ),
        check_vma=False,
    )
```

time: 194 us -> 164 us (0.85)
  blocking collectives: 57.8 us -> 25.8 us
  starting transfers between devices: 64 us -> 52.9 us
  waiting for transfers between devices: 44.2 us -> 53 us
  local copies, waits for them, and re-layouts: 11.4 us -> 14 us
    all_to_all x2 -> x1, blocking collectives: 57.8 us -> 16.2 us  [exchange(): return lax.all_to_all(x, axis, split_axis=0, concat_axis=0, tiled=False)]
    ppermute x2 -> x11, waiting for transfers between devices: 0.01 us -> 31.6 us  [the longest x9 20 us: swap(): lax.ppermute(x, axis, [(i, i ^ bit) for i in range(lax.axis_size(axis))])]
    all_to_all x6 -> x4, waiting for transfers between devices: 35.8 us -> 9.87 us  [exchange(): return lax.all_to_all(x, axis, split_axis=0, concat_axis=0, tiled=False)]
    ppermute x2 -> x11, starting transfers between devices: 5.8 us -> 22 us  [the longest x9 14.1 us: swap(): lax.ppermute(x, axis, [(i, i ^ bit) for i in range(lax.axis_size(axis))])]
    all_to_all x6 -> x4, starting transfers between devices: 36.9 us -> 21.4 us  [exchange(): return lax.all_to_all(x, axis, split_axis=0, concat_axis=0, tiled=False)]
    ppermute x8 -> x4, starting transfers between devices: 21.3 us -> 9.46 us  [neighbour(): return lax.ppermute(x, ('gx', 'gy'), pairs)]
    all_gather x0 -> x1, blocking collectives: none -> 9.63 us  [per_device(): gathered = lax.all_gather(payload, 'col')]
    reduce_sum x5 -> x1, other arithmetic: 3.72 us -> 0.06 us  [per_device(): level_part = exchange(level_part.astype(bf16), 'gx').astype(f32).sum(axis=0)]
  transfers between devices with their start and end apart: 16 -> 19, of which waited for: 7 -> 8; matrix products, arithmetic and copies ran while one was open for 5% -> 6% of each run, Pallas kernels for 3% -> 3%
where the time goes in v4:
time: 164 us; the launch traced here: 163 us
  waiting for transfers between devices  53 us (32%)
  starting transfers between devices  52.9 us (32%)
  blocking collectives  25.8 us (16%)
  local copies, waits for them, and re-layouts  14 us (9%)
  Pallas kernels  8.83 us (5%)
  other arithmetic  7.4 us (5%)
    all_to_all x4, starting transfers between devices, exchange(): return lax.all_to_all(x, axis, split_axis=0, concat_axis=0, tiled=False)  21.4 us
    ppermute x9, waiting for transfers between devices, swap(): lax.ppermute(x, axis, [(i, i ^ bit) for i in range(lax.axis_size(axis))])  20 us
    all_to_all x1, blocking collectives, exchange(): return lax.all_to_all(x, axis, split_axis=0, concat_axis=0, tiled=False)  16.2 us
    ppermute x9, starting transfers between devices, swap(): lax.ppermute(x, axis, [(i, i ^ bit) for i in range(lax.axis_size(axis))])  14.1 us
    ppermute x1, waiting for transfers between devices, per_device(): pre_after = lax.ppermute(edges[:, :1], 'col', downs)  11.6 us
    ppermute x4, waiting for transfers between devices, neighbour(): return lax.ppermute(x, ('gx', 'gy'), pairs)  11.5 us
    all_to_all x4, waiting for transfers between devices, exchange(): return lax.all_to_all(x, axis, split_axis=0, concat_axis=0, tiled=False)  9.87 us
    all_gather x1, blocking collectives, per_device(): gathered = lax.all_gather(payload, 'col')  9.63 us
  transfers between devices with their start and end apart: 19, of which 8 were waited for; matrix products, arithmetic and copies ran while one was open for 6% of the time, Pallas kernels for 3%

profile of v4, /device:TPU:1, one launch (start us, length us, event | category | flops | bytes accessed | tf_op | source)
XLA Modules:
  0.0 163.0 jit_solution(15934242263779826046)
XLA Ops:
  0.6 0.8 reshape.64.label_ref
  1.4 0.9 fusion.2
  2.3 9.6 %all-gather = bf16[2112,128]{1,0:T(8,128)(2,1)S(1)} all-gather(bf16[528,128]{1,0:T(8,128)(2,1)S(1)} %fusion.2), channel_id=2, replica_groups=mesh['gx'=8,'gy'=8,'col'=4] {'col'}, dimensions={0}, use_global_device_ids=true | all-gather | bytes 675840 | tf_op jit(solution)/shard_map/all_gather | solution.py:296
  12.0 0.8 copy-done.1
  12.8 0.6 shard_map.145
  13.4 2.5 %collective-permute-start = (bf16[128,512]{1,0:T(8,128)(2,1)S(1)}, bf16[128,512]{1,0:T(8,128)(2,1)S(1)}, u32[]{:S(2)}, u32[]{:S(2)}) collective-permute-start(bf16[128,512]{1,0:T(8,128)(2,1)S(1)} %get-tuple-element.24.refs_2_), channel_id=1, source_target_pairs={{0,32},{4,36},{8,40},{12,44},{16,48},{20,52},{24,56},{28,60},{32,6... | collective-permute-start | bytes 393224 | tf_op jit(solution)/shard_map/ppermute | solution.py:38
  15.9 1.3 collective-permute-start.1
  17.3 1.4 collective-permute-done.refs_0_
  18.7 4.2 %collective-permute-done.1.refs_3_ = bf16[128,512]{1,0:T(8,128)(2,1)S(1)} collective-permute-done((bf16[128,512]{1,0:T(8,128)(2,1)S(1)}, bf16[128,512]{1,0:T(8,128)(2,1)S(1)}, u32[]{:S(2)}, u32[]{:S(2)}) %collective-permute-start.1) | collective-permute-done | bytes 131104 | tf_op jit(solution)/shard_map/ppermute | solution.py:38
  22.9 4.4 %collective-permute-start.2 = (bf16[4,32,512]{2,1,0:T(8,128)(2,1)S(1)}, bf16[4,32,512]{2,1,0:T(8,128)(2,1)S(1)}, u32[]{:S(2)}, u32[]{:S(2)}) collective-permute-start(bf16[4,32,512]{2,1,0:T(8,128)(2,1)S(1)} %pad_maximum_fusion), channel_id=1, source_target_pairs={{0,4},{4,8},{8,12},{12,16},{16,20},{20,24},{24,28},{32,36},{36,40}... | collective-permute-start | bytes 393224 | tf_op jit(solution)/shard_map/ppermute | solution.py:38
  27.3 1.3 collective-permute-start.3
  28.6 0.6 collective-permute-done.2.refs_4_
  29.2 5.3 %collective-permute-done.3.refs_5_ = bf16[4,32,512]{2,1,0:T(8,128)(2,1)S(1)} collective-permute-done((bf16[4,32,512]{2,1,0:T(8,128)(2,1)S(1)}, bf16[4,32,512]{2,1,0:T(8,128)(2,1)S(1)}, u32[]{:S(2)}, u32[]{:S(2)}) %collective-permute-start.3) | collective-permute-done | bytes 131104 | tf_op jit(solution)/shard_map/ppermute | solution.py:38
  34.5 2.0 %copy-done = bf16[128,13824]{1,0:T(8,128)(2,1)S(1)} copy-done((bf16[128,13824]{1,0:T(8,128)(2,1)S(1)}, bf16[128,13824]{1,0:T(8,128)(2,1)}, u32[]{:S(2)}) %copy-start) | copy-done | bytes 3538968
  36.5 2.7 %shard_map.146 = (bf16[4,6,32,512]{3,2,1,0:T(8,128)(2,1)S(1)}, bf16[256,128]{1,0:T(8,128)(2,1)}, bf16[4,16,128]{2,1,0:T(8,128)(2,1)}) custom-call(bf16[128,512]{1,0:T(8,128)(2,1)S(1)} %collective-permute-done.refs_0_, bf16[128,512]{1,0:T(8,128)(2,1)S(1)} %get-tuple-element.25.refs_1_, bf16[128,512]{1,0:T(8,128)(2,1)S(1)} %get-tuple-element.24.refs_2_, ...), custom_call_target="tpu_custom_call" | custom-call | flops 905969664 | bytes 3538944 | tf_op jit(solution)/shard_map/pallas_call | solution.py:90
  39.2 5.7 %all-to-all-start = ((bf16[4,16,128]{2,1,0:T(8,128)(2,1)}), bf16[4,16,128]{2,1,0:T(8,128)(2,1)S(1)}, u32[]{:S(2)}, u32[]{:S(2)}) async-start(bf16[4,16,128]{2,1,0:T(8,128)(2,1)} %get-tuple-element.27), calls=%async_computation | async-start | bytes 32768 | tf_op jit(solution)/shard_map/all_to_all | solution.py:18
  44.9 2.6 %shard_map.147 = (bf16[8,224,128]{2,1,0:T(8,128)(2,1)S(1)}, bf16[8,224,128]{2,1,0:T(8,128)(2,1)S(1)}, bf16[8,224,128]{2,1,0:T(8,128)(2,1)S(1)}, bf16[8,224,128]{...) custom-call(s32[1]{0:T(128)} %bitcast.14.place_ref, ...), custom_call_target="tpu_custom_call" | custom-call | flops 905969664 | bytes 3670016 | tf_op jit(solution)/shard_map/pallas_call | solution.py:90
  47.5 0.7 copy-done.3
  48.3 16.2 %all_to_all.25 = bf16[8,80,128]{2,1,0:T(8,128)(2,1)S(1)} all-to-all(bf16[8,80,128]{2,1,0:T(8,128)(2,1)S(1)} %broadcast_in_dim.7), channel_id=1, replica_groups=mesh['gx'=8,'gy'=8,'col'=4] {'gx'}, dimensions={0} | all-to-all | bytes 327680 | tf_op jit(solution)/shard_map/all_to_all | solution.py:18
  64.6 1.0 broadcast_in_dim.8
  65.7 6.0 %all-to-all-start.2 = ((bf16[8,400,128]{2,1,0:T(8,128)(2,1)}), bf16[8,400,128]{2,1,0:T(8,128)(2,1)}, u32[]{:S(2)}, u32[]{:S(2)}) async-start(bf16[8,400,128]{2,1,0:T(8,128)(2,1)} %broadcast_in_dim.8), calls=%async_computation.2 | async-start | bytes 1638400 | tf_op jit(solution)/shard_map/all_to_all | solution.py:18
  71.7 3.0 %collective-permute-start.6 = (bf16[8,224,128]{2,1,0:T(8,128)(2,1)S(1)}, bf16[8,224,128]{2,1,0:T(8,128)(2,1)S(1)}, u32[]{:S(2)}, u32[]{:S(2)}) collective-permute-start(bf16[8,224,128]{2,1,0:T(8,128)(2,1)S(1)} %copy-done.4), channel_id=1, source_target_pairs={{0,4},{4,0},{8,12},{12,8},{16,20},{20,16},{24,28},{28,24},{1,5},{5... | collective-permute-start | bytes 1376264 | tf_op jit(solution)/shard_map/ppermute | solution.py:46
  74.8 1.2 collective-permute-start.7
  76.0 5.3 %collective-permute-start.5 = (bf16[8,1,16,128]{3,2,1,0:T(8,128)(2,1)S(1)}, bf16[8,1,16,128]{3,2,1,0:T(8,128)(2,1)S(1)}, u32[]{:S(2)}, u32[]{:S(2)}) collective-permute-start(bf16[8,1,16,128]{3,2,1,0:T(8,128)(2,1)S(1)} %get-tuple-element.54), channel_id=1, source_target_pairs={{1,0},{2,1},{3,2},{5,4},{6,5},{7,6},{9,8},{10,9},{11,10},{13,12},{... | collective-permute-start | bytes 98312 | tf_op jit(solution)/shard_map/ppermute | solution.py:359
  81.3 2.6 %collective-permute-start.4 = (bf16[8,1,16,128]{3,2,1,0:T(8,128)(2,1)S(1)}, bf16[8,1,16,128]{3,2,1,0:T(8,128)(2,1)S(1)}, u32[]{:S(2)}, u32[]{:S(2)}) collective-permute-start(bf16[8,1,16,128]{3,2,1,0:T(8,128)(2,1)S(1)} %get-tuple-element.55), channel_id=1, source_target_pairs={{0,1},{1,2},{2,3},{4,5},{5,6},{6,7},{8,9},{9,10},{10,11},{12,13},{... | collective-permute-start | bytes 98312 | tf_op jit(solution)/shard_map/ppermute | solution.py:358
  84.4 11.6 %collective-permute-done.5.after_ref = bf16[8,1,16,128]{3,2,1,0:T(8,128)(2,1)S(1)} collective-permute-done((bf16[8,1,16,128]{3,2,1,0:T(8,128)(2,1)S(1)}, bf16[8,1,16,128]{3,2,1,0:T(8,128)(2,1)S(1)}, u32[]{:S(2)}, u32[]{:S(2)}) %collective-permute-start.5) | collective-permute-done | bytes 32800 | tf_op jit(solution)/shard_map/ppermute | solution.py:359
  96.1 3.4 %collective-permute-start.9 = (bf16[8,224,128]{2,1,0:T(8,128)(2,1)}, bf16[8,224,128]{2,1,0:T(8,128)(2,1)}, u32[]{:S(2)}, u32[]{:S(2)}) collective-permute-start(bf16[8,224,128]{2,1,0:T(8,128)(2,1)} %get-tuple-element.37), channel_id=1, source_target_pairs={{0,16},{4,20},{8,24},{12,28},{16,0},{20,4},{24,8},{28,12},{1,17},{... | collective-permute-start | bytes 1376264 | tf_op jit(solution)/shard_map/ppermute | solution.py:46
  99.4 3.3 %collective-permute-start.10 = (bf16[8,224,128]{2,1,0:T(8,128)(2,1)}, bf16[8,224,128]{2,1,0:T(8,128)(2,1)}, u32[]{:S(2)}, u32[]{:S(2)}) collective-permute-start(bf16[8,224,128]{2,1,0:T(8,128)(2,1)} %get-tuple-element.38), channel_id=1, source_target_pairs={{0,20},{4,16},{8,28},{12,24},{16,4},{20,0},{24,12},{28,8},{1,21},{... | collective-permute-start | bytes 1376264 | tf_op jit(solution)/shard_map/ppermute | solution.py:46
  102.7 2.4 %collective-permute-start.11 = (bf16[8,224,128]{2,1,0:T(8,128)(2,1)S(1)}, bf16[8,224,128]{2,1,0:T(8,128)(2,1)}, u32[]{:S(2)}, u32[]{:S(2)}) collective-permute-start(bf16[8,224,128]{2,1,0:T(8,128)(2,1)S(1)} %get-tuple-element.39), channel_id=1, source_target_pairs={{0,24},{4,28},{8,16},{12,20},{16,8},{20,12},{24,0},{28,4},{1,25},{... | collective-permute-start | bytes 1376264 | tf_op jit(solution)/shard_map/ppermute | solution.py:46
  105.1 0.8 copy-done.12
  106.1 0.9 copy.27
  107.0 1.2 slice.83
  109.3 0.9 copy-done.5
  110.2 0.8 copy-done.8
  111.0 0.8 copy-done.10
  111.7 2.9 %shard_map.148 = (bf16[512,128]{1,0:T(8,128)(2,1)}, bf16[4,992,128]{2,1,0:T(8,128)(2,1)S(1)}) custom-call(bf16[768,512]{1,0:T(8,128)(2,1)S(1)} %bitcast.66, bf16[128,512]{1,0:T(8,128)(2,1)S(1)} %copy-done.5, bf16[8,1,16,128]{3,2,1,0:T(8,128)(2,1)S(1)} %copy-done.10, bf16[8,4,16,128]{3,2,1,0:T(8,128)(2,1)S(1)} %bitcast.68, ...), custom_call_target="tpu_custom_call" | custom-call | flops 905969664 | bytes 884736 | tf_op jit(solution)/shard_map/pallas_call | solution.py:90
  114.7 6.2 %all-to-all-start.3 = ((bf16[8,64,128]{2,1,0:T(8,128)(2,1)}), bf16[8,64,128]{2,1,0:T(8,128)(2,1)S(1)}, u32[]{:S(2)}, u32[]{:S(2)}) async-start(bf16[8,64,128]{2,1,0:T(8,128)(2,1)} %bitcast.23), calls=%async_computation.3 | async-start | bytes 262144 | tf_op jit(solution)/shard_map/all_to_all | solution.py:18
  121.0 14.7 %collective-permute-done.9 = bf16[8,224,128]{2,1,0:T(8,128)(2,1)} collective-permute-done((bf16[8,224,128]{2,1,0:T(8,128)(2,1)}, bf16[8,224,128]{2,1,0:T(8,128)(2,1)}, u32[]{:S(2)}, u32[]{:S(2)}) %collective-permute-start.9) | collective-permute-done | bytes 458784 | tf_op jit(solution)/shard_map/ppermute | solution.py:46
  135.7 5.3 %collective-permute-done.11 = bf16[8,224,128]{2,1,0:T(8,128)(2,1)} collective-permute-done((bf16[8,224,128]{2,1,0:T(8,128)(2,1)S(1)}, bf16[8,224,128]{2,1,0:T(8,128)(2,1)}, u32[]{:S(2)}, u32[]{:S(2)}) %collective-permute-start.11) | collective-permute-done | bytes 458784 | tf_op jit(solution)/shard_map/ppermute | solution.py:46
  141.0 3.1 %add_convert_fusion = bf16[8,224,128]{2,1,0:T(8,128)(2,1)} fusion(bf16[8,224,128]{2,1,0:T(8,128)(2,1)} %collective-permute-done.12, bf16[8,224,128]{2,1,0:T(8,128)(2,1)} %collective-permute-done.11, bf16[8,224,128]{2,1,0:T(8,128)(2,1)} %collective-permute-done.10, bf16[8,224,128]{2,1,0:T(8,128)(2,1)} %collective-permute-done.9, ...), kind=kLoop, calls=%fused_computation.2 | loop fusion | flops 3670016 | bytes 4128768 | tf_op jit(solution)/shard_map/convert_element_type | solution.py:377
  144.1 3.5 %all-to-all-start.4 = ((bf16[8,224,128]{2,1,0:T(8,128)(2,1)}), bf16[8,224,128]{2,1,0:T(8,128)(2,1)S(1)}, u32[]{:S(2)}, u32[]{:S(2)}) async-start(bf16[8,224,128]{2,1,0:T(8,128)(2,1)} %add_convert_fusion), calls=%async_computation.4 | async-start | bytes 917504 | tf_op jit(solution)/shard_map/all_to_all | solution.py:18
  147.6 1.4 convert_reduce_fusion.1
  149.0 0.6 copy.29
  149.6 1.2 convert_add_fusion
  151.0 9.9 %all-to-all-done.4 = bf16[8,224,128]{2,1,0:T(8,128)(2,1)S(1)} async-done(((bf16[8,224,128]{2,1,0:T(8,128)(2,1)}), bf16[8,224,128]{2,1,0:T(8,128)(2,1)S(1)}, u32[]{:S(2)}, u32[]{:S(2)}) %all-to-all-start.4) | async-done | bytes 458784 | tf_op jit(solution)/shard_map/all_to_all | solution.py:18
  160.9 0.7 fusion.3
  161.6 0.6 slice.87
  162.2 0.8 slice.86
  (57 shorter events, 2.4 us)
Async XLA Ops:
  0.6 44.3 %copy-start.6 = (bf16[2,4,32,128]{3,2,1,0:T(8,128)(2,1)S(1)}, bf16[2,4,32,128]{3,2,1,0:T(8,128)(2,1)}, u32[]{:S(2)}) copy-start(bf16[2,4,32,128]{3,2,1,0:T(8,128)(2,1)} %param.14) | copy-start | bytes 196612
  12.0 0.8 copy-start.1
  13.4 5.2 %collective-permute-start = (bf16[128,512]{1,0:T(8,128)(2,1)S(1)}, bf16[128,512]{1,0:T(8,128)(2,1)S(1)}, u32[]{:S(2)}, u32[]{:S(2)}) collective-permute-start(bf16[128,512]{1,0:T(8,128)(2,1)S(1)} %get-tuple-element.24.refs_2_), channel_id=1, source_target_pairs={{0,32},{4,36},{8,40},{12,44},{16,48},{20,52},{24,56},{28,60},{32,6... | collective-permute-start | bytes 393224 | tf_op jit(solution)/shard_map/ppermute | solution.py:38
  15.9 6.9 %collective-permute-start.1 = (bf16[128,512]{1,0:T(8,128)(2,1)S(1)}, bf16[128,512]{1,0:T(8,128)(2,1)S(1)}, u32[]{:S(2)}, u32[]{:S(2)}) collective-permute-start(bf16[128,512]{1,0:T(8,128)(2,1)S(1)} %get-tuple-element.25.refs_1_), channel_id=1, source_target_pairs={{32,0},{36,4},{40,8},{44,12},{48,16},{52,20},{56,24},{60,28},{64,3... | collective-permute-start | bytes 393224 | tf_op jit(solution)/shard_map/ppermute | solution.py:38
  22.9 6.3 %collective-permute-start.2 = (bf16[4,32,512]{2,1,0:T(8,128)(2,1)S(1)}, bf16[4,32,512]{2,1,0:T(8,128)(2,1)S(1)}, u32[]{:S(2)}, u32[]{:S(2)}) collective-permute-start(bf16[4,32,512]{2,1,0:T(8,128)(2,1)S(1)} %pad_maximum_fusion), channel_id=1, source_target_pairs={{0,4},{4,8},{8,12},{12,16},{16,20},{20,24},{24,28},{32,36},{36,40}... | collective-permute-start | bytes 393224 | tf_op jit(solution)/shard_map/ppermute | solution.py:38
  27.3 7.2 %collective-permute-start.3 = (bf16[4,32,512]{2,1,0:T(8,128)(2,1)S(1)}, bf16[4,32,512]{2,1,0:T(8,128)(2,1)S(1)}, u32[]{:S(2)}, u32[]{:S(2)}) collective-permute-start(bf16[4,32,512]{2,1,0:T(8,128)(2,1)S(1)} %pad_maximum_fusion.1), channel_id=1, source_target_pairs={{4,0},{8,4},{12,8},{16,12},{20,16},{24,20},{28,24},{36,32},{40,36}... | collective-permute-start | bytes 393224 | tf_op jit(solution)/shard_map/ppermute | solution.py:38
  34.5 2.0 %copy-start = (bf16[128,13824]{1,0:T(8,128)(2,1)S(1)}, bf16[128,13824]{1,0:T(8,128)(2,1)}, u32[]{:S(2)}) copy-start(bf16[128,13824]{1,0:T(8,128)(2,1)} %refs_6_.1) | copy-start | bytes 10616836
  39.2 9.1 %all-to-all-start = ((bf16[4,16,128]{2,1,0:T(8,128)(2,1)}), bf16[4,16,128]{2,1,0:T(8,128)(2,1)S(1)}, u32[]{:S(2)}, u32[]{:S(2)}) async-start(bf16[4,16,128]{2,1,0:T(8,128)(2,1)} %get-tuple-element.27), calls=%async_computation | async-start | bytes 32768 | tf_op jit(solution)/shard_map/all_to_all | solution.py:18
  44.9 31.0 %copy-start.13 = (bf16[8,16,4,128]{3,2,1,0:T(4,128)(2,1)S(1)}, bf16[8,16,4,128]{3,2,1,0:T(4,128)(2,1)}, u32[]{:S(2)}) copy-start(bf16[8,16,4,128]{3,2,1,0:T(4,128)(2,1)} %param.10) | copy-start | bytes 393220
  47.5 0.8 copy-start.3
  48.3 23.4 %copy-start.4 = (bf16[8,224,128]{2,1,0:T(8,128)(2,1)S(1)}, bf16[8,224,128]{2,1,0:T(8,128)(2,1)}, u32[]{:S(2)}) copy-start(bf16[8,224,128]{2,1,0:T(8,128)(2,1)} %copy-done.3) | copy-start | bytes 1376260
  65.7 41.3 %all-to-all-start.2 = ((bf16[8,400,128]{2,1,0:T(8,128)(2,1)}), bf16[8,400,128]{2,1,0:T(8,128)(2,1)}, u32[]{:S(2)}, u32[]{:S(2)}) async-start(bf16[8,400,128]{2,1,0:T(8,128)(2,1)} %broadcast_in_dim.8), calls=%async_computation.2 | async-start | bytes 1638400 | tf_op jit(solution)/shard_map/all_to_all | solution.py:18
  71.7 37.6 %copy-start.2 = (bf16[128,27,128]{2,0,1:T(8,128)(2,1)S(1)}, bf16[128,27,128]{2,0,1:T(8,128)(2,1)}, u32[]{:S(2)}) copy-start(bf16[128,27,128]{2,0,1:T(8,128)(2,1)} %param.12) | copy-start | bytes 2654212
  71.7 31.0 %collective-permute-start.6 = (bf16[8,224,128]{2,1,0:T(8,128)(2,1)S(1)}, bf16[8,224,128]{2,1,0:T(8,128)(2,1)S(1)}, u32[]{:S(2)}, u32[]{:S(2)}) collective-permute-start(bf16[8,224,128]{2,1,0:T(8,128)(2,1)S(1)} %copy-done.4), channel_id=1, source_target_pairs={{0,4},{4,0},{8,12},{12,8},{16,20},{20,16},{24,28},{28,24},{1,5},{5... | collective-permute-start | bytes 1376264 | tf_op jit(solution)/shard_map/ppermute | solution.py:46
  74.8 30.4 %collective-permute-start.7 = (bf16[8,224,128]{2,1,0:T(8,128)(2,1)S(1)}, bf16[8,224,128]{2,1,0:T(8,128)(2,1)S(1)}, u32[]{:S(2)}, u32[]{:S(2)}) collective-permute-start(bf16[8,224,128]{2,1,0:T(8,128)(2,1)S(1)} %get-tuple-element.35), channel_id=1, source_target_pairs={{0,8},{4,12},{8,0},{12,4},{16,24},{20,28},{24,16},{28,20},{1,9},{5... | collective-permute-start | bytes 1376264 | tf_op jit(solution)/shard_map/ppermute | solution.py:46
  76.0 20.1 %collective-permute-start.5 = (bf16[8,1,16,128]{3,2,1,0:T(8,128)(2,1)S(1)}, bf16[8,1,16,128]{3,2,1,0:T(8,128)(2,1)S(1)}, u32[]{:S(2)}, u32[]{:S(2)}) collective-permute-start(bf16[8,1,16,128]{3,2,1,0:T(8,128)(2,1)S(1)} %get-tuple-element.54), channel_id=1, source_target_pairs={{1,0},{2,1},{3,2},{5,4},{6,5},{7,6},{9,8},{10,9},{11,10},{13,12},{... | collective-permute-start | bytes 98312 | tf_op jit(solution)/shard_map/ppermute | solution.py:359
  81.3 18.1 %collective-permute-start.4 = (bf16[8,1,16,128]{3,2,1,0:T(8,128)(2,1)S(1)}, bf16[8,1,16,128]{3,2,1,0:T(8,128)(2,1)S(1)}, u32[]{:S(2)}, u32[]{:S(2)}) collective-permute-start(bf16[8,1,16,128]{3,2,1,0:T(8,128)(2,1)S(1)} %get-tuple-element.55), channel_id=1, source_target_pairs={{0,1},{1,2},{2,3},{4,5},{5,6},{6,7},{8,9},{9,10},{10,11},{12,13},{... | collective-permute-start | bytes 98312 | tf_op jit(solution)/shard_map/ppermute | solution.py:358
  83.9 37.0 %collective-permute-start.8 = (bf16[8,224,128]{2,1,0:T(8,128)(2,1)}, bf16[8,224,128]{2,1,0:T(8,128)(2,1)}, u32[]{:S(2)}, u32[]{:S(2)}) collective-permute-start(bf16[8,224,128]{2,1,0:T(8,128)(2,1)} %get-tuple-element.36), channel_id=1, source_target_pairs={{0,12},{4,8},{8,4},{12,0},{16,28},{20,24},{24,20},{28,16},{1,13},{... | collective-permute-start | bytes 1376264 | tf_op jit(solution)/shard_map/ppermute | solution.py:46
  96.1 13.2 %copy-start.7 = (bf16[8,1,16,128]{3,2,1,0:T(8,128)(2,1)}, bf16[8,1,16,128]{3,2,1,0:T(8,128)(2,1)S(1)}, u32[]{:S(2)}) copy-start(bf16[8,1,16,128]{3,2,1,0:T(8,128)(2,1)S(1)} %collective-permute-done.5.after_ref) | copy-start | bytes 98308
  96.1 39.6 %collective-permute-start.9 = (bf16[8,224,128]{2,1,0:T(8,128)(2,1)}, bf16[8,224,128]{2,1,0:T(8,128)(2,1)}, u32[]{:S(2)}, u32[]{:S(2)}) collective-permute-start(bf16[8,224,128]{2,1,0:T(8,128)(2,1)} %get-tuple-element.37), channel_id=1, source_target_pairs={{0,16},{4,20},{8,24},{12,28},{16,0},{20,4},{24,8},{28,12},{1,17},{... | collective-permute-start | bytes 1376264 | tf_op jit(solution)/shard_map/ppermute | solution.py:46
  99.4 9.9 %copy-start.9 = (bf16[8,1,16,128]{3,2,1,0:T(8,128)(2,1)}, bf16[8,1,16,128]{3,2,1,0:T(8,128)(2,1)S(1)}, u32[]{:S(2)}) copy-start(bf16[8,1,16,128]{3,2,1,0:T(8,128)(2,1)S(1)} %collective-permute-done.4.before_ref) | copy-start | bytes 98308
  99.4 36.3 %collective-permute-start.10 = (bf16[8,224,128]{2,1,0:T(8,128)(2,1)}, bf16[8,224,128]{2,1,0:T(8,128)(2,1)}, u32[]{:S(2)}, u32[]{:S(2)}) collective-permute-start(bf16[8,224,128]{2,1,0:T(8,128)(2,1)} %get-tuple-element.38), channel_id=1, source_target_pairs={{0,20},{4,16},{8,28},{12,24},{16,4},{20,0},{24,12},{28,8},{1,21},{... | collective-permute-start | bytes 1376264 | tf_op jit(solution)/shard_map/ppermute | solution.py:46
  102.7 2.4 %copy-start.11 = (bf16[8,224,128]{2,1,0:T(8,128)(2,1)}, bf16[8,224,128]{2,1,0:T(8,128)(2,1)S(1)}, u32[]{:S(2)}) copy-start(bf16[8,224,128]{2,1,0:T(8,128)(2,1)S(1)} %collective-permute-done.6) | copy-start | bytes 1376260
  102.7 38.2 %collective-permute-start.11 = (bf16[8,224,128]{2,1,0:T(8,128)(2,1)S(1)}, bf16[8,224,128]{2,1,0:T(8,128)(2,1)}, u32[]{:S(2)}, u32[]{:S(2)}) collective-permute-start(bf16[8,224,128]{2,1,0:T(8,128)(2,1)S(1)} %get-tuple-element.39), channel_id=1, source_target_pairs={{0,24},{4,28},{8,16},{12,20},{16,8},{20,12},{24,0},{28,4},{1,25},{... | collective-permute-start | bytes 1376264 | tf_op jit(solution)/shard_map/ppermute | solution.py:46
  105.1 0.8 copy-start.12
  105.9 35.1 %collective-permute-start.12 = (bf16[8,224,128]{2,1,0:T(8,128)(2,1)S(1)}, bf16[8,224,128]{2,1,0:T(8,128)(2,1)}, u32[]{:S(2)}, u32[]{:S(2)}) collective-permute-start(bf16[8,224,128]{2,1,0:T(8,128)(2,1)S(1)} %get-tuple-element.40), channel_id=1, source_target_pairs={{0,28},{4,24},{8,20},{12,16},{16,12},{20,8},{24,4},{28,0},{1,29},{... | collective-permute-start | bytes 1376264 | tf_op jit(solution)/shard_map/ppermute | solution.py:46
  109.3 0.9 copy-start.5
  110.2 0.8 copy-start.8
  111.0 0.8 copy-start.10
  114.7 29.4 %all-to-all-start.3 = ((bf16[8,64,128]{2,1,0:T(8,128)(2,1)}), bf16[8,64,128]{2,1,0:T(8,128)(2,1)S(1)}, u32[]{:S(2)}, u32[]{:S(2)}) async-start(bf16[8,64,128]{2,1,0:T(8,128)(2,1)} %bitcast.23), calls=%async_computation.3 | async-start | bytes 262144 | tf_op jit(solution)/shard_map/all_to_all | solution.py:18
  120.9 28.7 %collective-permute-start.13 = (bf16[2,992,128]{2,1,0:T(8,128)(2,1)S(1)}, bf16[2,992,128]{2,1,0:T(8,128)(2,1)}, u32[]{:S(2)}, u32[]{:S(2)}) collective-permute-start(bf16[2,992,128]{2,1,0:T(8,128)(2,1)S(1)} %dynamic-slice_bitcast_fusion), channel_id=1, source_target_pairs={{0,1},{1,0},{2,3},{3,2},{4,5},{5,4},{6,7},{7,6},{8,9},{9,8},{10,11... | collective-permute-start | bytes 1523720 | tf_op jit(solution)/shard_map/ppermute | solution.py:46
  144.1 16.7 %all-to-all-start.4 = ((bf16[8,224,128]{2,1,0:T(8,128)(2,1)}), bf16[8,224,128]{2,1,0:T(8,128)(2,1)S(1)}, u32[]{:S(2)}, u32[]{:S(2)}) async-start(bf16[8,224,128]{2,1,0:T(8,128)(2,1)} %add_convert_fusion), calls=%async_computation.4 | async-start | bytes 917504 | tf_op jit(solution)/shard_map/all_to_all | solution.py:18
  150.9 10.7 %collective-permute-start.14 = (bf16[992,128]{1,0:T(8,128)(2,1)S(1)}, bf16[992,128]{1,0:T(8,128)(2,1)S(1)}, u32[]{:S(2)}, u32[]{:S(2)}) collective-permute-start(bf16[992,128]{1,0:T(8,128)(2,1)S(1)} %fusion.1), channel_id=1, source_target_pairs={{0,2},{1,3},{2,0},{3,1},{4,6},{5,7},{6,4},{7,5},{8,10},{9,11},{10,... | collective-permute-start | bytes 761864 | tf_op jit(solution)/shard_map/ppermute | solution.py:46

commit v5 on v4

--- a/solution.py
+++ b/solution.py
@@ -86,12 +86,15 @@
     return jnp.where(place == edge, 0.0, pltpu.roll(x, step % rows, 0))
 
 
-def local_call(body, out_shapes, scratch, flops, moved_bytes, *args):
+def local_call(body, out_shapes, scratch, flops, moved_bytes, *args, stay=None):
     return pl.pallas_call(
         body,
         out_shape=list(out_shapes),
         in_specs=[
-            pl.BlockSpec(memory_space=pltpu.SMEM if a.ndim == 1 else pltpu.VMEM) for a in args
+            pl.BlockSpec(
+                memory_space=pl.ANY if k == stay else pltpu.SMEM if a.ndim == 1 else pltpu.VMEM
+            )
+            for k, a in enumerate(args)
         ],
         out_specs=[pl.BlockSpec(memory_space=pltpu.VMEM)] * len(out_shapes),
         scratch_shapes=scratch,
@@ -126,21 +129,36 @@
 
 
 def conv_kernel(*refs):
-    planes, (low_ref, high_ref, weight_ref) = refs[:-8], refs[-8:-5]
-    far_ref, out_ref, part_ref, acc_ref, pool_ref = refs[-5:]
+    side_ref, planes, (low_ref, high_ref, input_ref, weight_hbm) = refs[0], refs[1:-12], refs[-12:-8]
+    far_ref, out_ref, part_ref, send_ref, acc_ref, pool_ref, weight_ref, sems = refs[-8:]
     far_d, far_h, width, full = far_ref.shape
     depth, height = far_d - 2, far_h - 2
     inner = out_ref.shape[1]
     rows = depth * height * width
+    copies = []
+    for k in range(9):
+        span = pl.ds(3 * k * full, 3 * full)
+        copies.append(
+            pltpu.make_async_copy(weight_hbm.at[:, span], weight_ref.at[:, span], sems.at[k])
+        )
+        copies[k].start()
     for d, plane_ref in enumerate(planes):
         far_ref[d, 1 : 1 + height] = plane_ref[...].reshape(height, width, full)
     far_ref[:, 0] = low_ref[...]
     far_ref[:, far_h - 1] = high_ref[...]
+    sent = far_d // 2
+    send_ref[: sent * far_h * width] = far_ref[pl.ds(sent * side_ref[0], sent)].reshape(-1, full)
+    piece_rows = rows * inner // full
+    for c in range(full // inner):
+        send_ref[sent * far_h * width :, c * inner : (c + 1) * inner] = input_ref[
+            c * piece_rows : (c + 1) * piece_rows
+        ]
     total = jnp.zeros((rows, inner), jnp.float32)
     terms = [total] * 3
     for a in STEPS:
         for b in STEPS:
             piece = far_ref[1 - a : 1 - a + depth, 1 - b : 1 - b + height].reshape(rows, full)
+            copies[3 * (a + 1) + b + 1].wait()
             for c in STEPS:
                 tap = 9 * (a + 1) + 3 * (b + 1) + c + 1
                 terms[c + 1] += dot_nt(piece, weight_ref[:, tap * full : (tap + 1) * full])
@@ -173,33 +191,46 @@
         ).astype(jnp.bfloat16)
 
 
-def kernel_grad_kernel(chunk, place_ref, far_ref, input_ref, *refs):
-    out_refs, all_ref, turn_ref = refs[:-2], refs[-2], refs[-1]
+def kernel_grad_kernel(chunk, place_ref, far_ref, input_ref, got_ref, *refs):
+    out_refs, (all_ref, flat_ref, pair_ref, turn_ref, wide_ref) = refs[:-5], refs[-5:]
     far_d, far_h, width, full = far_ref.shape
     depth, height = far_d - 2, far_h - 2
     rows, inner = input_ref.shape
     by_height, by_depth, window, _ = all_ref.shape
     lanes = height * width
-    flat = input_ref[...].astype(jnp.float32)
-    wide = jnp.concatenate([moved(flat, -c, width).astype(jnp.bfloat16) for c in STEPS], axis=1)
-    for d in range(far_d):
+    side, at_y = place_ref[0], place_ref[1]
+    sent = far_d // 2
+    pair_ref[pl.ds(depth * side, far_d)] = far_ref[...]
+    pair_ref[pl.ds(far_d * (1 - side), depth)] = got_ref[: sent * far_h * width].reshape(
+        sent, far_h, width, full
+    )
+    piece_rows = rows * inner // full
+    other = jnp.concatenate(
+        [
+            got_ref[sent * far_h * width :, c * inner : (c + 1) * inner]
+            for c in range(full // inner)
+        ],
+        axis=0,
+    )
+    for c in STEPS:
+        wide_ref[c + 1, side] = moved(input_ref[...].astype(jnp.float32), -c, width).astype(jnp.bfloat16)
+        wide_ref[c + 1, 1 - side] = moved(other.astype(jnp.float32), -c, width).astype(jnp.bfloat16)
+    for d in range(far_d + depth):
         for b in range(3):
-            turn_ref[d, b] = far_ref[d, b : b + height].reshape(lanes, full).T
-    for a in STEPS:
-        for b in STEPS:
-            turned = jnp.concatenate([turn_ref[1 - a + d, 1 - b] for d in range(depth)], axis=1)
-            terms = dot_nn(turned, wide).astype(jnp.bfloat16)
-            for c in range(3):
-                first = (9 * (a + 1) + 3 * (b + 1) + c) * full
-                for owner in range(by_depth * by_height):
-                    start = owner * chunk // 16 * 16
-                    low, high = max(start, first), min(start + window, first + full)
-                    if low < high:
-                        all_ref[owner % by_height, owner // by_height, low - start : high - start] = terms[
-                            low - first : high - first, c * inner : (c + 1) * inner
-                        ]
+            turn_ref[d, b] = pair_ref[d, b : b + height].reshape(lanes, full).T
+    half = full // 2
+    for step in range(TAPS // 2 + 1):
+        tap = TAPS // 2 * side + step
+        a, b, c = tap // 9, lax.rem(tap // 3, 3), lax.rem(tap, 3)
+        turned = jnp.concatenate([turn_ref[2 - a + d, 2 - b] for d in range(2 * depth)], axis=1)
+        terms = dot_nn(turned, wide_ref[c].reshape(2 * rows, inner))
+        first = pl.multiple_of(step * full + half - half * side, half)
+        flat_ref[pl.ds(first, full)] = terms.astype(jnp.bfloat16)
+    for owner in range(by_depth * by_height):
+        start = half + owner * chunk // 16 * 16
+        all_ref[owner % by_height, owner // by_height] = flat_ref[start : start + window]
     for k, out_ref in enumerate(out_refs):
-        out_ref[...] = all_ref[place_ref[0] ^ k]
+        out_ref[...] = all_ref[at_y ^ k]
 
 
 def bottom_kernel(
@@ -209,11 +240,15 @@
     pre_ref,
     after_ref,
     source_ref,
-    weight_ref,
+    weight_hbm,
     part_ref,
     both_ref,
     shift_ref,
+    weight_ref,
+    sem,
 ):
+    copy = pltpu.make_async_copy(weight_hbm, weight_ref, sem)
+    copy.start()
     _, far_d, far_w, height, filters = shift_ref.shape
     depth, width = far_d - 2, far_w - 2
     rows = depth * width * height
@@ -239,6 +274,7 @@
         both_ref[cc, TAPS * thin :] = up_part[:, cc * inner : (cc + 1) * inner]
     turned = source_ref[...].T
     total = jnp.zeros((rows, channels), jnp.float32)
+    copy.wait()
     for a in STEPS:
         for b in STEPS:
             tap = 9 * (a + 1) + 3 * (b + 1)
@@ -312,24 +348,33 @@
 
     window = (wide + 7) // 8 * 8
     cells = half_d * half_h * window
-    far, level_input_grad, parts = local_call(
+    side = lax.rem(at_x, 2).astype(jnp.int32)
+    flat_input = level_input.reshape(rows, inner)
+    far, level_input_grad, parts, send = local_call(
         conv_kernel,
         (
             struct((far_d, far_h, width, full), bf16),
             struct((rows, inner), bf16),
             struct((nc, cells, inner), bf16),
+            struct((far_d // 2 * far_h * width + rows * inner // full, full), bf16),
         ),
         [
             pltpu.VMEM((width, inner), f32),
             pltpu.VMEM((half_d, half_h, half_w + 24, inner), f32),
+            pltpu.VMEM(level_weight.shape, bf16),
+            pltpu.SemaphoreType.DMA((9,)),
         ],
         2 * rows * full * TAPS * inner,
         2 * level_weight.size,
+        side.reshape(1),
         *planes,
         low,
         high,
+        flat_input,
         level_weight,
-    )
+        stay=len(planes) + 4,
+    )
+    got = swap(send, "gx", 1)
     level_input_grad = level_input_grad.reshape(level_input.shape)
 
     relayed = exchange(parts, "col").reshape(nc * cells, inner)
@@ -338,17 +383,22 @@
     span = chunk + 8 if chunk % 16 else chunk
     level_parts = local_call(
         functools.partial(kernel_grad_kernel, chunk),
-        [struct((nx, span, inner), bf16)] * ny,
+        [struct((nx // 2, span, inner), bf16)] * ny,
         [
-            pltpu.VMEM((ny, nx, span, inner), bf16),
-            pltpu.VMEM((far_d, 3, full, lanes), bf16),
+            pltpu.VMEM((ny, nx // 2, span, inner), bf16),
+            pltpu.VMEM(((TAPS + 2) * full // 2, inner), bf16),
+            pltpu.VMEM((far_d + depth, far_h, width, full), bf16),
+            pltpu.VMEM((far_d + depth, 3, full, lanes), bf16),
+            pltpu.VMEM((3, 2, rows, inner), bf16),
         ],
         2 * rows * full * TAPS * inner,
         2 * nx * ny * span * inner,
-        jnp.full((1,), at_y, jnp.int32),
+        jnp.stack([side, at_y.astype(jnp.int32)]),
         far,
-        level_input.reshape(rows, inner),
-    )
+        flat_input,
+        got,
+    )
+    terms = [level_parts[0]] + [swap(level_parts[k], "gy", k) for k in range(1, ny)]
     relayed = behind(relayed, level_parts[0])
 
     turned_pre = pre_bottom.transpose(0, 2, 1, 3)
@@ -360,6 +410,7 @@
 
     by_depth = spread(jnp.concatenate([relayed, aux_part]), "gx")
     aux_sum = by_depth[:, nc * cells :].astype(f32).sum(axis=0).astype(bf16)
+    by_depth = behind(by_depth, *terms[1 : ny // 2])
     line = by_depth[:, : nc * cells].reshape(nx, nc, half_d * half_h, window, inner)[:, :, :, :wide]
     split = nx * nc * half_d * half_h * wide
     by_height = spread(jnp.concatenate([line.reshape(split, inner), aux_sum]), "gy")
@@ -371,10 +422,18 @@
         .reshape(bottom_d * wide * bottom_h, full)
     )
 
-    level_part = level_parts[0].astype(f32)
-    for k in range(1, ny):
-        level_part += swap(level_parts[k], "gy", k).astype(f32)
-    level_part = exchange(level_part.astype(bf16), "gx").astype(f32).sum(axis=0)
+    level_part = sum(t.astype(f32) for t in terms).astype(bf16)
+    down_wide = behind(down_wide, level_part)
+    pairs = nx // 2
+    level_sum = jnp.zeros((span, inner), f32)
+    for step in range(pairs):
+        chosen = lax.dynamic_index_in_dim(
+            level_part, lax.rem(at_x // 2 + step, pairs), 0, keepdims=False
+        )
+        level_sum += lax.ppermute(
+            chosen, "gx", [(i, i % 2 * pairs + (i // 2 + step) % pairs) for i in range(nx)]
+        ).astype(f32)
+    level_part = level_sum
     if span != chunk:
         odd = lax.rem(at_y + at_x * ny, 2)
         level_part = jnp.where(odd == 1, level_part[span - chunk :], level_part[:chunk])
@@ -389,7 +448,11 @@
             struct((bottom_rows, channel_width), bf16),
             struct((nc, TAPS * thin + filters, inner), bf16),
         ),
-        [pltpu.VMEM((3, bottom_d + 2, wide, bottom_h, filters), bf16)],
+        [
+            pltpu.VMEM((3, bottom_d + 2, wide, bottom_h, filters), bf16),
+            pltpu.VMEM((TAPS, channel_width, filters), bf16),
+            pltpu.SemaphoreType.DMA(()),
+        ],
         4 * bottom_rows * channel_width * TAPS * filters,
         2 * bottom_weight.size,
         down_wide,
@@ -399,6 +462,7 @@
         pre_after,
         bottom_input.transpose(0, 2, 1, 3).reshape(bottom_rows, channel_width),
         bottom_weight.transpose(1, 0, 2),
+        stay=6,
     )
     share = bottom_d // ny
     bottom_input_grad = (

time: 164 us -> 157 us (0.957)
  starting transfers between devices: 52.9 us -> 80.6 us
  waiting for transfers between devices: 53 us -> 36.2 us
  blocking collectives: 25.8 us -> 9.63 us
  local copies, waits for them, and re-layouts: 14 us -> 10.1 us
  Pallas kernels: 8.83 us -> 11.9 us
  other arithmetic: 7.4 us -> 5.01 us
    all_to_all x1 -> x0, blocking collectives: 16.2 us -> none  [exchange(): return lax.all_to_all(x, axis, split_axis=0, concat_axis=0, tiled=False)]
    ppermute x0 -> x4, starting transfers between devices: none -> 12.9 us  [per_device(): lax.ppermute(chosen, 'gx', [(i, i % 2 * pairs + (i // 2 + step) % pairs)...]
    ppermute x1, waiting for transfers between devices: 11.6 us -> 0.01 us  [per_device(): pre_after = lax.ppermute(edges[:, :1], 'col', downs)]
    ppermute x1, starting transfers between devices: 2.58 us -> 13.2 us  [per_device(): pre_before = lax.ppermute(edges[:, -1:], 'col', ups)]
    ppermute x0 -> x4, waiting for transfers between devices: none -> 6.17 us  [per_device(): lax.ppermute(chosen, 'gx', [(i, i % 2 * pairs + (i // 2 + step) % pairs)...]
    ppermute x9 -> x10, waiting for transfers between devices: 20 us -> 14.2 us  [swap(): lax.ppermute(x, axis, [(i, i ^ bit) for i in range(lax.axis_size(axis))])]
    all_to_all x4, waiting for transfers between devices: 9.87 us -> 4.27 us  [exchange(): return lax.all_to_all(x, axis, split_axis=0, concat_axis=0, tiled=False)]
    pallas_call x4, Pallas kernels: 8.83 us -> 11.9 us  [local_call(): pl.pallas_call(body, out_shape=list(out_shapes), in_specs=[pl.BlockSpec(m...]
  transfers between devices with their start and end apart: 19 -> 24, of which waited for: 8 -> 13; matrix products, arithmetic and copies ran while one was open for 6% -> 4% of each run, Pallas kernels for 3% -> 2%
where the time goes in v5:
time: 157 us; the launch traced here: 155 us
  starting transfers between devices  80.6 us (51%)
  waiting for transfers between devices  36.2 us (23%)
  Pallas kernels  11.9 us (8%)
  local copies, waits for them, and re-layouts  10.1 us (6%)
  blocking collectives  9.63 us (6%)
  other arithmetic  5.01 us (3%)
    all_to_all x4, starting transfers between devices, exchange(): return lax.all_to_all(x, axis, split_axis=0, concat_axis=0, tiled=False)  22.4 us
    ppermute x10, starting transfers between devices, swap(): lax.ppermute(x, axis, [(i, i ^ bit) for i in range(lax.axis_size(axis))])  15.6 us
    ppermute x10, waiting for transfers between devices, swap(): lax.ppermute(x, axis, [(i, i ^ bit) for i in range(lax.axis_size(axis))])  14.2 us
    ppermute x1, starting transfers between devices, per_device(): pre_before = lax.ppermute(edges[:, -1:], 'col', ups)  13.2 us
    ppermute x4, starting transfers between devices, per_device(): lax.ppermute(chosen, 'gx', [(i, i % 2 * pairs + (i // 2 + step) % pairs)...  12.9 us
    pallas_call x4, Pallas kernels, local_call(): pl.pallas_call(body, out_shape=list(out_shapes), in_specs=[pl.BlockSpec(m...  11.9 us
    ppermute x4, waiting for transfers between devices, neighbour(): return lax.ppermute(x, ('gx', 'gy'), pairs)  11.5 us
    all_gather x1, blocking collectives, per_device(): gathered = lax.all_gather(payload, 'col')  9.63 us
  transfers between devices with their start and end apart: 24, of which 13 were waited for; matrix products, arithmetic and copies ran while one was open for 4% of the time, Pallas kernels for 2%

profile of v5, /device:TPU:1, one launch (start us, length us, event | category | flops | bytes accessed | tf_op | source)
XLA Modules:
  0.0 154.6 jit_solution(7522422221556359718)
XLA Ops:
  0.6 0.8 reshape.68.label_ref
  1.4 0.9 fusion.2
  2.3 9.6 %all-gather = bf16[2112,128]{1,0:T(8,128)(2,1)S(1)} all-gather(bf16[528,128]{1,0:T(8,128)(2,1)S(1)} %fusion.2), channel_id=2, replica_groups=mesh['gx'=8,'gy'=8,'col'=4] {'col'}, dimensions={0}, use_global_device_ids=true | all-gather | bytes 675840 | tf_op jit(solution)/shard_map/all_gather | solution.py:332
  12.0 0.8 copy-done.1
  13.4 2.5 %collective-permute-start = (bf16[128,512]{1,0:T(8,128)(2,1)S(1)}, bf16[128,512]{1,0:T(8,128)(2,1)S(1)}, u32[]{:S(2)}, u32[]{:S(2)}) collective-permute-start(bf16[128,512]{1,0:T(8,128)(2,1)S(1)} %get-tuple-element.27.refs_3_), channel_id=1, source_target_pairs={{0,32},{4,36},{8,40},{12,44},{16,48},{20,52},{24,56},{28,60},{32,6... | collective-permute-start | bytes 393224 | tf_op jit(solution)/shard_map/ppermute | solution.py:38
  15.9 1.3 collective-permute-start.1
  17.3 1.4 collective-permute-done.refs_1_
  18.7 4.2 %collective-permute-done.1.refs_4_ = bf16[128,512]{1,0:T(8,128)(2,1)S(1)} collective-permute-done((bf16[128,512]{1,0:T(8,128)(2,1)S(1)}, bf16[128,512]{1,0:T(8,128)(2,1)S(1)}, u32[]{:S(2)}, u32[]{:S(2)}) %collective-permute-start.1) | collective-permute-done | bytes 131104 | tf_op jit(solution)/shard_map/ppermute | solution.py:38
  22.9 4.4 %collective-permute-start.2 = (bf16[4,32,512]{2,1,0:T(8,128)(2,1)S(1)}, bf16[4,32,512]{2,1,0:T(8,128)(2,1)S(1)}, u32[]{:S(2)}, u32[]{:S(2)}) collective-permute-start(bf16[4,32,512]{2,1,0:T(8,128)(2,1)S(1)} %pad_maximum_fusion), channel_id=1, source_target_pairs={{0,4},{4,8},{8,12},{12,16},{16,20},{20,24},{24,28},{32,36},{36,40}... | collective-permute-start | bytes 393224 | tf_op jit(solution)/shard_map/ppermute | solution.py:38
  27.3 1.3 collective-permute-start.3
  29.2 5.3 %collective-permute-done.3.refs_6_ = bf16[4,32,512]{2,1,0:T(8,128)(2,1)S(1)} collective-permute-done((bf16[4,32,512]{2,1,0:T(8,128)(2,1)S(1)}, bf16[4,32,512]{2,1,0:T(8,128)(2,1)S(1)}, u32[]{:S(2)}, u32[]{:S(2)}) %collective-permute-start.3) | collective-permute-done | bytes 131104 | tf_op jit(solution)/shard_map/ppermute | solution.py:38
  34.5 2.0 %copy-done = bf16[128,13824]{1,0:T(8,128)(2,1)S(1)} copy-done((bf16[128,13824]{1,0:T(8,128)(2,1)S(1)}, bf16[128,13824]{1,0:T(8,128)(2,1)}, u32[]{:S(2)}) %copy-start) | copy-done | bytes 3538968
  36.5 0.8 copy-done.2
  37.3 4.6 %shard_map.146 = (bf16[4,6,32,512]{3,2,1,0:T(8,128)(2,1)S(1)}, bf16[256,128]{1,0:T(8,128)(2,1)}, bf16[4,16,128]{2,1,0:T(8,128)(2,1)}, bf16[448,512]{1,0:T(8,128)(2,1)S(1)}) custom-call(s32[1]{0:T(128)} %bitcast.refs_0_, bf16[128,512]{1,0:T(8,128)(2,1)S(1)} %collective-permute-done.refs_1_, bf16[128,512]{1,0:T(8,128)(2,1)S(1)} %get-tuple-element.28.refs_2_, ...), custom_call_target="tpu_custom_call" | custom-call | flops 905969664 | bytes 3538944 | tf_op jit(solution)/shard_map/pallas_call | solution.py:90
  41.9 1.7 %collective-permute-start.4 = (bf16[448,512]{1,0:T(8,128)(2,1)S(1)}, bf16[448,512]{1,0:T(8,128)(2,1)S(1)}, u32[]{:S(2)}, u32[]{:S(2)}) collective-permute-start(bf16[448,512]{1,0:T(8,128)(2,1)S(1)} %get-tuple-element.32), channel_id=1, source_target_pairs={{0,32},{32,0},{64,96},{96,64},{128,160},{160,128},{192,224},{224,1... | collective-permute-start | bytes 1376264 | tf_op jit(solution)/shard_map/ppermute | solution.py:46
  43.7 6.0 %all-to-all-start = ((bf16[4,16,128]{2,1,0:T(8,128)(2,1)}), bf16[4,16,128]{2,1,0:T(8,128)(2,1)S(1)}, u32[]{:S(2)}, u32[]{:S(2)}) async-start(bf16[4,16,128]{2,1,0:T(8,128)(2,1)} %get-tuple-element.30), calls=%async_computation | async-start | bytes 32768 | tf_op jit(solution)/shard_map/all_to_all | solution.py:18
  49.7 2.1 %collective-permute-done.4.got_ref = bf16[448,512]{1,0:T(8,128)(2,1)S(1)} collective-permute-done((bf16[448,512]{1,0:T(8,128)(2,1)S(1)}, bf16[448,512]{1,0:T(8,128)(2,1)S(1)}, u32[]{:S(2)}, u32[]{:S(2)}) %collective-permute-start.4) | collective-permute-done | bytes 458784 | tf_op jit(solution)/shard_map/ppermute | solution.py:46
  51.9 3.6 %shard_map.147 = (bf16[4,224,128]{2,1,0:T(8,128)(2,1)S(1)}, bf16[4,224,128]{2,1,0:T(8,128)(2,1)S(1)}, bf16[4,224,128]{2,1,0:T(8,128)(2,1)S(1)}, bf16[4,224,128]{...) custom-call(s32[2]{0:T(128)S(1)} %pad_add_fusion.place_ref, ...), custom_call_target="tpu_custom_call" | custom-call | flops 905969664 | bytes 3670016 | tf_op jit(solution)/shard_map/pallas_call | solution.py:90
  55.5 0.7 broadcast_in_dim.4
  56.2 7.1 %all-to-all-start.1 = ((bf16[8,80,128]{2,1,0:T(8,128)(2,1)}), bf16[8,80,128]{2,1,0:T(8,128)(2,1)S(1)}, u32[]{:S(2)}, u32[]{:S(2)}) async-start(bf16[8,80,128]{2,1,0:T(8,128)(2,1)} %broadcast_in_dim.4), calls=%async_computation.1 | async-start | bytes 327680 | tf_op jit(solution)/shard_map/all_to_all | solution.py:18
  63.3 2.4 %collective-permute-start.5 = (bf16[4,224,128]{2,1,0:T(8,128)(2,1)S(1)}, bf16[4,224,128]{2,1,0:T(8,128)(2,1)S(1)}, u32[]{:S(2)}, u32[]{:S(2)}) collective-permute-start(bf16[4,224,128]{2,1,0:T(8,128)(2,1)S(1)} %get-tuple-element.36), channel_id=1, source_target_pairs={{0,4},{4,0},{8,12},{12,8},{16,20},{20,16},{24,28},{28,24},{1,5},{5... | collective-permute-start | bytes 688136 | tf_op jit(solution)/shard_map/ppermute | solution.py:46
  65.8 1.3 collective-permute-start.6
  67.5 2.2 %collective-permute-done.5 = bf16[4,224,128]{2,1,0:T(8,128)(2,1)S(1)} collective-permute-done((bf16[4,224,128]{2,1,0:T(8,128)(2,1)S(1)}, bf16[4,224,128]{2,1,0:T(8,128)(2,1)S(1)}, u32[]{:S(2)}, u32[]{:S(2)}) %collective-permute-start.5) | collective-permute-done | bytes 229408 | tf_op jit(solution)/shard_map/ppermute | solution.py:46
  69.7 1.1 collective-permute-done.6
  70.8 5.4 %collective-permute-done.7 = bf16[4,224,128]{2,1,0:T(8,128)(2,1)S(1)} collective-permute-done((bf16[4,224,128]{2,1,0:T(8,128)(2,1)S(1)}, bf16[4,224,128]{2,1,0:T(8,128)(2,1)S(1)}, u32[]{:S(2)}, u32[]{:S(2)}) %collective-permute-start.7) | collective-permute-done | bytes 229408 | tf_op jit(solution)/shard_map/ppermute | solution.py:46
  76.4 1.0 broadcast_in_dim.5
  77.4 4.7 %all-to-all-start.2 = ((bf16[8,400,128]{2,1,0:T(8,128)(2,1)}), bf16[8,400,128]{2,1,0:T(8,128)(2,1)S(1)}, u32[]{:S(2)}, u32[]{:S(2)}) async-start(bf16[8,400,128]{2,1,0:T(8,128)(2,1)} %broadcast_in_dim.5), calls=%async_computation.2 | async-start | bytes 1638400 | tf_op jit(solution)/shard_map/all_to_all | solution.py:18
  82.1 3.0 %collective-permute-start.8 = (bf16[4,224,128]{2,1,0:T(8,128)(2,1)S(1)}, bf16[4,224,128]{2,1,0:T(8,128)(2,1)S(1)}, u32[]{:S(2)}, u32[]{:S(2)}) collective-permute-start(bf16[4,224,128]{2,1,0:T(8,128)(2,1)S(1)} %get-tuple-element.40), channel_id=1, source_target_pairs={{0,16},{4,20},{8,24},{12,28},{16,0},{20,4},{24,8},{28,12},{1,17},{... | collective-permute-start | bytes 688136 | tf_op jit(solution)/shard_map/ppermute | solution.py:46
  85.1 2.7 %collective-permute-start.9 = (bf16[4,224,128]{2,1,0:T(8,128)(2,1)S(1)}, bf16[4,224,128]{2,1,0:T(8,128)(2,1)}, u32[]{:S(2)}, u32[]{:S(2)}) collective-permute-start(bf16[4,224,128]{2,1,0:T(8,128)(2,1)S(1)} %get-tuple-element.41), channel_id=1, source_target_pairs={{0,20},{4,16},{8,28},{12,24},{16,4},{20,0},{24,12},{28,8},{1,21},{... | collective-permute-start | bytes 688136 | tf_op jit(solution)/shard_map/ppermute | solution.py:46
  87.7 2.4 %collective-permute-start.10 = (bf16[4,224,128]{2,1,0:T(8,128)(2,1)S(1)}, bf16[4,224,128]{2,1,0:T(8,128)(2,1)}, u32[]{:S(2)}, u32[]{:S(2)}) collective-permute-start(bf16[4,224,128]{2,1,0:T(8,128)(2,1)S(1)} %get-tuple-element.42), channel_id=1, source_target_pairs={{0,24},{4,28},{8,16},{12,20},{16,8},{20,12},{24,0},{28,4},{1,25},{... | collective-permute-start | bytes 688136 | tf_op jit(solution)/shard_map/ppermute | solution.py:46
  90.2 0.6 fusion.4
  90.9 7.0 %collective-permute-start.13 = (bf16[8,1,16,128]{3,2,1,0:T(8,128)(2,1)}, bf16[8,1,16,128]{3,2,1,0:T(8,128)(2,1)S(1)}, u32[]{:S(2)}, u32[]{:S(2)}) collective-permute-start(bf16[8,1,16,128]{3,2,1,0:T(8,128)(2,1)} %get-tuple-element.64), channel_id=1, source_target_pairs={{1,0},{2,1},{3,2},{5,4},{6,5},{7,6},{9,8},{10,9},{11,10},{13,12},{... | collective-permute-start | bytes 98312 | tf_op jit(solution)/shard_map/ppermute | solution.py:409
  97.9 13.2 %collective-permute-start.12 = (bf16[8,1,16,128]{3,2,1,0:T(8,128)(2,1)S(1)}, bf16[8,1,16,128]{3,2,1,0:T(8,128)(2,1)S(1)}, u32[]{:S(2)}, u32[]{:S(2)}) collective-permute-start(bf16[8,1,16,128]{3,2,1,0:T(8,128)(2,1)S(1)} %get-tuple-element.65), channel_id=1, source_target_pairs={{0,1},{1,2},{2,3},{4,5},{5,6},{6,7},{8,9},{9,10},{10,11},{12,13},{... | collective-permute-start | bytes 98312 | tf_op jit(solution)/shard_map/ppermute | solution.py:408
  111.1 3.1 %collective-permute-done.10 = bf16[4,224,128]{2,1,0:T(8,128)(2,1)} collective-permute-done((bf16[4,224,128]{2,1,0:T(8,128)(2,1)S(1)}, bf16[4,224,128]{2,1,0:T(8,128)(2,1)}, u32[]{:S(2)}, u32[]{:S(2)}) %collective-permute-start.10) | collective-permute-done | bytes 229408 | tf_op jit(solution)/shard_map/ppermute | solution.py:46
  114.2 1.4 add_convert_fusion
  116.8 3.1 %shard_map.148 = (bf16[512,128]{1,0:T(8,128)(2,1)}, bf16[4,992,128]{2,1,0:T(8,128)(2,1)S(1)}) custom-call(bf16[768,512]{1,0:T(8,128)(2,1)S(1)} %bitcast.75, bf16[128,512]{1,0:T(8,128)(2,1)S(1)} %copy-done.5, bf16[8,1,16,128]{3,2,1,0:T(8,128)(2,1)S(1)} %collective-permute-done.12.before_ref, bf16[8,4,16,128]{3,2,1,0:T(8,128)(2,1)S(1)} %bitcast.77, ...), custom_call_target="tpu_custom_call" | custom-call | flops 905969664 | bytes 884736 | tf_op jit(solution)/shard_map/pallas_call | solution.py:90
  120.0 1.4 collective-permute-start.18
  121.4 0.7 collective-permute-start.14
  122.0 8.5 %collective-permute-start.17 = (bf16[224,128]{1,0:T(8,128)(2,1)S(1)}, bf16[224,128]{1,0:T(8,128)(2,1)S(1)}, u32[]{:S(2)}, u32[]{:S(2)}) collective-permute-start(bf16[224,128]{1,0:T(8,128)(2,1)S(1)} %get-tuple-element.61), channel_id=1, source_target_pairs={{0,96},{32,224},{64,0},{96,128},{128,32},{160,160},{192,64},{224,1... | collective-permute-start | bytes 172040 | tf_op jit(solution)/shard_map/ppermute | solution.py:433
  130.7 3.6 %collective-permute-start.15 = (bf16[224,128]{1,0:T(8,128)(2,1)S(1)}, bf16[224,128]{1,0:T(8,128)(2,1)S(1)}, u32[]{:S(2)}, u32[]{:S(2)}) collective-permute-start(bf16[224,128]{1,0:T(8,128)(2,1)S(1)} %get-tuple-element.63), channel_id=1, source_target_pairs={{0,32},{32,160},{64,64},{96,192},{128,96},{160,224},{192,0},{224,1... | collective-permute-start | bytes 172040 | tf_op jit(solution)/shard_map/ppermute | solution.py:433
  134.4 3.2 %collective-permute-done.16 = bf16[224,128]{1,0:T(8,128)(2,1)S(1)} collective-permute-done((bf16[224,128]{1,0:T(8,128)(2,1)S(1)}, bf16[224,128]{1,0:T(8,128)(2,1)S(1)}, u32[]{:S(2)}, u32[]{:S(2)}) %collective-permute-start.16) | collective-permute-done | bytes 57376 | tf_op jit(solution)/shard_map/ppermute | solution.py:433
  137.7 2.9 %collective-permute-done.15 = bf16[224,128]{1,0:T(8,128)(2,1)S(1)} collective-permute-done((bf16[224,128]{1,0:T(8,128)(2,1)S(1)}, bf16[224,128]{1,0:T(8,128)(2,1)S(1)}, u32[]{:S(2)}, u32[]{:S(2)}) %collective-permute-start.15) | collective-permute-done | bytes 57376 | tf_op jit(solution)/shard_map/ppermute | solution.py:433
  140.6 4.6 %all-to-all-start.3 = ((bf16[8,64,128]{2,1,0:T(8,128)(2,1)}), bf16[8,64,128]{2,1,0:T(8,128)(2,1)S(1)}, u32[]{:S(2)}, u32[]{:S(2)}) async-start(bf16[8,64,128]{2,1,0:T(8,128)(2,1)} %bitcast.24), calls=%async_computation.3 | async-start | bytes 262144 | tf_op jit(solution)/shard_map/all_to_all | solution.py:18
  145.2 1.2 convert_add_fusion
  146.7 0.7 fusion.3
  148.0 4.3 %all-to-all-done.3 = bf16[8,64,128]{2,1,0:T(8,128)(2,1)S(1)} async-done(((bf16[8,64,128]{2,1,0:T(8,128)(2,1)}), bf16[8,64,128]{2,1,0:T(8,128)(2,1)S(1)}, u32[]{:S(2)}, u32[]{:S(2)}) %all-to-all-start.3) | async-done | bytes 131104 | tf_op jit(solution)/shard_map/all_to_all | solution.py:18
  153.1 0.6 slice.86
  153.8 0.8 slice.85
  (56 shorter events, 5.0 us)
Async XLA Ops:
  1.4 50.5 %copy-start.3 = (bf16[2,4,32,128]{3,2,1,0:T(8,128)(2,1)S(1)}, bf16[2,4,32,128]{3,2,1,0:T(8,128)(2,1)}, u32[]{:S(2)}) copy-start(bf16[2,4,32,128]{3,2,1,0:T(8,128)(2,1)} %param.14) | copy-start | bytes 196612
  12.0 0.8 copy-start.1
  13.4 5.2 %collective-permute-start = (bf16[128,512]{1,0:T(8,128)(2,1)S(1)}, bf16[128,512]{1,0:T(8,128)(2,1)S(1)}, u32[]{:S(2)}, u32[]{:S(2)}) collective-permute-start(bf16[128,512]{1,0:T(8,128)(2,1)S(1)} %get-tuple-element.27.refs_3_), channel_id=1, source_target_pairs={{0,32},{4,36},{8,40},{12,44},{16,48},{20,52},{24,56},{28,60},{32,6... | collective-permute-start | bytes 393224 | tf_op jit(solution)/shard_map/ppermute | solution.py:38
  15.9 6.9 %collective-permute-start.1 = (bf16[128,512]{1,0:T(8,128)(2,1)S(1)}, bf16[128,512]{1,0:T(8,128)(2,1)S(1)}, u32[]{:S(2)}, u32[]{:S(2)}) collective-permute-start(bf16[128,512]{1,0:T(8,128)(2,1)S(1)} %get-tuple-element.28.refs_2_), channel_id=1, source_target_pairs={{32,0},{36,4},{40,8},{44,12},{48,16},{52,20},{56,24},{60,28},{64,3... | collective-permute-start | bytes 393224 | tf_op jit(solution)/shard_map/ppermute | solution.py:38
  22.9 6.3 %collective-permute-start.2 = (bf16[4,32,512]{2,1,0:T(8,128)(2,1)S(1)}, bf16[4,32,512]{2,1,0:T(8,128)(2,1)S(1)}, u32[]{:S(2)}, u32[]{:S(2)}) collective-permute-start(bf16[4,32,512]{2,1,0:T(8,128)(2,1)S(1)} %pad_maximum_fusion), channel_id=1, source_target_pairs={{0,4},{4,8},{8,12},{12,16},{16,20},{20,24},{24,28},{32,36},{36,40}... | collective-permute-start | bytes 393224 | tf_op jit(solution)/shard_map/ppermute | solution.py:38
  27.3 7.2 %collective-permute-start.3 = (bf16[4,32,512]{2,1,0:T(8,128)(2,1)S(1)}, bf16[4,32,512]{2,1,0:T(8,128)(2,1)S(1)}, u32[]{:S(2)}, u32[]{:S(2)}) collective-permute-start(bf16[4,32,512]{2,1,0:T(8,128)(2,1)S(1)} %pad_maximum_fusion.1), channel_id=1, source_target_pairs={{4,0},{8,4},{12,8},{16,12},{20,16},{24,20},{28,24},{36,32},{40,36}... | collective-permute-start | bytes 393224 | tf_op jit(solution)/shard_map/ppermute | solution.py:38
  34.5 2.0 %copy-start = (bf16[128,13824]{1,0:T(8,128)(2,1)S(1)}, bf16[128,13824]{1,0:T(8,128)(2,1)}, u32[]{:S(2)}) copy-start(bf16[128,13824]{1,0:T(8,128)(2,1)} %refs_8_.1) | copy-start | bytes 10616836
  36.5 0.8 copy-start.2
  41.9 9.9 %collective-permute-start.4 = (bf16[448,512]{1,0:T(8,128)(2,1)S(1)}, bf16[448,512]{1,0:T(8,128)(2,1)S(1)}, u32[]{:S(2)}, u32[]{:S(2)}) collective-permute-start(bf16[448,512]{1,0:T(8,128)(2,1)S(1)} %get-tuple-element.32), channel_id=1, source_target_pairs={{0,32},{32,0},{64,96},{96,64},{128,160},{160,128},{192,224},{224,1... | collective-permute-start | bytes 1376264 | tf_op jit(solution)/shard_map/ppermute | solution.py:46
  43.7 11.8 %all-to-all-start = ((bf16[4,16,128]{2,1,0:T(8,128)(2,1)}), bf16[4,16,128]{2,1,0:T(8,128)(2,1)S(1)}, u32[]{:S(2)}, u32[]{:S(2)}) async-start(bf16[4,16,128]{2,1,0:T(8,128)(2,1)} %get-tuple-element.30), calls=%async_computation | async-start | bytes 32768 | tf_op jit(solution)/shard_map/all_to_all | solution.py:18
  51.9 38.3 %copy-start.6 = (bf16[8,16,4,128]{3,2,1,0:T(4,128)(2,1)S(1)}, bf16[8,16,4,128]{3,2,1,0:T(4,128)(2,1)}, u32[]{:S(2)}) copy-start(bf16[8,16,4,128]{3,2,1,0:T(4,128)(2,1)} %param.10) | copy-start | bytes 393220
  51.9 38.3 %copy-start.7 = (bf16[8,16,4,128]{3,2,1,0:T(4,128)(2,1)S(1)}, bf16[8,16,4,128]{3,2,1,0:T(4,128)(2,1)}, u32[]{:S(2)}) copy-start(bf16[8,16,4,128]{3,2,1,0:T(4,128)(2,1)} %param.11) | copy-start | bytes 393220
  56.2 20.0 %all-to-all-start.1 = ((bf16[8,80,128]{2,1,0:T(8,128)(2,1)}), bf16[8,80,128]{2,1,0:T(8,128)(2,1)S(1)}, u32[]{:S(2)}, u32[]{:S(2)}) async-start(bf16[8,80,128]{2,1,0:T(8,128)(2,1)} %broadcast_in_dim.4), calls=%async_computation.1 | async-start | bytes 327680 | tf_op jit(solution)/shard_map/all_to_all | solution.py:18
  63.3 6.4 %collective-permute-start.5 = (bf16[4,224,128]{2,1,0:T(8,128)(2,1)S(1)}, bf16[4,224,128]{2,1,0:T(8,128)(2,1)S(1)}, u32[]{:S(2)}, u32[]{:S(2)}) collective-permute-start(bf16[4,224,128]{2,1,0:T(8,128)(2,1)S(1)} %get-tuple-element.36), channel_id=1, source_target_pairs={{0,4},{4,0},{8,12},{12,8},{16,20},{20,16},{24,28},{28,24},{1,5},{5... | collective-permute-start | bytes 688136 | tf_op jit(solution)/shard_map/ppermute | solution.py:46
  65.8 5.1 %collective-permute-start.6 = (bf16[4,224,128]{2,1,0:T(8,128)(2,1)S(1)}, bf16[4,224,128]{2,1,0:T(8,128)(2,1)S(1)}, u32[]{:S(2)}, u32[]{:S(2)}) collective-permute-start(bf16[4,224,128]{2,1,0:T(8,128)(2,1)S(1)} %get-tuple-element.37), channel_id=1, source_target_pairs={{0,8},{4,12},{8,0},{12,4},{16,24},{20,28},{24,16},{28,20},{1,9},{5... | collective-permute-start | bytes 688136 | tf_op jit(solution)/shard_map/ppermute | solution.py:46
  67.1 9.2 %collective-permute-start.7 = (bf16[4,224,128]{2,1,0:T(8,128)(2,1)S(1)}, bf16[4,224,128]{2,1,0:T(8,128)(2,1)S(1)}, u32[]{:S(2)}, u32[]{:S(2)}) collective-permute-start(bf16[4,224,128]{2,1,0:T(8,128)(2,1)S(1)} %get-tuple-element.38), channel_id=1, source_target_pairs={{0,12},{4,8},{8,4},{12,0},{16,28},{20,24},{24,20},{28,16},{1,13},{... | collective-permute-start | bytes 688136 | tf_op jit(solution)/shard_map/ppermute | solution.py:46
  77.4 38.2 %all-to-all-start.2 = ((bf16[8,400,128]{2,1,0:T(8,128)(2,1)}), bf16[8,400,128]{2,1,0:T(8,128)(2,1)S(1)}, u32[]{:S(2)}, u32[]{:S(2)}) async-start(bf16[8,400,128]{2,1,0:T(8,128)(2,1)} %broadcast_in_dim.5), calls=%async_computation.2 | async-start | bytes 1638400 | tf_op jit(solution)/shard_map/all_to_all | solution.py:18
  82.1 15.8 %collective-permute-start.8 = (bf16[4,224,128]{2,1,0:T(8,128)(2,1)S(1)}, bf16[4,224,128]{2,1,0:T(8,128)(2,1)S(1)}, u32[]{:S(2)}, u32[]{:S(2)}) collective-permute-start(bf16[4,224,128]{2,1,0:T(8,128)(2,1)S(1)} %get-tuple-element.40), channel_id=1, source_target_pairs={{0,16},{4,20},{8,24},{12,28},{16,0},{20,4},{24,8},{28,12},{1,17},{... | collective-permute-start | bytes 688136 | tf_op jit(solution)/shard_map/ppermute | solution.py:46
  85.1 26.0 %collective-permute-start.9 = (bf16[4,224,128]{2,1,0:T(8,128)(2,1)S(1)}, bf16[4,224,128]{2,1,0:T(8,128)(2,1)}, u32[]{:S(2)}, u32[]{:S(2)}) collective-permute-start(bf16[4,224,128]{2,1,0:T(8,128)(2,1)S(1)} %get-tuple-element.41), channel_id=1, source_target_pairs={{0,20},{4,16},{8,28},{12,24},{16,4},{20,0},{24,12},{28,8},{1,21},{... | collective-permute-start | bytes 688136 | tf_op jit(solution)/shard_map/ppermute | solution.py:46
  87.7 26.4 %collective-permute-start.10 = (bf16[4,224,128]{2,1,0:T(8,128)(2,1)S(1)}, bf16[4,224,128]{2,1,0:T(8,128)(2,1)}, u32[]{:S(2)}, u32[]{:S(2)}) collective-permute-start(bf16[4,224,128]{2,1,0:T(8,128)(2,1)S(1)} %get-tuple-element.42), channel_id=1, source_target_pairs={{0,24},{4,28},{8,16},{12,20},{16,8},{20,12},{24,0},{28,4},{1,25},{... | collective-permute-start | bytes 688136 | tf_op jit(solution)/shard_map/ppermute | solution.py:46
  90.1 24.0 %collective-permute-start.11 = (bf16[4,224,128]{2,1,0:T(8,128)(2,1)S(1)}, bf16[4,224,128]{2,1,0:T(8,128)(2,1)}, u32[]{:S(2)}, u32[]{:S(2)}) collective-permute-start(bf16[4,224,128]{2,1,0:T(8,128)(2,1)S(1)} %get-tuple-element.43), channel_id=1, source_target_pairs={{0,28},{4,24},{8,20},{12,16},{16,12},{20,8},{24,4},{28,0},{1,29},{... | collective-permute-start | bytes 688136 | tf_op jit(solution)/shard_map/ppermute | solution.py:46
  90.9 25.9 %collective-permute-start.13 = (bf16[8,1,16,128]{3,2,1,0:T(8,128)(2,1)}, bf16[8,1,16,128]{3,2,1,0:T(8,128)(2,1)S(1)}, u32[]{:S(2)}, u32[]{:S(2)}) collective-permute-start(bf16[8,1,16,128]{3,2,1,0:T(8,128)(2,1)} %get-tuple-element.64), channel_id=1, source_target_pairs={{1,0},{2,1},{3,2},{5,4},{6,5},{7,6},{9,8},{10,9},{11,10},{13,12},{... | collective-permute-start | bytes 98312 | tf_op jit(solution)/shard_map/ppermute | solution.py:409
  97.9 18.8 %collective-permute-start.12 = (bf16[8,1,16,128]{3,2,1,0:T(8,128)(2,1)S(1)}, bf16[8,1,16,128]{3,2,1,0:T(8,128)(2,1)S(1)}, u32[]{:S(2)}, u32[]{:S(2)}) collective-permute-start(bf16[8,1,16,128]{3,2,1,0:T(8,128)(2,1)S(1)} %get-tuple-element.65), channel_id=1, source_target_pairs={{0,1},{1,2},{2,3},{4,5},{5,6},{6,7},{8,9},{9,10},{10,11},{12,13},{... | collective-permute-start | bytes 98312 | tf_op jit(solution)/shard_map/ppermute | solution.py:408
  115.6 1.2 copy-start.4
  115.6 1.2 copy-start.5
  120.0 25.2 %collective-permute-start.18 = (bf16[2,992,128]{2,1,0:T(8,128)(2,1)S(1)}, bf16[2,992,128]{2,1,0:T(8,128)(2,1)}, u32[]{:S(2)}, u32[]{:S(2)}) collective-permute-start(bf16[2,992,128]{2,1,0:T(8,128)(2,1)S(1)} %dynamic-slice_bitcast_fusion), channel_id=1, source_target_pairs={{0,1},{1,0},{2,3},{3,2},{4,5},{5,4},{6,7},{7,6},{8,9},{9,8},{10,11... | collective-permute-start | bytes 1523720 | tf_op jit(solution)/shard_map/ppermute | solution.py:46
  121.4 13.0 %collective-permute-start.14 = (bf16[224,128]{1,0:T(8,128)(2,1)S(1)}, bf16[224,128]{1,0:T(8,128)(2,1)S(1)}, u32[]{:S(2)}, u32[]{:S(2)}) collective-permute-start(bf16[224,128]{1,0:T(8,128)(2,1)S(1)} %get-tuple-element.60), channel_id=1, source_target_pairs={{0,0},{32,128},{64,32},{96,160},{128,64},{160,192},{192,96},{224,2... | collective-permute-start | bytes 172040 | tf_op jit(solution)/shard_map/ppermute | solution.py:433
  122.0 12.4 %collective-permute-start.17 = (bf16[224,128]{1,0:T(8,128)(2,1)S(1)}, bf16[224,128]{1,0:T(8,128)(2,1)S(1)}, u32[]{:S(2)}, u32[]{:S(2)}) collective-permute-start(bf16[224,128]{1,0:T(8,128)(2,1)S(1)} %get-tuple-element.61), channel_id=1, source_target_pairs={{0,96},{32,224},{64,0},{96,128},{128,32},{160,160},{192,64},{224,1... | collective-permute-start | bytes 172040 | tf_op jit(solution)/shard_map/ppermute | solution.py:433
  130.6 7.1 %collective-permute-start.16 = (bf16[224,128]{1,0:T(8,128)(2,1)S(1)}, bf16[224,128]{1,0:T(8,128)(2,1)S(1)}, u32[]{:S(2)}, u32[]{:S(2)}) collective-permute-start(bf16[224,128]{1,0:T(8,128)(2,1)S(1)} %get-tuple-element.62), channel_id=1, source_target_pairs={{0,64},{32,192},{64,96},{96,224},{128,0},{160,128},{192,32},{224,1... | collective-permute-start | bytes 172040 | tf_op jit(solution)/shard_map/ppermute | solution.py:433
  130.7 9.9 %collective-permute-start.15 = (bf16[224,128]{1,0:T(8,128)(2,1)S(1)}, bf16[224,128]{1,0:T(8,128)(2,1)S(1)}, u32[]{:S(2)}, u32[]{:S(2)}) collective-permute-start(bf16[224,128]{1,0:T(8,128)(2,1)S(1)} %get-tuple-element.63), channel_id=1, source_target_pairs={{0,32},{32,160},{64,64},{96,192},{128,96},{160,224},{192,0},{224,1... | collective-permute-start | bytes 172040 | tf_op jit(solution)/shard_map/ppermute | solution.py:433
  140.6 11.6 %all-to-all-start.3 = ((bf16[8,64,128]{2,1,0:T(8,128)(2,1)}), bf16[8,64,128]{2,1,0:T(8,128)(2,1)S(1)}, u32[]{:S(2)}, u32[]{:S(2)}) async-start(bf16[8,64,128]{2,1,0:T(8,128)(2,1)} %bitcast.24), calls=%async_computation.3 | async-start | bytes 262144 | tf_op jit(solution)/shard_map/all_to_all | solution.py:18
  146.4 6.7 %collective-permute-start.19 = (bf16[992,128]{1,0:T(8,128)(2,1)S(1)}, bf16[992,128]{1,0:T(8,128)(2,1)S(1)}, u32[]{:S(2)}, u32[]{:S(2)}) collective-permute-start(bf16[992,128]{1,0:T(8,128)(2,1)S(1)} %fusion.1), channel_id=1, source_target_pairs={{0,2},{1,3},{2,0},{3,1},{4,6},{5,7},{6,4},{7,5},{8,10},{9,11},{10,... | collective-permute-start | bytes 761864 | tf_op jit(solution)/shard_map/ppermute | solution.py:46

commit v6 on v5

--- a/solution.py
+++ b/solution.py
@@ -11,6 +11,7 @@
 CLASS_ROWS = 16
 TAPS = 27
 VMEM_LIMIT = 48 * 1024 * 1024
+VMEM_MORE = 56 * 1024 * 1024
 STEPS = (-1, 0, 1)
 
 
@@ -52,12 +53,14 @@
     return take(own), take(1 - own)
 
 
-def summed_by_pairs(x, axis, bits):
+def summed_by_pairs(x, axis, bits, first):
     names = bits_of(axis)
     x = x.reshape((2,) * len(names) + x.shape[1:])
     left = list(names)
     steps = []
     for bit in bits:
+        if bit == bits[-1]:
+            x = behind(x, first)
         own, other = mine_and_other(x, axis, bit, left.index(bit))
         left.remove(bit)
         x = own.astype(jnp.float32) + swap(other.astype(jnp.bfloat16), axis, bit).astype(jnp.float32)
@@ -92,14 +95,14 @@
         out_shape=list(out_shapes),
         in_specs=[
             pl.BlockSpec(
-                memory_space=pl.ANY if k == stay else pltpu.SMEM if a.ndim == 1 else pltpu.VMEM
+                memory_space=pltpu.HBM if k == stay else pltpu.SMEM if a.ndim == 1 else pltpu.VMEM
             )
             for k, a in enumerate(args)
         ],
         out_specs=[pl.BlockSpec(memory_space=pltpu.VMEM)] * len(out_shapes),
         scratch_shapes=scratch,
         cost_estimate=pl.CostEstimate(flops=flops, bytes_accessed=moved_bytes, transcendentals=0),
-        compiler_params=pltpu.CompilerParams(vmem_limit_bytes=VMEM_LIMIT),
+        compiler_params=pltpu.CompilerParams(vmem_limit_bytes=VMEM_LIMIT if stay is None else VMEM_MORE),
     )(*args)
 
 
@@ -423,21 +426,7 @@
     )
 
     level_part = sum(t.astype(f32) for t in terms).astype(bf16)
-    down_wide = behind(down_wide, level_part)
-    pairs = nx // 2
-    level_sum = jnp.zeros((span, inner), f32)
-    for step in range(pairs):
-        chosen = lax.dynamic_index_in_dim(
-            level_part, lax.rem(at_x // 2 + step, pairs), 0, keepdims=False
-        )
-        level_sum += lax.ppermute(
-            chosen, "gx", [(i, i % 2 * pairs + (i // 2 + step) % pairs) for i in range(nx)]
-        ).astype(f32)
-    level_part = level_sum
-    if span != chunk:
-        odd = lax.rem(at_y + at_x * ny, 2)
-        level_part = jnp.where(odd == 1, level_part[span - chunk :], level_part[:chunk])
-    level_weight_grad = level_part.T
+    down_wide = behind(down_wide, terms[ny // 2])
 
     bottom_rows = bottom_d * block * bottom_h
     channel_width = bottom_weight.shape[0]
@@ -464,16 +453,32 @@
         bottom_weight.transpose(1, 0, 2),
         stay=6,
     )
+    part = exchange(part.reshape(ny, bottom_rows // ny, channel_width), "gy")
+    pairs = nx // 2
+    level_sum = jnp.zeros((span, inner), f32)
+    for step in range(pairs):
+        if step == pairs // 2:
+            level_part = behind(level_part, part)
+        chosen = lax.dynamic_index_in_dim(
+            level_part, lax.rem(at_x // 2 + step, pairs), 0, keepdims=False
+        )
+        level_sum += lax.ppermute(
+            chosen, "gx", [(i, i % 2 * pairs + (i // 2 + step) % pairs) for i in range(nx)]
+        ).astype(f32)
+    level_part = level_sum
+    if span != chunk:
+        odd = lax.rem(at_y + at_x * ny, 2)
+        level_part = jnp.where(odd == 1, level_part[span - chunk :], level_part[:chunk])
+    level_weight_grad = level_part.T
     share = bottom_d // ny
     bottom_input_grad = (
-        exchange(part.reshape(ny, bottom_rows // ny, channel_width), "gy")
-        .astype(f32)
+        part.astype(f32)
         .sum(axis=0)
         .astype(bf16)
         .reshape(share, block, bottom_h, channel_width)
         .transpose(0, 2, 1, 3)
     )
-    both, _ = summed_by_pairs(both, "col", bits_of("col")[::-1])
+    both, _ = summed_by_pairs(both, "col", bits_of("col")[::-1], part)
     bottom_weight_grad = both[: TAPS * thin].reshape(TAPS, thin, filters).transpose(1, 0, 2)
     up_weight_grad = both[TAPS * thin :]
     return (

time: 157 us -> 151 us (0.962)
  the two profiles are of different devices: /device:TPU:1 before, /device:TPU:6 now
where the time goes in v6:
time: 151 us; the launch traced here: 150 us
  starting transfers between devices  71.9 us (48%)
  waiting for transfers between devices  35.4 us (23%)
  Pallas kernels  16.1 us (11%)
  local copies, waits for them, and re-layouts  13.2 us (9%)
  blocking collectives  6.87 us (5%)
  other arithmetic  5.12 us (3%)
    all_to_all x4, starting transfers between devices, exchange(): return lax.all_to_all(x, axis, split_axis=0, concat_axis=0, tiled=False)  25.2 us
    ppermute x10, waiting for transfers between devices, swap(): lax.ppermute(x, axis, [(i, i ^ bit) for i in range(lax.axis_size(axis))])  22 us
    pallas_call x4, Pallas kernels, local_call(): pl.pallas_call(body, out_shape=list(out_shapes), in_specs=[pl.BlockSpec(m...  16.1 us
    ppermute x4, starting transfers between devices, per_device(): lax.ppermute(chosen, 'gx', [(i, i % 2 * pairs + (i // 2 + step) % pairs)...  15.2 us
    ppermute x10, starting transfers between devices, swap(): lax.ppermute(x, axis, [(i, i ^ bit) for i in range(lax.axis_size(axis))])  14.7 us
    ppermute x4, starting transfers between devices, neighbour(): return lax.ppermute(x, ('gx', 'gy'), pairs)  12.5 us
    ppermute x4, waiting for transfers between devices, neighbour(): return lax.ppermute(x, ('gx', 'gy'), pairs)  12.4 us
    all_gather x1, blocking collectives, per_device(): gathered = lax.all_gather(payload, 'col')  6.87 us
  transfers between devices with their start and end apart: 24, of which 12 were waited for; matrix products, arithmetic and copies ran while one was open for 6% of the time, Pallas kernels for 6%

profile of v6, /device:TPU:6, one launch (start us, length us, event | category | flops | bytes accessed | tf_op | source)
XLA Modules:
  0.0 149.5 jit_solution(13547526344747480226)
XLA Ops:
  0.6 0.8 reshape.68.label_ref
  1.4 0.9 fusion.2
  2.3 6.9 %all-gather = bf16[2112,128]{1,0:T(8,128)(2,1)S(1)} all-gather(bf16[528,128]{1,0:T(8,128)(2,1)S(1)} %fusion.2), channel_id=2, replica_groups=mesh['gx'=8,'gy'=8,'col'=4] {'col'}, dimensions={0}, use_global_device_ids=true | all-gather | bytes 675840 | tf_op jit(solution)/shard_map/all_gather | solution.py:335
  9.2 0.8 copy-done.2
  10.7 3.8 %collective-permute-start = (bf16[128,512]{1,0:T(8,128)(2,1)S(1)}, bf16[128,512]{1,0:T(8,128)(2,1)S(1)}, u32[]{:S(2)}, u32[]{:S(2)}) collective-permute-start(bf16[128,512]{1,0:T(8,128)(2,1)S(1)} %get-tuple-element.29.refs_3_), channel_id=1, source_target_pairs={{0,32},{4,36},{8,40},{12,44},{16,48},{20,52},{24,56},{28,60},{32,6... | collective-permute-start | bytes 393224 | tf_op jit(solution)/shard_map/ppermute | solution.py:39
  14.5 1.3 collective-permute-start.1
  15.8 1.9 %collective-permute-done.refs_1_ = bf16[128,512]{1,0:T(8,128)(2,1)S(1)} collective-permute-done((bf16[128,512]{1,0:T(8,128)(2,1)S(1)}, bf16[128,512]{1,0:T(8,128)(2,1)S(1)}, u32[]{:S(2)}, u32[]{:S(2)}) %collective-permute-start) | collective-permute-done | bytes 131104 | tf_op jit(solution)/shard_map/ppermute | solution.py:39
  17.8 4.3 %collective-permute-done.1.refs_4_ = bf16[128,512]{1,0:T(8,128)(2,1)S(1)} collective-permute-done((bf16[128,512]{1,0:T(8,128)(2,1)S(1)}, bf16[128,512]{1,0:T(8,128)(2,1)S(1)}, u32[]{:S(2)}, u32[]{:S(2)}) %collective-permute-start.1) | collective-permute-done | bytes 131104 | tf_op jit(solution)/shard_map/ppermute | solution.py:39
  22.1 4.3 %collective-permute-start.2 = (bf16[4,32,512]{2,1,0:T(8,128)(2,1)S(1)}, bf16[4,32,512]{2,1,0:T(8,128)(2,1)S(1)}, u32[]{:S(2)}, u32[]{:S(2)}) collective-permute-start(bf16[4,32,512]{2,1,0:T(8,128)(2,1)S(1)} %pad_maximum_fusion), channel_id=1, source_target_pairs={{0,4},{4,8},{8,12},{12,16},{16,20},{20,24},{24,28},{32,36},{36,40}... | collective-permute-start | bytes 393224 | tf_op jit(solution)/shard_map/ppermute | solution.py:39
  26.4 3.0 %collective-permute-start.3 = (bf16[4,32,512]{2,1,0:T(8,128)(2,1)S(1)}, bf16[4,32,512]{2,1,0:T(8,128)(2,1)S(1)}, u32[]{:S(2)}, u32[]{:S(2)}) collective-permute-start(bf16[4,32,512]{2,1,0:T(8,128)(2,1)S(1)} %pad_maximum_fusion.1), channel_id=1, source_target_pairs={{4,0},{8,4},{12,8},{16,12},{20,16},{24,20},{28,24},{36,32},{40,36}... | collective-permute-start | bytes 393224 | tf_op jit(solution)/shard_map/ppermute | solution.py:39
  29.5 1.0 collective-permute-done.2.refs_5_
  30.5 5.3 %collective-permute-done.3.refs_6_ = bf16[4,32,512]{2,1,0:T(8,128)(2,1)S(1)} collective-permute-done((bf16[4,32,512]{2,1,0:T(8,128)(2,1)S(1)}, bf16[4,32,512]{2,1,0:T(8,128)(2,1)S(1)}, u32[]{:S(2)}, u32[]{:S(2)}) %collective-permute-start.3) | collective-permute-done | bytes 131104 | tf_op jit(solution)/shard_map/ppermute | solution.py:39
  36.4 6.5 %shard_map.146 = (bf16[4,6,32,512]{3,2,1,0:T(8,128)(2,1)}, bf16[256,128]{1,0:T(8,128)(2,1)}, bf16[4,16,128]{2,1,0:T(8,128)(2,1)}, bf16[448,512]{1,0:T(8,128)(2,1)}) custom-call(s32[1]{0:T(128)} %bitcast.refs_0_, bf16[128,512]{1,0:T(8,128)(2,1)} %copy-done.6, bf16[128,512]{1,0:T(8,128)(2,1)} %copy-done, bf16[128,512]{1,0:T(8,128)(2,1)} %copy-done.1, ...), custom_call_target="tpu_custom_call" | custom-call | flops 905969664 | bytes 3538944 | tf_op jit(solution)/shard_map/pallas_call | solution.py:93
  42.9 2.0 %collective-permute-start.4 = (bf16[448,512]{1,0:T(8,128)(2,1)}, bf16[448,512]{1,0:T(8,128)(2,1)S(1)}, u32[]{:S(2)}, u32[]{:S(2)}) collective-permute-start(bf16[448,512]{1,0:T(8,128)(2,1)} %get-tuple-element.34), channel_id=1, source_target_pairs={{0,32},{32,0},{64,96},{96,64},{128,160},{160,128},{192,224},{224,1... | collective-permute-start | bytes 1376264 | tf_op jit(solution)/shard_map/ppermute | solution.py:47
  45.0 3.5 %all-to-all-start = ((bf16[4,16,128]{2,1,0:T(8,128)(2,1)}), bf16[4,16,128]{2,1,0:T(8,128)(2,1)S(1)}, u32[]{:S(2)}, u32[]{:S(2)}) async-start(bf16[4,16,128]{2,1,0:T(8,128)(2,1)} %get-tuple-element.32), calls=%async_computation | async-start | bytes 32768 | tf_op jit(solution)/shard_map/all_to_all | solution.py:19
  48.5 5.3 %collective-permute-done.4.got_ref = bf16[448,512]{1,0:T(8,128)(2,1)S(1)} collective-permute-done((bf16[448,512]{1,0:T(8,128)(2,1)}, bf16[448,512]{1,0:T(8,128)(2,1)S(1)}, u32[]{:S(2)}, u32[]{:S(2)}) %collective-permute-start.4) | collective-permute-done | bytes 458784 | tf_op jit(solution)/shard_map/ppermute | solution.py:47
  53.8 1.1 copy-done.4
  55.0 3.6 %shard_map.147 = (bf16[4,224,128]{2,1,0:T(8,128)(2,1)S(1)}, bf16[4,224,128]{2,1,0:T(8,128)(2,1)S(1)}, bf16[4,224,128]{2,1,0:T(8,128)(2,1)S(1)}, bf16[4,224,128]{...) custom-call(s32[2]{0:T(128)S(1)} %pad_add_fusion.place_ref, ...), custom_call_target="tpu_custom_call" | custom-call | flops 905969664 | bytes 3670016 | tf_op jit(solution)/shard_map/pallas_call | solution.py:93
  58.6 0.7 broadcast_in_dim.4
  59.3 7.8 %all-to-all-start.1 = ((bf16[8,80,128]{2,1,0:T(8,128)(2,1)}), bf16[8,80,128]{2,1,0:T(8,128)(2,1)S(1)}, u32[]{:S(2)}, u32[]{:S(2)}) async-start(bf16[8,80,128]{2,1,0:T(8,128)(2,1)} %broadcast_in_dim.4), calls=%async_computation.1 | async-start | bytes 327680 | tf_op jit(solution)/shard_map/all_to_all | solution.py:19
  67.6 1.6 %collective-permute-start.6 = (bf16[4,224,128]{2,1,0:T(8,128)(2,1)S(1)}, bf16[4,224,128]{2,1,0:T(8,128)(2,1)S(1)}, u32[]{:S(2)}, u32[]{:S(2)}) collective-permute-start(bf16[4,224,128]{2,1,0:T(8,128)(2,1)S(1)} %get-tuple-element.39), channel_id=1, source_target_pairs={{0,8},{4,12},{8,0},{12,4},{16,24},{20,28},{24,16},{28,20},{1,9},{5... | collective-permute-start | bytes 688136 | tf_op jit(solution)/shard_map/ppermute | solution.py:47
  69.2 2.8 %collective-permute-start.7 = (bf16[4,224,128]{2,1,0:T(8,128)(2,1)S(1)}, bf16[4,224,128]{2,1,0:T(8,128)(2,1)}, u32[]{:S(2)}, u32[]{:S(2)}) collective-permute-start(bf16[4,224,128]{2,1,0:T(8,128)(2,1)S(1)} %get-tuple-element.40), channel_id=1, source_target_pairs={{0,12},{4,8},{8,4},{12,0},{16,28},{20,24},{24,20},{28,16},{1,13},{... | collective-permute-start | bytes 688136 | tf_op jit(solution)/shard_map/ppermute | solution.py:47
  72.1 3.1 %collective-permute-done.5 = bf16[4,224,128]{2,1,0:T(8,128)(2,1)S(1)} collective-permute-done((bf16[4,224,128]{2,1,0:T(8,128)(2,1)S(1)}, bf16[4,224,128]{2,1,0:T(8,128)(2,1)S(1)}, u32[]{:S(2)}, u32[]{:S(2)}) %collective-permute-start.5) | collective-permute-done | bytes 229408 | tf_op jit(solution)/shard_map/ppermute | solution.py:47
  75.1 1.0 collective-permute-done.6
  76.1 0.7 copy-done.11
  76.8 1.9 %collective-permute-done.7 = bf16[4,224,128]{2,1,0:T(8,128)(2,1)} collective-permute-done((bf16[4,224,128]{2,1,0:T(8,128)(2,1)S(1)}, bf16[4,224,128]{2,1,0:T(8,128)(2,1)}, u32[]{:S(2)}, u32[]{:S(2)}) %collective-permute-start.7) | collective-permute-done | bytes 229408 | tf_op jit(solution)/shard_map/ppermute | solution.py:47
  78.8 1.0 broadcast_in_dim.5
  79.8 7.1 %all-to-all-start.2 = ((bf16[8,400,128]{2,1,0:T(8,128)(2,1)}), bf16[8,400,128]{2,1,0:T(8,128)(2,1)S(1)}, u32[]{:S(2)}, u32[]{:S(2)}) async-start(bf16[8,400,128]{2,1,0:T(8,128)(2,1)} %broadcast_in_dim.5), calls=%async_computation.2 | async-start | bytes 1638400 | tf_op jit(solution)/shard_map/all_to_all | solution.py:19
  86.9 3.1 %collective-permute-start.8 = (bf16[4,224,128]{2,1,0:T(8,128)(2,1)S(1)}, bf16[4,224,128]{2,1,0:T(8,128)(2,1)S(1)}, u32[]{:S(2)}, u32[]{:S(2)}) collective-permute-start(bf16[4,224,128]{2,1,0:T(8,128)(2,1)S(1)} %get-tuple-element.42), channel_id=1, source_target_pairs={{0,16},{4,20},{8,24},{12,28},{16,0},{20,4},{24,8},{28,12},{1,17},{... | collective-permute-start | bytes 688136 | tf_op jit(solution)/shard_map/ppermute | solution.py:47
  90.0 1.9 %collective-permute-start.10 = (bf16[8,1,16,128]{3,2,1,0:T(8,128)(2,1)S(1)}, bf16[8,1,16,128]{3,2,1,0:T(8,128)(2,1)S(1)}, u32[]{:S(2)}, u32[]{:S(2)}) collective-permute-start(bf16[8,1,16,128]{3,2,1,0:T(8,128)(2,1)S(1)} %get-tuple-element.68), channel_id=1, source_target_pairs={{1,0},{2,1},{3,2},{5,4},{6,5},{7,6},{9,8},{10,9},{11,10},{13,12},{... | collective-permute-start | bytes 98312 | tf_op jit(solution)/shard_map/ppermute | solution.py:412
  91.9 2.4 %collective-permute-start.9 = (bf16[8,1,16,128]{3,2,1,0:T(8,128)(2,1)S(1)}, bf16[8,1,16,128]{3,2,1,0:T(8,128)(2,1)S(1)}, u32[]{:S(2)}, u32[]{:S(2)}) collective-permute-start(bf16[8,1,16,128]{3,2,1,0:T(8,128)(2,1)S(1)} %get-tuple-element.69), channel_id=1, source_target_pairs={{0,1},{1,2},{2,3},{4,5},{5,6},{6,7},{8,9},{9,10},{10,11},{12,13},{... | collective-permute-start | bytes 98312 | tf_op jit(solution)/shard_map/ppermute | solution.py:411
  94.4 3.2 %collective-permute-start.12 = (bf16[4,224,128]{2,1,0:T(8,128)(2,1)S(1)}, bf16[4,224,128]{2,1,0:T(8,128)(2,1)}, u32[]{:S(2)}, u32[]{:S(2)}) collective-permute-start(bf16[4,224,128]{2,1,0:T(8,128)(2,1)S(1)} %get-tuple-element.47), channel_id=1, source_target_pairs={{0,24},{4,28},{8,16},{12,20},{16,8},{20,12},{24,0},{28,4},{1,25},{... | collective-permute-start | bytes 688136 | tf_op jit(solution)/shard_map/ppermute | solution.py:47
  97.6 2.6 %collective-permute-done.8 = bf16[4,224,128]{2,1,0:T(8,128)(2,1)S(1)} collective-permute-done((bf16[4,224,128]{2,1,0:T(8,128)(2,1)S(1)}, bf16[4,224,128]{2,1,0:T(8,128)(2,1)S(1)}, u32[]{:S(2)}, u32[]{:S(2)}) %collective-permute-start.8) | collective-permute-done | bytes 229408 | tf_op jit(solution)/shard_map/ppermute | solution.py:47
  100.2 1.1 collective-permute-start.13
  101.3 0.7 copy.27
  103.1 1.0 copy.35
  104.7 5.3 %shard_map.148 = (bf16[512,128]{1,0:T(8,128)(2,1)}, bf16[4,992,128]{2,1,0:T(8,128)(2,1)}) custom-call(bf16[768,512]{1,0:T(8,128)(2,1)} %bitcast.81, bf16[128,512]{1,0:T(8,128)(2,1)} %up_ref.1, bf16[8,1,16,128]{3,2,1,0:T(8,128)(2,1)} %copy-done.20, bf16[8,4,16,128]{3,2,1,0:T(8,128)(2,1)} %bitcast.85, bf16[8,1,16,128]{3,2,1,0:T(8,128)(2,1)} %copy-done.19, ...), custom_call_target="tpu_custom_call" | custom-call | flops 905969664 | bytes 884736 | tf_op jit(solution)/shard_map/pallas_call | solution.py:93
  110.0 1.9 %dynamic-slice_bitcast_fusion = bf16[2,992,128]{2,1,0:T(8,128)(2,1)} fusion(bf16[2,2,992,128]{3,2,1,0:T(8,128)(2,1)} %bitcast.79, s32[]{:T(128)S(6)} %select_n.66), kind=kLoop, calls=%fused_computation.4 | loop fusion | bytes 1015812 | tf_op jit(solution)/shard_map/jit(dynamic_index_in_dim)/squeeze | solution.py:53
  112.0 3.0 %collective-permute-done.12 = bf16[4,224,128]{2,1,0:T(8,128)(2,1)} collective-permute-done((bf16[4,224,128]{2,1,0:T(8,128)(2,1)S(1)}, bf16[4,224,128]{2,1,0:T(8,128)(2,1)}, u32[]{:S(2)}, u32[]{:S(2)}) %collective-permute-start.12) | collective-permute-done | bytes 229408 | tf_op jit(solution)/shard_map/ppermute | solution.py:47
  115.0 1.5 %add_convert_fusion = bf16[4,224,128]{2,1,0:T(8,128)(2,1)S(1)} fusion(bf16[4,224,128]{2,1,0:T(8,128)(2,1)} %collective-permute-done.13, bf16[4,224,128]{2,1,0:T(8,128)(2,1)} %collective-permute-done.12, bf16[4,224,128]{2,1,0:T(8,128)(2,1)} %collective-permute-done.11, bf16[4,224,128]{2,1,0:T(8,128)(2,1)S(1)} %copy-done.14, ...), kind=kLoop, calls=%fused_computation.5 | loop fusion | flops 1835008 | bytes 2064384 | tf_op jit(solution)/shard_map/convert_element_type | solution.py:428
  116.6 6.8 %all-to-all-start.3 = ((bf16[8,64,128]{2,1,0:T(8,128)(2,1)}), bf16[8,64,128]{2,1,0:T(8,128)(2,1)S(1)}, u32[]{:S(2)}, u32[]{:S(2)}) async-start(bf16[8,64,128]{2,1,0:T(8,128)(2,1)} %bitcast.88), calls=%async_computation.3 | async-start | bytes 262144 | tf_op jit(solution)/shard_map/all_to_all | solution.py:19
  123.4 0.7 collective-permute-start.14
  124.1 8.7 %collective-permute-start.15 = (bf16[224,128]{1,0:T(8,128)(2,1)S(1)}, bf16[224,128]{1,0:T(8,128)(2,1)S(1)}, u32[]{:S(2)}, u32[]{:S(2)}) collective-permute-start(bf16[224,128]{1,0:T(8,128)(2,1)S(1)} %get-tuple-element.65), channel_id=1, source_target_pairs={{0,32},{32,160},{64,64},{96,192},{128,96},{160,224},{192,0},{224,1... | collective-permute-start | bytes 172040 | tf_op jit(solution)/shard_map/ppermute | solution.py:465
  134.2 5.7 %collective-permute-start.17 = (bf16[224,128]{1,0:T(8,128)(2,1)S(1)}, bf16[224,128]{1,0:T(8,128)(2,1)S(1)}, u32[]{:S(2)}, u32[]{:S(2)}) collective-permute-start(bf16[224,128]{1,0:T(8,128)(2,1)S(1)} %get-tuple-element.67), channel_id=1, source_target_pairs={{0,96},{32,224},{64,0},{96,128},{128,32},{160,160},{192,64},{224,1... | collective-permute-start | bytes 172040 | tf_op jit(solution)/shard_map/ppermute | solution.py:465
  139.9 1.1 convert_add_fusion
  141.3 0.9 collective-permute-done.16
  142.9 5.1 %collective-permute-done.19 = bf16[992,128]{1,0:T(8,128)(2,1)S(1)} collective-permute-done((bf16[992,128]{1,0:T(8,128)(2,1)S(1)}, bf16[992,128]{1,0:T(8,128)(2,1)S(1)}, u32[]{:S(2)}, u32[]{:S(2)}) %collective-permute-start.19) | collective-permute-done | bytes 253984 | tf_op jit(solution)/shard_map/ppermute | solution.py:47
  148.8 0.8 slice.85
  (83 shorter events, 6.8 us)
Async XLA Ops:
  1.4 52.4 %copy-start.3 = (bf16[2,4,32,128]{3,2,1,0:T(8,128)(2,1)S(1)}, bf16[2,4,32,128]{3,2,1,0:T(8,128)(2,1)}, u32[]{:S(2)}) copy-start(bf16[2,4,32,128]{3,2,1,0:T(8,128)(2,1)} %param.14) | copy-start | bytes 196612
  9.2 0.8 copy-start.2
  10.6 25.1 %copy-start = (bf16[128,512]{1,0:T(8,128)(2,1)}, bf16[128,512]{1,0:T(8,128)(2,1)S(1)}, u32[]{:S(2)}) copy-start(bf16[128,512]{1,0:T(8,128)(2,1)S(1)} %get-tuple-element.30.refs_2_) | copy-start | bytes 393220
  10.7 25.1 %copy-start.1 = (bf16[128,512]{1,0:T(8,128)(2,1)}, bf16[128,512]{1,0:T(8,128)(2,1)S(1)}, u32[]{:S(2)}) copy-start(bf16[128,512]{1,0:T(8,128)(2,1)S(1)} %get-tuple-element.29.refs_3_) | copy-start | bytes 393220
  10.7 7.1 %collective-permute-start = (bf16[128,512]{1,0:T(8,128)(2,1)S(1)}, bf16[128,512]{1,0:T(8,128)(2,1)S(1)}, u32[]{:S(2)}, u32[]{:S(2)}) collective-permute-start(bf16[128,512]{1,0:T(8,128)(2,1)S(1)} %get-tuple-element.29.refs_3_), channel_id=1, source_target_pairs={{0,32},{4,36},{8,40},{12,44},{16,48},{20,52},{24,56},{28,60},{32,6... | collective-permute-start | bytes 393224 | tf_op jit(solution)/shard_map/ppermute | solution.py:39
  14.5 7.5 %collective-permute-start.1 = (bf16[128,512]{1,0:T(8,128)(2,1)S(1)}, bf16[128,512]{1,0:T(8,128)(2,1)S(1)}, u32[]{:S(2)}, u32[]{:S(2)}) collective-permute-start(bf16[128,512]{1,0:T(8,128)(2,1)S(1)} %get-tuple-element.30.refs_2_), channel_id=1, source_target_pairs={{32,0},{36,4},{40,8},{44,12},{48,16},{52,20},{56,24},{60,28},{64,3... | collective-permute-start | bytes 393224 | tf_op jit(solution)/shard_map/ppermute | solution.py:39
  17.7 18.0 %copy-start.6 = (bf16[128,512]{1,0:T(8,128)(2,1)}, bf16[128,512]{1,0:T(8,128)(2,1)S(1)}, u32[]{:S(2)}) copy-start(bf16[128,512]{1,0:T(8,128)(2,1)S(1)} %collective-permute-done.refs_1_) | copy-start | bytes 393220
  22.0 13.7 %copy-start.7 = (bf16[128,512]{1,0:T(8,128)(2,1)}, bf16[128,512]{1,0:T(8,128)(2,1)S(1)}, u32[]{:S(2)}) copy-start(bf16[128,512]{1,0:T(8,128)(2,1)S(1)} %collective-permute-done.1.refs_4_) | copy-start | bytes 393220
  22.1 8.4 %collective-permute-start.2 = (bf16[4,32,512]{2,1,0:T(8,128)(2,1)S(1)}, bf16[4,32,512]{2,1,0:T(8,128)(2,1)S(1)}, u32[]{:S(2)}, u32[]{:S(2)}) collective-permute-start(bf16[4,32,512]{2,1,0:T(8,128)(2,1)S(1)} %pad_maximum_fusion), channel_id=1, source_target_pairs={{0,4},{4,8},{8,12},{12,16},{16,20},{20,24},{24,28},{32,36},{36,40}... | collective-permute-start | bytes 393224 | tf_op jit(solution)/shard_map/ppermute | solution.py:39
  26.4 9.3 %collective-permute-start.3 = (bf16[4,32,512]{2,1,0:T(8,128)(2,1)S(1)}, bf16[4,32,512]{2,1,0:T(8,128)(2,1)S(1)}, u32[]{:S(2)}, u32[]{:S(2)}) collective-permute-start(bf16[4,32,512]{2,1,0:T(8,128)(2,1)S(1)} %pad_maximum_fusion.1), channel_id=1, source_target_pairs={{4,0},{8,4},{12,8},{16,12},{20,16},{24,20},{28,24},{36,32},{40,36}... | collective-permute-start | bytes 393224 | tf_op jit(solution)/shard_map/ppermute | solution.py:39
  30.5 5.3 %copy-start.15 = (bf16[4,32,512]{2,1,0:T(8,128)(2,1)}, bf16[4,32,512]{2,1,0:T(8,128)(2,1)S(1)}, u32[]{:S(2)}) copy-start(bf16[4,32,512]{2,1,0:T(8,128)(2,1)S(1)} %collective-permute-done.2.refs_5_) | copy-start | bytes 393220
  35.7 0.6 copy-start.16
  42.9 10.9 %collective-permute-start.4 = (bf16[448,512]{1,0:T(8,128)(2,1)}, bf16[448,512]{1,0:T(8,128)(2,1)S(1)}, u32[]{:S(2)}, u32[]{:S(2)}) collective-permute-start(bf16[448,512]{1,0:T(8,128)(2,1)} %get-tuple-element.34), channel_id=1, source_target_pairs={{0,32},{32,0},{64,96},{96,64},{128,160},{160,128},{192,224},{224,1... | collective-permute-start | bytes 1376264 | tf_op jit(solution)/shard_map/ppermute | solution.py:47
  45.0 13.6 %all-to-all-start = ((bf16[4,16,128]{2,1,0:T(8,128)(2,1)}), bf16[4,16,128]{2,1,0:T(8,128)(2,1)S(1)}, u32[]{:S(2)}, u32[]{:S(2)}) async-start(bf16[4,16,128]{2,1,0:T(8,128)(2,1)} %get-tuple-element.32), calls=%async_computation | async-start | bytes 32768 | tf_op jit(solution)/shard_map/all_to_all | solution.py:19
  53.8 1.1 copy-start.4
  55.0 31.9 %copy-start.17 = (bf16[8,16,4,128]{3,2,1,0:T(4,128)(2,1)S(1)}, bf16[8,16,4,128]{3,2,1,0:T(4,128)(2,1)}, u32[]{:S(2)}) copy-start(bf16[8,16,4,128]{3,2,1,0:T(4,128)(2,1)} %param.10) | copy-start | bytes 393220
  55.0 46.4 %copy-start.18 = (bf16[8,16,4,128]{3,2,1,0:T(4,128)(2,1)S(1)}, bf16[8,16,4,128]{3,2,1,0:T(4,128)(2,1)}, u32[]{:S(2)}) copy-start(bf16[8,16,4,128]{3,2,1,0:T(4,128)(2,1)} %param.11) | copy-start | bytes 393220
  59.3 19.4 %all-to-all-start.1 = ((bf16[8,80,128]{2,1,0:T(8,128)(2,1)}), bf16[8,80,128]{2,1,0:T(8,128)(2,1)S(1)}, u32[]{:S(2)}, u32[]{:S(2)}) async-start(bf16[8,80,128]{2,1,0:T(8,128)(2,1)} %broadcast_in_dim.4), calls=%async_computation.1 | async-start | bytes 327680 | tf_op jit(solution)/shard_map/all_to_all | solution.py:19
  67.1 8.1 %collective-permute-start.5 = (bf16[4,224,128]{2,1,0:T(8,128)(2,1)S(1)}, bf16[4,224,128]{2,1,0:T(8,128)(2,1)S(1)}, u32[]{:S(2)}, u32[]{:S(2)}) collective-permute-start(bf16[4,224,128]{2,1,0:T(8,128)(2,1)S(1)} %get-tuple-element.38), channel_id=1, source_target_pairs={{0,4},{4,0},{8,12},{12,8},{16,20},{20,16},{24,28},{28,24},{1,5},{5... | collective-permute-start | bytes 688136 | tf_op jit(solution)/shard_map/ppermute | solution.py:47
  67.6 8.5 %collective-permute-start.6 = (bf16[4,224,128]{2,1,0:T(8,128)(2,1)S(1)}, bf16[4,224,128]{2,1,0:T(8,128)(2,1)S(1)}, u32[]{:S(2)}, u32[]{:S(2)}) collective-permute-start(bf16[4,224,128]{2,1,0:T(8,128)(2,1)S(1)} %get-tuple-element.39), channel_id=1, source_target_pairs={{0,8},{4,12},{8,0},{12,4},{16,24},{20,28},{24,16},{28,20},{1,9},{5... | collective-permute-start | bytes 688136 | tf_op jit(solution)/shard_map/ppermute | solution.py:47
  69.2 9.5 %collective-permute-start.7 = (bf16[4,224,128]{2,1,0:T(8,128)(2,1)S(1)}, bf16[4,224,128]{2,1,0:T(8,128)(2,1)}, u32[]{:S(2)}, u32[]{:S(2)}) collective-permute-start(bf16[4,224,128]{2,1,0:T(8,128)(2,1)S(1)} %get-tuple-element.40), channel_id=1, source_target_pairs={{0,12},{4,8},{8,4},{12,0},{16,28},{20,24},{24,20},{28,16},{1,13},{... | collective-permute-start | bytes 688136 | tf_op jit(solution)/shard_map/ppermute | solution.py:47
  75.1 3.6 %copy-start.9 = (bf16[4,224,128]{2,1,0:T(8,128)(2,1)}, bf16[4,224,128]{2,1,0:T(8,128)(2,1)S(1)}, u32[]{:S(2)}) copy-start(bf16[4,224,128]{2,1,0:T(8,128)(2,1)S(1)} %collective-permute-done.5) | copy-start | bytes 688132
  76.1 0.7 copy-start.11
  79.8 22.2 %all-to-all-start.2 = ((bf16[8,400,128]{2,1,0:T(8,128)(2,1)}), bf16[8,400,128]{2,1,0:T(8,128)(2,1)S(1)}, u32[]{:S(2)}, u32[]{:S(2)}) async-start(bf16[8,400,128]{2,1,0:T(8,128)(2,1)} %broadcast_in_dim.5), calls=%async_computation.2 | async-start | bytes 1638400 | tf_op jit(solution)/shard_map/all_to_all | solution.py:19
  86.9 17.2 %copy-start.8 = (bf16[8,16,4,128]{3,1,2,0:T(8,128)(2,1)}, bf16[8,16,4,128]{3,1,2,0:T(8,128)(2,1)S(1)}, u32[]{:S(2)}) copy-start(bf16[8,16,4,128]{3,1,2,0:T(8,128)(2,1)S(1)} %copy.36) | copy-start | bytes 393220
  86.9 13.3 %collective-permute-start.8 = (bf16[4,224,128]{2,1,0:T(8,128)(2,1)S(1)}, bf16[4,224,128]{2,1,0:T(8,128)(2,1)S(1)}, u32[]{:S(2)}, u32[]{:S(2)}) collective-permute-start(bf16[4,224,128]{2,1,0:T(8,128)(2,1)S(1)} %get-tuple-element.42), channel_id=1, source_target_pairs={{0,16},{4,20},{8,24},{12,28},{16,0},{20,4},{24,8},{28,12},{1,17},{... | collective-permute-start | bytes 688136 | tf_op jit(solution)/shard_map/ppermute | solution.py:47
  90.0 14.1 %collective-permute-start.10 = (bf16[8,1,16,128]{3,2,1,0:T(8,128)(2,1)S(1)}, bf16[8,1,16,128]{3,2,1,0:T(8,128)(2,1)S(1)}, u32[]{:S(2)}, u32[]{:S(2)}) collective-permute-start(bf16[8,1,16,128]{3,2,1,0:T(8,128)(2,1)S(1)} %get-tuple-element.68), channel_id=1, source_target_pairs={{1,0},{2,1},{3,2},{5,4},{6,5},{7,6},{9,8},{10,9},{11,10},{13,12},{... | collective-permute-start | bytes 98312 | tf_op jit(solution)/shard_map/ppermute | solution.py:412
  91.9 12.2 %collective-permute-start.9 = (bf16[8,1,16,128]{3,2,1,0:T(8,128)(2,1)S(1)}, bf16[8,1,16,128]{3,2,1,0:T(8,128)(2,1)S(1)}, u32[]{:S(2)}, u32[]{:S(2)}) collective-permute-start(bf16[8,1,16,128]{3,2,1,0:T(8,128)(2,1)S(1)} %get-tuple-element.69), channel_id=1, source_target_pairs={{0,1},{1,2},{2,3},{4,5},{5,6},{6,7},{8,9},{9,10},{10,11},{12,13},{... | collective-permute-start | bytes 98312 | tf_op jit(solution)/shard_map/ppermute | solution.py:411
  94.3 17.7 %collective-permute-start.11 = (bf16[4,224,128]{2,1,0:T(8,128)(2,1)S(1)}, bf16[4,224,128]{2,1,0:T(8,128)(2,1)}, u32[]{:S(2)}, u32[]{:S(2)}) collective-permute-start(bf16[4,224,128]{2,1,0:T(8,128)(2,1)S(1)} %get-tuple-element.46), channel_id=1, source_target_pairs={{0,20},{4,16},{8,28},{12,24},{16,4},{20,0},{24,12},{28,8},{1,21},{... | collective-permute-start | bytes 688136 | tf_op jit(solution)/shard_map/ppermute | solution.py:47
  94.4 20.6 %collective-permute-start.12 = (bf16[4,224,128]{2,1,0:T(8,128)(2,1)S(1)}, bf16[4,224,128]{2,1,0:T(8,128)(2,1)}, u32[]{:S(2)}, u32[]{:S(2)}) collective-permute-start(bf16[4,224,128]{2,1,0:T(8,128)(2,1)S(1)} %get-tuple-element.47), channel_id=1, source_target_pairs={{0,24},{4,28},{8,16},{12,20},{16,8},{20,12},{24,0},{28,4},{1,25},{... | collective-permute-start | bytes 688136 | tf_op jit(solution)/shard_map/ppermute | solution.py:47
  100.2 2.4 %copy-start.13 = (bf16[4,224,128]{2,1,0:T(8,128)(2,1)}, bf16[4,224,128]{2,1,0:T(8,128)(2,1)S(1)}, u32[]{:S(2)}) copy-start(bf16[4,224,128]{2,1,0:T(8,128)(2,1)S(1)} %collective-permute-done.8) | copy-start | bytes 688132
  100.2 14.8 %collective-permute-start.13 = (bf16[4,224,128]{2,1,0:T(8,128)(2,1)S(1)}, bf16[4,224,128]{2,1,0:T(8,128)(2,1)}, u32[]{:S(2)}, u32[]{:S(2)}) collective-permute-start(bf16[4,224,128]{2,1,0:T(8,128)(2,1)S(1)} %get-tuple-element.48), channel_id=1, source_target_pairs={{0,28},{4,24},{8,20},{12,16},{16,12},{20,8},{24,4},{28,0},{1,29},{... | collective-permute-start | bytes 688136 | tf_op jit(solution)/shard_map/ppermute | solution.py:47
  102.6 12.4 %copy-start.10 = (bf16[4,224,128]{2,1,0:T(8,128)(2,1)S(1)}, bf16[4,224,128]{2,1,0:T(8,128)(2,1)}, u32[]{:S(2)}) copy-start(bf16[4,224,128]{2,1,0:T(8,128)(2,1)} %copy-done.9) | copy-start | bytes 688132
  102.6 12.4 %copy-start.12 = (bf16[4,224,128]{2,1,0:T(8,128)(2,1)S(1)}, bf16[4,224,128]{2,1,0:T(8,128)(2,1)}, u32[]{:S(2)}) copy-start(bf16[4,224,128]{2,1,0:T(8,128)(2,1)} %copy-done.11) | copy-start | bytes 688132
  102.6 12.4 %copy-start.14 = (bf16[4,224,128]{2,1,0:T(8,128)(2,1)S(1)}, bf16[4,224,128]{2,1,0:T(8,128)(2,1)}, u32[]{:S(2)}) copy-start(bf16[4,224,128]{2,1,0:T(8,128)(2,1)} %copy-done.13) | copy-start | bytes 688132
  104.1 0.6 copy-start.19
  104.1 0.6 copy-start.20
  110.0 29.9 %copy-start.5 = (bf16[4,992,128]{2,1,0:T(8,128)(2,1)S(1)}, bf16[4,992,128]{2,1,0:T(8,128)(2,1)}, u32[]{:S(2)}) copy-start(bf16[4,992,128]{2,1,0:T(8,128)(2,1)} %get-tuple-element.50) | copy-start | bytes 3047428
  112.0 27.9 %collective-permute-start.18 = (bf16[2,992,128]{2,1,0:T(8,128)(2,1)}, bf16[2,992,128]{2,1,0:T(8,128)(2,1)}, u32[]{:S(2)}, u32[]{:S(2)}) collective-permute-start(bf16[2,992,128]{2,1,0:T(8,128)(2,1)} %dynamic-slice_bitcast_fusion), channel_id=1, source_target_pairs={{0,1},{1,0},{2,3},{3,2},{4,5},{5,4},{6,7},{7,6},{8,9},{9,8},{10,11... | collective-permute-start | bytes 1523720 | tf_op jit(solution)/shard_map/ppermute | solution.py:47
  116.6 16.9 %all-to-all-start.3 = ((bf16[8,64,128]{2,1,0:T(8,128)(2,1)}), bf16[8,64,128]{2,1,0:T(8,128)(2,1)S(1)}, u32[]{:S(2)}, u32[]{:S(2)}) async-start(bf16[8,64,128]{2,1,0:T(8,128)(2,1)} %bitcast.88), calls=%async_computation.3 | async-start | bytes 262144 | tf_op jit(solution)/shard_map/all_to_all | solution.py:19
  123.4 17.9 %collective-permute-start.14 = (bf16[224,128]{1,0:T(8,128)(2,1)S(1)}, bf16[224,128]{1,0:T(8,128)(2,1)S(1)}, u32[]{:S(2)}, u32[]{:S(2)}) collective-permute-start(bf16[224,128]{1,0:T(8,128)(2,1)S(1)} %get-tuple-element.64), channel_id=1, source_target_pairs={{0,0},{32,128},{64,32},{96,160},{128,64},{160,192},{192,96},{224,2... | collective-permute-start | bytes 172040 | tf_op jit(solution)/shard_map/ppermute | solution.py:465
  124.1 17.2 %collective-permute-start.15 = (bf16[224,128]{1,0:T(8,128)(2,1)S(1)}, bf16[224,128]{1,0:T(8,128)(2,1)S(1)}, u32[]{:S(2)}, u32[]{:S(2)}) collective-permute-start(bf16[224,128]{1,0:T(8,128)(2,1)S(1)} %get-tuple-element.65), channel_id=1, source_target_pairs={{0,32},{32,160},{64,64},{96,192},{128,96},{160,224},{192,0},{224,1... | collective-permute-start | bytes 172040 | tf_op jit(solution)/shard_map/ppermute | solution.py:465
  134.1 8.2 %collective-permute-start.16 = (bf16[224,128]{1,0:T(8,128)(2,1)S(1)}, bf16[224,128]{1,0:T(8,128)(2,1)S(1)}, u32[]{:S(2)}, u32[]{:S(2)}) collective-permute-start(bf16[224,128]{1,0:T(8,128)(2,1)S(1)} %get-tuple-element.66), channel_id=1, source_target_pairs={{0,64},{32,192},{64,96},{96,224},{128,0},{160,128},{192,32},{224,1... | collective-permute-start | bytes 172040 | tf_op jit(solution)/shard_map/ppermute | solution.py:465
  134.2 8.1 %collective-permute-start.17 = (bf16[224,128]{1,0:T(8,128)(2,1)S(1)}, bf16[224,128]{1,0:T(8,128)(2,1)S(1)}, u32[]{:S(2)}, u32[]{:S(2)}) collective-permute-start(bf16[224,128]{1,0:T(8,128)(2,1)S(1)} %get-tuple-element.67), channel_id=1, source_target_pairs={{0,96},{32,224},{64,0},{96,128},{128,32},{160,160},{192,64},{224,1... | collective-permute-start | bytes 172040 | tf_op jit(solution)/shard_map/ppermute | solution.py:465
  141.1 7.0 %collective-permute-start.19 = (bf16[992,128]{1,0:T(8,128)(2,1)S(1)}, bf16[992,128]{1,0:T(8,128)(2,1)S(1)}, u32[]{:S(2)}, u32[]{:S(2)}) collective-permute-start(bf16[992,128]{1,0:T(8,128)(2,1)S(1)} %fusion.1), channel_id=1, source_target_pairs={{0,2},{1,3},{2,0},{3,1},{4,6},{5,7},{6,4},{7,5},{8,10},{9,11},{10,... | collective-permute-start | bytes 761864 | tf_op jit(solution)/shard_map/ppermute | solution.py:47

commit v7 on v6

--- a/solution.py
+++ b/solution.py
@@ -11,7 +11,7 @@
 CLASS_ROWS = 16
 TAPS = 27
 VMEM_LIMIT = 48 * 1024 * 1024
-VMEM_MORE = 56 * 1024 * 1024
+VMEM_MORE = 60 * 1024 * 1024
 STEPS = (-1, 0, 1)
 
 
@@ -28,23 +28,19 @@
     return lax.optimization_barrier((x,) + others)[0]
 
 
-def neighbour(x, depth, height):
-    nx, ny = lax.axis_size("gx"), lax.axis_size("gy")
-    pairs = [
-        (i * ny + j, (i + depth) * ny + j + height)
-        for i in range(nx)
-        for j in range(ny)
-        if 0 <= i + depth < nx and 0 <= j + height < ny
-    ]
-    return lax.ppermute(x, ("gx", "gy"), pairs)
-
-
 def bits_of(axis):
     return [1 << k for k in reversed(range(lax.axis_size(axis).bit_length() - 1))]
 
 
 def swap(x, axis, bit):
     return lax.ppermute(x, axis, [(i, i ^ bit) for i in range(lax.axis_size(axis))])
+
+
+def swap_odd(x, axis):
+    last = lax.axis_size(axis) - 1
+    return lax.ppermute(
+        x, axis, [(i, i + 1 if i % 2 else i - 1) for i in range(1, last)]
+    )
 
 
 def mine_and_other(x, axis, bit, dim):
@@ -106,8 +102,10 @@
     )(*args)
 
 
-def class_kernel(gathered_ref, own_ref, label_ref, *out_refs):
-    plane_refs, aux_ref = out_refs[:-1], out_refs[-1]
+def class_kernel(
+    side_ref, gathered_ref, own_ref, label_ref, later_ref, grad_ref, even_ref, odd_ref, aux_ref
+):
+    del later_ref
     groups, rows, inner = gathered_ref.shape[0], own_ref.shape[0], own_ref.shape[1]
     logits = jnp.zeros((CLASS_ROWS, rows), jnp.float32)
     for c in range(groups):
@@ -124,33 +122,43 @@
         weight = gathered_ref[c, 2 * rows : 2 * rows + CLASS_ROWS]
         total = gathered_ref[c, rows : 2 * rows].astype(jnp.float32) + dot_tn(logit_grad, weight)
         active = gathered_ref[c, :rows].astype(jnp.float32) > 0
-        grad = jnp.where(active, total, 0.0).astype(jnp.bfloat16)
-        size = rows // len(plane_refs)
-        for d, plane_ref in enumerate(plane_refs):
-            plane_ref[:, c * inner : (c + 1) * inner] = grad[d * size : (d + 1) * size]
+        grad_ref[:, c * inner : (c + 1) * inner] = jnp.where(active, total, 0.0).astype(jnp.bfloat16)
+    size = even_ref.shape[0]
+    first = pl.multiple_of((rows - size) * side_ref[0], size)
+    even_ref[...] = grad_ref[pl.ds(rows - size - first, size)]
+    odd_ref[...] = grad_ref[pl.ds(first, size)]
     aux_ref[...] = dot_nn(logit_grad, jnp.maximum(own_ref[...], 0)).astype(jnp.bfloat16)
 
 
-def conv_kernel(*refs):
-    side_ref, planes, (low_ref, high_ref, input_ref, weight_hbm) = refs[0], refs[1:-12], refs[-12:-8]
-    far_ref, out_ref, part_ref, send_ref, acc_ref, pool_ref, weight_ref, sems = refs[-8:]
+def conv_kernel(
+    side_ref,
+    grad_ref,
+    even_x_ref,
+    odd_x_ref,
+    even_y_ref,
+    odd_y_ref,
+    input_ref,
+    edge_ref,
+    weight_ref,
+    far_ref,
+    out_ref,
+    part_ref,
+    send_ref,
+    acc_ref,
+    pool_ref,
+):
     far_d, far_h, width, full = far_ref.shape
     depth, height = far_d - 2, far_h - 2
     inner = out_ref.shape[1]
     rows = depth * height * width
-    copies = []
-    for k in range(9):
-        span = pl.ds(3 * k * full, 3 * full)
-        copies.append(
-            pltpu.make_async_copy(weight_hbm.at[:, span], weight_ref.at[:, span], sems.at[k])
-        )
-        copies[k].start()
-    for d, plane_ref in enumerate(planes):
-        far_ref[d, 1 : 1 + height] = plane_ref[...].reshape(height, width, full)
-    far_ref[:, 0] = low_ref[...]
-    far_ref[:, far_h - 1] = high_ref[...]
+    side_x, side_y = side_ref[0], side_ref[1]
+    far_ref[1 : 1 + depth, 1 : 1 + height] = grad_ref[...].reshape(depth, height, width, full)
+    far_ref[(far_d - 1) * (1 - side_x), 1 : 1 + height] = even_x_ref[...].reshape(height, width, full)
+    far_ref[(far_d - 1) * side_x, 1 : 1 + height] = odd_x_ref[...].reshape(height, width, full)
+    far_ref[:, (far_h - 1) * (1 - side_y)] = even_y_ref[...]
+    far_ref[:, (far_h - 1) * side_y] = odd_y_ref[...]
     sent = far_d // 2
-    send_ref[: sent * far_h * width] = far_ref[pl.ds(sent * side_ref[0], sent)].reshape(-1, full)
+    send_ref[: sent * far_h * width] = far_ref[pl.ds(sent * side_x, sent)].reshape(-1, full)
     piece_rows = rows * inner // full
     for c in range(full // inner):
         send_ref[sent * far_h * width :, c * inner : (c + 1) * inner] = input_ref[
@@ -161,7 +169,6 @@
     for a in STEPS:
         for b in STEPS:
             piece = far_ref[1 - a : 1 - a + depth, 1 - b : 1 - b + height].reshape(rows, full)
-            copies[3 * (a + 1) + b + 1].wait()
             for c in STEPS:
                 tap = 9 * (a + 1) + 3 * (b + 1) + c + 1
                 terms[c + 1] += dot_nt(piece, weight_ref[:, tap * full : (tap + 1) * full])
@@ -172,7 +179,8 @@
     half_d, half_h, half_w = depth // 2, height // 2, width // 2
     nc = part_ref.shape[0]
     block = half_w // nc
-    window = part_ref.shape[1] // (half_d * half_h)
+    cells = part_ref.shape[1] - edge_ref.shape[1]
+    window = cells // (half_d * half_h)
     pool_ref[...] = jnp.zeros_like(pool_ref)
     lines = total.reshape(depth, height, width, inner)
     for d in range(half_d):
@@ -188,7 +196,8 @@
             )
     for c in range(nc):
         start = 7 + c * block
-        part_ref[c] = jnp.concatenate(
+        part_ref[c, cells:] = edge_ref[c]
+        part_ref[c, :cells] = jnp.concatenate(
             [pool_ref[d, h, start : start + window] for d in range(half_d) for h in range(half_h)],
             axis=0,
         ).astype(jnp.bfloat16)
@@ -237,31 +246,13 @@
 
 
 def bottom_kernel(
-    down_ref,
-    up_ref,
-    before_ref,
-    pre_ref,
-    after_ref,
-    source_ref,
-    weight_hbm,
-    part_ref,
-    both_ref,
-    shift_ref,
-    weight_ref,
-    sem,
+    down_ref, up_ref, before_ref, pre_ref, after_ref, weight_ref, part_ref, shift_ref
 ):
-    copy = pltpu.make_async_copy(weight_hbm, weight_ref, sem)
-    copy.start()
     _, far_d, far_w, height, filters = shift_ref.shape
     depth, width = far_d - 2, far_w - 2
     rows = depth * width * height
-    channels = source_ref.shape[1]
-    groups = both_ref.shape[0]
-    thin = channels // groups
-    full = down_ref.shape[1]
-    inner = full // groups
+    channels = part_ref.shape[1]
     back = dot_nt(down_ref[...], up_ref[...])
-    own_saved = pre_ref[...].reshape(rows, filters)
     saved = jnp.concatenate([before_ref[...], pre_ref[...], after_ref[...]], axis=1)
     saved = saved.reshape(depth * far_w * height, filters)
     grad = jnp.where(saved.astype(jnp.float32) > 0, back, 0.0)
@@ -271,13 +262,7 @@
         shift_ref[b + 1, 1 : 1 + depth] = (
             moved(grad, b, height).astype(jnp.bfloat16).reshape(depth, far_w, height, filters)
         )
-    own_down = down_ref[...].reshape(depth, far_w, height, full)[:, 1 : 1 + width].reshape(rows, full)
-    up_part = dot_tn(jnp.maximum(own_saved, 0), own_down).astype(jnp.bfloat16)
-    for cc in range(groups):
-        both_ref[cc, TAPS * thin :] = up_part[:, cc * inner : (cc + 1) * inner]
-    turned = source_ref[...].T
     total = jnp.zeros((rows, channels), jnp.float32)
-    copy.wait()
     for a in STEPS:
         for b in STEPS:
             tap = 9 * (a + 1) + 3 * (b + 1)
@@ -290,13 +275,39 @@
             )
             weight = jnp.concatenate([weight_ref[tap + c] for c in range(3)], axis=1)
             total += dot_nt(piece, weight)
+    part_ref[...] = total.astype(jnp.bfloat16)
+
+
+def bottom_weight_kernel(down_ref, pre_ref, source_ref, shift_ref, both_ref):
+    _, far_d, far_w, height, filters = shift_ref.shape
+    depth, width = far_d - 2, far_w - 2
+    rows, channels = source_ref.shape
+    groups = both_ref.shape[0]
+    thin = channels // groups
+    full = down_ref.shape[1]
+    inner = full // groups
+    own_down = down_ref[...].reshape(depth, far_w, height, full)[:, 1 : 1 + width].reshape(rows, full)
+    own_saved = pre_ref[...].reshape(rows, filters)
+    up_part = dot_tn(jnp.maximum(own_saved, 0), own_down).astype(jnp.bfloat16)
+    for cc in range(groups):
+        both_ref[cc, TAPS * thin :] = up_part[:, cc * inner : (cc + 1) * inner]
+    turned = source_ref[...].T
+    for a in STEPS:
+        for b in STEPS:
+            tap = 9 * (a + 1) + 3 * (b + 1)
+            piece = jnp.concatenate(
+                [
+                    shift_ref[b + 1, 1 - a : 1 - a + depth, 1 - c : 1 - c + width].reshape(rows, filters)
+                    for c in STEPS
+                ],
+                axis=1,
+            )
             terms = dot_nn(turned, piece).astype(jnp.bfloat16)
             for c in range(3):
                 for cc in range(groups):
                     both_ref[cc, (tap + c) * thin : (tap + c + 1) * thin] = terms[
                         cc * thin : (cc + 1) * thin, c * filters : (c + 1) * filters
                     ]
-    part_ref[...] = total.astype(jnp.bfloat16)
 
 
 def per_device(
@@ -312,7 +323,7 @@
     aux_weight,
 ):
     nx, ny, nc = (lax.axis_size(a) for a in ("gx", "gy", "col"))
-    at_x, at_y = lax.axis_index("gx"), lax.axis_index("gy")
+    at_x, at_y, at_c = (lax.axis_index(a) for a in ("gx", "gy", "col"))
     depth, height, width, inner = level_input.shape
     full = inner * nc
     rows = depth * height * width
@@ -334,53 +345,88 @@
     )
     gathered = lax.all_gather(payload, "col")
     lanes = height * width
-    *planes, aux_part = local_call(
+    side_x, side_y = at_x % 2, at_y % 2
+    sides = jnp.stack([side_x, side_y]).astype(jnp.int32)
+    level_pre_grad, even_x, odd_x, aux_part = local_call(
         class_kernel,
-        [struct((lanes, full), bf16)] * depth + [struct((CLASS_ROWS, inner), bf16)],
+        (
+            struct((rows, full), bf16),
+            struct((lanes, full), bf16),
+            struct((lanes, full), bf16),
+            struct((CLASS_ROWS, inner), bf16),
+        ),
         [],
         6 * rows * full * CLASS_ROWS,
         2 * gathered.size,
+        sides,
         gathered,
         own_pre,
         labels.reshape(1, rows),
-    )
-
-    planes = [neighbour(planes[-1], 1, 0)] + planes + [neighbour(planes[0], -1, 0)]
-    low = neighbour(jnp.stack([p[lanes - width :] for p in planes]), 0, 1)
-    high = neighbour(jnp.stack([p[:width] for p in planes]), 0, -1)
+        level_weight,
+        stay=4,
+    )
+
+    even_x = swap(even_x, "gx", 1)
+    odd_x = swap_odd(odd_x, "gx")
+
+    def lines(start):
+        take = lambda x: x[start : start + width]
+        before = jnp.where(side_x == 1, take(even_x), take(odd_x))
+        after = jnp.where(side_x == 1, take(odd_x), take(even_x))
+        own = level_pre_grad.reshape(depth, lanes, full)
+        return jnp.stack([before] + [take(own[d]) for d in range(depth)] + [after])
+
+    first, last = lines(0), lines(lanes - width)
+    even_y = swap(jnp.where(side_y == 1, first, last), "gy", 1)
+    odd_y = swap_odd(jnp.where(side_y == 1, last, first), "gy")
+
+    turned_pre = pre_bottom.transpose(0, 2, 1, 3)
+    edges = jnp.stack(
+        [
+            jnp.where(at_c < c, turned_pre[:, -1], turned_pre[:, 0]).reshape(-1, filters)
+            for c in range(nc)
+        ]
+    )
 
     window = (wide + 7) // 8 * 8
     cells = half_d * half_h * window
-    side = lax.rem(at_x, 2).astype(jnp.int32)
     flat_input = level_input.reshape(rows, inner)
     far, level_input_grad, parts, send = local_call(
         conv_kernel,
         (
             struct((far_d, far_h, width, full), bf16),
             struct((rows, inner), bf16),
-            struct((nc, cells, inner), bf16),
+            struct((nc, cells + edges.shape[1], inner), bf16),
             struct((far_d // 2 * far_h * width + rows * inner // full, full), bf16),
         ),
         [
             pltpu.VMEM((width, inner), f32),
             pltpu.VMEM((half_d, half_h, half_w + 24, inner), f32),
-            pltpu.VMEM(level_weight.shape, bf16),
-            pltpu.SemaphoreType.DMA((9,)),
         ],
         2 * rows * full * TAPS * inner,
         2 * level_weight.size,
-        side.reshape(1),
-        *planes,
-        low,
-        high,
+        sides,
+        level_pre_grad,
+        even_x,
+        odd_x,
+        even_y,
+        odd_y,
         flat_input,
+        edges,
         level_weight,
-        stay=len(planes) + 4,
     )
     got = swap(send, "gx", 1)
     level_input_grad = level_input_grad.reshape(level_input.shape)
 
-    relayed = exchange(parts, "col").reshape(nc * cells, inner)
+    relayed = exchange(parts, "col")
+    edges = relayed[:, cells:].reshape(nc, bottom_d, 1, bottom_h, filters)
+    relayed = relayed[:, :cells].reshape(nc * cells, inner)
+
+    def edge_of(c):
+        found = lax.dynamic_index_in_dim(edges, jnp.clip(c, 0, nc - 1), 0, keepdims=False)
+        return jnp.where((c >= 0) & (c < nc), found, jnp.zeros_like(found))
+
+    pre_before, pre_after = edge_of(at_c - 1), edge_of(at_c + 1)
 
     chunk = TAPS * full // (nx * ny)
     span = chunk + 8 if chunk % 16 else chunk
@@ -396,20 +442,13 @@
         ],
         2 * rows * full * TAPS * inner,
         2 * nx * ny * span * inner,
-        jnp.stack([side, at_y.astype(jnp.int32)]),
+        jnp.stack([side_x, at_y]).astype(jnp.int32),
         far,
         flat_input,
         got,
     )
     terms = [level_parts[0]] + [swap(level_parts[k], "gy", k) for k in range(1, ny)]
     relayed = behind(relayed, level_parts[0])
-
-    turned_pre = pre_bottom.transpose(0, 2, 1, 3)
-    edges = behind(turned_pre, parts)
-    ups = [(i, i + 1) for i in range(nc - 1)]
-    downs = [(j, i) for i, j in ups]
-    pre_before = lax.ppermute(edges[:, -1:], "col", ups)
-    pre_after = lax.ppermute(edges[:, :1], "col", downs)
 
     by_depth = spread(jnp.concatenate([relayed, aux_part]), "gx")
     aux_sum = by_depth[:, nc * cells :].astype(f32).sum(axis=0).astype(bf16)
@@ -431,27 +470,32 @@
     bottom_rows = bottom_d * block * bottom_h
     channel_width = bottom_weight.shape[0]
     thin = channel_width // nc
-    part, both = local_call(
+    part, shifts = local_call(
         bottom_kernel,
         (
             struct((bottom_rows, channel_width), bf16),
-            struct((nc, TAPS * thin + filters, inner), bf16),
+            struct((3, bottom_d + 2, wide, bottom_h, filters), bf16),
         ),
-        [
-            pltpu.VMEM((3, bottom_d + 2, wide, bottom_h, filters), bf16),
-            pltpu.VMEM((TAPS, channel_width, filters), bf16),
-            pltpu.SemaphoreType.DMA(()),
-        ],
-        4 * bottom_rows * channel_width * TAPS * filters,
+        [],
+        2 * bottom_rows * channel_width * TAPS * filters,
         2 * bottom_weight.size,
         down_wide,
         up_weight,
         pre_before,
         turned_pre,
         pre_after,
+        bottom_weight.transpose(1, 0, 2),
+    )
+    (both,) = local_call(
+        bottom_weight_kernel,
+        [struct((nc, TAPS * thin + filters, inner), bf16)],
+        [],
+        2 * bottom_rows * channel_width * TAPS * filters,
+        2 * bottom_weight.size,
+        down_wide,
+        turned_pre,
         bottom_input.transpose(0, 2, 1, 3).reshape(bottom_rows, channel_width),
-        bottom_weight.transpose(1, 0, 2),
-        stay=6,
+        shifts,
     )
     part = exchange(part.reshape(ny, bottom_rows // ny, channel_width), "gy")
     pairs = nx // 2

time: 151 us -> 153 us (1.013)
  the two profiles are of different devices: /device:TPU:6 before, /device:TPU:1 now
where the time goes in v7:
time: 153 us; the launch traced here: 150 us
  starting transfers between devices  77.6 us (51%)
  waiting for transfers between devices  27 us (18%)
  local copies, waits for them, and re-layouts  14.8 us (10%)
  Pallas kernels  13.1 us (9%)
  blocking collectives  10.1 us (7%)
  other arithmetic  6.63 us (4%)
    ppermute x12, starting transfers between devices, swap(): lax.ppermute(x, axis, [(i, i ^ bit) for i in range(lax.axis_size(axis))])  40.1 us
    ppermute x12, waiting for transfers between devices, swap(): lax.ppermute(x, axis, [(i, i ^ bit) for i in range(lax.axis_size(axis))])  21.6 us
    all_to_all x4, starting transfers between devices, exchange(): return lax.all_to_all(x, axis, split_axis=0, concat_axis=0, tiled=False)  21.4 us
    ppermute x4, starting transfers between devices, per_device(): lax.ppermute(chosen, 'gx', [(i, i % 2 * pairs + (i // 2 + step) % pairs)...  14.1 us
    pallas_call x5, Pallas kernels, local_call(): pl.pallas_call(body, out_shape=list(out_shapes), in_specs=[pl.BlockSpec(m...  13.1 us
    all_gather x1, blocking collectives, per_device(): gathered = lax.all_gather(payload, 'col')  10.1 us
    unnamed x42, local copies, waits for them, and re-layouts  6.9 us
    all_to_all x4, waiting for transfers between devices, exchange(): return lax.all_to_all(x, axis, split_axis=0, concat_axis=0, tiled=False)  5.4 us
  transfers between devices with their start and end apart: 22, of which 9 were waited for; matrix products, arithmetic and copies ran while one was open for 6% of the time, Pallas kernels for 2%

profile of v7, /device:TPU:1, one launch (start us, length us, event | category | flops | bytes accessed | tf_op | source)
XLA Modules:
  0.0 150.4 jit_solution(8274184997388802496)
XLA Ops:
  0.7 1.5 reshape.183.label_ref
  2.1 0.9 fusion.2
  3.0 10.1 %all-gather = bf16[2112,128]{1,0:T(8,128)(2,1)} all-gather(bf16[528,128]{1,0:T(8,128)(2,1)S(1)} %fusion.2), channel_id=2, replica_groups=mesh['gx'=8,'gy'=8,'col'=4] {'col'}, dimensions={0}, use_global_device_ids=true | all-gather | bytes 675840 | tf_op jit(solution)/shard_map/all_gather | solution.py:346
  13.8 2.5 %shard_map.145 = (bf16[256,512]{1,0:T(8,128)(2,1)}, bf16[128,512]{1,0:T(8,128)(2,1)}, bf16[128,512]{1,0:T(8,128)(2,1)}, bf16[16,128]{1,0:T(8,128)(2,1)}) custom-call(s32[2]{0:T(128)} %pad_add_fusion.side_ref, bf16[4,528,128]{2,1,0:T(8,128)(2,1)} %bitcast.97, bf16[256,128]{1,0:T(8,128)(2,1)} %bitcast.102, s32[1,256]{1,0:T(1,128)} %reshape.183.label_ref, ...), custom_call_target="tpu_custom_call" | custom-call | flops 12582912 | bytes 540672 | tf_op jit(solution)/shard_map/pallas_call | solution.py:89
  16.9 1.3 collective-permute-start.1
  18.2 0.9 copy.39
  19.1 0.9 slice_bitcast_fusion.3
  20.0 1.5 %collective-permute-done.even_x_ref = bf16[128,512]{1,0:T(8,128)(2,1)} collective-permute-done((bf16[128,512]{1,0:T(8,128)(2,1)}, bf16[128,512]{1,0:T(8,128)(2,1)}, u32[]{:S(2)}, u32[]{:S(2)}) %collective-permute-start) | collective-permute-done | bytes 131104 | tf_op jit(solution)/shard_map/ppermute | solution.py:36
  21.5 0.8 select_bitcast_fusion.5
  23.1 4.7 %collective-permute-start.2 = (bf16[4,32,512]{2,1,0:T(8,128)(2,1)S(1)}, bf16[4,32,512]{2,1,0:T(8,128)(2,1)S(1)}, u32[]{:S(2)}, u32[]{:S(2)}) collective-permute-start(bf16[4,32,512]{2,1,0:T(8,128)(2,1)S(1)} %get-tuple-element.65), channel_id=1, source_target_pairs={{0,4},{4,0},{8,12},{12,8},{16,20},{20,16},{24,28},{28,24},{1,5},{5... | collective-permute-start | bytes 393224 | tf_op jit(solution)/shard_map/ppermute | solution.py:36
  27.8 5.4 %collective-permute-done.2.even_y_ref = bf16[4,32,512]{2,1,0:T(8,128)(2,1)S(1)} collective-permute-done((bf16[4,32,512]{2,1,0:T(8,128)(2,1)S(1)}, bf16[4,32,512]{2,1,0:T(8,128)(2,1)S(1)}, u32[]{:S(2)}, u32[]{:S(2)}) %collective-permute-start.2) | collective-permute-done | bytes 131104 | tf_op jit(solution)/shard_map/ppermute | solution.py:36
  33.3 0.9 copy-done.4
  34.2 0.8 copy-done.7
  35.0 3.8 %shard_map.146 = (bf16[4,6,32,512]{3,2,1,0:T(8,128)(2,1)S(1)}, bf16[256,128]{1,0:T(8,128)(2,1)}, bf16[4,144,128]{2,1,0:T(8,128)(2,1)S(1)}, bf16[448,512]{1,0:T(8,128)(2,1)}) custom-call(s32[2]{0:T(128)S(1)} %copy-done.9, bf16[256,512]{1,0:T(8,128)(2,1)S(1)} %copy-done.4, bf16[128,512]{1,0:T(8,128)(2,1)} %collective-permute-done.even_x_ref, ...), custom_call_target="tpu_custom_call" | custom-call | flops 905969664 | bytes 3538944 | tf_op jit(solution)/shard_map/pallas_call | solution.py:89
  38.8 0.9 copy-done.10
  39.7 4.4 %collective-permute-start.4 = (bf16[448,512]{1,0:T(8,128)(2,1)}, bf16[448,512]{1,0:T(8,128)(2,1)S(1)}, u32[]{:S(2)}, u32[]{:S(2)}) collective-permute-start(bf16[448,512]{1,0:T(8,128)(2,1)} %get-tuple-element.35), channel_id=1, source_target_pairs={{0,32},{32,0},{64,96},{96,64},{128,160},{160,128},{192,224},{224,1... | collective-permute-start | bytes 1376264 | tf_op jit(solution)/shard_map/ppermute | solution.py:36
  44.2 5.7 %all-to-all-start = ((bf16[4,144,128]{2,1,0:T(8,128)(2,1)}), bf16[4,144,128]{2,1,0:T(8,128)(2,1)S(1)}, u32[]{:S(2)}, u32[]{:S(2)}) async-start(bf16[4,144,128]{2,1,0:T(8,128)(2,1)} %copy-done.5), calls=%async_computation | async-start | bytes 294912 | tf_op jit(solution)/shard_map/all_to_all | solution.py:19
  50.0 3.9 %all-to-all-done = bf16[4,144,128]{2,1,0:T(8,128)(2,1)S(1)} async-done(((bf16[4,144,128]{2,1,0:T(8,128)(2,1)}), bf16[4,144,128]{2,1,0:T(8,128)(2,1)S(1)}, u32[]{:S(2)}, u32[]{:S(2)}) %all-to-all-start) | async-done | bytes 147488 | tf_op jit(solution)/shard_map/all_to_all | solution.py:19
  54.0 0.8 copy-done.8
  54.8 1.1 copy-done.11
  55.9 3.6 %shard_map.147 = (bf16[4,224,128]{2,1,0:T(8,128)(2,1)S(1)}, bf16[4,224,128]{2,1,0:T(8,128)(2,1)S(1)}, bf16[4,224,128]{2,1,0:T(8,128)(2,1)S(1)}, bf16[4,224,128]{...) custom-call(s32[2]{0:T(128)S(1)} %pad_add_fusion.1.place_ref, ...), custom_call_target="tpu_custom_call" | custom-call | flops 905969664 | bytes 3670016 | tf_op jit(solution)/shard_map/pallas_call | solution.py:89
  59.6 0.7 broadcast_in_dim.4
  60.3 6.7 %all-to-all-start.1 = ((bf16[8,80,128]{2,1,0:T(8,128)(2,1)}), bf16[8,80,128]{2,1,0:T(8,128)(2,1)S(1)}, u32[]{:S(2)}, u32[]{:S(2)}) async-start(bf16[8,80,128]{2,1,0:T(8,128)(2,1)} %broadcast_in_dim.4), calls=%async_computation.1 | async-start | bytes 327680 | tf_op jit(solution)/shard_map/all_to_all | solution.py:19
  67.0 1.3 collective-permute-start.5
  68.3 2.3 %collective-permute-start.6 = (bf16[4,224,128]{2,1,0:T(8,128)(2,1)S(1)}, bf16[4,224,128]{2,1,0:T(8,128)(2,1)S(1)}, u32[]{:S(2)}, u32[]{:S(2)}) collective-permute-start(bf16[4,224,128]{2,1,0:T(8,128)(2,1)S(1)} %get-tuple-element.40), channel_id=1, source_target_pairs={{0,8},{4,12},{8,0},{12,4},{16,24},{20,28},{24,16},{28,20},{1,9},{5... | collective-permute-start | bytes 688136 | tf_op jit(solution)/shard_map/ppermute | solution.py:36
  71.2 2.2 %collective-permute-done.5 = bf16[4,224,128]{2,1,0:T(8,128)(2,1)S(1)} collective-permute-done((bf16[4,224,128]{2,1,0:T(8,128)(2,1)S(1)}, bf16[4,224,128]{2,1,0:T(8,128)(2,1)S(1)}, u32[]{:S(2)}, u32[]{:S(2)}) %collective-permute-start.5) | collective-permute-done | bytes 229408 | tf_op jit(solution)/shard_map/ppermute | solution.py:36
  73.4 0.9 collective-permute-done.6
  74.3 5.7 %collective-permute-done.7 = bf16[4,224,128]{2,1,0:T(8,128)(2,1)S(1)} collective-permute-done((bf16[4,224,128]{2,1,0:T(8,128)(2,1)S(1)}, bf16[4,224,128]{2,1,0:T(8,128)(2,1)S(1)}, u32[]{:S(2)}, u32[]{:S(2)}) %collective-permute-start.7) | collective-permute-done | bytes 229408 | tf_op jit(solution)/shard_map/ppermute | solution.py:36
  80.1 1.0 broadcast_in_dim.5
  81.2 4.0 %all-to-all-start.2 = ((bf16[8,400,128]{2,1,0:T(8,128)(2,1)}), bf16[8,400,128]{2,1,0:T(8,128)(2,1)S(1)}, u32[]{:S(2)}, u32[]{:S(2)}) async-start(bf16[8,400,128]{2,1,0:T(8,128)(2,1)} %broadcast_in_dim.5), calls=%async_computation.2 | async-start | bytes 1638400 | tf_op jit(solution)/shard_map/all_to_all | solution.py:19
  85.2 3.0 %collective-permute-start.8 = (bf16[4,224,128]{2,1,0:T(8,128)(2,1)S(1)}, bf16[4,224,128]{2,1,0:T(8,128)(2,1)}, u32[]{:S(2)}, u32[]{:S(2)}) collective-permute-start(bf16[4,224,128]{2,1,0:T(8,128)(2,1)S(1)} %get-tuple-element.43), channel_id=1, source_target_pairs={{0,16},{4,20},{8,24},{12,28},{16,0},{20,4},{24,8},{28,12},{1,17},{... | collective-permute-start | bytes 688136 | tf_op jit(solution)/shard_map/ppermute | solution.py:36
  88.2 1.0 copy.30
  89.3 2.8 %collective-permute-start.9 = (bf16[4,224,128]{2,1,0:T(8,128)(2,1)S(1)}, bf16[4,224,128]{2,1,0:T(8,128)(2,1)}, u32[]{:S(2)}, u32[]{:S(2)}) collective-permute-start(bf16[4,224,128]{2,1,0:T(8,128)(2,1)S(1)} %get-tuple-element.46), channel_id=1, source_target_pairs={{0,20},{4,16},{8,28},{12,24},{16,4},{20,0},{24,12},{28,8},{1,21},{... | collective-permute-start | bytes 688136 | tf_op jit(solution)/shard_map/ppermute | solution.py:36
  92.1 2.4 %collective-permute-start.10 = (bf16[4,224,128]{2,1,0:T(8,128)(2,1)S(1)}, bf16[4,224,128]{2,1,0:T(8,128)(2,1)}, u32[]{:S(2)}, u32[]{:S(2)}) collective-permute-start(bf16[4,224,128]{2,1,0:T(8,128)(2,1)S(1)} %get-tuple-element.47), channel_id=1, source_target_pairs={{0,24},{4,28},{8,16},{12,20},{16,8},{20,12},{24,0},{28,4},{1,25},{... | collective-permute-start | bytes 688136 | tf_op jit(solution)/shard_map/ppermute | solution.py:36
  94.6 1.4 all-to-all-done.2
  97.2 1.1 collective-permute-done.8
  98.4 2.3 %shard_map.148 = (bf16[512,128]{1,0:T(8,128)(2,1)}, bf16[3,10,6,16,128]{4,3,2,1,0:T(8,128)(2,1)S(1)}) custom-call(bf16[768,512]{1,0:T(8,128)(2,1)S(1)} %bitcast.84, bf16[128,512]{1,0:T(8,128)(2,1)S(1)} %copy-done.6, bf16[8,1,16,128]{3,2,1,0:T(8,128)(2,1)S(1)} %get-tuple-element.79.before_ref, bf16[8,4,16,128]{3,2,1,0:T(8,128)(2,1)S(1)} %bitcast.89, ...), custom_call_target="tpu_custom_call" | custom-call | flops 452984832 | bytes 884736 | tf_op jit(solution)/shard_map/pallas_call | solution.py:89
  100.7 0.9 shard_map.149
  101.6 0.8 dynamic-slice_bitcast_fusion
  102.4 17.1 %collective-permute-start.16 = (bf16[2,992,128]{2,1,0:T(8,128)(2,1)}, bf16[2,992,128]{2,1,0:T(8,128)(2,1)}, u32[]{:S(2)}, u32[]{:S(2)}) collective-permute-start(bf16[2,992,128]{2,1,0:T(8,128)(2,1)} %dynamic-slice_bitcast_fusion), channel_id=1, source_target_pairs={{0,1},{1,0},{2,3},{3,2},{4,5},{5,4},{6,7},{7,6},{8,9},{9,8},{10,11... | collective-permute-start | bytes 1523720 | tf_op jit(solution)/shard_map/ppermute | solution.py:36
  119.5 1.5 %add_convert_fusion = bf16[4,224,128]{2,1,0:T(8,128)(2,1)S(1)} fusion(bf16[4,224,128]{2,1,0:T(8,128)(2,1)} %collective-permute-done.11, bf16[4,224,128]{2,1,0:T(8,128)(2,1)} %collective-permute-done.10, bf16[4,224,128]{2,1,0:T(8,128)(2,1)} %collective-permute-done.9, bf16[4,224,128]{2,1,0:T(8,128)(2,1)} %collective-permute-done.8, ...), kind=kLoop, calls=%fused_computation.5 | loop fusion | flops 1835008 | bytes 2064384 | tf_op jit(solution)/shard_map/convert_element_type | solution.py:467
  121.1 4.9 %all-to-all-start.3 = ((bf16[8,64,128]{2,1,0:T(8,128)(2,1)}), bf16[8,64,128]{2,1,0:T(8,128)(2,1)S(1)}, u32[]{:S(2)}, u32[]{:S(2)}) async-start(bf16[8,64,128]{2,1,0:T(8,128)(2,1)} %bitcast.31), calls=%async_computation.3 | async-start | bytes 262144 | tf_op jit(solution)/shard_map/all_to_all | solution.py:19
  126.6 8.2 %collective-permute-start.13 = (bf16[224,128]{1,0:T(8,128)(2,1)S(1)}, bf16[224,128]{1,0:T(8,128)(2,1)S(1)}, u32[]{:S(2)}, u32[]{:S(2)}) collective-permute-start(bf16[224,128]{1,0:T(8,128)(2,1)S(1)} %get-tuple-element.75), channel_id=1, source_target_pairs={{0,32},{32,160},{64,64},{96,192},{128,96},{160,224},{192,0},{224,1... | collective-permute-start | bytes 172040 | tf_op jit(solution)/shard_map/ppermute | solution.py:509
  136.2 5.1 %collective-permute-start.15 = (bf16[224,128]{1,0:T(8,128)(2,1)S(1)}, bf16[224,128]{1,0:T(8,128)(2,1)S(1)}, u32[]{:S(2)}, u32[]{:S(2)}) collective-permute-start(bf16[224,128]{1,0:T(8,128)(2,1)S(1)} %get-tuple-element.77), channel_id=1, source_target_pairs={{0,96},{32,224},{64,0},{96,128},{128,32},{160,160},{192,64},{224,1... | collective-permute-start | bytes 172040 | tf_op jit(solution)/shard_map/ppermute | solution.py:509
  141.4 1.2 convert_add_fusion
  142.6 1.0 collective-permute-start.17
  144.3 4.7 %collective-permute-done.17 = bf16[992,128]{1,0:T(8,128)(2,1)S(1)} collective-permute-done((bf16[992,128]{1,0:T(8,128)(2,1)S(1)}, bf16[992,128]{1,0:T(8,128)(2,1)S(1)}, u32[]{:S(2)}, u32[]{:S(2)}) %collective-permute-start.17) | collective-permute-done | bytes 253984 | tf_op jit(solution)/shard_map/ppermute | solution.py:36
  149.6 0.8 slice.119
  (79 shorter events, 7.5 us)
Async XLA Ops:
  0.6 32.6 %copy-start = (bf16[128,13824]{1,0:T(8,128)(2,1)S(1)}, bf16[128,13824]{1,0:T(8,128)(2,1)}, u32[]{:S(2)}) copy-start(bf16[128,13824]{1,0:T(8,128)(2,1)} %weight_ref.1) | copy-start | bytes 10616836
  13.8 19.5 %copy-start.9 = (s32[2]{0:T(128)S(1)}, s32[2]{0:T(128)}, u32[]{:S(2)}) copy-start(s32[2]{0:T(128)} %pad_add_fusion.side_ref) | copy-start | bytes 28
  16.3 5.3 %collective-permute-start = (bf16[128,512]{1,0:T(8,128)(2,1)}, bf16[128,512]{1,0:T(8,128)(2,1)}, u32[]{:S(2)}, u32[]{:S(2)}) collective-permute-start(bf16[128,512]{1,0:T(8,128)(2,1)} %get-tuple-element.30), channel_id=1, source_target_pairs={{0,32},{32,0},{64,96},{96,64},{128,160},{160,128},{192,224},{224,1... | collective-permute-start | bytes 393224 | tf_op jit(solution)/shard_map/ppermute | solution.py:36
  16.9 4.7 %collective-permute-start.1 = (bf16[128,512]{1,0:T(8,128)(2,1)}, bf16[128,512]{1,0:T(8,128)(2,1)}, u32[]{:S(2)}, u32[]{:S(2)}) collective-permute-start(bf16[128,512]{1,0:T(8,128)(2,1)} %get-tuple-element.31), channel_id=1, source_target_pairs={{32,64},{64,32},{96,128},{128,96},{160,192},{192,160},{33,65},{65,... | collective-permute-start | bytes 393224 | tf_op jit(solution)/shard_map/ppermute | solution.py:41
  19.1 8.6 %copy-start.1 = (bf16[8,16,4,128]{3,1,2,0:T(8,128)(2,1)}, bf16[8,16,4,128]{3,1,2,0:T(8,128)(2,1)S(1)}, u32[]{:S(2)}) copy-start(bf16[8,16,4,128]{3,1,2,0:T(8,128)(2,1)S(1)} %copy.39) | copy-start | bytes 393220
  22.4 5.4 %collective-permute-start.3 = (bf16[4,32,512]{2,1,0:T(8,128)(2,1)S(1)}, bf16[4,32,512]{2,1,0:T(8,128)(2,1)S(1)}, u32[]{:S(2)}, u32[]{:S(2)}) collective-permute-start(bf16[4,32,512]{2,1,0:T(8,128)(2,1)S(1)} %get-tuple-element.64), channel_id=1, source_target_pairs={{4,8},{8,4},{12,16},{16,12},{20,24},{24,20},{5,9},{9,5},{13,17},{1... | collective-permute-start | bytes 393224 | tf_op jit(solution)/shard_map/ppermute | solution.py:41
  23.1 10.2 %collective-permute-start.2 = (bf16[4,32,512]{2,1,0:T(8,128)(2,1)S(1)}, bf16[4,32,512]{2,1,0:T(8,128)(2,1)S(1)}, u32[]{:S(2)}, u32[]{:S(2)}) collective-permute-start(bf16[4,32,512]{2,1,0:T(8,128)(2,1)S(1)} %get-tuple-element.65), channel_id=1, source_target_pairs={{0,4},{4,0},{8,12},{12,8},{16,20},{20,16},{24,28},{28,24},{1,5},{5... | collective-permute-start | bytes 393224 | tf_op jit(solution)/shard_map/ppermute | solution.py:36
  33.3 1.0 copy-start.4
  34.2 0.8 copy-start.7
  35.0 24.5 %copy-start.18 = (bf16[16,128]{1,0:T(8,128)(2,1)S(1)}, bf16[16,128]{1,0:T(8,128)(2,1)}, u32[]{:S(2)}) copy-start(bf16[16,128]{1,0:T(8,128)(2,1)} %get-tuple-element.38) | copy-start | bytes 12292
  38.8 0.9 copy-start.10
  39.7 4.4 %copy-start.5 = (bf16[4,144,128]{2,1,0:T(8,128)(2,1)}, bf16[4,144,128]{2,1,0:T(8,128)(2,1)S(1)}, u32[]{:S(2)}) copy-start(bf16[4,144,128]{2,1,0:T(8,128)(2,1)S(1)} %get-tuple-element.33) | copy-start | bytes 442372
  39.7 14.2 %collective-permute-start.4 = (bf16[448,512]{1,0:T(8,128)(2,1)}, bf16[448,512]{1,0:T(8,128)(2,1)S(1)}, u32[]{:S(2)}, u32[]{:S(2)}) collective-permute-start(bf16[448,512]{1,0:T(8,128)(2,1)} %get-tuple-element.35), channel_id=1, source_target_pairs={{0,32},{32,0},{64,96},{96,64},{128,160},{160,128},{192,224},{224,1... | collective-permute-start | bytes 1376264 | tf_op jit(solution)/shard_map/ppermute | solution.py:36
  44.2 9.8 %all-to-all-start = ((bf16[4,144,128]{2,1,0:T(8,128)(2,1)}), bf16[4,144,128]{2,1,0:T(8,128)(2,1)S(1)}, u32[]{:S(2)}, u32[]{:S(2)}) async-start(bf16[4,144,128]{2,1,0:T(8,128)(2,1)} %copy-done.5), calls=%async_computation | async-start | bytes 294912 | tf_op jit(solution)/shard_map/all_to_all | solution.py:19
  54.0 0.8 copy-start.8
  54.8 1.1 copy-start.11
  60.3 19.8 %all-to-all-start.1 = ((bf16[8,80,128]{2,1,0:T(8,128)(2,1)}), bf16[8,80,128]{2,1,0:T(8,128)(2,1)S(1)}, u32[]{:S(2)}, u32[]{:S(2)}) async-start(bf16[8,80,128]{2,1,0:T(8,128)(2,1)} %broadcast_in_dim.4), calls=%async_computation.1 | async-start | bytes 327680 | tf_op jit(solution)/shard_map/all_to_all | solution.py:19
  67.0 6.4 %collective-permute-start.5 = (bf16[4,224,128]{2,1,0:T(8,128)(2,1)S(1)}, bf16[4,224,128]{2,1,0:T(8,128)(2,1)S(1)}, u32[]{:S(2)}, u32[]{:S(2)}) collective-permute-start(bf16[4,224,128]{2,1,0:T(8,128)(2,1)S(1)} %get-tuple-element.39), channel_id=1, source_target_pairs={{0,4},{4,0},{8,12},{12,8},{16,20},{20,16},{24,28},{28,24},{1,5},{5... | collective-permute-start | bytes 688136 | tf_op jit(solution)/shard_map/ppermute | solution.py:36
  68.3 6.0 %collective-permute-start.6 = (bf16[4,224,128]{2,1,0:T(8,128)(2,1)S(1)}, bf16[4,224,128]{2,1,0:T(8,128)(2,1)S(1)}, u32[]{:S(2)}, u32[]{:S(2)}) collective-permute-start(bf16[4,224,128]{2,1,0:T(8,128)(2,1)S(1)} %get-tuple-element.40), channel_id=1, source_target_pairs={{0,8},{4,12},{8,0},{12,4},{16,24},{20,28},{24,16},{28,20},{1,9},{5... | collective-permute-start | bytes 688136 | tf_op jit(solution)/shard_map/ppermute | solution.py:36
  70.6 9.4 %collective-permute-start.7 = (bf16[4,224,128]{2,1,0:T(8,128)(2,1)S(1)}, bf16[4,224,128]{2,1,0:T(8,128)(2,1)S(1)}, u32[]{:S(2)}, u32[]{:S(2)}) collective-permute-start(bf16[4,224,128]{2,1,0:T(8,128)(2,1)S(1)} %get-tuple-element.41), channel_id=1, source_target_pairs={{0,12},{4,8},{8,4},{12,0},{16,28},{20,24},{24,20},{28,16},{1,13},{... | collective-permute-start | bytes 688136 | tf_op jit(solution)/shard_map/ppermute | solution.py:36
  73.4 14.8 %copy-start.12 = (bf16[4,224,128]{2,1,0:T(8,128)(2,1)}, bf16[4,224,128]{2,1,0:T(8,128)(2,1)S(1)}, u32[]{:S(2)}) copy-start(bf16[4,224,128]{2,1,0:T(8,128)(2,1)S(1)} %collective-permute-done.5) | copy-start | bytes 688132
  74.3 5.7 %copy-start.14 = (bf16[4,224,128]{2,1,0:T(8,128)(2,1)}, bf16[4,224,128]{2,1,0:T(8,128)(2,1)S(1)}, u32[]{:S(2)}) copy-start(bf16[4,224,128]{2,1,0:T(8,128)(2,1)S(1)} %collective-permute-done.6) | copy-start | bytes 688132
  80.0 1.1 copy-start.16
  81.2 14.9 %all-to-all-start.2 = ((bf16[8,400,128]{2,1,0:T(8,128)(2,1)}), bf16[8,400,128]{2,1,0:T(8,128)(2,1)S(1)}, u32[]{:S(2)}, u32[]{:S(2)}) async-start(bf16[8,400,128]{2,1,0:T(8,128)(2,1)} %broadcast_in_dim.5), calls=%async_computation.2 | async-start | bytes 1638400 | tf_op jit(solution)/shard_map/all_to_all | solution.py:19
  85.2 13.1 %collective-permute-start.8 = (bf16[4,224,128]{2,1,0:T(8,128)(2,1)S(1)}, bf16[4,224,128]{2,1,0:T(8,128)(2,1)}, u32[]{:S(2)}, u32[]{:S(2)}) collective-permute-start(bf16[4,224,128]{2,1,0:T(8,128)(2,1)S(1)} %get-tuple-element.43), channel_id=1, source_target_pairs={{0,16},{4,20},{8,24},{12,28},{16,0},{20,4},{24,8},{28,12},{1,17},{... | collective-permute-start | bytes 688136 | tf_op jit(solution)/shard_map/ppermute | solution.py:36
  88.2 10.2 %copy-start.2 = (bf16[8,16,4,128]{3,1,2,0:T(8,128)(2,1)S(1)}, bf16[8,16,4,128]{3,1,2,0:T(8,128)(2,1)}, u32[]{:S(2)}) copy-start(bf16[8,16,4,128]{3,1,2,0:T(8,128)(2,1)} %copy-done.1) | copy-start | bytes 393220
  88.2 10.2 %copy-start.3 = (bf16[128,27,128]{2,0,1:T(8,128)(2,1)S(1)}, bf16[128,27,128]{2,0,1:T(8,128)(2,1)}, u32[]{:S(2)}) copy-start(bf16[128,27,128]{2,0,1:T(8,128)(2,1)} %param.12) | copy-start | bytes 2654212
  88.2 10.2 %copy-start.6 = (bf16[128,512]{1,0:T(8,128)(2,1)S(1)}, bf16[128,512]{1,0:T(8,128)(2,1)}, u32[]{:S(2)}) copy-start(bf16[128,512]{1,0:T(8,128)(2,1)} %up_ref.1) | copy-start | bytes 393220
  89.3 30.1 %collective-permute-start.9 = (bf16[4,224,128]{2,1,0:T(8,128)(2,1)S(1)}, bf16[4,224,128]{2,1,0:T(8,128)(2,1)}, u32[]{:S(2)}, u32[]{:S(2)}) collective-permute-start(bf16[4,224,128]{2,1,0:T(8,128)(2,1)S(1)} %get-tuple-element.46), channel_id=1, source_target_pairs={{0,20},{4,16},{8,28},{12,24},{16,4},{20,0},{24,12},{28,8},{1,21},{... | collective-permute-start | bytes 688136 | tf_op jit(solution)/shard_map/ppermute | solution.py:36
  92.1 27.4 %collective-permute-start.10 = (bf16[4,224,128]{2,1,0:T(8,128)(2,1)S(1)}, bf16[4,224,128]{2,1,0:T(8,128)(2,1)}, u32[]{:S(2)}, u32[]{:S(2)}) collective-permute-start(bf16[4,224,128]{2,1,0:T(8,128)(2,1)S(1)} %get-tuple-element.47), channel_id=1, source_target_pairs={{0,24},{4,28},{8,16},{12,20},{16,8},{20,12},{24,0},{28,4},{1,25},{... | collective-permute-start | bytes 688136 | tf_op jit(solution)/shard_map/ppermute | solution.py:36
  94.5 25.0 %collective-permute-start.11 = (bf16[4,224,128]{2,1,0:T(8,128)(2,1)S(1)}, bf16[4,224,128]{2,1,0:T(8,128)(2,1)}, u32[]{:S(2)}, u32[]{:S(2)}) collective-permute-start(bf16[4,224,128]{2,1,0:T(8,128)(2,1)S(1)} %get-tuple-element.48), channel_id=1, source_target_pairs={{0,28},{4,24},{8,20},{12,16},{16,12},{20,8},{24,4},{28,0},{1,29},{... | collective-permute-start | bytes 688136 | tf_op jit(solution)/shard_map/ppermute | solution.py:36
  97.1 22.4 %copy-start.13 = (bf16[4,224,128]{2,1,0:T(8,128)(2,1)S(1)}, bf16[4,224,128]{2,1,0:T(8,128)(2,1)}, u32[]{:S(2)}) copy-start(bf16[4,224,128]{2,1,0:T(8,128)(2,1)} %copy-done.12) | copy-start | bytes 688132
  97.1 22.4 %copy-start.15 = (bf16[4,224,128]{2,1,0:T(8,128)(2,1)S(1)}, bf16[4,224,128]{2,1,0:T(8,128)(2,1)}, u32[]{:S(2)}) copy-start(bf16[4,224,128]{2,1,0:T(8,128)(2,1)} %copy-done.14) | copy-start | bytes 688132
  97.1 22.4 %copy-start.17 = (bf16[4,224,128]{2,1,0:T(8,128)(2,1)S(1)}, bf16[4,224,128]{2,1,0:T(8,128)(2,1)}, u32[]{:S(2)}) copy-start(bf16[4,224,128]{2,1,0:T(8,128)(2,1)} %copy-done.16) | copy-start | bytes 688132
  102.4 38.9 %collective-permute-start.16 = (bf16[2,992,128]{2,1,0:T(8,128)(2,1)}, bf16[2,992,128]{2,1,0:T(8,128)(2,1)}, u32[]{:S(2)}, u32[]{:S(2)}) collective-permute-start(bf16[2,992,128]{2,1,0:T(8,128)(2,1)} %dynamic-slice_bitcast_fusion), channel_id=1, source_target_pairs={{0,1},{1,0},{2,3},{3,2},{4,5},{5,4},{6,7},{7,6},{8,9},{9,8},{10,11... | collective-permute-start | bytes 1523720 | tf_op jit(solution)/shard_map/ppermute | solution.py:36
  121.1 14.4 %all-to-all-start.3 = ((bf16[8,64,128]{2,1,0:T(8,128)(2,1)}), bf16[8,64,128]{2,1,0:T(8,128)(2,1)S(1)}, u32[]{:S(2)}, u32[]{:S(2)}) async-start(bf16[8,64,128]{2,1,0:T(8,128)(2,1)} %bitcast.31), calls=%async_computation.3 | async-start | bytes 262144 | tf_op jit(solution)/shard_map/all_to_all | solution.py:19
  126.0 17.6 %collective-permute-start.12 = (bf16[224,128]{1,0:T(8,128)(2,1)S(1)}, bf16[224,128]{1,0:T(8,128)(2,1)S(1)}, u32[]{:S(2)}, u32[]{:S(2)}) collective-permute-start(bf16[224,128]{1,0:T(8,128)(2,1)S(1)} %get-tuple-element.74), channel_id=1, source_target_pairs={{0,0},{32,128},{64,32},{96,160},{128,64},{160,192},{192,96},{224,2... | collective-permute-start | bytes 172040 | tf_op jit(solution)/shard_map/ppermute | solution.py:509
  126.6 16.9 %collective-permute-start.13 = (bf16[224,128]{1,0:T(8,128)(2,1)S(1)}, bf16[224,128]{1,0:T(8,128)(2,1)S(1)}, u32[]{:S(2)}, u32[]{:S(2)}) collective-permute-start(bf16[224,128]{1,0:T(8,128)(2,1)S(1)} %get-tuple-element.75), channel_id=1, source_target_pairs={{0,32},{32,160},{64,64},{96,192},{128,96},{160,224},{192,0},{224,1... | collective-permute-start | bytes 172040 | tf_op jit(solution)/shard_map/ppermute | solution.py:509
  136.1 7.4 %collective-permute-start.14 = (bf16[224,128]{1,0:T(8,128)(2,1)S(1)}, bf16[224,128]{1,0:T(8,128)(2,1)S(1)}, u32[]{:S(2)}, u32[]{:S(2)}) collective-permute-start(bf16[224,128]{1,0:T(8,128)(2,1)S(1)} %get-tuple-element.76), channel_id=1, source_target_pairs={{0,64},{32,192},{64,96},{96,224},{128,0},{160,128},{192,32},{224,1... | collective-permute-start | bytes 172040 | tf_op jit(solution)/shard_map/ppermute | solution.py:509
  136.2 7.4 %collective-permute-start.15 = (bf16[224,128]{1,0:T(8,128)(2,1)S(1)}, bf16[224,128]{1,0:T(8,128)(2,1)S(1)}, u32[]{:S(2)}, u32[]{:S(2)}) collective-permute-start(bf16[224,128]{1,0:T(8,128)(2,1)S(1)} %get-tuple-element.77), channel_id=1, source_target_pairs={{0,96},{32,224},{64,0},{96,128},{128,32},{160,160},{192,64},{224,1... | collective-permute-start | bytes 172040 | tf_op jit(solution)/shard_map/ppermute | solution.py:509
  142.6 6.3 %collective-permute-start.17 = (bf16[992,128]{1,0:T(8,128)(2,1)S(1)}, bf16[992,128]{1,0:T(8,128)(2,1)S(1)}, u32[]{:S(2)}, u32[]{:S(2)}) collective-permute-start(bf16[992,128]{1,0:T(8,128)(2,1)S(1)} %fusion.1), channel_id=1, source_target_pairs={{0,2},{1,3},{2,0},{3,1},{4,6},{5,7},{6,4},{7,5},{8,10},{9,11},{10,... | collective-permute-start | bytes 761864 | tf_op jit(solution)/shard_map/ppermute | solution.py:36

commit v8 on v7

--- a/solution.py
+++ b/solution.py
@@ -49,19 +49,16 @@
     return take(own), take(1 - own)
 
 
-def summed_by_pairs(x, axis, bits, first):
-    names = bits_of(axis)
-    x = x.reshape((2,) * len(names) + x.shape[1:])
-    left = list(names)
-    steps = []
-    for bit in bits:
-        if bit == bits[-1]:
+def summed_by_pairs(x, axis, bits, order, first=None):
+    x = x.reshape((2,) * len(bits) + x.shape[1:])
+    left = list(bits)
+    for bit in order:
+        if bit == order[-1] and first is not None:
             x = behind(x, first)
         own, other = mine_and_other(x, axis, bit, left.index(bit))
         left.remove(bit)
         x = own.astype(jnp.float32) + swap(other.astype(jnp.bfloat16), axis, bit).astype(jnp.float32)
-        steps.append(x)
-    return x, steps
+    return x
 
 
 def dot_nn(a, b):
@@ -102,10 +99,19 @@
     )(*args)
 
 
-def class_kernel(
-    side_ref, gathered_ref, own_ref, label_ref, later_ref, grad_ref, even_ref, odd_ref, aux_ref
-):
+def pack_kernel(saved_ref, cotangent_ref, weight_ref, later_ref, out_ref):
     del later_ref
+    rows, inner = saved_ref.shape
+    out_ref[:rows] = saved_ref[...]
+    out_ref[rows : 2 * rows] = cotangent_ref[...]
+    spare = CLASS_ROWS - weight_ref.shape[0]
+    out_ref[2 * rows :] = jnp.concatenate(
+        [weight_ref[...].astype(jnp.float32), jnp.zeros((spare, inner), jnp.float32)], axis=0
+    ).astype(jnp.bfloat16)
+
+
+def class_kernel(gathered_ref, own_ref, label_ref, grad_ref, even_ref, odd_ref, aux_ref):
+    side = lax.rem(lax.axis_index("gx"), 2)
     groups, rows, inner = gathered_ref.shape[0], own_ref.shape[0], own_ref.shape[1]
     logits = jnp.zeros((CLASS_ROWS, rows), jnp.float32)
     for c in range(groups):
@@ -116,7 +122,15 @@
     logits = jnp.where(real, logits, -jnp.inf)
     powers = jnp.exp(logits - jnp.max(logits, axis=0, keepdims=True))
     probabilities = powers / jnp.sum(powers, axis=0, keepdims=True)
-    onehot = jnp.where(place == label_ref[...], 1.0, 0.0)
+    labels = jnp.concatenate(
+        [
+            label_ref[d, h : h + 1]
+            for d in range(label_ref.shape[0])
+            for h in range(label_ref.shape[1])
+        ],
+        axis=1,
+    )
+    onehot = jnp.where(place == labels, 1.0, 0.0)
     logit_grad = jnp.where(real, probabilities - onehot, 0.0).astype(jnp.bfloat16)
     for c in range(groups):
         weight = gathered_ref[c, 2 * rows : 2 * rows + CLASS_ROWS]
@@ -124,14 +138,13 @@
         active = gathered_ref[c, :rows].astype(jnp.float32) > 0
         grad_ref[:, c * inner : (c + 1) * inner] = jnp.where(active, total, 0.0).astype(jnp.bfloat16)
     size = even_ref.shape[0]
-    first = pl.multiple_of((rows - size) * side_ref[0], size)
+    first = pl.multiple_of((rows - size) * side, size)
     even_ref[...] = grad_ref[pl.ds(rows - size - first, size)]
     odd_ref[...] = grad_ref[pl.ds(first, size)]
     aux_ref[...] = dot_nn(logit_grad, jnp.maximum(own_ref[...], 0)).astype(jnp.bfloat16)
 
 
 def conv_kernel(
-    side_ref,
     grad_ref,
     even_x_ref,
     odd_x_ref,
@@ -151,7 +164,7 @@
     depth, height = far_d - 2, far_h - 2
     inner = out_ref.shape[1]
     rows = depth * height * width
-    side_x, side_y = side_ref[0], side_ref[1]
+    side_x, side_y = (lax.rem(lax.axis_index(a), 2) for a in ("gx", "gy"))
     far_ref[1 : 1 + depth, 1 : 1 + height] = grad_ref[...].reshape(depth, height, width, full)
     far_ref[(far_d - 1) * (1 - side_x), 1 : 1 + height] = even_x_ref[...].reshape(height, width, full)
     far_ref[(far_d - 1) * side_x, 1 : 1 + height] = odd_x_ref[...].reshape(height, width, full)
@@ -203,14 +216,14 @@
         ).astype(jnp.bfloat16)
 
 
-def kernel_grad_kernel(chunk, place_ref, far_ref, input_ref, got_ref, *refs):
+def kernel_grad_kernel(chunk, far_ref, input_ref, got_ref, *refs):
     out_refs, (all_ref, flat_ref, pair_ref, turn_ref, wide_ref) = refs[:-5], refs[-5:]
     far_d, far_h, width, full = far_ref.shape
     depth, height = far_d - 2, far_h - 2
     rows, inner = input_ref.shape
     by_height, by_depth, window, _ = all_ref.shape
     lanes = height * width
-    side, at_y = place_ref[0], place_ref[1]
+    side, at_y = lax.rem(lax.axis_index("gx"), 2), lax.axis_index("gy")
     sent = far_d // 2
     pair_ref[pl.ds(depth * side, far_d)] = far_ref[...]
     pair_ref[pl.ds(far_d * (1 - side), depth)] = got_ref[: sent * far_h * width].reshape(
@@ -230,19 +243,26 @@
     for d in range(far_d + depth):
         for b in range(3):
             turn_ref[d, b] = pair_ref[d, b : b + height].reshape(lanes, full).T
-    half = full // 2
-    for step in range(TAPS // 2 + 1):
-        tap = TAPS // 2 * side + step
-        a, b, c = tap // 9, lax.rem(tap // 3, 3), lax.rem(tap, 3)
-        turned = jnp.concatenate([turn_ref[2 - a + d, 2 - b] for d in range(2 * depth)], axis=1)
-        terms = dot_nn(turned, wide_ref[c].reshape(2 * rows, inner))
-        first = pl.multiple_of(step * full + half - half * side, half)
-        flat_ref[pl.ds(first, full)] = terms.astype(jnp.bfloat16)
-    for owner in range(by_depth * by_height):
-        start = half + owner * chunk // 16 * 16
-        all_ref[owner % by_height, owner // by_height] = flat_ref[start : start + window]
+    span = chunk * by_height
+    grain = 16
+    for m in range(by_depth):
+        begin = span * (2 * m + side)
+        for step in range((span - 1) // full + 2):
+            tap = begin // full + step
+
+            @pl.when(tap * full < begin + span)
+            def _():
+                a, b, c = tap // 9, lax.rem(tap // 3, 3), lax.rem(tap, 3)
+                turned = jnp.concatenate([turn_ref[2 - a + d, 2 - b] for d in range(2 * depth)], axis=1)
+                terms = dot_nn(turned, wide_ref[c].reshape(2 * rows, inner))
+                first = pl.multiple_of(tap * full - begin + full, grain)
+                flat_ref[m, pl.ds(first, full)] = terms.astype(jnp.bfloat16)
+
+        for j in range(by_height):
+            start = full + j * chunk // grain * grain
+            all_ref[j, m] = flat_ref[m, start : start + window]
     for k, out_ref in enumerate(out_refs):
-        out_ref[...] = all_ref[at_y ^ k]
+        out_ref[...] = all_ref[pl.ds(2 * (at_y // 2 ^ k), 2)]
 
 
 def bottom_kernel(
@@ -336,17 +356,21 @@
     struct = jax.ShapeDtypeStruct
 
     own_pre = pre_level.reshape(rows, inner)
-    payload = jnp.concatenate(
-        [
-            own_pre,
-            level_cotangent.reshape(rows, inner),
-            jnp.pad(aux_weight.T, ((0, CLASS_ROWS - CLASSES), (0, 0))),
-        ]
+    (payload,) = local_call(
+        pack_kernel,
+        [struct((2 * rows + CLASS_ROWS, inner), bf16)],
+        [],
+        0,
+        2 * pre_level.size,
+        own_pre,
+        level_cotangent.reshape(rows, inner),
+        aux_weight.T,
+        level_weight,
+        stay=3,
     )
     gathered = lax.all_gather(payload, "col")
     lanes = height * width
     side_x, side_y = at_x % 2, at_y % 2
-    sides = jnp.stack([side_x, side_y]).astype(jnp.int32)
     level_pre_grad, even_x, odd_x, aux_part = local_call(
         class_kernel,
         (
@@ -358,12 +382,9 @@
         [],
         6 * rows * full * CLASS_ROWS,
         2 * gathered.size,
-        sides,
         gathered,
         own_pre,
-        labels.reshape(1, rows),
-        level_weight,
-        stay=4,
+        labels,
     )
 
     even_x = swap(even_x, "gx", 1)
@@ -405,7 +426,6 @@
         ],
         2 * rows * full * TAPS * inner,
         2 * level_weight.size,
-        sides,
         level_pre_grad,
         even_x,
         odd_x,
@@ -432,27 +452,26 @@
     span = chunk + 8 if chunk % 16 else chunk
     level_parts = local_call(
         functools.partial(kernel_grad_kernel, chunk),
-        [struct((nx // 2, span, inner), bf16)] * ny,
+        [struct((2, nx // 2, span, inner), bf16)] * (ny // 2),
         [
             pltpu.VMEM((ny, nx // 2, span, inner), bf16),
-            pltpu.VMEM(((TAPS + 2) * full // 2, inner), bf16),
+            pltpu.VMEM((nx // 2, (chunk * ny - 1) // full * full + 4 * full, inner), bf16),
             pltpu.VMEM((far_d + depth, far_h, width, full), bf16),
             pltpu.VMEM((far_d + depth, 3, full, lanes), bf16),
             pltpu.VMEM((3, 2, rows, inner), bf16),
         ],
         2 * rows * full * TAPS * inner,
         2 * nx * ny * span * inner,
-        jnp.stack([side_x, at_y]).astype(jnp.int32),
         far,
         flat_input,
         got,
     )
-    terms = [level_parts[0]] + [swap(level_parts[k], "gy", k) for k in range(1, ny)]
+    terms = [level_parts[0]] + [swap(level_parts[k], "gy", 2 * k) for k in range(1, ny // 2)]
     relayed = behind(relayed, level_parts[0])
 
     by_depth = spread(jnp.concatenate([relayed, aux_part]), "gx")
     aux_sum = by_depth[:, nc * cells :].astype(f32).sum(axis=0).astype(bf16)
-    by_depth = behind(by_depth, *terms[1 : ny // 2])
+    by_depth = behind(by_depth, terms[1], terms[-1])
     line = by_depth[:, : nc * cells].reshape(nx, nc, half_d * half_h, window, inner)[:, :, :, :wide]
     split = nx * nc * half_d * half_h * wide
     by_height = spread(jnp.concatenate([line.reshape(split, inner), aux_sum]), "gy")
@@ -464,8 +483,9 @@
         .reshape(bottom_d * wide * bottom_h, full)
     )
 
-    level_part = sum(t.astype(f32) for t in terms).astype(bf16)
-    down_wide = behind(down_wide, terms[ny // 2])
+    down_wide = behind(down_wide, terms[ny // 4])
+    level_part = sum(t.astype(f32) for t in terms)
+    level_part = summed_by_pairs(level_part, "gy", [1], [1])
 
     bottom_rows = bottom_d * block * bottom_h
     channel_width = bottom_weight.shape[0]
@@ -498,18 +518,7 @@
         shifts,
     )
     part = exchange(part.reshape(ny, bottom_rows // ny, channel_width), "gy")
-    pairs = nx // 2
-    level_sum = jnp.zeros((span, inner), f32)
-    for step in range(pairs):
-        if step == pairs // 2:
-            level_part = behind(level_part, part)
-        chosen = lax.dynamic_index_in_dim(
-            level_part, lax.rem(at_x // 2 + step, pairs), 0, keepdims=False
-        )
-        level_sum += lax.ppermute(
-            chosen, "gx", [(i, i % 2 * pairs + (i // 2 + step) % pairs) for i in range(nx)]
-        ).astype(f32)
-    level_part = level_sum
+    level_part = summed_by_pairs(level_part, "gx", bits_of("gx")[:-1], bits_of("gx")[-2::-1], part)
     if span != chunk:
         odd = lax.rem(at_y + at_x * ny, 2)
         level_part = jnp.where(odd == 1, level_part[span - chunk :], level_part[:chunk])
@@ -522,7 +531,7 @@
         .reshape(share, block, bottom_h, channel_width)
         .transpose(0, 2, 1, 3)
     )
-    both, _ = summed_by_pairs(both, "col", bits_of("col")[::-1], part)
+    both = summed_by_pairs(both, "col", bits_of("col"), bits_of("col")[::-1], part)
     bottom_weight_grad = both[: TAPS * thin].reshape(TAPS, thin, filters).transpose(1, 0, 2)
     up_weight_grad = both[TAPS * thin :]
     return (

time: 153 us -> 137 us (0.90)
  starting transfers between devices: 77.6 us -> 53.2 us
  blocking collectives: 10.1 us -> 19 us
  waiting for transfers between devices: 27 us -> 32 us
  local copies, waits for them, and re-layouts: 14.8 us -> 10.3 us
  Pallas kernels: 13.1 us -> 16.1 us
  other arithmetic: 6.63 us -> 3.99 us
    ppermute x4 -> x0, starting transfers between devices: 14.1 us -> none  [per_device(): lax.ppermute(chosen, 'gx', [(i, i % 2 * pairs + (i // 2 + step) % pairs)...]
    all_to_all x4 -> x3, waiting for transfers between devices: 5.4 us -> 14.8 us  [exchange(): return lax.all_to_all(x, axis, split_axis=0, concat_axis=0, tiled=False)]
    all_to_all x0 -> x1, blocking collectives: none -> 9.16 us  [exchange(): return lax.all_to_all(x, axis, split_axis=0, concat_axis=0, tiled=False)]
    all_to_all x4 -> x3, starting transfers between devices: 21.4 us -> 14.8 us  [exchange(): return lax.all_to_all(x, axis, split_axis=0, concat_axis=0, tiled=False)]
    ppermute x12 -> x11, waiting for transfers between devices: 21.6 us -> 17.3 us  [swap(): lax.ppermute(x, axis, [(i, i ^ bit) for i in range(lax.axis_size(axis))])]
    ppermute x12 -> x11, starting transfers between devices: 40.1 us -> 36.4 us  [swap(): lax.ppermute(x, axis, [(i, i ^ bit) for i in range(lax.axis_size(axis))])]
    pallas_call x5 -> x6, Pallas kernels: 13.1 us -> 16.1 us  [local_call(): pl.pallas_call(body, out_shape=list(out_shapes), in_specs=[pl.BlockSpec(m...]
    unnamed x42 -> x32, local copies, waits for them, and re-layouts: 6.9 us -> 4.75 us
  transfers between devices with their start and end apart: 22 -> 16, of which waited for: 9 -> 6; matrix products, arithmetic and copies ran while one was open for 6% -> 7% of each run, Pallas kernels for 2% -> 2%
where the time goes in v8:
time: 137 us; the launch traced here: 136 us
  starting transfers between devices  53.2 us (39%)
  waiting for transfers between devices  32 us (23%)
  blocking collectives  19 us (14%)
  Pallas kernels  16.1 us (12%)
  local copies, waits for them, and re-layouts  10.3 us (8%)
  other arithmetic  3.99 us (3%)
    ppermute x11, starting transfers between devices, swap(): lax.ppermute(x, axis, [(i, i ^ bit) for i in range(lax.axis_size(axis))])  36.4 us
    ppermute x11, waiting for transfers between devices, swap(): lax.ppermute(x, axis, [(i, i ^ bit) for i in range(lax.axis_size(axis))])  17.3 us
    pallas_call x6, Pallas kernels, local_call(): pl.pallas_call(body, out_shape=list(out_shapes), in_specs=[pl.BlockSpec(m...  16.1 us
    all_to_all x3, starting transfers between devices, exchange(): return lax.all_to_all(x, axis, split_axis=0, concat_axis=0, tiled=False)  14.8 us
    all_to_all x3, waiting for transfers between devices, exchange(): return lax.all_to_all(x, axis, split_axis=0, concat_axis=0, tiled=False)  14.8 us
    all_gather x1, blocking collectives, per_device(): gathered = lax.all_gather(payload, 'col')  9.83 us
    all_to_all x1, blocking collectives, exchange(): return lax.all_to_all(x, axis, split_axis=0, concat_axis=0, tiled=False)  9.16 us
    unnamed x32, local copies, waits for them, and re-layouts  4.75 us
  transfers between devices with their start and end apart: 16, of which 6 were waited for; matrix products, arithmetic and copies ran while one was open for 7% of the time, Pallas kernels for 2%

profile of v8, /device:TPU:1, one launch (start us, length us, event | category | flops | bytes accessed | tf_op | source)
XLA Modules:
  0.0 135.6 jit_solution(9554350076900728210)
XLA Ops:
  0.7 1.7 %shard_map.145 = bf16[528,128]{1,0:T(8,128)(2,1)} custom-call(bf16[256,128]{1,0:T(8,128)(2,1)} %bitcast.100, bf16[256,128]{1,0:T(8,128)(2,1)} %bitcast.118, bf16[14,128]{1,0:T(8,128)(2,1)} %bitcast.120, bf16[128,13824]{1,0:T(8,128)(2,1)} %weight_ref.1), custom_call_target="tpu_custom_call" | custom-call | bytes 65536 | tf_op jit(solution)/shard_map/pallas_call | solution.py:86
  2.4 9.8 %all-gather = bf16[2112,128]{1,0:T(8,128)(2,1)S(1)} all-gather(bf16[528,128]{1,0:T(8,128)(2,1)} %shard_map.145), channel_id=2, replica_groups=mesh['gx'=8,'gy'=8,'col'=4] {'col'}, dimensions={0}, use_global_device_ids=true | all-gather | bytes 675840 | tf_op jit(solution)/shard_map/all_gather | solution.py:371
  12.2 1.3 shard_map.146
  13.5 0.7 copy-done.4
  14.2 0.6 collective-permute-start
  14.8 1.3 collective-permute-start.1
  16.1 1.0 copy.43
  17.1 0.9 slice_bitcast_fusion.3
  18.0 1.5 %collective-permute-done.even_x_ref = bf16[128,512]{1,0:T(8,128)(2,1)} collective-permute-done((bf16[128,512]{1,0:T(8,128)(2,1)}, bf16[128,512]{1,0:T(8,128)(2,1)}, u32[]{:S(2)}, u32[]{:S(2)}) %collective-permute-start) | collective-permute-done | bytes 131104 | tf_op jit(solution)/shard_map/ppermute | solution.py:36
  19.5 0.8 select_bitcast_fusion.5
  20.4 0.7 collective-permute-start.3
  21.0 4.6 %collective-permute-start.2 = (bf16[4,32,512]{2,1,0:T(8,128)(2,1)S(1)}, bf16[4,32,512]{2,1,0:T(8,128)(2,1)S(1)}, u32[]{:S(2)}, u32[]{:S(2)}) collective-permute-start(bf16[4,32,512]{2,1,0:T(8,128)(2,1)S(1)} %get-tuple-element.57), channel_id=1, source_target_pairs={{0,4},{4,0},{8,12},{12,8},{16,20},{20,16},{24,28},{28,24},{1,5},{5... | collective-permute-start | bytes 393224 | tf_op jit(solution)/shard_map/ppermute | solution.py:36
  25.7 5.4 %collective-permute-done.2.even_y_ref = bf16[4,32,512]{2,1,0:T(8,128)(2,1)S(1)} collective-permute-done((bf16[4,32,512]{2,1,0:T(8,128)(2,1)S(1)}, bf16[4,32,512]{2,1,0:T(8,128)(2,1)S(1)}, u32[]{:S(2)}, u32[]{:S(2)}) %collective-permute-start.2) | collective-permute-done | bytes 131104 | tf_op jit(solution)/shard_map/ppermute | solution.py:36
  31.2 0.9 copy-done.5
  32.1 0.8 copy-done.8
  33.0 3.7 %shard_map.147 = (bf16[4,6,32,512]{3,2,1,0:T(8,128)(2,1)S(1)}, bf16[256,128]{1,0:T(8,128)(2,1)}, bf16[4,144,128]{2,1,0:T(8,128)(2,1)S(1)}, bf16[448,512]{1,0:T(8,128)(2,1)S(1)}) custom-call(bf16[256,512]{1,0:T(8,128)(2,1)S(1)} %copy-done.5, bf16[128,512]{1,0:T(8,128)(2,1)} %collective-permute-done.even_x_ref, ...), custom_call_target="tpu_custom_call" | custom-call | flops 905969664 | bytes 3538944 | tf_op jit(solution)/shard_map/pallas_call | solution.py:86
  36.6 4.4 %collective-permute-start.4 = (bf16[448,512]{1,0:T(8,128)(2,1)S(1)}, bf16[448,512]{1,0:T(8,128)(2,1)S(1)}, u32[]{:S(2)}, u32[]{:S(2)}) collective-permute-start(bf16[448,512]{1,0:T(8,128)(2,1)S(1)} %get-tuple-element.31), channel_id=1, source_target_pairs={{0,32},{32,0},{64,96},{96,64},{128,160},{160,128},{192,224},{224,1... | collective-permute-start | bytes 1376264 | tf_op jit(solution)/shard_map/ppermute | solution.py:36
  41.1 9.2 %all_to_all.20 = bf16[4,144,128]{2,1,0:T(8,128)(2,1)S(1)} all-to-all(bf16[4,144,128]{2,1,0:T(8,128)(2,1)S(1)} %get-tuple-element.29), channel_id=1, replica_groups=mesh['gx'=8,'gy'=8,'col'=4] {'col'}, dimensions={0} | all-to-all | bytes 294912 | tf_op jit(solution)/shard_map/all_to_all | solution.py:19
  50.2 6.2 %shard_map.148 = (bf16[2,4,224,128]{3,2,1,0:T(8,128)(2,1)S(1)}, bf16[2,4,224,128]{3,2,1,0:T(8,128)(2,1)S(1)}, bf16[2,4,224,128]{3,2,1,0:T(8,128)(2,1)S(1)}, bf16[2,4,224,128]{3,2,1,0:T(8,128)(2,1)S(1)}) custom-call(bf16[4,6,32,512]{3,2,1,0:T(8,128)(2,1)S(1)} %get-tuple-element.30.far_ref, bf16[256,128]{1,0:T(8,128)(2,1)S(1)} %bitcast.103, ...), custom_call_target="tpu_custom_call" | custom-call | flops 905969664 | bytes 3670016 | tf_op jit(solution)/shard_map/pallas_call | solution.py:86
  56.5 1.6 %collective-permute-start.5 = (bf16[2,4,224,128]{3,2,1,0:T(8,128)(2,1)S(1)}, bf16[2,4,224,128]{3,2,1,0:T(8,128)(2,1)S(1)}, u32[]{:S(2)}, u32[]{:S(2)}) collective-permute-start(bf16[2,4,224,128]{3,2,1,0:T(8,128)(2,1)S(1)} %get-tuple-element.35), channel_id=1, source_target_pairs={{0,8},{4,12},{8,0},{12,4},{16,24},{20,28},{24,16},{28,20},{1,9},{5... | collective-permute-start | bytes 1376264 | tf_op jit(solution)/shard_map/ppermute | solution.py:36
  58.1 2.2 %collective-permute-start.6 = (bf16[2,4,224,128]{3,2,1,0:T(8,128)(2,1)S(1)}, bf16[2,4,224,128]{3,2,1,0:T(8,128)(2,1)S(1)}, u32[]{:S(2)}, u32[]{:S(2)}) collective-permute-start(bf16[2,4,224,128]{3,2,1,0:T(8,128)(2,1)S(1)} %get-tuple-element.36), channel_id=1, source_target_pairs={{0,24},{4,28},{8,16},{12,20},{16,8},{20,12},{24,0},{28,4},{1,25},{... | collective-permute-start | bytes 1376264 | tf_op jit(solution)/shard_map/ppermute | solution.py:36
  60.3 0.7 broadcast_in_dim.4
  61.0 7.0 %all-to-all-start.1 = ((bf16[8,80,128]{2,1,0:T(8,128)(2,1)}), bf16[8,80,128]{2,1,0:T(8,128)(2,1)S(1)}, u32[]{:S(2)}, u32[]{:S(2)}) async-start(bf16[8,80,128]{2,1,0:T(8,128)(2,1)} %broadcast_in_dim.4), calls=%async_computation.1 | async-start | bytes 327680 | tf_op jit(solution)/shard_map/all_to_all | solution.py:19
  68.0 8.4 %all-to-all-done.1 = bf16[8,80,128]{2,1,0:T(8,128)(2,1)S(1)} async-done(((bf16[8,80,128]{2,1,0:T(8,128)(2,1)}), bf16[8,80,128]{2,1,0:T(8,128)(2,1)S(1)}, u32[]{:S(2)}, u32[]{:S(2)}) %all-to-all-start.1) | async-done | bytes 163872 | tf_op jit(solution)/shard_map/all_to_all | solution.py:19
  76.5 1.1 broadcast_in_dim.5
  77.6 3.7 %all-to-all-start.2 = ((bf16[8,400,128]{2,1,0:T(8,128)(2,1)}), bf16[8,400,128]{2,1,0:T(8,128)(2,1)S(1)}, u32[]{:S(2)}, u32[]{:S(2)}) async-start(bf16[8,400,128]{2,1,0:T(8,128)(2,1)} %broadcast_in_dim.5), calls=%async_computation.2 | async-start | bytes 1638400 | tf_op jit(solution)/shard_map/all_to_all | solution.py:19
  81.4 1.5 %convert_add_fusion.1 = f32[2,4,224,128]{3,2,1,0:T(8,128)S(1)} fusion(bf16[2,4,224,128]{3,2,1,0:T(8,128)(2,1)} %copy-done.12, bf16[2,4,224,128]{3,2,1,0:T(8,128)(2,1)} %collective-permute-done.7, bf16[2,4,224,128]{3,2,1,0:T(8,128)(2,1)} %copy-done.11, bf16[2,4,224,128]{3,2,1,0:T(8,128)(2,1)S(1)} %get-tuple-element.32), kind=kLoop, calls=%fused_computation.1 | loop fusion | flops 1605632 | bytes 2752512 | tf_op jit(solution)/shard_map/add | solution.py:487
  82.9 3.0 %collective-permute-start.8 = (bf16[4,224,128]{2,1,0:T(8,128)(2,1)S(1)}, bf16[4,224,128]{2,1,0:T(8,128)(2,1)S(1)}, u32[]{:S(2)}, u32[]{:S(2)}) collective-permute-start(bf16[4,224,128]{2,1,0:T(8,128)(2,1)S(1)} %fusion.1), channel_id=1, source_target_pairs={{0,4},{4,0},{8,12},{12,8},{16,20},{20,16},{24,28},{28,24},{1,5},{5... | collective-permute-start | bytes 688136 | tf_op jit(solution)/shard_map/ppermute | solution.py:36
  86.0 6.2 %collective-permute-done.8 = bf16[4,224,128]{2,1,0:T(8,128)(2,1)S(1)} collective-permute-done((bf16[4,224,128]{2,1,0:T(8,128)(2,1)S(1)}, bf16[4,224,128]{2,1,0:T(8,128)(2,1)S(1)}, u32[]{:S(2)}, u32[]{:S(2)}) %collective-permute-start.8) | collective-permute-done | bytes 229408 | tf_op jit(solution)/shard_map/ppermute | solution.py:36
  92.4 0.1 collective-permute-start.9
  92.5 0.5 copy.36
  93.1 0.4 copy.30
  93.5 0.1 copy.42
  93.6 2.3 %shard_map.149 = (bf16[512,128]{1,0:T(8,128)(2,1)}, bf16[3,10,6,16,128]{4,3,2,1,0:T(8,128)(2,1)S(1)}) custom-call(bf16[768,512]{1,0:T(8,128)(2,1)S(1)} %bitcast.90, bf16[128,512]{1,0:T(8,128)(2,1)S(1)} %copy-done.7, bf16[8,1,16,128]{3,2,1,0:T(8,128)(2,1)S(1)} %get-tuple-element.67.before_ref, bf16[8,4,16,128]{3,2,1,0:T(8,128)(2,1)S(1)} %bitcast.96, ...), custom_call_target="tpu_custom_call" | custom-call | flops 452984832 | bytes 884736 | tf_op jit(solution)/shard_map/pallas_call | solution.py:86
  96.0 0.9 shard_map.150
  96.9 0.8 dynamic-slice_bitcast_fusion
  97.7 12.9 %collective-permute-start.11 = (bf16[2,992,128]{2,1,0:T(8,128)(2,1)}, bf16[2,992,128]{2,1,0:T(8,128)(2,1)S(1)}, u32[]{:S(2)}, u32[]{:S(2)}) collective-permute-start(bf16[2,992,128]{2,1,0:T(8,128)(2,1)} %dynamic-slice_bitcast_fusion), channel_id=1, source_target_pairs={{0,1},{1,0},{2,3},{3,2},{4,5},{5,4},{6,7},{7,6},{8,9},{9,8},{10,11... | collective-permute-start | bytes 1523720 | tf_op jit(solution)/shard_map/ppermute | solution.py:36
  110.6 4.0 %all-to-all-start.3 = ((bf16[8,64,128]{2,1,0:T(8,128)(2,1)}), bf16[8,64,128]{2,1,0:T(8,128)(2,1)S(1)}, u32[]{:S(2)}, u32[]{:S(2)}) async-start(bf16[8,64,128]{2,1,0:T(8,128)(2,1)} %bitcast.28), calls=%async_computation.3 | async-start | bytes 262144 | tf_op jit(solution)/shard_map/all_to_all | solution.py:19
  114.6 0.6 convert_reduce_fusion
  115.2 6.4 %all-to-all-done.3 = bf16[8,64,128]{2,1,0:T(8,128)(2,1)S(1)} async-done(((bf16[8,64,128]{2,1,0:T(8,128)(2,1)}), bf16[8,64,128]{2,1,0:T(8,128)(2,1)S(1)}, u32[]{:S(2)}, u32[]{:S(2)}) %all-to-all-start.3) | async-done | bytes 131104 | tf_op jit(solution)/shard_map/all_to_all | solution.py:19
  121.7 0.6 copy.35
  122.3 4.1 %collective-permute-start.10 = (bf16[224,128]{1,0:T(8,128)(2,1)S(1)}, bf16[224,128]{1,0:T(8,128)(2,1)S(1)}, u32[]{:S(2)}, u32[]{:S(2)}) collective-permute-start(bf16[224,128]{1,0:T(8,128)(2,1)S(1)} %fusion.4), channel_id=1, source_target_pairs={{0,128},{32,160},{64,192},{96,224},{128,0},{160,32},{192,64},{224,... | collective-permute-start | bytes 172040 | tf_op jit(solution)/shard_map/ppermute | solution.py:36
  126.4 0.1 convert_add_fusion
  126.6 2.8 %collective-permute-start.12 = (bf16[992,128]{1,0:T(8,128)(2,1)S(1)}, bf16[992,128]{1,0:T(8,128)(2,1)S(1)}, u32[]{:S(2)}, u32[]{:S(2)}) collective-permute-start(bf16[992,128]{1,0:T(8,128)(2,1)S(1)} %fusion), channel_id=1, source_target_pairs={{0,2},{1,3},{2,0},{3,1},{4,6},{5,7},{6,4},{7,5},{8,10},{9,11},{10,... | collective-permute-start | bytes 761864 | tf_op jit(solution)/shard_map/ppermute | solution.py:36
  129.4 0.7 fusion.3
  130.1 4.1 %collective-permute-done.12 = bf16[992,128]{1,0:T(8,128)(2,1)S(1)} collective-permute-done((bf16[992,128]{1,0:T(8,128)(2,1)S(1)}, bf16[992,128]{1,0:T(8,128)(2,1)S(1)}, u32[]{:S(2)}, u32[]{:S(2)}) %collective-permute-start.12) | collective-permute-done | bytes 253984 | tf_op jit(solution)/shard_map/ppermute | solution.py:36
  134.2 0.6 slice.120
  134.8 0.8 slice.119
  (58 shorter events, 0.6 us)
Async XLA Ops:
  0.6 30.5 %copy-start = (bf16[128,13824]{1,0:T(8,128)(2,1)S(1)}, bf16[128,13824]{1,0:T(8,128)(2,1)}, u32[]{:S(2)}) copy-start(bf16[128,13824]{1,0:T(8,128)(2,1)} %weight_ref.1) | copy-start | bytes 10616836
  0.6 11.5 %copy-start.6 = (bf16[2,4,32,128]{3,2,1,0:T(8,128)(2,1)S(1)}, bf16[2,4,32,128]{3,2,1,0:T(8,128)(2,1)}, u32[]{:S(2)}) copy-start(bf16[2,4,32,128]{3,2,1,0:T(8,128)(2,1)} %param.15) | copy-start | bytes 196612
  0.7 11.5 %copy-start.10 = (s32[2,4,32]{2,1,0:T(4,128)S(1)}, s32[2,4,32]{2,1,0:T(4,128)}, u32[]{:S(2)}) copy-start(s32[2,4,32]{2,1,0:T(4,128)} %label_ref.1) | copy-start | bytes 3076
  13.5 0.7 copy-start.4
  14.2 5.3 %collective-permute-start = (bf16[128,512]{1,0:T(8,128)(2,1)}, bf16[128,512]{1,0:T(8,128)(2,1)}, u32[]{:S(2)}, u32[]{:S(2)}) collective-permute-start(bf16[128,512]{1,0:T(8,128)(2,1)} %get-tuple-element.26), channel_id=1, source_target_pairs={{0,32},{32,0},{64,96},{96,64},{128,160},{160,128},{192,224},{224,1... | collective-permute-start | bytes 393224 | tf_op jit(solution)/shard_map/ppermute | solution.py:36
  14.8 4.7 %collective-permute-start.1 = (bf16[128,512]{1,0:T(8,128)(2,1)}, bf16[128,512]{1,0:T(8,128)(2,1)}, u32[]{:S(2)}, u32[]{:S(2)}) collective-permute-start(bf16[128,512]{1,0:T(8,128)(2,1)} %get-tuple-element.27), channel_id=1, source_target_pairs={{32,64},{64,32},{96,128},{128,96},{160,192},{192,160},{33,65},{65,... | collective-permute-start | bytes 393224 | tf_op jit(solution)/shard_map/ppermute | solution.py:41
  16.1 34.1 %copy-start.9 = (bf16[2,4,32,128]{3,2,1,0:T(8,128)(2,1)S(1)}, bf16[2,4,32,128]{3,2,1,0:T(8,128)(2,1)}, u32[]{:S(2)}) copy-start(bf16[2,4,32,128]{3,2,1,0:T(8,128)(2,1)} %param.14) | copy-start | bytes 196612
  17.1 8.6 %copy-start.1 = (bf16[8,16,4,128]{3,1,2,0:T(8,128)(2,1)}, bf16[8,16,4,128]{3,1,2,0:T(8,128)(2,1)S(1)}, u32[]{:S(2)}) copy-start(bf16[8,16,4,128]{3,1,2,0:T(8,128)(2,1)S(1)} %copy.43) | copy-start | bytes 393220
  20.4 5.4 %collective-permute-start.3 = (bf16[4,32,512]{2,1,0:T(8,128)(2,1)S(1)}, bf16[4,32,512]{2,1,0:T(8,128)(2,1)S(1)}, u32[]{:S(2)}, u32[]{:S(2)}) collective-permute-start(bf16[4,32,512]{2,1,0:T(8,128)(2,1)S(1)} %get-tuple-element.56), channel_id=1, source_target_pairs={{4,8},{8,4},{12,16},{16,12},{20,24},{24,20},{5,9},{9,5},{13,17},{1... | collective-permute-start | bytes 393224 | tf_op jit(solution)/shard_map/ppermute | solution.py:41
  21.0 10.1 %collective-permute-start.2 = (bf16[4,32,512]{2,1,0:T(8,128)(2,1)S(1)}, bf16[4,32,512]{2,1,0:T(8,128)(2,1)S(1)}, u32[]{:S(2)}, u32[]{:S(2)}) collective-permute-start(bf16[4,32,512]{2,1,0:T(8,128)(2,1)S(1)} %get-tuple-element.57), channel_id=1, source_target_pairs={{0,4},{4,0},{8,12},{12,8},{16,20},{20,16},{24,28},{28,24},{1,5},{5... | collective-permute-start | bytes 393224 | tf_op jit(solution)/shard_map/ppermute | solution.py:36
  31.2 1.0 copy-start.5
  32.1 0.8 copy-start.8
  36.6 13.6 %collective-permute-start.4 = (bf16[448,512]{1,0:T(8,128)(2,1)S(1)}, bf16[448,512]{1,0:T(8,128)(2,1)S(1)}, u32[]{:S(2)}, u32[]{:S(2)}) collective-permute-start(bf16[448,512]{1,0:T(8,128)(2,1)S(1)} %get-tuple-element.31), channel_id=1, source_target_pairs={{0,32},{32,0},{64,96},{96,64},{128,160},{160,128},{192,224},{224,1... | collective-permute-start | bytes 1376264 | tf_op jit(solution)/shard_map/ppermute | solution.py:36
  56.5 20.0 %collective-permute-start.5 = (bf16[2,4,224,128]{3,2,1,0:T(8,128)(2,1)S(1)}, bf16[2,4,224,128]{3,2,1,0:T(8,128)(2,1)S(1)}, u32[]{:S(2)}, u32[]{:S(2)}) collective-permute-start(bf16[2,4,224,128]{3,2,1,0:T(8,128)(2,1)S(1)} %get-tuple-element.35), channel_id=1, source_target_pairs={{0,8},{4,12},{8,0},{12,4},{16,24},{20,28},{24,16},{28,20},{1,9},{5... | collective-permute-start | bytes 1376264 | tf_op jit(solution)/shard_map/ppermute | solution.py:36
  58.1 18.3 %collective-permute-start.6 = (bf16[2,4,224,128]{3,2,1,0:T(8,128)(2,1)S(1)}, bf16[2,4,224,128]{3,2,1,0:T(8,128)(2,1)S(1)}, u32[]{:S(2)}, u32[]{:S(2)}) collective-permute-start(bf16[2,4,224,128]{3,2,1,0:T(8,128)(2,1)S(1)} %get-tuple-element.36), channel_id=1, source_target_pairs={{0,24},{4,28},{8,16},{12,20},{16,8},{20,12},{24,0},{28,4},{1,25},{... | collective-permute-start | bytes 1376264 | tf_op jit(solution)/shard_map/ppermute | solution.py:36
  60.3 25.6 %copy-start.13 = (bf16[8,16,4,128]{3,2,1,0:T(4,128)(2,1)S(1)}, bf16[8,16,4,128]{3,2,1,0:T(4,128)(2,1)}, u32[]{:S(2)}) copy-start(bf16[8,16,4,128]{3,2,1,0:T(4,128)(2,1)} %param.11) | copy-start | bytes 393220
  61.0 15.4 %all-to-all-start.1 = ((bf16[8,80,128]{2,1,0:T(8,128)(2,1)}), bf16[8,80,128]{2,1,0:T(8,128)(2,1)S(1)}, u32[]{:S(2)}, u32[]{:S(2)}) async-start(bf16[8,80,128]{2,1,0:T(8,128)(2,1)} %broadcast_in_dim.4), calls=%async_computation.1 | async-start | bytes 327680 | tf_op jit(solution)/shard_map/all_to_all | solution.py:19
  68.0 13.4 %collective-permute-start.7 = (bf16[2,4,224,128]{3,2,1,0:T(8,128)(2,1)S(1)}, bf16[2,4,224,128]{3,2,1,0:T(8,128)(2,1)}, u32[]{:S(2)}, u32[]{:S(2)}) collective-permute-start(bf16[2,4,224,128]{3,2,1,0:T(8,128)(2,1)S(1)} %get-tuple-element.38), channel_id=1, source_target_pairs={{0,16},{4,20},{8,24},{12,28},{16,0},{20,4},{24,8},{28,12},{1,17},{... | collective-permute-start | bytes 1376264 | tf_op jit(solution)/shard_map/ppermute | solution.py:36
  76.4 1.2 copy-start.11
  76.4 4.9 %copy-start.12 = (bf16[2,4,224,128]{3,2,1,0:T(8,128)(2,1)}, bf16[2,4,224,128]{3,2,1,0:T(8,128)(2,1)S(1)}, u32[]{:S(2)}) copy-start(bf16[2,4,224,128]{3,2,1,0:T(8,128)(2,1)S(1)} %collective-permute-done.6) | copy-start | bytes 1376260
  77.6 14.8 %all-to-all-start.2 = ((bf16[8,400,128]{2,1,0:T(8,128)(2,1)}), bf16[8,400,128]{2,1,0:T(8,128)(2,1)S(1)}, u32[]{:S(2)}, u32[]{:S(2)}) async-start(bf16[8,400,128]{2,1,0:T(8,128)(2,1)} %broadcast_in_dim.5), calls=%async_computation.2 | async-start | bytes 1638400 | tf_op jit(solution)/shard_map/all_to_all | solution.py:19
  82.9 9.3 %collective-permute-start.8 = (bf16[4,224,128]{2,1,0:T(8,128)(2,1)S(1)}, bf16[4,224,128]{2,1,0:T(8,128)(2,1)S(1)}, u32[]{:S(2)}, u32[]{:S(2)}) collective-permute-start(bf16[4,224,128]{2,1,0:T(8,128)(2,1)S(1)} %fusion.1), channel_id=1, source_target_pairs={{0,4},{4,0},{8,12},{12,8},{16,20},{20,16},{24,28},{28,24},{1,5},{5... | collective-permute-start | bytes 688136 | tf_op jit(solution)/shard_map/ppermute | solution.py:36
  92.3 1.3 copy-start.2
  92.3 1.3 copy-start.3
  92.3 1.3 copy-start.7
  92.4 22.2 %collective-permute-start.9 = (bf16[2,224,128]{2,1,0:T(8,128)(2,1)S(1)}, bf16[2,224,128]{2,1,0:T(8,128)(2,1)S(1)}, u32[]{:S(2)}, u32[]{:S(2)}) collective-permute-start(bf16[2,224,128]{2,1,0:T(8,128)(2,1)S(1)} %fusion.2), channel_id=1, source_target_pairs={{0,64},{32,96},{64,0},{96,32},{128,192},{160,224},{192,128},{224,1... | collective-permute-start | bytes 344072 | tf_op jit(solution)/shard_map/ppermute | solution.py:36
  97.7 28.7 %collective-permute-start.11 = (bf16[2,992,128]{2,1,0:T(8,128)(2,1)}, bf16[2,992,128]{2,1,0:T(8,128)(2,1)S(1)}, u32[]{:S(2)}, u32[]{:S(2)}) collective-permute-start(bf16[2,992,128]{2,1,0:T(8,128)(2,1)} %dynamic-slice_bitcast_fusion), channel_id=1, source_target_pairs={{0,1},{1,0},{2,3},{3,2},{4,5},{5,4},{6,7},{7,6},{8,9},{9,8},{10,11... | collective-permute-start | bytes 1523720 | tf_op jit(solution)/shard_map/ppermute | solution.py:36
  110.6 11.1 %all-to-all-start.3 = ((bf16[8,64,128]{2,1,0:T(8,128)(2,1)}), bf16[8,64,128]{2,1,0:T(8,128)(2,1)S(1)}, u32[]{:S(2)}, u32[]{:S(2)}) async-start(bf16[8,64,128]{2,1,0:T(8,128)(2,1)} %bitcast.28), calls=%async_computation.3 | async-start | bytes 262144 | tf_op jit(solution)/shard_map/all_to_all | solution.py:19
  122.3 7.1 %collective-permute-start.10 = (bf16[224,128]{1,0:T(8,128)(2,1)S(1)}, bf16[224,128]{1,0:T(8,128)(2,1)S(1)}, u32[]{:S(2)}, u32[]{:S(2)}) collective-permute-start(bf16[224,128]{1,0:T(8,128)(2,1)S(1)} %fusion.4), channel_id=1, source_target_pairs={{0,128},{32,160},{64,192},{96,224},{128,0},{160,32},{192,64},{224,... | collective-permute-start | bytes 172040 | tf_op jit(solution)/shard_map/ppermute | solution.py:36
  126.6 7.6 %collective-permute-start.12 = (bf16[992,128]{1,0:T(8,128)(2,1)S(1)}, bf16[992,128]{1,0:T(8,128)(2,1)S(1)}, u32[]{:S(2)}, u32[]{:S(2)}) collective-permute-start(bf16[992,128]{1,0:T(8,128)(2,1)S(1)} %fusion), channel_id=1, source_target_pairs={{0,2},{1,3},{2,0},{3,1},{4,6},{5,7},{6,4},{7,5},{8,10},{9,11},{10,... | collective-permute-start | bytes 761864 | tf_op jit(solution)/shard_map/ppermute | solution.py:36

commit v9 on v8

--- a/solution.py
+++ b/solution.py
@@ -10,7 +10,7 @@
 CLASSES = 14
 CLASS_ROWS = 16
 TAPS = 27
-VMEM_LIMIT = 48 * 1024 * 1024
+VMEM_LIMIT = 24 * 1024 * 1024
 VMEM_MORE = 60 * 1024 * 1024
 STEPS = (-1, 0, 1)
 
@@ -467,11 +467,10 @@
         got,
     )
     terms = [level_parts[0]] + [swap(level_parts[k], "gy", 2 * k) for k in range(1, ny // 2)]
-    relayed = behind(relayed, level_parts[0])
 
     by_depth = spread(jnp.concatenate([relayed, aux_part]), "gx")
     aux_sum = by_depth[:, nc * cells :].astype(f32).sum(axis=0).astype(bf16)
-    by_depth = behind(by_depth, terms[1], terms[-1])
+    by_depth = behind(by_depth, level_parts[0])
     line = by_depth[:, : nc * cells].reshape(nx, nc, half_d * half_h, window, inner)[:, :, :, :wide]
     split = nx * nc * half_d * half_h * wide
     by_height = spread(jnp.concatenate([line.reshape(split, inner), aux_sum]), "gy")
@@ -483,7 +482,7 @@
         .reshape(bottom_d * wide * bottom_h, full)
     )
 
-    down_wide = behind(down_wide, terms[ny // 4])
+    down_wide = behind(down_wide, terms[1], terms[-1])
     level_part = sum(t.astype(f32) for t in terms)
     level_part = summed_by_pairs(level_part, "gy", [1], [1])
 
@@ -531,7 +530,7 @@
         .reshape(share, block, bottom_h, channel_width)
         .transpose(0, 2, 1, 3)
     )
-    both = summed_by_pairs(both, "col", bits_of("col"), bits_of("col")[::-1], part)
+    both = summed_by_pairs(behind(both, part), "col", bits_of("col"), bits_of("col")[::-1])
     bottom_weight_grad = both[: TAPS * thin].reshape(TAPS, thin, filters).transpose(1, 0, 2)
     up_weight_grad = both[TAPS * thin :]
     return (

time: 137 us -> 145 us (1.058)
  waiting for transfers between devices: 32 us -> 40.4 us
  starting transfers between devices: 53.2 us -> 48.5 us
  local copies, waits for them, and re-layouts: 10.3 us -> 13.4 us
  other arithmetic: 3.99 us -> 5.76 us
    ppermute x11, waiting for transfers between devices: 17.3 us -> 35.4 us  [swap(): lax.ppermute(x, axis, [(i, i ^ bit) for i in range(lax.axis_size(axis))])]
    all_to_all x3, waiting for transfers between devices: 14.8 us -> 4.97 us  [exchange(): return lax.all_to_all(x, axis, split_axis=0, concat_axis=0, tiled=False)]
    ppermute x11, starting transfers between devices: 36.4 us -> 30.6 us  [swap(): lax.ppermute(x, axis, [(i, i ^ bit) for i in range(lax.axis_size(axis))])]
    unnamed x32 -> x36, local copies, waits for them, and re-layouts: 4.75 us -> 8.75 us
  transfers between devices with their start and end apart: 16 -> 16, of which waited for: 6 -> 9; matrix products, arithmetic and copies ran while one was open for 7% -> 7% of each run, Pallas kernels for 2% -> 7%
where the time goes in v9:
time: 145 us; the launch traced here: 144 us
  starting transfers between devices  48.5 us (33%)
  waiting for transfers between devices  40.4 us (28%)
  blocking collectives  19 us (13%)
  Pallas kernels  16.3 us (11%)
  local copies, waits for them, and re-layouts  13.4 us (9%)
  other arithmetic  5.76 us (4%)
    ppermute x11, waiting for transfers between devices, swap(): lax.ppermute(x, axis, [(i, i ^ bit) for i in range(lax.axis_size(axis))])  35.4 us
    ppermute x11, starting transfers between devices, swap(): lax.ppermute(x, axis, [(i, i ^ bit) for i in range(lax.axis_size(axis))])  30.6 us
    pallas_call x6, Pallas kernels, local_call(): pl.pallas_call(body, out_shape=list(out_shapes), in_specs=[pl.BlockSpec(m...  16.3 us
    all_to_all x3, starting transfers between devices, exchange(): return lax.all_to_all(x, axis, split_axis=0, concat_axis=0, tiled=False)  15.9 us
    all_gather x1, blocking collectives, per_device(): gathered = lax.all_gather(payload, 'col')  9.83 us
    all_to_all x1, blocking collectives, exchange(): return lax.all_to_all(x, axis, split_axis=0, concat_axis=0, tiled=False)  9.16 us
    unnamed x36, local copies, waits for them, and re-layouts  8.75 us
    all_to_all x3, waiting for transfers between devices, exchange(): return lax.all_to_all(x, axis, split_axis=0, concat_axis=0, tiled=False)  4.97 us
  transfers between devices with their start and end apart: 16, of which 9 were waited for; matrix products, arithmetic and copies ran while one was open for 7% of the time, Pallas kernels for 7%

profile of v9, /device:TPU:1, one launch (start us, length us, event | category | flops | bytes accessed | tf_op | source)
XLA Modules:
  0.0 144.3 jit_solution(5698286653633594939)
XLA Ops:
  0.7 1.7 %shard_map.145 = bf16[528,128]{1,0:T(8,128)(2,1)} custom-call(bf16[256,128]{1,0:T(8,128)(2,1)} %bitcast.100, bf16[256,128]{1,0:T(8,128)(2,1)} %bitcast.118, bf16[14,128]{1,0:T(8,128)(2,1)} %bitcast.120, bf16[128,13824]{1,0:T(8,128)(2,1)} %weight_ref.1), custom_call_target="tpu_custom_call" | custom-call | bytes 65536 | tf_op jit(solution)/shard_map/pallas_call | solution.py:86
  2.4 9.8 %all-gather = bf16[2112,128]{1,0:T(8,128)(2,1)S(1)} all-gather(bf16[528,128]{1,0:T(8,128)(2,1)} %shard_map.145), channel_id=2, replica_groups=mesh['gx'=8,'gy'=8,'col'=4] {'col'}, dimensions={0}, use_global_device_ids=true | all-gather | bytes 675840 | tf_op jit(solution)/shard_map/all_gather | solution.py:371
  12.2 1.4 shard_map.146
  13.6 0.7 copy-done.4
  14.9 1.3 collective-permute-start.1
  16.2 0.9 copy.43
  17.1 0.9 slice_bitcast_fusion.3
  18.0 1.5 %collective-permute-done.even_x_ref = bf16[128,512]{1,0:T(8,128)(2,1)} collective-permute-done((bf16[128,512]{1,0:T(8,128)(2,1)}, bf16[128,512]{1,0:T(8,128)(2,1)}, u32[]{:S(2)}, u32[]{:S(2)}) %collective-permute-start) | collective-permute-done | bytes 131104 | tf_op jit(solution)/shard_map/ppermute | solution.py:36
  19.5 0.8 select_bitcast_fusion.5
  20.4 0.7 collective-permute-start.3
  21.1 4.6 %collective-permute-start.2 = (bf16[4,32,512]{2,1,0:T(8,128)(2,1)S(1)}, bf16[4,32,512]{2,1,0:T(8,128)(2,1)S(1)}, u32[]{:S(2)}, u32[]{:S(2)}) collective-permute-start(bf16[4,32,512]{2,1,0:T(8,128)(2,1)S(1)} %get-tuple-element.55), channel_id=1, source_target_pairs={{0,4},{4,0},{8,12},{12,8},{16,20},{20,16},{24,28},{28,24},{1,5},{5... | collective-permute-start | bytes 393224 | tf_op jit(solution)/shard_map/ppermute | solution.py:36
  25.8 5.4 %collective-permute-done.2.even_y_ref = bf16[4,32,512]{2,1,0:T(8,128)(2,1)S(1)} collective-permute-done((bf16[4,32,512]{2,1,0:T(8,128)(2,1)S(1)}, bf16[4,32,512]{2,1,0:T(8,128)(2,1)S(1)}, u32[]{:S(2)}, u32[]{:S(2)}) %collective-permute-start.2) | collective-permute-done | bytes 131104 | tf_op jit(solution)/shard_map/ppermute | solution.py:36
  31.2 0.9 copy-done.5
  32.2 0.8 copy-done.8
  33.0 3.8 %shard_map.147 = (bf16[4,6,32,512]{3,2,1,0:T(8,128)(2,1)S(1)}, bf16[256,128]{1,0:T(8,128)(2,1)}, bf16[4,144,128]{2,1,0:T(8,128)(2,1)S(1)}, bf16[448,512]{1,0:T(8,128)(2,1)}) custom-call(bf16[256,512]{1,0:T(8,128)(2,1)S(1)} %copy-done.5, bf16[128,512]{1,0:T(8,128)(2,1)} %collective-permute-done.even_x_ref, bf16[128,512]{1,0:T(8,128)(2,1)} %collective-permute-done.1.odd_x_ref, ...), custom_call_target="tpu_custom_call" | custom-call | flops 905969664 | bytes 3538944 | tf_op jit(solution)/shard_map/pallas_call | solution.py:86
  36.8 0.9 copy-done.11
  37.7 4.5 %collective-permute-start.4 = (bf16[448,512]{1,0:T(8,128)(2,1)}, bf16[448,512]{1,0:T(8,128)(2,1)S(1)}, u32[]{:S(2)}, u32[]{:S(2)}) collective-permute-start(bf16[448,512]{1,0:T(8,128)(2,1)} %get-tuple-element.31), channel_id=1, source_target_pairs={{0,32},{32,0},{64,96},{96,64},{128,160},{160,128},{192,224},{224,1... | collective-permute-start | bytes 1376264 | tf_op jit(solution)/shard_map/ppermute | solution.py:36
  42.1 9.2 %all_to_all.20 = bf16[4,144,128]{2,1,0:T(8,128)(2,1)S(1)} all-to-all(bf16[4,144,128]{2,1,0:T(8,128)(2,1)S(1)} %get-tuple-element.28), channel_id=1, replica_groups=mesh['gx'=8,'gy'=8,'col'=4] {'col'}, dimensions={0} | all-to-all | bytes 294912 | tf_op jit(solution)/shard_map/all_to_all | solution.py:19
  51.3 0.7 broadcast_in_dim.4
  52.0 6.7 %all-to-all-start.1 = ((bf16[8,80,128]{2,1,0:T(8,128)(2,1)}), bf16[8,80,128]{2,1,0:T(8,128)(2,1)S(1)}, u32[]{:S(2)}, u32[]{:S(2)}) async-start(bf16[8,80,128]{2,1,0:T(8,128)(2,1)} %broadcast_in_dim.4), calls=%async_computation.1 | async-start | bytes 327680 | tf_op jit(solution)/shard_map/all_to_all | solution.py:19
  58.7 0.8 copy-done.9
  59.5 1.1 copy-done.12
  60.6 6.2 %shard_map.148 = (bf16[2,4,224,128]{3,2,1,0:T(8,128)(2,1)S(1)}, bf16[2,4,224,128]{3,2,1,0:T(8,128)(2,1)S(1)}, bf16[2,4,224,128]{3,2,1,0:T(8,128)(2,1)S(1)}, bf16[2,4,224,128]{3,2,1,0:T(8,128)(2,1)S(1)}) custom-call(bf16[4,6,32,512]{3,2,1,0:T(8,128)(2,1)S(1)} %copy-done.12, bf16[256,128]{1,0:T(8,128)(2,1)S(1)} %bitcast.103, ...), custom_call_target="tpu_custom_call" | custom-call | flops 905969664 | bytes 3670016 | tf_op jit(solution)/shard_map/pallas_call | solution.py:86
  66.8 1.4 collective-permute-start.5
  68.2 1.9 %collective-permute-start.6 = (bf16[2,4,224,128]{3,2,1,0:T(8,128)(2,1)S(1)}, bf16[2,4,224,128]{3,2,1,0:T(8,128)(2,1)}, u32[]{:S(2)}, u32[]{:S(2)}) collective-permute-start(bf16[2,4,224,128]{3,2,1,0:T(8,128)(2,1)S(1)} %get-tuple-element.35), channel_id=1, source_target_pairs={{0,24},{4,28},{8,16},{12,20},{16,8},{20,12},{24,0},{28,4},{1,25},{... | collective-permute-start | bytes 1376264 | tf_op jit(solution)/shard_map/ppermute | solution.py:36
  70.5 1.0 broadcast_in_dim.5
  71.5 5.2 %all-to-all-start.2 = ((bf16[8,400,128]{2,1,0:T(8,128)(2,1)}), bf16[8,400,128]{2,1,0:T(8,128)(2,1)S(1)}, u32[]{:S(2)}, u32[]{:S(2)}) async-start(bf16[8,400,128]{2,1,0:T(8,128)(2,1)} %broadcast_in_dim.5), calls=%async_computation.2 | async-start | bytes 1638400 | tf_op jit(solution)/shard_map/all_to_all | solution.py:19
  76.7 1.7 %collective-permute-done.5 = bf16[2,4,224,128]{3,2,1,0:T(8,128)(2,1)S(1)} collective-permute-done((bf16[2,4,224,128]{3,2,1,0:T(8,128)(2,1)S(1)}, bf16[2,4,224,128]{3,2,1,0:T(8,128)(2,1)S(1)}, u32[]{:S(2)}, u32[]{:S(2)}) %collective-permute-start.5) | collective-permute-done | bytes 458784 | tf_op jit(solution)/shard_map/ppermute | solution.py:36
  78.4 13.7 %collective-permute-done.6 = bf16[2,4,224,128]{3,2,1,0:T(8,128)(2,1)} collective-permute-done((bf16[2,4,224,128]{3,2,1,0:T(8,128)(2,1)S(1)}, bf16[2,4,224,128]{3,2,1,0:T(8,128)(2,1)}, u32[]{:S(2)}, u32[]{:S(2)}) %collective-permute-start.6) | collective-permute-done | bytes 458784 | tf_op jit(solution)/shard_map/ppermute | solution.py:36
  92.1 2.6 %collective-permute-done.7 = bf16[2,4,224,128]{3,2,1,0:T(8,128)(2,1)} collective-permute-done((bf16[2,4,224,128]{3,2,1,0:T(8,128)(2,1)S(1)}, bf16[2,4,224,128]{3,2,1,0:T(8,128)(2,1)}, u32[]{:S(2)}, u32[]{:S(2)}) %collective-permute-start.7) | collective-permute-done | bytes 458784 | tf_op jit(solution)/shard_map/ppermute | solution.py:36
  94.7 1.4 convert_add_fusion.1
  96.1 0.9 copy-done.14
  97.0 2.1 %collective-permute-start.8 = (bf16[4,224,128]{2,1,0:T(8,128)(2,1)S(1)}, bf16[4,224,128]{2,1,0:T(8,128)(2,1)}, u32[]{:S(2)}, u32[]{:S(2)}) collective-permute-start(bf16[4,224,128]{2,1,0:T(8,128)(2,1)S(1)} %fusion.1), channel_id=1, source_target_pairs={{0,4},{4,0},{8,12},{12,8},{16,20},{20,16},{24,28},{28,24},{1,5},{5... | collective-permute-start | bytes 688136 | tf_op jit(solution)/shard_map/ppermute | solution.py:36
  100.6 2.3 %shard_map.149 = (bf16[512,128]{1,0:T(8,128)(2,1)}, bf16[3,10,6,16,128]{4,3,2,1,0:T(8,128)(2,1)S(1)}) custom-call(bf16[768,512]{1,0:T(8,128)(2,1)S(1)} %bitcast.90, bf16[128,512]{1,0:T(8,128)(2,1)S(1)} %copy-done.7, bf16[8,1,16,128]{3,2,1,0:T(8,128)(2,1)S(1)} %get-tuple-element.65.before_ref, bf16[8,4,16,128]{3,2,1,0:T(8,128)(2,1)S(1)} %bitcast.96, ...), custom_call_target="tpu_custom_call" | custom-call | flops 452984832 | bytes 884736 | tf_op jit(solution)/shard_map/pallas_call | solution.py:86
  103.0 4.1 %all-to-all-start.3 = ((bf16[8,64,128]{2,1,0:T(8,128)(2,1)}), bf16[8,64,128]{2,1,0:T(8,128)(2,1)S(1)}, u32[]{:S(2)}, u32[]{:S(2)}) async-start(bf16[8,64,128]{2,1,0:T(8,128)(2,1)} %bitcast.28), calls=%async_computation.3 | async-start | bytes 262144 | tf_op jit(solution)/shard_map/all_to_all | solution.py:19
  107.1 1.2 bitcast_add_fusion.1
  108.3 0.9 shard_map.150
  109.1 5.0 %all-to-all-done.3 = bf16[8,64,128]{2,1,0:T(8,128)(2,1)S(1)} async-done(((bf16[8,64,128]{2,1,0:T(8,128)(2,1)}), bf16[8,64,128]{2,1,0:T(8,128)(2,1)S(1)}, u32[]{:S(2)}, u32[]{:S(2)}) %all-to-all-start.3) | async-done | bytes 131104 | tf_op jit(solution)/shard_map/all_to_all | solution.py:19
  114.2 6.9 %collective-permute-start.11 = (bf16[2,992,128]{2,1,0:T(8,128)(2,1)S(1)}, bf16[2,992,128]{2,1,0:T(8,128)(2,1)S(1)}, u32[]{:S(2)}, u32[]{:S(2)}) collective-permute-start(bf16[2,992,128]{2,1,0:T(8,128)(2,1)S(1)} %dynamic-slice_bitcast_fusion), channel_id=1, source_target_pairs={{0,1},{1,0},{2,3},{3,2},{4,5},{5,4},{6,7},{7,6},{8,9},{9,8},{10,11... | collective-permute-start | bytes 1523720 | tf_op jit(solution)/shard_map/ppermute | solution.py:36
  121.1 2.4 %collective-permute-start.9 = (bf16[2,224,128]{2,1,0:T(8,128)(2,1)S(1)}, bf16[2,224,128]{2,1,0:T(8,128)(2,1)S(1)}, u32[]{:S(2)}, u32[]{:S(2)}) collective-permute-start(bf16[2,224,128]{2,1,0:T(8,128)(2,1)S(1)} %fusion.2), channel_id=1, source_target_pairs={{0,64},{32,96},{64,0},{96,32},{128,192},{160,224},{192,128},{224,1... | collective-permute-start | bytes 344072 | tf_op jit(solution)/shard_map/ppermute | solution.py:36
  123.5 1.4 convert_reduce_fusion
  124.9 4.4 %collective-permute-done.9 = bf16[2,224,128]{2,1,0:T(8,128)(2,1)S(1)} collective-permute-done((bf16[2,224,128]{2,1,0:T(8,128)(2,1)S(1)}, bf16[2,224,128]{2,1,0:T(8,128)(2,1)S(1)}, u32[]{:S(2)}, u32[]{:S(2)}) %collective-permute-start.9) | collective-permute-done | bytes 114720 | tf_op jit(solution)/shard_map/ppermute | solution.py:36
  130.0 5.7 %collective-permute-start.10 = (bf16[224,128]{1,0:T(8,128)(2,1)S(1)}, bf16[224,128]{1,0:T(8,128)(2,1)S(1)}, u32[]{:S(2)}, u32[]{:S(2)}) collective-permute-start(bf16[224,128]{1,0:T(8,128)(2,1)S(1)} %fusion.4), channel_id=1, source_target_pairs={{0,128},{32,160},{64,192},{96,224},{128,0},{160,32},{192,64},{224,... | collective-permute-start | bytes 172040 | tf_op jit(solution)/shard_map/ppermute | solution.py:36
  136.1 1.1 collective-permute-done.10
  137.3 0.7 fusion.3
  137.9 4.9 %collective-permute-done.12 = bf16[992,128]{1,0:T(8,128)(2,1)S(1)} collective-permute-done((bf16[992,128]{1,0:T(8,128)(2,1)S(1)}, bf16[992,128]{1,0:T(8,128)(2,1)S(1)}, u32[]{:S(2)}, u32[]{:S(2)}) %collective-permute-start.12) | collective-permute-done | bytes 253984 | tf_op jit(solution)/shard_map/ppermute | solution.py:36
  142.9 0.6 slice.120
  143.5 0.8 slice.119
  (62 shorter events, 3.7 us)
Async XLA Ops:
  0.6 30.6 %copy-start = (bf16[128,13824]{1,0:T(8,128)(2,1)S(1)}, bf16[128,13824]{1,0:T(8,128)(2,1)}, u32[]{:S(2)}) copy-start(bf16[128,13824]{1,0:T(8,128)(2,1)} %weight_ref.1) | copy-start | bytes 10616836
  0.6 11.5 %copy-start.6 = (bf16[2,4,32,128]{3,2,1,0:T(8,128)(2,1)S(1)}, bf16[2,4,32,128]{3,2,1,0:T(8,128)(2,1)}, u32[]{:S(2)}) copy-start(bf16[2,4,32,128]{3,2,1,0:T(8,128)(2,1)} %param.15) | copy-start | bytes 196612
  0.7 11.5 %copy-start.10 = (s32[2,4,32]{2,1,0:T(4,128)S(1)}, s32[2,4,32]{2,1,0:T(4,128)}, u32[]{:S(2)}) copy-start(s32[2,4,32]{2,1,0:T(4,128)} %label_ref.1) | copy-start | bytes 3076
  13.6 0.7 copy-start.4
  14.3 5.3 %collective-permute-start = (bf16[128,512]{1,0:T(8,128)(2,1)}, bf16[128,512]{1,0:T(8,128)(2,1)}, u32[]{:S(2)}, u32[]{:S(2)}) collective-permute-start(bf16[128,512]{1,0:T(8,128)(2,1)} %get-tuple-element.25), channel_id=1, source_target_pairs={{0,32},{32,0},{64,96},{96,64},{128,160},{160,128},{192,224},{224,1... | collective-permute-start | bytes 393224 | tf_op jit(solution)/shard_map/ppermute | solution.py:36
  14.9 4.7 %collective-permute-start.1 = (bf16[128,512]{1,0:T(8,128)(2,1)}, bf16[128,512]{1,0:T(8,128)(2,1)}, u32[]{:S(2)}, u32[]{:S(2)}) collective-permute-start(bf16[128,512]{1,0:T(8,128)(2,1)} %get-tuple-element.26), channel_id=1, source_target_pairs={{32,64},{64,32},{96,128},{128,96},{160,192},{192,160},{33,65},{65,... | collective-permute-start | bytes 393224 | tf_op jit(solution)/shard_map/ppermute | solution.py:41
  17.1 8.6 %copy-start.1 = (bf16[8,16,4,128]{3,1,2,0:T(8,128)(2,1)}, bf16[8,16,4,128]{3,1,2,0:T(8,128)(2,1)S(1)}, u32[]{:S(2)}) copy-start(bf16[8,16,4,128]{3,1,2,0:T(8,128)(2,1)S(1)} %copy.43) | copy-start | bytes 393220
  20.4 5.4 %collective-permute-start.3 = (bf16[4,32,512]{2,1,0:T(8,128)(2,1)S(1)}, bf16[4,32,512]{2,1,0:T(8,128)(2,1)S(1)}, u32[]{:S(2)}, u32[]{:S(2)}) collective-permute-start(bf16[4,32,512]{2,1,0:T(8,128)(2,1)S(1)} %get-tuple-element.54), channel_id=1, source_target_pairs={{4,8},{8,4},{12,16},{16,12},{20,24},{24,20},{5,9},{9,5},{13,17},{1... | collective-permute-start | bytes 393224 | tf_op jit(solution)/shard_map/ppermute | solution.py:41
  21.1 10.1 %collective-permute-start.2 = (bf16[4,32,512]{2,1,0:T(8,128)(2,1)S(1)}, bf16[4,32,512]{2,1,0:T(8,128)(2,1)S(1)}, u32[]{:S(2)}, u32[]{:S(2)}) collective-permute-start(bf16[4,32,512]{2,1,0:T(8,128)(2,1)S(1)} %get-tuple-element.55), channel_id=1, source_target_pairs={{0,4},{4,0},{8,12},{12,8},{16,20},{20,16},{24,28},{28,24},{1,5},{5... | collective-permute-start | bytes 393224 | tf_op jit(solution)/shard_map/ppermute | solution.py:36
  31.2 1.0 copy-start.5
  32.2 0.8 copy-start.8
  36.8 0.9 copy-start.11
  37.7 21.0 %collective-permute-start.4 = (bf16[448,512]{1,0:T(8,128)(2,1)}, bf16[448,512]{1,0:T(8,128)(2,1)S(1)}, u32[]{:S(2)}, u32[]{:S(2)}) collective-permute-start(bf16[448,512]{1,0:T(8,128)(2,1)} %get-tuple-element.31), channel_id=1, source_target_pairs={{0,32},{32,0},{64,96},{96,64},{128,160},{160,128},{192,224},{224,1... | collective-permute-start | bytes 1376264 | tf_op jit(solution)/shard_map/ppermute | solution.py:36
  52.0 18.4 %all-to-all-start.1 = ((bf16[8,80,128]{2,1,0:T(8,128)(2,1)}), bf16[8,80,128]{2,1,0:T(8,128)(2,1)S(1)}, u32[]{:S(2)}, u32[]{:S(2)}) async-start(bf16[8,80,128]{2,1,0:T(8,128)(2,1)} %broadcast_in_dim.4), calls=%async_computation.1 | async-start | bytes 327680 | tf_op jit(solution)/shard_map/all_to_all | solution.py:19
  58.6 0.8 copy-start.9
  59.5 1.1 copy-start.12
  66.8 32.2 %copy-start.15 = (bf16[8,16,4,128]{3,2,1,0:T(4,128)(2,1)S(1)}, bf16[8,16,4,128]{3,2,1,0:T(4,128)(2,1)}, u32[]{:S(2)}) copy-start(bf16[8,16,4,128]{3,2,1,0:T(4,128)(2,1)} %param.11) | copy-start | bytes 393220
  66.8 11.6 %collective-permute-start.5 = (bf16[2,4,224,128]{3,2,1,0:T(8,128)(2,1)S(1)}, bf16[2,4,224,128]{3,2,1,0:T(8,128)(2,1)S(1)}, u32[]{:S(2)}, u32[]{:S(2)}) collective-permute-start(bf16[2,4,224,128]{3,2,1,0:T(8,128)(2,1)S(1)} %get-tuple-element.34), channel_id=1, source_target_pairs={{0,8},{4,12},{8,0},{12,4},{16,24},{20,28},{24,16},{28,20},{1,9},{5... | collective-permute-start | bytes 1376264 | tf_op jit(solution)/shard_map/ppermute | solution.py:36
  68.2 23.9 %collective-permute-start.6 = (bf16[2,4,224,128]{3,2,1,0:T(8,128)(2,1)S(1)}, bf16[2,4,224,128]{3,2,1,0:T(8,128)(2,1)}, u32[]{:S(2)}, u32[]{:S(2)}) collective-permute-start(bf16[2,4,224,128]{3,2,1,0:T(8,128)(2,1)S(1)} %get-tuple-element.35), channel_id=1, source_target_pairs={{0,24},{4,28},{8,16},{12,20},{16,8},{20,12},{24,0},{28,4},{1,25},{... | collective-permute-start | bytes 1376264 | tf_op jit(solution)/shard_map/ppermute | solution.py:36
  70.2 24.5 %collective-permute-start.7 = (bf16[2,4,224,128]{3,2,1,0:T(8,128)(2,1)S(1)}, bf16[2,4,224,128]{3,2,1,0:T(8,128)(2,1)}, u32[]{:S(2)}, u32[]{:S(2)}) collective-permute-start(bf16[2,4,224,128]{3,2,1,0:T(8,128)(2,1)S(1)} %get-tuple-element.38), channel_id=1, source_target_pairs={{0,16},{4,20},{8,24},{12,28},{16,0},{20,4},{24,8},{28,12},{1,17},{... | collective-permute-start | bytes 1376264 | tf_op jit(solution)/shard_map/ppermute | solution.py:36
  71.5 27.7 %all-to-all-start.2 = ((bf16[8,400,128]{2,1,0:T(8,128)(2,1)}), bf16[8,400,128]{2,1,0:T(8,128)(2,1)S(1)}, u32[]{:S(2)}, u32[]{:S(2)}) async-start(bf16[8,400,128]{2,1,0:T(8,128)(2,1)} %broadcast_in_dim.5), calls=%async_computation.2 | async-start | bytes 1638400 | tf_op jit(solution)/shard_map/all_to_all | solution.py:19
  96.0 0.9 copy-start.14
  97.0 10.0 %collective-permute-start.8 = (bf16[4,224,128]{2,1,0:T(8,128)(2,1)S(1)}, bf16[4,224,128]{2,1,0:T(8,128)(2,1)}, u32[]{:S(2)}, u32[]{:S(2)}) collective-permute-start(bf16[4,224,128]{2,1,0:T(8,128)(2,1)S(1)} %fusion.1), channel_id=1, source_target_pairs={{0,4},{4,0},{8,12},{12,8},{16,20},{20,16},{24,28},{28,24},{1,5},{5... | collective-permute-start | bytes 688136 | tf_op jit(solution)/shard_map/ppermute | solution.py:36
  99.1 1.3 copy-start.2
  99.1 1.5 %copy-start.3 = (bf16[128,27,128]{2,0,1:T(8,128)(2,1)S(1)}, bf16[128,27,128]{2,0,1:T(8,128)(2,1)}, u32[]{:S(2)}) copy-start(bf16[128,27,128]{2,0,1:T(8,128)(2,1)} %param.12) | copy-start | bytes 2654212
  99.1 1.5 %copy-start.7 = (bf16[128,512]{1,0:T(8,128)(2,1)S(1)}, bf16[128,512]{1,0:T(8,128)(2,1)}, u32[]{:S(2)}) copy-start(bf16[128,512]{1,0:T(8,128)(2,1)} %up_ref.1) | copy-start | bytes 393220
  99.2 1.1 copy-start.13
  103.0 11.2 %all-to-all-start.3 = ((bf16[8,64,128]{2,1,0:T(8,128)(2,1)}), bf16[8,64,128]{2,1,0:T(8,128)(2,1)S(1)}, u32[]{:S(2)}, u32[]{:S(2)}) async-start(bf16[8,64,128]{2,1,0:T(8,128)(2,1)} %bitcast.28), calls=%async_computation.3 | async-start | bytes 262144 | tf_op jit(solution)/shard_map/all_to_all | solution.py:19
  114.2 21.5 %collective-permute-start.11 = (bf16[2,992,128]{2,1,0:T(8,128)(2,1)S(1)}, bf16[2,992,128]{2,1,0:T(8,128)(2,1)S(1)}, u32[]{:S(2)}, u32[]{:S(2)}) collective-permute-start(bf16[2,992,128]{2,1,0:T(8,128)(2,1)S(1)} %dynamic-slice_bitcast_fusion), channel_id=1, source_target_pairs={{0,1},{1,0},{2,3},{3,2},{4,5},{5,4},{6,7},{7,6},{8,9},{9,8},{10,11... | collective-permute-start | bytes 1523720 | tf_op jit(solution)/shard_map/ppermute | solution.py:36
  121.1 8.2 %collective-permute-start.9 = (bf16[2,224,128]{2,1,0:T(8,128)(2,1)S(1)}, bf16[2,224,128]{2,1,0:T(8,128)(2,1)S(1)}, u32[]{:S(2)}, u32[]{:S(2)}) collective-permute-start(bf16[2,224,128]{2,1,0:T(8,128)(2,1)S(1)} %fusion.2), channel_id=1, source_target_pairs={{0,64},{32,96},{64,0},{96,32},{128,192},{160,224},{192,128},{224,1... | collective-permute-start | bytes 344072 | tf_op jit(solution)/shard_map/ppermute | solution.py:36
  130.0 7.3 %collective-permute-start.10 = (bf16[224,128]{1,0:T(8,128)(2,1)S(1)}, bf16[224,128]{1,0:T(8,128)(2,1)S(1)}, u32[]{:S(2)}, u32[]{:S(2)}) collective-permute-start(bf16[224,128]{1,0:T(8,128)(2,1)S(1)} %fusion.4), channel_id=1, source_target_pairs={{0,128},{32,160},{64,192},{96,224},{128,0},{160,32},{192,64},{224,... | collective-permute-start | bytes 172040 | tf_op jit(solution)/shard_map/ppermute | solution.py:36
  135.9 7.0 %collective-permute-start.12 = (bf16[992,128]{1,0:T(8,128)(2,1)S(1)}, bf16[992,128]{1,0:T(8,128)(2,1)S(1)}, u32[]{:S(2)}, u32[]{:S(2)}) collective-permute-start(bf16[992,128]{1,0:T(8,128)(2,1)S(1)} %fusion), channel_id=1, source_target_pairs={{0,2},{1,3},{2,0},{3,1},{4,6},{5,7},{6,4},{7,5},{8,10},{9,11},{10,... | collective-permute-start | bytes 761864 | tf_op jit(solution)/shard_map/ppermute | solution.py:36

commit v10 on v9

--- a/solution.py
+++ b/solution.py
@@ -13,6 +13,7 @@
 VMEM_LIMIT = 24 * 1024 * 1024
 VMEM_MORE = 60 * 1024 * 1024
 STEPS = (-1, 0, 1)
+HALVES = ((0, (0, 3)), (0, (1, 2)), (1, (0, 1)), (1, (3, 2)))
 
 
 def exchange(x, axis):
@@ -88,7 +89,7 @@
         out_shape=list(out_shapes),
         in_specs=[
             pl.BlockSpec(
-                memory_space=pltpu.HBM if k == stay else pltpu.SMEM if a.ndim == 1 else pltpu.VMEM
+                memory_space=pltpu.HBM if stay is not None and k >= stay else pltpu.SMEM if a.ndim == 1 else pltpu.VMEM
             )
             for k, a in enumerate(args)
         ],
@@ -99,8 +100,8 @@
     )(*args)
 
 
-def pack_kernel(saved_ref, cotangent_ref, weight_ref, later_ref, out_ref):
-    del later_ref
+def pack_kernel(saved_ref, cotangent_ref, weight_ref, *refs):
+    out_ref = refs[-1]
     rows, inner = saved_ref.shape
     out_ref[:rows] = saved_ref[...]
     out_ref[rows : 2 * rows] = cotangent_ref[...]
@@ -261,8 +262,9 @@
         for j in range(by_height):
             start = full + j * chunk // grain * grain
             all_ref[j, m] = flat_ref[m, start : start + window]
-    for k, out_ref in enumerate(out_refs):
-        out_ref[...] = all_ref[pl.ds(2 * (at_y // 2 ^ k), 2)]
+    for (q, pairs), out_ref in zip(HALVES, out_refs):
+        for slot, k in enumerate(pairs):
+            out_ref[slot] = all_ref[2 * (at_y // 2 ^ k) + q]
 
 
 def bottom_kernel(
@@ -366,6 +368,9 @@
         level_cotangent.reshape(rows, inner),
         aux_weight.T,
         level_weight,
+        level_input.reshape(rows, inner),
+        up_weight,
+        bottom_weight.transpose(1, 0, 2),
         stay=3,
     )
     gathered = lax.all_gather(payload, "col")
@@ -452,7 +457,7 @@
     span = chunk + 8 if chunk % 16 else chunk
     level_parts = local_call(
         functools.partial(kernel_grad_kernel, chunk),
-        [struct((2, nx // 2, span, inner), bf16)] * (ny // 2),
+        [struct((2, nx // 2, span, inner), bf16)] * 4,
         [
             pltpu.VMEM((ny, nx // 2, span, inner), bf16),
             pltpu.VMEM((nx // 2, (chunk * ny - 1) // full * full + 4 * full, inner), bf16),
@@ -466,11 +471,16 @@
         flat_input,
         got,
     )
-    terms = [level_parts[0]] + [swap(level_parts[k], "gy", 2 * k) for k in range(1, ny // 2)]
+    def first_sum(kept, sent, bit):
+        return kept.astype(f32) + swap(sent, "gy", bit).astype(f32)
+
+    even_sum = first_sum(level_parts[0], level_parts[1], 2)
+    odd_sum = first_sum(level_parts[2], level_parts[3], 6)
+    relayed = behind(relayed, level_parts[0])
 
     by_depth = spread(jnp.concatenate([relayed, aux_part]), "gx")
     aux_sum = by_depth[:, nc * cells :].astype(f32).sum(axis=0).astype(bf16)
-    by_depth = behind(by_depth, level_parts[0])
+    by_depth = behind(by_depth, even_sum, odd_sum)
     line = by_depth[:, : nc * cells].reshape(nx, nc, half_d * half_h, window, inner)[:, :, :, :wide]
     split = nx * nc * half_d * half_h * wide
     by_height = spread(jnp.concatenate([line.reshape(split, inner), aux_sum]), "gy")
@@ -482,9 +492,10 @@
         .reshape(bottom_d * wide * bottom_h, full)
     )
 
-    down_wide = behind(down_wide, terms[1], terms[-1])
-    level_part = sum(t.astype(f32) for t in terms)
-    level_part = summed_by_pairs(level_part, "gy", [1], [1])
+    even_sum = first_sum(even_sum[0], even_sum[1].astype(bf16), 6)
+    odd_sum = first_sum(odd_sum[0], odd_sum[1].astype(bf16), 2)
+    level_part = summed_by_pairs(jnp.stack([even_sum, odd_sum]), "gy", [1], [1])
+    down_wide = behind(down_wide, level_part)
 
     bottom_rows = bottom_d * block * bottom_h
     channel_width = bottom_weight.shape[0]

time: 145 us -> 140 us (0.966)
  waiting for transfers between devices: 40.4 us -> 31.6 us
  starting transfers between devices: 48.5 us -> 52 us
  local copies, waits for them, and re-layouts: 13.4 us -> 10.4 us
  other arithmetic: 5.76 us -> 8.61 us
    ppermute x11 -> x12, waiting for transfers between devices: 35.4 us -> 19.5 us  [swap(): lax.ppermute(x, axis, [(i, i ^ bit) for i in range(lax.axis_size(axis))])]
    all_to_all x3, waiting for transfers between devices: 4.97 us -> 12.1 us  [exchange(): return lax.all_to_all(x, axis, split_axis=0, concat_axis=0, tiled=False)]
    unnamed x36 -> x30, local copies, waits for them, and re-layouts: 8.75 us -> 5.02 us
    ppermute x11 -> x12, starting transfers between devices: 30.6 us -> 33.2 us  [swap(): lax.ppermute(x, axis, [(i, i ^ bit) for i in range(lax.axis_size(axis))])]
    another operation x0 -> x2, other arithmetic: none -> 2.1 us  [per_device(): level_part = summed_by_pairs(jnp.stack([even_sum, odd_sum]), 'gy', [1], [1])]
  transfers between devices with their start and end apart: 16 -> 17, of which waited for: 9 -> 7; matrix products, arithmetic and copies ran while one was open for 7% -> 9% of each run, Pallas kernels for 7% -> 1%
where the time goes in v10:
time: 140 us; the launch traced here: 139 us
  starting transfers between devices  52 us (37%)
  waiting for transfers between devices  31.6 us (23%)
  blocking collectives  19 us (14%)
  Pallas kernels  16.1 us (12%)
  local copies, waits for them, and re-layouts  10.4 us (7%)
  other arithmetic  8.61 us (6%)
    ppermute x12, starting transfers between devices, swap(): lax.ppermute(x, axis, [(i, i ^ bit) for i in range(lax.axis_size(axis))])  33.2 us
    ppermute x12, waiting for transfers between devices, swap(): lax.ppermute(x, axis, [(i, i ^ bit) for i in range(lax.axis_size(axis))])  19.5 us
    all_to_all x3, starting transfers between devices, exchange(): return lax.all_to_all(x, axis, split_axis=0, concat_axis=0, tiled=False)  16.8 us
    pallas_call x6, Pallas kernels, local_call(): pl.pallas_call(body, out_shape=list(out_shapes), in_specs=[pl.BlockSpec(m...  16.1 us
    all_to_all x3, waiting for transfers between devices, exchange(): return lax.all_to_all(x, axis, split_axis=0, concat_axis=0, tiled=False)  12.1 us
    all_gather x1, blocking collectives, per_device(): gathered = lax.all_gather(payload, 'col')  9.83 us
    all_to_all x1, blocking collectives, exchange(): return lax.all_to_all(x, axis, split_axis=0, concat_axis=0, tiled=False)  9.16 us
    unnamed x30, local copies, waits for them, and re-layouts  5.02 us
  transfers between devices with their start and end apart: 17, of which 7 were waited for; matrix products, arithmetic and copies ran while one was open for 9% of the time, Pallas kernels for 1%

profile of v10, /device:TPU:1, one launch (start us, length us, event | category | flops | bytes accessed | tf_op | source)
XLA Modules:
  0.0 138.8 jit_solution(17198315225654432339)
XLA Ops:
  0.7 1.7 %shard_map.145 = bf16[528,128]{1,0:T(8,128)(2,1)} custom-call(bf16[256,128]{1,0:T(8,128)(2,1)} %bitcast.126, bf16[256,128]{1,0:T(8,128)(2,1)} %bitcast.140, bf16[14,128]{1,0:T(8,128)(2,1)} %bitcast.144, bf16[128,13824]{1,0:T(8,128)(2,1)} %weight_ref.1, bf16[256,128]{1,0:T(8,128)(2,1)} %bitcast.123, bf16[128,512]{1,0:T(8,128)(2,1)} %up_ref.1, ...), custom_call_target="tpu_custom_call" | custom-call | bytes 65536 | tf_op jit(solution)/shard_map/pallas_call | solution.py:87
  2.4 9.8 %all-gather = bf16[2112,128]{1,0:T(8,128)(2,1)S(1)} all-gather(bf16[528,128]{1,0:T(8,128)(2,1)} %shard_map.145), channel_id=2, replica_groups=mesh['gx'=8,'gy'=8,'col'=4] {'col'}, dimensions={0}, use_global_device_ids=true | all-gather | bytes 675840 | tf_op jit(solution)/shard_map/all_gather | solution.py:376
  12.2 1.3 shard_map.146
  13.5 0.7 copy-done.4
  14.2 0.6 collective-permute-start
  14.8 1.3 collective-permute-start.1
  16.1 0.9 copy.43
  17.1 0.9 slice_bitcast_fusion.5
  17.9 1.5 %collective-permute-done.even_x_ref = bf16[128,512]{1,0:T(8,128)(2,1)} collective-permute-done((bf16[128,512]{1,0:T(8,128)(2,1)}, bf16[128,512]{1,0:T(8,128)(2,1)}, u32[]{:S(2)}, u32[]{:S(2)}) %collective-permute-start) | collective-permute-done | bytes 131104 | tf_op jit(solution)/shard_map/ppermute | solution.py:37
  19.5 0.8 select_bitcast_fusion.5
  20.4 0.7 collective-permute-start.3
  21.0 4.6 %collective-permute-start.2 = (bf16[4,32,512]{2,1,0:T(8,128)(2,1)S(1)}, bf16[4,32,512]{2,1,0:T(8,128)(2,1)S(1)}, u32[]{:S(2)}, u32[]{:S(2)}) collective-permute-start(bf16[4,32,512]{2,1,0:T(8,128)(2,1)S(1)} %get-tuple-element.57), channel_id=1, source_target_pairs={{0,4},{4,0},{8,12},{12,8},{16,20},{20,16},{24,28},{28,24},{1,5},{5... | collective-permute-start | bytes 393224 | tf_op jit(solution)/shard_map/ppermute | solution.py:37
  25.7 5.4 %collective-permute-done.2.even_y_ref = bf16[4,32,512]{2,1,0:T(8,128)(2,1)S(1)} collective-permute-done((bf16[4,32,512]{2,1,0:T(8,128)(2,1)S(1)}, bf16[4,32,512]{2,1,0:T(8,128)(2,1)S(1)}, u32[]{:S(2)}, u32[]{:S(2)}) %collective-permute-start.2) | collective-permute-done | bytes 131104 | tf_op jit(solution)/shard_map/ppermute | solution.py:37
  31.2 0.9 copy-done.5
  32.1 0.8 copy-done.7
  33.0 3.7 %shard_map.147 = (bf16[4,6,32,512]{3,2,1,0:T(8,128)(2,1)S(1)}, bf16[256,128]{1,0:T(8,128)(2,1)}, bf16[4,144,128]{2,1,0:T(8,128)(2,1)S(1)}, bf16[448,512]{1,0:T(8,128)(2,1)S(1)}) custom-call(bf16[256,512]{1,0:T(8,128)(2,1)S(1)} %copy-done.5, bf16[128,512]{1,0:T(8,128)(2,1)} %collective-permute-done.even_x_ref, ...), custom_call_target="tpu_custom_call" | custom-call | flops 905969664 | bytes 3538944 | tf_op jit(solution)/shard_map/pallas_call | solution.py:87
  36.7 4.4 %collective-permute-start.4 = (bf16[448,512]{1,0:T(8,128)(2,1)S(1)}, bf16[448,512]{1,0:T(8,128)(2,1)S(1)}, u32[]{:S(2)}, u32[]{:S(2)}) collective-permute-start(bf16[448,512]{1,0:T(8,128)(2,1)S(1)} %get-tuple-element.31), channel_id=1, source_target_pairs={{0,32},{32,0},{64,96},{96,64},{128,160},{160,128},{192,224},{224,1... | collective-permute-start | bytes 1376264 | tf_op jit(solution)/shard_map/ppermute | solution.py:37
  41.1 9.2 %all_to_all.20 = bf16[4,144,128]{2,1,0:T(8,128)(2,1)S(1)} all-to-all(bf16[4,144,128]{2,1,0:T(8,128)(2,1)S(1)} %get-tuple-element.29), channel_id=1, replica_groups=mesh['gx'=8,'gy'=8,'col'=4] {'col'}, dimensions={0} | all-to-all | bytes 294912 | tf_op jit(solution)/shard_map/all_to_all | solution.py:20
  50.3 6.2 %shard_map.148 = (bf16[2,4,224,128]{3,2,1,0:T(8,128)(2,1)S(1)}, bf16[2,4,224,128]{3,2,1,0:T(8,128)(2,1)S(1)}, bf16[2,4,224,128]{3,2,1,0:T(8,128)(2,1)S(1)}, bf16[2,4,224,128]{3,2,1,0:T(8,128)(2,1)S(1)}) custom-call(bf16[4,6,32,512]{3,2,1,0:T(8,128)(2,1)S(1)} %get-tuple-element.30.far_ref, bf16[256,128]{1,0:T(8,128)(2,1)S(1)} %bitcast.125, ...), custom_call_target="tpu_custom_call" | custom-call | flops 905969664 | bytes 3670016 | tf_op jit(solution)/shard_map/pallas_call | solution.py:87
  56.5 1.4 %collective-permute-start.5 = (bf16[2,4,224,128]{3,2,1,0:T(8,128)(2,1)S(1)}, bf16[2,4,224,128]{3,2,1,0:T(8,128)(2,1)}, u32[]{:S(2)}, u32[]{:S(2)}) collective-permute-start(bf16[2,4,224,128]{3,2,1,0:T(8,128)(2,1)S(1)} %get-tuple-element.35), channel_id=1, source_target_pairs={{0,8},{4,12},{8,0},{12,4},{16,24},{20,28},{24,16},{28,20},{1,9},{5... | collective-permute-start | bytes 1376264 | tf_op jit(solution)/shard_map/ppermute | solution.py:37
  57.9 0.7 broadcast_in_dim.4
  58.6 7.2 %all-to-all-start.1 = ((bf16[8,80,128]{2,1,0:T(8,128)(2,1)}), bf16[8,80,128]{2,1,0:T(8,128)(2,1)S(1)}, u32[]{:S(2)}, u32[]{:S(2)}) async-start(bf16[8,80,128]{2,1,0:T(8,128)(2,1)} %broadcast_in_dim.4), calls=%async_computation.1 | async-start | bytes 327680 | tf_op jit(solution)/shard_map/all_to_all | solution.py:20
  65.8 2.3 %collective-permute-start.6 = (bf16[2,4,224,128]{3,2,1,0:T(8,128)(2,1)S(1)}, bf16[2,4,224,128]{3,2,1,0:T(8,128)(2,1)}, u32[]{:S(2)}, u32[]{:S(2)}) collective-permute-start(bf16[2,4,224,128]{3,2,1,0:T(8,128)(2,1)S(1)} %get-tuple-element.37), channel_id=1, source_target_pairs={{0,24},{4,28},{8,16},{12,20},{16,8},{20,12},{24,0},{28,4},{1,25},{... | collective-permute-start | bytes 1376264 | tf_op jit(solution)/shard_map/ppermute | solution.py:37
  68.0 6.1 %all-to-all-done.1 = bf16[8,80,128]{2,1,0:T(8,128)(2,1)S(1)} async-done(((bf16[8,80,128]{2,1,0:T(8,128)(2,1)}), bf16[8,80,128]{2,1,0:T(8,128)(2,1)S(1)}, u32[]{:S(2)}, u32[]{:S(2)}) %all-to-all-start.1) | async-done | bytes 163872 | tf_op jit(solution)/shard_map/all_to_all | solution.py:20
  74.2 1.1 convert_add_fusion.2
  75.3 2.6 %collective-permute-start.7 = (bf16[4,224,128]{2,1,0:T(8,128)(2,1)S(1)}, bf16[4,224,128]{2,1,0:T(8,128)(2,1)}, u32[]{:S(2)}, u32[]{:S(2)}) collective-permute-start(bf16[4,224,128]{2,1,0:T(8,128)(2,1)S(1)} %fusion.10), channel_id=1, source_target_pairs={{0,24},{4,28},{8,16},{12,20},{16,8},{20,12},{24,0},{28,4},{1,25},{... | collective-permute-start | bytes 688136 | tf_op jit(solution)/shard_map/ppermute | solution.py:37
  77.9 1.1 convert_add_fusion.1
  79.0 0.7 fusion.11
  79.9 1.0 broadcast_in_dim.5
  80.9 4.8 %all-to-all-start.2 = ((bf16[8,400,128]{2,1,0:T(8,128)(2,1)}), bf16[8,400,128]{2,1,0:T(8,128)(2,1)S(1)}, u32[]{:S(2)}, u32[]{:S(2)}) async-start(bf16[8,400,128]{2,1,0:T(8,128)(2,1)} %broadcast_in_dim.5), calls=%async_computation.2 | async-start | bytes 1638400 | tf_op jit(solution)/shard_map/all_to_all | solution.py:20
  85.7 1.0 fusion.8
  86.7 1.1 fusion.6
  88.0 3.0 %collective-permute-start.9 = (bf16[4,224,128]{2,1,0:T(8,128)(2,1)S(1)}, bf16[4,224,128]{2,1,0:T(8,128)(2,1)S(1)}, u32[]{:S(2)}, u32[]{:S(2)}) collective-permute-start(bf16[4,224,128]{2,1,0:T(8,128)(2,1)S(1)} %fusion.12), channel_id=1, source_target_pairs={{0,4},{4,0},{8,12},{12,8},{16,20},{20,16},{24,28},{28,24},{1,5},{5... | collective-permute-start | bytes 688136 | tf_op jit(solution)/shard_map/ppermute | solution.py:37
  91.1 7.1 %collective-permute-done.9 = bf16[4,224,128]{2,1,0:T(8,128)(2,1)S(1)} collective-permute-done((bf16[4,224,128]{2,1,0:T(8,128)(2,1)S(1)}, bf16[4,224,128]{2,1,0:T(8,128)(2,1)S(1)}, u32[]{:S(2)}, u32[]{:S(2)}) %collective-permute-start.9) | collective-permute-done | bytes 229408 | tf_op jit(solution)/shard_map/ppermute | solution.py:37
  99.8 2.3 %shard_map.149 = (bf16[512,128]{1,0:T(8,128)(2,1)}, bf16[3,10,6,16,128]{4,3,2,1,0:T(8,128)(2,1)S(1)}) custom-call(bf16[768,512]{1,0:T(8,128)(2,1)S(1)} %bitcast.112, bf16[128,512]{1,0:T(8,128)(2,1)S(1)} %copy-done.6, bf16[8,1,16,128]{3,2,1,0:T(8,128)(2,1)S(1)} %get-tuple-element.67.before_ref, bf16[8,4,16,128]{3,2,1,0:T(8,128)(2,1)S(1)} %bitcast.120, ...), custom_call_target="tpu_custom_call" | custom-call | flops 452984832 | bytes 884736 | tf_op jit(solution)/shard_map/pallas_call | solution.py:87
  102.1 4.8 %all-to-all-start.3 = ((bf16[8,64,128]{2,1,0:T(8,128)(2,1)}), bf16[8,64,128]{2,1,0:T(8,128)(2,1)S(1)}, u32[]{:S(2)}, u32[]{:S(2)}) async-start(bf16[8,64,128]{2,1,0:T(8,128)(2,1)} %bitcast.36), calls=%async_computation.3 | async-start | bytes 262144 | tf_op jit(solution)/shard_map/all_to_all | solution.py:20
  107.1 0.9 shard_map.150
  108.0 6.0 %all-to-all-done.3 = bf16[8,64,128]{2,1,0:T(8,128)(2,1)S(1)} async-done(((bf16[8,64,128]{2,1,0:T(8,128)(2,1)}), bf16[8,64,128]{2,1,0:T(8,128)(2,1)S(1)}, u32[]{:S(2)}, u32[]{:S(2)}) %all-to-all-start.3) | async-done | bytes 131104 | tf_op jit(solution)/shard_map/all_to_all | solution.py:20
  114.0 7.1 %collective-permute-start.12 = (bf16[2,992,128]{2,1,0:T(8,128)(2,1)S(1)}, bf16[2,992,128]{2,1,0:T(8,128)(2,1)S(1)}, u32[]{:S(2)}, u32[]{:S(2)}) collective-permute-start(bf16[2,992,128]{2,1,0:T(8,128)(2,1)S(1)} %dynamic-slice_bitcast_fusion), channel_id=1, source_target_pairs={{0,1},{1,0},{2,3},{3,2},{4,5},{5,4},{6,7},{7,6},{8,9},{9,8},{10,11... | collective-permute-start | bytes 1523720 | tf_op jit(solution)/shard_map/ppermute | solution.py:37
  121.1 0.9 bitcast_add_fusion.1
  122.1 1.4 convert_reduce_fusion
  123.5 0.6 copy.35
  124.1 5.2 %collective-permute-start.11 = (bf16[224,128]{1,0:T(8,128)(2,1)S(1)}, bf16[224,128]{1,0:T(8,128)(2,1)S(1)}, u32[]{:S(2)}, u32[]{:S(2)}) collective-permute-start(bf16[224,128]{1,0:T(8,128)(2,1)S(1)} %fusion.15), channel_id=1, source_target_pairs={{0,128},{32,160},{64,192},{96,224},{128,0},{160,32},{192,64},{224,... | collective-permute-start | bytes 172040 | tf_op jit(solution)/shard_map/ppermute | solution.py:37
  129.4 1.8 %collective-permute-start.13 = (bf16[992,128]{1,0:T(8,128)(2,1)S(1)}, bf16[992,128]{1,0:T(8,128)(2,1)S(1)}, u32[]{:S(2)}, u32[]{:S(2)}) collective-permute-start(bf16[992,128]{1,0:T(8,128)(2,1)S(1)} %fusion.9), channel_id=1, source_target_pairs={{0,2},{1,3},{2,0},{3,1},{4,6},{5,7},{6,4},{7,5},{8,10},{9,11},{10,... | collective-permute-start | bytes 761864 | tf_op jit(solution)/shard_map/ppermute | solution.py:37
  131.5 0.7 fusion.14
  132.1 5.2 %collective-permute-done.13 = bf16[992,128]{1,0:T(8,128)(2,1)S(1)} collective-permute-done((bf16[992,128]{1,0:T(8,128)(2,1)S(1)}, bf16[992,128]{1,0:T(8,128)(2,1)S(1)}, u32[]{:S(2)}, u32[]{:S(2)}) %collective-permute-start.13) | collective-permute-done | bytes 253984 | tf_op jit(solution)/shard_map/ppermute | solution.py:37
  137.4 0.6 slice.142
  138.0 0.8 slice.141
  (63 shorter events, 2.7 us)
Async XLA Ops:
  0.6 11.6 %copy-start.8 = (bf16[2,4,32,128]{3,2,1,0:T(8,128)(2,1)S(1)}, bf16[2,4,32,128]{3,2,1,0:T(8,128)(2,1)}, u32[]{:S(2)}) copy-start(bf16[2,4,32,128]{3,2,1,0:T(8,128)(2,1)} %param.15) | copy-start | bytes 196612
  0.6 11.5 %copy-start.9 = (s32[2,4,32]{2,1,0:T(4,128)S(1)}, s32[2,4,32]{2,1,0:T(4,128)}, u32[]{:S(2)}) copy-start(s32[2,4,32]{2,1,0:T(4,128)} %label_ref.1) | copy-start | bytes 3076
  0.7 30.5 %copy-start = (bf16[128,13824]{1,0:T(8,128)(2,1)S(1)}, bf16[128,13824]{1,0:T(8,128)(2,1)}, u32[]{:S(2)}) copy-start(bf16[128,13824]{1,0:T(8,128)(2,1)} %weight_ref.1) | copy-start | bytes 10616836
  13.5 0.7 copy-start.4
  14.2 5.3 %collective-permute-start = (bf16[128,512]{1,0:T(8,128)(2,1)}, bf16[128,512]{1,0:T(8,128)(2,1)}, u32[]{:S(2)}, u32[]{:S(2)}) collective-permute-start(bf16[128,512]{1,0:T(8,128)(2,1)} %get-tuple-element.26), channel_id=1, source_target_pairs={{0,32},{32,0},{64,96},{96,64},{128,160},{160,128},{192,224},{224,1... | collective-permute-start | bytes 393224 | tf_op jit(solution)/shard_map/ppermute | solution.py:37
  14.8 4.7 %collective-permute-start.1 = (bf16[128,512]{1,0:T(8,128)(2,1)}, bf16[128,512]{1,0:T(8,128)(2,1)}, u32[]{:S(2)}, u32[]{:S(2)}) collective-permute-start(bf16[128,512]{1,0:T(8,128)(2,1)} %get-tuple-element.27), channel_id=1, source_target_pairs={{32,64},{64,32},{96,128},{128,96},{160,192},{192,160},{33,65},{65,... | collective-permute-start | bytes 393224 | tf_op jit(solution)/shard_map/ppermute | solution.py:42
  17.1 8.6 %copy-start.2 = (bf16[8,16,4,128]{3,1,2,0:T(8,128)(2,1)}, bf16[8,16,4,128]{3,1,2,0:T(8,128)(2,1)S(1)}, u32[]{:S(2)}) copy-start(bf16[8,16,4,128]{3,1,2,0:T(8,128)(2,1)S(1)} %copy.43) | copy-start | bytes 393220
  20.4 5.4 %collective-permute-start.3 = (bf16[4,32,512]{2,1,0:T(8,128)(2,1)S(1)}, bf16[4,32,512]{2,1,0:T(8,128)(2,1)S(1)}, u32[]{:S(2)}, u32[]{:S(2)}) collective-permute-start(bf16[4,32,512]{2,1,0:T(8,128)(2,1)S(1)} %get-tuple-element.56), channel_id=1, source_target_pairs={{4,8},{8,4},{12,16},{16,12},{20,24},{24,20},{5,9},{9,5},{13,17},{1... | collective-permute-start | bytes 393224 | tf_op jit(solution)/shard_map/ppermute | solution.py:42
  21.0 10.1 %collective-permute-start.2 = (bf16[4,32,512]{2,1,0:T(8,128)(2,1)S(1)}, bf16[4,32,512]{2,1,0:T(8,128)(2,1)S(1)}, u32[]{:S(2)}, u32[]{:S(2)}) collective-permute-start(bf16[4,32,512]{2,1,0:T(8,128)(2,1)S(1)} %get-tuple-element.57), channel_id=1, source_target_pairs={{0,4},{4,0},{8,12},{12,8},{16,20},{20,16},{24,28},{28,24},{1,5},{5... | collective-permute-start | bytes 393224 | tf_op jit(solution)/shard_map/ppermute | solution.py:37
  31.2 1.0 copy-start.5
  32.1 0.8 copy-start.7
  36.7 13.6 %collective-permute-start.4 = (bf16[448,512]{1,0:T(8,128)(2,1)S(1)}, bf16[448,512]{1,0:T(8,128)(2,1)S(1)}, u32[]{:S(2)}, u32[]{:S(2)}) collective-permute-start(bf16[448,512]{1,0:T(8,128)(2,1)S(1)} %get-tuple-element.31), channel_id=1, source_target_pairs={{0,32},{32,0},{64,96},{96,64},{128,160},{160,128},{192,224},{224,1... | collective-permute-start | bytes 1376264 | tf_op jit(solution)/shard_map/ppermute | solution.py:37
  56.5 17.7 %collective-permute-start.5 = (bf16[2,4,224,128]{3,2,1,0:T(8,128)(2,1)S(1)}, bf16[2,4,224,128]{3,2,1,0:T(8,128)(2,1)}, u32[]{:S(2)}, u32[]{:S(2)}) collective-permute-start(bf16[2,4,224,128]{3,2,1,0:T(8,128)(2,1)S(1)} %get-tuple-element.35), channel_id=1, source_target_pairs={{0,8},{4,12},{8,0},{12,4},{16,24},{20,28},{24,16},{28,20},{1,9},{5... | collective-permute-start | bytes 1376264 | tf_op jit(solution)/shard_map/ppermute | solution.py:37
  58.6 15.6 %all-to-all-start.1 = ((bf16[8,80,128]{2,1,0:T(8,128)(2,1)}), bf16[8,80,128]{2,1,0:T(8,128)(2,1)S(1)}, u32[]{:S(2)}, u32[]{:S(2)}) async-start(bf16[8,80,128]{2,1,0:T(8,128)(2,1)} %broadcast_in_dim.4), calls=%async_computation.1 | async-start | bytes 327680 | tf_op jit(solution)/shard_map/all_to_all | solution.py:20
  65.8 12.1 %collective-permute-start.6 = (bf16[2,4,224,128]{3,2,1,0:T(8,128)(2,1)S(1)}, bf16[2,4,224,128]{3,2,1,0:T(8,128)(2,1)}, u32[]{:S(2)}, u32[]{:S(2)}) collective-permute-start(bf16[2,4,224,128]{3,2,1,0:T(8,128)(2,1)S(1)} %get-tuple-element.37), channel_id=1, source_target_pairs={{0,24},{4,28},{8,16},{12,20},{16,8},{20,12},{24,0},{28,4},{1,25},{... | collective-permute-start | bytes 1376264 | tf_op jit(solution)/shard_map/ppermute | solution.py:37
  75.3 10.4 %collective-permute-start.7 = (bf16[4,224,128]{2,1,0:T(8,128)(2,1)S(1)}, bf16[4,224,128]{2,1,0:T(8,128)(2,1)}, u32[]{:S(2)}, u32[]{:S(2)}) collective-permute-start(bf16[4,224,128]{2,1,0:T(8,128)(2,1)S(1)} %fusion.10), channel_id=1, source_target_pairs={{0,24},{4,28},{8,16},{12,20},{16,8},{20,12},{24,0},{28,4},{1,25},{... | collective-permute-start | bytes 688136 | tf_op jit(solution)/shard_map/ppermute | solution.py:37
  79.0 1.9 %copy-start.11 = (f32[2,4,224,128]{3,2,1,0:T(8,128)}, f32[2,4,224,128]{3,2,1,0:T(8,128)S(1)}, u32[]{:S(2)}) copy-start(f32[2,4,224,128]{3,2,1,0:T(8,128)S(1)} %convert_add_fusion.1) | copy-start | bytes 2752516
  79.0 12.0 %copy-start.12 = (bf16[8,16,4,128]{3,2,1,0:T(4,128)(2,1)S(1)}, bf16[8,16,4,128]{3,2,1,0:T(4,128)(2,1)}, u32[]{:S(2)}) copy-start(bf16[8,16,4,128]{3,2,1,0:T(4,128)(2,1)} %param.11) | copy-start | bytes 393220
  79.8 6.9 %collective-permute-start.8 = (bf16[4,224,128]{2,1,0:T(8,128)(2,1)}, bf16[4,224,128]{2,1,0:T(8,128)(2,1)}, u32[]{:S(2)}, u32[]{:S(2)}) collective-permute-start(bf16[4,224,128]{2,1,0:T(8,128)(2,1)} %fusion.11), channel_id=1, source_target_pairs={{0,8},{4,12},{8,0},{12,4},{16,24},{20,28},{24,16},{28,20},{1,9},{5... | collective-permute-start | bytes 688136 | tf_op jit(solution)/shard_map/ppermute | solution.py:37
  80.9 17.4 %all-to-all-start.2 = ((bf16[8,400,128]{2,1,0:T(8,128)(2,1)}), bf16[8,400,128]{2,1,0:T(8,128)(2,1)S(1)}, u32[]{:S(2)}, u32[]{:S(2)}) async-start(bf16[8,400,128]{2,1,0:T(8,128)(2,1)} %broadcast_in_dim.5), calls=%async_computation.2 | async-start | bytes 1638400 | tf_op jit(solution)/shard_map/all_to_all | solution.py:20
  88.0 10.2 %collective-permute-start.9 = (bf16[4,224,128]{2,1,0:T(8,128)(2,1)S(1)}, bf16[4,224,128]{2,1,0:T(8,128)(2,1)S(1)}, u32[]{:S(2)}, u32[]{:S(2)}) collective-permute-start(bf16[4,224,128]{2,1,0:T(8,128)(2,1)S(1)} %fusion.12), channel_id=1, source_target_pairs={{0,4},{4,0},{8,12},{12,8},{16,20},{20,16},{24,28},{28,24},{1,5},{5... | collective-permute-start | bytes 688136 | tf_op jit(solution)/shard_map/ppermute | solution.py:37
  98.3 1.5 %copy-start.1 = (bf16[128,27,128]{2,0,1:T(8,128)(2,1)S(1)}, bf16[128,27,128]{2,0,1:T(8,128)(2,1)}, u32[]{:S(2)}) copy-start(bf16[128,27,128]{2,0,1:T(8,128)(2,1)} %param.12) | copy-start | bytes 2654212
  98.3 1.5 %copy-start.3 = (bf16[8,16,4,128]{3,1,2,0:T(8,128)(2,1)S(1)}, bf16[8,16,4,128]{3,1,2,0:T(8,128)(2,1)}, u32[]{:S(2)}) copy-start(bf16[8,16,4,128]{3,1,2,0:T(8,128)(2,1)} %copy-done.2) | copy-start | bytes 393220
  98.3 1.5 %copy-start.6 = (bf16[128,512]{1,0:T(8,128)(2,1)S(1)}, bf16[128,512]{1,0:T(8,128)(2,1)}, u32[]{:S(2)}) copy-start(bf16[128,512]{1,0:T(8,128)(2,1)} %up_ref.1) | copy-start | bytes 393220
  98.3 1.0 copy-start.10
  102.1 11.9 %all-to-all-start.3 = ((bf16[8,64,128]{2,1,0:T(8,128)(2,1)}), bf16[8,64,128]{2,1,0:T(8,128)(2,1)S(1)}, u32[]{:S(2)}, u32[]{:S(2)}) async-start(bf16[8,64,128]{2,1,0:T(8,128)(2,1)} %bitcast.36), calls=%async_computation.3 | async-start | bytes 262144 | tf_op jit(solution)/shard_map/all_to_all | solution.py:20
  107.0 14.2 %collective-permute-start.10 = (bf16[2,224,128]{2,1,0:T(8,128)(2,1)S(1)}, bf16[2,224,128]{2,1,0:T(8,128)(2,1)}, u32[]{:S(2)}, u32[]{:S(2)}) collective-permute-start(bf16[2,224,128]{2,1,0:T(8,128)(2,1)S(1)} %fusion.13), channel_id=1, source_target_pairs={{0,64},{32,96},{64,0},{96,32},{128,192},{160,224},{192,128},{224,1... | collective-permute-start | bytes 344072 | tf_op jit(solution)/shard_map/ppermute | solution.py:37
  114.0 15.2 %collective-permute-start.12 = (bf16[2,992,128]{2,1,0:T(8,128)(2,1)S(1)}, bf16[2,992,128]{2,1,0:T(8,128)(2,1)S(1)}, u32[]{:S(2)}, u32[]{:S(2)}) collective-permute-start(bf16[2,992,128]{2,1,0:T(8,128)(2,1)S(1)} %dynamic-slice_bitcast_fusion), channel_id=1, source_target_pairs={{0,1},{1,0},{2,3},{3,2},{4,5},{5,4},{6,7},{7,6},{8,9},{9,8},{10,11... | collective-permute-start | bytes 1523720 | tf_op jit(solution)/shard_map/ppermute | solution.py:37
  124.1 7.4 %collective-permute-start.11 = (bf16[224,128]{1,0:T(8,128)(2,1)S(1)}, bf16[224,128]{1,0:T(8,128)(2,1)S(1)}, u32[]{:S(2)}, u32[]{:S(2)}) collective-permute-start(bf16[224,128]{1,0:T(8,128)(2,1)S(1)} %fusion.15), channel_id=1, source_target_pairs={{0,128},{32,160},{64,192},{96,224},{128,0},{160,32},{192,64},{224,... | collective-permute-start | bytes 172040 | tf_op jit(solution)/shard_map/ppermute | solution.py:37
  129.4 7.9 %collective-permute-start.13 = (bf16[992,128]{1,0:T(8,128)(2,1)S(1)}, bf16[992,128]{1,0:T(8,128)(2,1)S(1)}, u32[]{:S(2)}, u32[]{:S(2)}) collective-permute-start(bf16[992,128]{1,0:T(8,128)(2,1)S(1)} %fusion.9), channel_id=1, source_target_pairs={{0,2},{1,3},{2,0},{3,1},{4,6},{5,7},{6,4},{7,5},{8,10},{9,11},{10,... | collective-permute-start | bytes 761864 | tf_op jit(solution)/shard_map/ppermute | solution.py:37

commit v11 on v10

--- a/solution.py
+++ b/solution.py
@@ -218,11 +218,12 @@
 
 
 def kernel_grad_kernel(chunk, far_ref, input_ref, got_ref, *refs):
-    out_refs, (all_ref, flat_ref, pair_ref, turn_ref, wide_ref) = refs[:-5], refs[-5:]
+    out_refs, (flat_ref, pair_ref, turn_ref, wide_ref) = refs[:-4], refs[-4:]
     far_d, far_h, width, full = far_ref.shape
     depth, height = far_d - 2, far_h - 2
     rows, inner = input_ref.shape
-    by_height, by_depth, window, _ = all_ref.shape
+    by_height = lax.axis_size("gy")
+    _, by_depth, window, _ = out_refs[0].shape
     lanes = height * width
     side, at_y = lax.rem(lax.axis_index("gx"), 2), lax.axis_index("gy")
     sent = far_d // 2
@@ -259,12 +260,11 @@
                 first = pl.multiple_of(tap * full - begin + full, grain)
                 flat_ref[m, pl.ds(first, full)] = terms.astype(jnp.bfloat16)
 
-        for j in range(by_height):
-            start = full + j * chunk // grain * grain
-            all_ref[j, m] = flat_ref[m, start : start + window]
-    for (q, pairs), out_ref in zip(HALVES, out_refs):
-        for slot, k in enumerate(pairs):
-            out_ref[slot] = all_ref[2 * (at_y // 2 ^ k) + q]
+        for (q, pairs), out_ref in zip(HALVES, out_refs):
+            for slot, k in enumerate(pairs):
+                owner = 2 * (at_y // 2 ^ k) + q
+                start = pl.multiple_of(full + owner * chunk // grain * grain, grain)
+                out_ref[slot, m] = flat_ref[m, pl.ds(start, window)]
 
 
 def bottom_kernel(
@@ -300,7 +300,8 @@
     part_ref[...] = total.astype(jnp.bfloat16)
 
 
-def bottom_weight_kernel(down_ref, pre_ref, source_ref, shift_ref, both_ref):
+def bottom_weight_kernel(down_ref, pre_ref, source_ref, shift_ref, *refs):
+    out_refs, both_ref = refs[:-1], refs[-1]
     _, far_d, far_w, height, filters = shift_ref.shape
     depth, width = far_d - 2, far_w - 2
     rows, channels = source_ref.shape
@@ -330,6 +331,9 @@
                     both_ref[cc, (tap + c) * thin : (tap + c + 1) * thin] = terms[
                         cc * thin : (cc + 1) * thin, c * filters : (c + 1) * filters
                     ]
+    at_c = lax.axis_index("col")
+    for k, out_ref in enumerate(out_refs):
+        out_ref[...] = both_ref[at_c ^ k]
 
 
 def per_device(
@@ -459,7 +463,6 @@
         functools.partial(kernel_grad_kernel, chunk),
         [struct((2, nx // 2, span, inner), bf16)] * 4,
         [
-            pltpu.VMEM((ny, nx // 2, span, inner), bf16),
             pltpu.VMEM((nx // 2, (chunk * ny - 1) // full * full + 4 * full, inner), bf16),
             pltpu.VMEM((far_d + depth, far_h, width, full), bf16),
             pltpu.VMEM((far_d + depth, 3, full, lanes), bf16),
@@ -480,7 +483,6 @@
 
     by_depth = spread(jnp.concatenate([relayed, aux_part]), "gx")
     aux_sum = by_depth[:, nc * cells :].astype(f32).sum(axis=0).astype(bf16)
-    by_depth = behind(by_depth, even_sum, odd_sum)
     line = by_depth[:, : nc * cells].reshape(nx, nc, half_d * half_h, window, inner)[:, :, :, :wide]
     split = nx * nc * half_d * half_h * wide
     by_height = spread(jnp.concatenate([line.reshape(split, inner), aux_sum]), "gy")
@@ -494,8 +496,8 @@
 
     even_sum = first_sum(even_sum[0], even_sum[1].astype(bf16), 6)
     odd_sum = first_sum(odd_sum[0], odd_sum[1].astype(bf16), 2)
+    down_wide = behind(down_wide, even_sum, odd_sum)
     level_part = summed_by_pairs(jnp.stack([even_sum, odd_sum]), "gy", [1], [1])
-    down_wide = behind(down_wide, level_part)
 
     bottom_rows = bottom_d * block * bottom_h
     channel_width = bottom_weight.shape[0]
@@ -516,10 +518,10 @@
         pre_after,
         bottom_weight.transpose(1, 0, 2),
     )
-    (both,) = local_call(
+    both = local_call(
         bottom_weight_kernel,
-        [struct((nc, TAPS * thin + filters, inner), bf16)],
-        [],
+        [struct((TAPS * thin + filters, inner), bf16)] * nc,
+        [pltpu.VMEM((nc, TAPS * thin + filters, inner), bf16)],
         2 * bottom_rows * channel_width * TAPS * filters,
         2 * bottom_weight.size,
         down_wide,
@@ -541,7 +543,9 @@
         .reshape(share, block, bottom_h, channel_width)
         .transpose(0, 2, 1, 3)
     )
-    both = summed_by_pairs(behind(both, part), "col", bits_of("col"), bits_of("col")[::-1])
+    both = sum(
+        (both[k] if k == 0 else swap(both[k], "col", k)).astype(f32) for k in range(nc)
+    )
     bottom_weight_grad = both[: TAPS * thin].reshape(TAPS, thin, filters).transpose(1, 0, 2)
     up_weight_grad = both[TAPS * thin :]
     return (

time: 140 us -> 134 us (0.957)
  other arithmetic: 8.61 us -> 4.49 us
  starting transfers between devices: 52 us -> 48.5 us
    ppermute x12 -> x13, waiting for transfers between devices: 19.5 us -> 27.7 us  [swap(): lax.ppermute(x, axis, [(i, i ^ bit) for i in range(lax.axis_size(axis))])]
    all_to_all x3, waiting for transfers between devices: 12.1 us -> 4.29 us  [exchange(): return lax.all_to_all(x, axis, split_axis=0, concat_axis=0, tiled=False)]
    ppermute x12 -> x13, starting transfers between devices: 33.2 us -> 29.3 us  [swap(): lax.ppermute(x, axis, [(i, i ^ bit) for i in range(lax.axis_size(axis))])]
    another operation x2 -> x0, other arithmetic: 2.1 us -> none  [per_device(): level_part = summed_by_pairs(jnp.stack([even_sum, odd_sum]), 'gy', [1], [1])]
    add x2 -> x4, other arithmetic: 2.23 us -> 0.27 us  [first_sum(): return kept.astype(f32) + swap(sent, 'gy', bit).astype(f32)]
    unnamed x30 -> x26, local copies, waits for them, and re-layouts: 5.02 us -> 4.71 us
  transfers between devices with their start and end apart: 17 -> 18, of which waited for: 7 -> 8; matrix products, arithmetic and copies ran while one was open for 9% -> 8% of each run, Pallas kernels for 1% -> 2%
where the time goes in v11:
time: 134 us; the launch traced here: 132 us
  starting transfers between devices  48.5 us (36%)
  waiting for transfers between devices  31.9 us (24%)
  blocking collectives  19 us (14%)
  Pallas kernels  16 us (12%)
  local copies, waits for them, and re-layouts  11.2 us (8%)
  other arithmetic  4.49 us (3%)
    ppermute x13, starting transfers between devices, swap(): lax.ppermute(x, axis, [(i, i ^ bit) for i in range(lax.axis_size(axis))])  29.3 us
    ppermute x13, waiting for transfers between devices, swap(): lax.ppermute(x, axis, [(i, i ^ bit) for i in range(lax.axis_size(axis))])  27.7 us
    all_to_all x3, starting transfers between devices, exchange(): return lax.all_to_all(x, axis, split_axis=0, concat_axis=0, tiled=False)  17.3 us
    pallas_call x6, Pallas kernels, local_call(): pl.pallas_call(body, out_shape=list(out_shapes), in_specs=[pl.BlockSpec(m...  16 us
    all_gather x1, blocking collectives, per_device(): gathered = lax.all_gather(payload, 'col')  9.83 us
    all_to_all x1, blocking collectives, exchange(): return lax.all_to_all(x, axis, split_axis=0, concat_axis=0, tiled=False)  9.16 us
    unnamed x26, local copies, waits for them, and re-layouts  4.71 us
    all_to_all x3, waiting for transfers between devices, exchange(): return lax.all_to_all(x, axis, split_axis=0, concat_axis=0, tiled=False)  4.29 us
  transfers between devices with their start and end apart: 18, of which 8 were waited for; matrix products, arithmetic and copies ran while one was open for 8% of the time, Pallas kernels for 2%

profile of v11, /device:TPU:1, one launch (start us, length us, event | category | flops | bytes accessed | tf_op | source)
XLA Modules:
  0.0 132.1 jit_solution(10318326686509530579)
XLA Ops:
  0.7 1.7 %shard_map.145 = bf16[528,128]{1,0:T(8,128)(2,1)} custom-call(bf16[256,128]{1,0:T(8,128)(2,1)} %bitcast.106, bf16[256,128]{1,0:T(8,128)(2,1)} %bitcast.124, bf16[14,128]{1,0:T(8,128)(2,1)} %bitcast.128, bf16[128,13824]{1,0:T(8,128)(2,1)} %weight_ref.1, bf16[256,128]{1,0:T(8,128)(2,1)} %bitcast.103, bf16[128,512]{1,0:T(8,128)(2,1)} %up_ref.1, ...), custom_call_target="tpu_custom_call" | custom-call | bytes 65536 | tf_op jit(solution)/shard_map/pallas_call | solution.py:87
  2.4 9.8 %all-gather = bf16[2112,128]{1,0:T(8,128)(2,1)S(1)} all-gather(bf16[528,128]{1,0:T(8,128)(2,1)} %shard_map.145), channel_id=2, replica_groups=mesh['gx'=8,'gy'=8,'col'=4] {'col'}, dimensions={0}, use_global_device_ids=true | all-gather | bytes 675840 | tf_op jit(solution)/shard_map/all_gather | solution.py:380
  12.2 1.3 %shard_map.146 = (bf16[256,512]{1,0:T(8,128)(2,1)S(1)}, bf16[128,512]{1,0:T(8,128)(2,1)}, bf16[128,512]{1,0:T(8,128)(2,1)}, bf16[16,128]{1,0:T(8,128)(2,1)S(1)}) custom-call(bf16[4,528,128]{2,1,0:T(8,128)(2,1)S(1)} %bitcast.98, bf16[256,128]{1,0:T(8,128)(2,1)S(1)} %bitcast.107, s32[2,4,32]{2,1,0:T(4,128)S(1)} %copy-done.9), custom_call_target="tpu_custom_call" | custom-call | flops 12582912 | bytes 540672 | tf_op jit(solution)/shard_map/pallas_call | solution.py:87
  13.5 0.7 copy-done.4
  14.2 0.6 collective-permute-start
  14.8 1.3 collective-permute-start.1
  16.1 0.9 copy.39
  17.1 0.9 slice_bitcast_fusion.5
  17.9 1.5 %collective-permute-done.even_x_ref = bf16[128,512]{1,0:T(8,128)(2,1)} collective-permute-done((bf16[128,512]{1,0:T(8,128)(2,1)}, bf16[128,512]{1,0:T(8,128)(2,1)}, u32[]{:S(2)}, u32[]{:S(2)}) %collective-permute-start) | collective-permute-done | bytes 131104 | tf_op jit(solution)/shard_map/ppermute | solution.py:37
  19.5 0.8 select_bitcast_fusion.5
  20.4 0.7 collective-permute-start.3
  21.0 4.6 %collective-permute-start.2 = (bf16[4,32,512]{2,1,0:T(8,128)(2,1)S(1)}, bf16[4,32,512]{2,1,0:T(8,128)(2,1)S(1)}, u32[]{:S(2)}, u32[]{:S(2)}) collective-permute-start(bf16[4,32,512]{2,1,0:T(8,128)(2,1)S(1)} %get-tuple-element.61), channel_id=1, source_target_pairs={{0,4},{4,0},{8,12},{12,8},{16,20},{20,16},{24,28},{28,24},{1,5},{5... | collective-permute-start | bytes 393224 | tf_op jit(solution)/shard_map/ppermute | solution.py:37
  25.7 5.4 %collective-permute-done.2.even_y_ref = bf16[4,32,512]{2,1,0:T(8,128)(2,1)S(1)} collective-permute-done((bf16[4,32,512]{2,1,0:T(8,128)(2,1)S(1)}, bf16[4,32,512]{2,1,0:T(8,128)(2,1)S(1)}, u32[]{:S(2)}, u32[]{:S(2)}) %collective-permute-start.2) | collective-permute-done | bytes 131104 | tf_op jit(solution)/shard_map/ppermute | solution.py:37
  31.2 0.9 copy-done.5
  32.1 0.8 copy-done.7
  33.0 3.7 %shard_map.147 = (bf16[4,6,32,512]{3,2,1,0:T(8,128)(2,1)S(1)}, bf16[256,128]{1,0:T(8,128)(2,1)}, bf16[4,144,128]{2,1,0:T(8,128)(2,1)S(1)}, bf16[448,512]{1,0:T(8,128)(2,1)S(1)}) custom-call(bf16[256,512]{1,0:T(8,128)(2,1)S(1)} %copy-done.5, bf16[128,512]{1,0:T(8,128)(2,1)} %collective-permute-done.even_x_ref, ...), custom_call_target="tpu_custom_call" | custom-call | flops 905969664 | bytes 3538944 | tf_op jit(solution)/shard_map/pallas_call | solution.py:87
  36.6 4.4 %collective-permute-start.4 = (bf16[448,512]{1,0:T(8,128)(2,1)S(1)}, bf16[448,512]{1,0:T(8,128)(2,1)S(1)}, u32[]{:S(2)}, u32[]{:S(2)}) collective-permute-start(bf16[448,512]{1,0:T(8,128)(2,1)S(1)} %get-tuple-element.33), channel_id=1, source_target_pairs={{0,32},{32,0},{64,96},{96,64},{128,160},{160,128},{192,224},{224,1... | collective-permute-start | bytes 1376264 | tf_op jit(solution)/shard_map/ppermute | solution.py:37
  41.1 9.2 %all_to_all.20 = bf16[4,144,128]{2,1,0:T(8,128)(2,1)S(1)} all-to-all(bf16[4,144,128]{2,1,0:T(8,128)(2,1)S(1)} %get-tuple-element.31), channel_id=1, replica_groups=mesh['gx'=8,'gy'=8,'col'=4] {'col'}, dimensions={0} | all-to-all | bytes 294912 | tf_op jit(solution)/shard_map/all_to_all | solution.py:20
  50.2 6.1 %shard_map.148 = (bf16[2,4,224,128]{3,2,1,0:T(8,128)(2,1)S(1)}, bf16[2,4,224,128]{3,2,1,0:T(8,128)(2,1)S(1)}, bf16[2,4,224,128]{3,2,1,0:T(8,128)(2,1)S(1)}, bf16[2,4,224,128]{3,2,1,0:T(8,128)(2,1)S(1)}) custom-call(bf16[4,6,32,512]{3,2,1,0:T(8,128)(2,1)S(1)} %get-tuple-element.32.far_ref, bf16[256,128]{1,0:T(8,128)(2,1)S(1)} %bitcast.105, ...), custom_call_target="tpu_custom_call" | custom-call | flops 905969664 | bytes 3670016 | tf_op jit(solution)/shard_map/pallas_call | solution.py:87
  56.3 0.7 broadcast_in_dim.4
  57.0 6.7 %all-to-all-start.1 = ((bf16[8,80,128]{2,1,0:T(8,128)(2,1)}), bf16[8,80,128]{2,1,0:T(8,128)(2,1)S(1)}, u32[]{:S(2)}, u32[]{:S(2)}) async-start(bf16[8,80,128]{2,1,0:T(8,128)(2,1)} %broadcast_in_dim.4), calls=%async_computation.1 | async-start | bytes 327680 | tf_op jit(solution)/shard_map/all_to_all | solution.py:20
  63.7 1.8 %collective-permute-start.5 = (bf16[2,4,224,128]{3,2,1,0:T(8,128)(2,1)S(1)}, bf16[2,4,224,128]{3,2,1,0:T(8,128)(2,1)S(1)}, u32[]{:S(2)}, u32[]{:S(2)}) collective-permute-start(bf16[2,4,224,128]{3,2,1,0:T(8,128)(2,1)S(1)} %get-tuple-element.37), channel_id=1, source_target_pairs={{0,8},{4,12},{8,0},{12,4},{16,24},{20,28},{24,16},{28,20},{1,9},{5... | collective-permute-start | bytes 1376264 | tf_op jit(solution)/shard_map/ppermute | solution.py:37
  65.5 2.3 %collective-permute-start.7 = (bf16[2,4,224,128]{3,2,1,0:T(8,128)(2,1)S(1)}, bf16[2,4,224,128]{3,2,1,0:T(8,128)(2,1)S(1)}, u32[]{:S(2)}, u32[]{:S(2)}) collective-permute-start(bf16[2,4,224,128]{3,2,1,0:T(8,128)(2,1)S(1)} %get-tuple-element.39), channel_id=1, source_target_pairs={{0,24},{4,28},{8,16},{12,20},{16,8},{20,12},{24,0},{28,4},{1,25},{... | collective-permute-start | bytes 1376264 | tf_op jit(solution)/shard_map/ppermute | solution.py:37
  67.8 4.3 %all-to-all-done.1 = bf16[8,80,128]{2,1,0:T(8,128)(2,1)S(1)} async-done(((bf16[8,80,128]{2,1,0:T(8,128)(2,1)}), bf16[8,80,128]{2,1,0:T(8,128)(2,1)S(1)}, u32[]{:S(2)}, u32[]{:S(2)}) %all-to-all-start.1) | async-done | bytes 163872 | tf_op jit(solution)/shard_map/all_to_all | solution.py:20
  72.2 1.0 broadcast_in_dim.5
  73.2 5.8 %all-to-all-start.2 = ((bf16[8,400,128]{2,1,0:T(8,128)(2,1)}), bf16[8,400,128]{2,1,0:T(8,128)(2,1)}, u32[]{:S(2)}, u32[]{:S(2)}) async-start(bf16[8,400,128]{2,1,0:T(8,128)(2,1)} %broadcast_in_dim.5), calls=%async_computation.2 | async-start | bytes 1638400 | tf_op jit(solution)/shard_map/all_to_all | solution.py:20
  79.2 2.9 %collective-permute-start.6 = (bf16[4,224,128]{2,1,0:T(8,128)(2,1)S(1)}, bf16[4,224,128]{2,1,0:T(8,128)(2,1)S(1)}, u32[]{:S(2)}, u32[]{:S(2)}) collective-permute-start(bf16[4,224,128]{2,1,0:T(8,128)(2,1)S(1)} %fusion.7), channel_id=1, source_target_pairs={{0,24},{4,28},{8,16},{12,20},{16,8},{20,12},{24,0},{28,4},{1,25},{... | collective-permute-start | bytes 688136 | tf_op jit(solution)/shard_map/ppermute | solution.py:37
  82.4 8.3 %collective-permute-done.6 = bf16[4,224,128]{2,1,0:T(8,128)(2,1)S(1)} collective-permute-done((bf16[4,224,128]{2,1,0:T(8,128)(2,1)S(1)}, bf16[4,224,128]{2,1,0:T(8,128)(2,1)S(1)}, u32[]{:S(2)}, u32[]{:S(2)}) %collective-permute-start.6) | collective-permute-done | bytes 229408 | tf_op jit(solution)/shard_map/ppermute | solution.py:37
  90.8 3.2 %collective-permute-done.8 = bf16[4,224,128]{2,1,0:T(8,128)(2,1)S(1)} collective-permute-done((bf16[4,224,128]{2,1,0:T(8,128)(2,1)S(1)}, bf16[4,224,128]{2,1,0:T(8,128)(2,1)S(1)}, u32[]{:S(2)}, u32[]{:S(2)}) %collective-permute-start.8) | collective-permute-done | bytes 229408 | tf_op jit(solution)/shard_map/ppermute | solution.py:37
  94.1 3.9 %collective-permute-start.9 = (bf16[4,224,128]{2,1,0:T(8,128)(2,1)S(1)}, bf16[4,224,128]{2,1,0:T(8,128)(2,1)S(1)}, u32[]{:S(2)}, u32[]{:S(2)}) collective-permute-start(bf16[4,224,128]{2,1,0:T(8,128)(2,1)S(1)} %fusion.9), channel_id=1, source_target_pairs={{0,4},{4,0},{8,12},{12,8},{16,20},{20,16},{24,28},{28,24},{1,5},{5... | collective-permute-start | bytes 688136 | tf_op jit(solution)/shard_map/ppermute | solution.py:37
  98.1 3.3 %collective-permute-done.9 = bf16[4,224,128]{2,1,0:T(8,128)(2,1)S(1)} collective-permute-done((bf16[4,224,128]{2,1,0:T(8,128)(2,1)S(1)}, bf16[4,224,128]{2,1,0:T(8,128)(2,1)S(1)}, u32[]{:S(2)}, u32[]{:S(2)}) %collective-permute-start.9) | collective-permute-done | bytes 229408 | tf_op jit(solution)/shard_map/ppermute | solution.py:37
  101.5 0.7 fusion.10
  102.2 1.2 slice.134
  103.4 0.5 copy.33
  104.5 2.3 %shard_map.149 = (bf16[512,128]{1,0:T(8,128)(2,1)}, bf16[3,10,6,16,128]{4,3,2,1,0:T(8,128)(2,1)S(1)}) custom-call(bf16[768,512]{1,0:T(8,128)(2,1)S(1)} %bitcast.94, bf16[128,512]{1,0:T(8,128)(2,1)S(1)} %copy-done.6, bf16[8,1,16,128]{3,2,1,0:T(8,128)(2,1)S(1)} %get-tuple-element.71.before_ref, bf16[8,4,16,128]{3,2,1,0:T(8,128)(2,1)S(1)} %bitcast.100, ...), custom_call_target="tpu_custom_call" | custom-call | flops 452984832 | bytes 884736 | tf_op jit(solution)/shard_map/pallas_call | solution.py:87
  106.8 4.8 %all-to-all-start.3 = ((bf16[8,64,128]{2,1,0:T(8,128)(2,1)}), bf16[8,64,128]{2,1,0:T(8,128)(2,1)S(1)}, u32[]{:S(2)}, u32[]{:S(2)}) async-start(bf16[8,64,128]{2,1,0:T(8,128)(2,1)} %bitcast.32), calls=%async_computation.3 | async-start | bytes 262144 | tf_op jit(solution)/shard_map/all_to_all | solution.py:20
  111.6 0.9 shard_map.150
  112.5 4.1 %collective-permute-start.12 = (bf16[992,128]{1,0:T(8,128)(2,1)S(1)}, bf16[992,128]{1,0:T(8,128)(2,1)S(1)}, u32[]{:S(2)}, u32[]{:S(2)}) collective-permute-start(bf16[992,128]{1,0:T(8,128)(2,1)S(1)} %get-tuple-element.45), channel_id=1, source_target_pairs={{0,1},{1,0},{2,3},{3,2},{4,5},{5,4},{6,7},{7,6},{8,9},{9,8},{10,11... | collective-permute-start | bytes 761864 | tf_op jit(solution)/shard_map/ppermute | solution.py:37
  116.7 1.7 %collective-permute-start.13 = (bf16[992,128]{1,0:T(8,128)(2,1)S(1)}, bf16[992,128]{1,0:T(8,128)(2,1)S(1)}, u32[]{:S(2)}, u32[]{:S(2)}) collective-permute-start(bf16[992,128]{1,0:T(8,128)(2,1)S(1)} %get-tuple-element.46), channel_id=1, source_target_pairs={{0,2},{1,3},{2,0},{3,1},{4,6},{5,7},{6,4},{7,5},{8,10},{9,11},{10,... | collective-permute-start | bytes 761864 | tf_op jit(solution)/shard_map/ppermute | solution.py:37
  118.5 0.9 bitcast_add_fusion
  119.4 2.6 %collective-permute-start.11 = (bf16[224,128]{1,0:T(8,128)(2,1)S(1)}, bf16[224,128]{1,0:T(8,128)(2,1)S(1)}, u32[]{:S(2)}, u32[]{:S(2)}) collective-permute-start(bf16[224,128]{1,0:T(8,128)(2,1)S(1)} %fusion.12), channel_id=1, source_target_pairs={{0,128},{32,160},{64,192},{96,224},{128,0},{160,32},{192,64},{224,... | collective-permute-start | bytes 172040 | tf_op jit(solution)/shard_map/ppermute | solution.py:37
  122.0 1.4 %convert_reduce_fusion = f32[14,128]{1,0:T(8,128)} fusion(bf16[8,400,128]{2,1,0:T(8,128)(2,1)} %all-to-all-done.2), kind=kLoop, calls=%fused_computation.36 | loop fusion | flops 26880 | bytes 35840 | tf_op jit(solution)/shard_map/reduce_sum | solution.py:489
  123.4 0.6 copy.32
  124.1 2.4 %collective-permute-done.11 = bf16[224,128]{1,0:T(8,128)(2,1)S(1)} collective-permute-done((bf16[224,128]{1,0:T(8,128)(2,1)S(1)}, bf16[224,128]{1,0:T(8,128)(2,1)S(1)}, u32[]{:S(2)}, u32[]{:S(2)}) %collective-permute-start.11) | collective-permute-done | bytes 57376 | tf_op jit(solution)/shard_map/ppermute | solution.py:37
  126.5 0.7 fusion.11
  127.1 3.4 %collective-permute-done.14 = bf16[992,128]{1,0:T(8,128)(2,1)S(1)} collective-permute-done((bf16[992,128]{1,0:T(8,128)(2,1)S(1)}, bf16[992,128]{1,0:T(8,128)(2,1)S(1)}, u32[]{:S(2)}, u32[]{:S(2)}) %collective-permute-start.14) | collective-permute-done | bytes 253984 | tf_op jit(solution)/shard_map/ppermute | solution.py:37
  130.7 0.6 slice.143
  131.3 0.8 slice.142
  (58 shorter events, 1.6 us)
Async XLA Ops:
  0.6 11.6 %copy-start.8 = (bf16[2,4,32,128]{3,2,1,0:T(8,128)(2,1)S(1)}, bf16[2,4,32,128]{3,2,1,0:T(8,128)(2,1)}, u32[]{:S(2)}) copy-start(bf16[2,4,32,128]{3,2,1,0:T(8,128)(2,1)} %param.15) | copy-start | bytes 196612
  0.6 11.5 %copy-start.9 = (s32[2,4,32]{2,1,0:T(4,128)S(1)}, s32[2,4,32]{2,1,0:T(4,128)}, u32[]{:S(2)}) copy-start(s32[2,4,32]{2,1,0:T(4,128)} %label_ref.1) | copy-start | bytes 3076
  0.7 30.5 %copy-start = (bf16[128,13824]{1,0:T(8,128)(2,1)S(1)}, bf16[128,13824]{1,0:T(8,128)(2,1)}, u32[]{:S(2)}) copy-start(bf16[128,13824]{1,0:T(8,128)(2,1)} %weight_ref.1) | copy-start | bytes 10616836
  13.5 0.7 copy-start.4
  14.2 5.3 %collective-permute-start = (bf16[128,512]{1,0:T(8,128)(2,1)}, bf16[128,512]{1,0:T(8,128)(2,1)}, u32[]{:S(2)}, u32[]{:S(2)}) collective-permute-start(bf16[128,512]{1,0:T(8,128)(2,1)} %get-tuple-element.28), channel_id=1, source_target_pairs={{0,32},{32,0},{64,96},{96,64},{128,160},{160,128},{192,224},{224,1... | collective-permute-start | bytes 393224 | tf_op jit(solution)/shard_map/ppermute | solution.py:37
  14.8 4.7 %collective-permute-start.1 = (bf16[128,512]{1,0:T(8,128)(2,1)}, bf16[128,512]{1,0:T(8,128)(2,1)}, u32[]{:S(2)}, u32[]{:S(2)}) collective-permute-start(bf16[128,512]{1,0:T(8,128)(2,1)} %get-tuple-element.29), channel_id=1, source_target_pairs={{32,64},{64,32},{96,128},{128,96},{160,192},{192,160},{33,65},{65,... | collective-permute-start | bytes 393224 | tf_op jit(solution)/shard_map/ppermute | solution.py:42
  17.1 8.6 %copy-start.2 = (bf16[8,16,4,128]{3,1,2,0:T(8,128)(2,1)}, bf16[8,16,4,128]{3,1,2,0:T(8,128)(2,1)S(1)}, u32[]{:S(2)}) copy-start(bf16[8,16,4,128]{3,1,2,0:T(8,128)(2,1)S(1)} %copy.39) | copy-start | bytes 393220
  20.4 5.4 %collective-permute-start.3 = (bf16[4,32,512]{2,1,0:T(8,128)(2,1)S(1)}, bf16[4,32,512]{2,1,0:T(8,128)(2,1)S(1)}, u32[]{:S(2)}, u32[]{:S(2)}) collective-permute-start(bf16[4,32,512]{2,1,0:T(8,128)(2,1)S(1)} %get-tuple-element.60), channel_id=1, source_target_pairs={{4,8},{8,4},{12,16},{16,12},{20,24},{24,20},{5,9},{9,5},{13,17},{1... | collective-permute-start | bytes 393224 | tf_op jit(solution)/shard_map/ppermute | solution.py:42
  21.0 10.1 %collective-permute-start.2 = (bf16[4,32,512]{2,1,0:T(8,128)(2,1)S(1)}, bf16[4,32,512]{2,1,0:T(8,128)(2,1)S(1)}, u32[]{:S(2)}, u32[]{:S(2)}) collective-permute-start(bf16[4,32,512]{2,1,0:T(8,128)(2,1)S(1)} %get-tuple-element.61), channel_id=1, source_target_pairs={{0,4},{4,0},{8,12},{12,8},{16,20},{20,16},{24,28},{28,24},{1,5},{5... | collective-permute-start | bytes 393224 | tf_op jit(solution)/shard_map/ppermute | solution.py:37
  31.2 1.0 copy-start.5
  32.1 0.8 copy-start.7
  36.6 13.6 %collective-permute-start.4 = (bf16[448,512]{1,0:T(8,128)(2,1)S(1)}, bf16[448,512]{1,0:T(8,128)(2,1)S(1)}, u32[]{:S(2)}, u32[]{:S(2)}) collective-permute-start(bf16[448,512]{1,0:T(8,128)(2,1)S(1)} %get-tuple-element.33), channel_id=1, source_target_pairs={{0,32},{32,0},{64,96},{96,64},{128,160},{160,128},{192,224},{224,1... | collective-permute-start | bytes 1376264 | tf_op jit(solution)/shard_map/ppermute | solution.py:37
  57.0 15.1 %all-to-all-start.1 = ((bf16[8,80,128]{2,1,0:T(8,128)(2,1)}), bf16[8,80,128]{2,1,0:T(8,128)(2,1)S(1)}, u32[]{:S(2)}, u32[]{:S(2)}) async-start(bf16[8,80,128]{2,1,0:T(8,128)(2,1)} %broadcast_in_dim.4), calls=%async_computation.1 | async-start | bytes 327680 | tf_op jit(solution)/shard_map/all_to_all | solution.py:20
  63.7 15.3 %collective-permute-start.5 = (bf16[2,4,224,128]{3,2,1,0:T(8,128)(2,1)S(1)}, bf16[2,4,224,128]{3,2,1,0:T(8,128)(2,1)S(1)}, u32[]{:S(2)}, u32[]{:S(2)}) collective-permute-start(bf16[2,4,224,128]{3,2,1,0:T(8,128)(2,1)S(1)} %get-tuple-element.37), channel_id=1, source_target_pairs={{0,8},{4,12},{8,0},{12,4},{16,24},{20,28},{24,16},{28,20},{1,9},{5... | collective-permute-start | bytes 1376264 | tf_op jit(solution)/shard_map/ppermute | solution.py:37
  65.5 16.6 %collective-permute-start.7 = (bf16[2,4,224,128]{3,2,1,0:T(8,128)(2,1)S(1)}, bf16[2,4,224,128]{3,2,1,0:T(8,128)(2,1)S(1)}, u32[]{:S(2)}, u32[]{:S(2)}) collective-permute-start(bf16[2,4,224,128]{3,2,1,0:T(8,128)(2,1)S(1)} %get-tuple-element.39), channel_id=1, source_target_pairs={{0,24},{4,28},{8,16},{12,20},{16,8},{20,12},{24,0},{28,4},{1,25},{... | collective-permute-start | bytes 1376264 | tf_op jit(solution)/shard_map/ppermute | solution.py:37
  73.2 29.0 %all-to-all-start.2 = ((bf16[8,400,128]{2,1,0:T(8,128)(2,1)}), bf16[8,400,128]{2,1,0:T(8,128)(2,1)}, u32[]{:S(2)}, u32[]{:S(2)}) async-start(bf16[8,400,128]{2,1,0:T(8,128)(2,1)} %broadcast_in_dim.5), calls=%async_computation.2 | async-start | bytes 1638400 | tf_op jit(solution)/shard_map/all_to_all | solution.py:20
  79.1 18.8 %copy-start.10 = (bf16[8,16,4,128]{3,2,1,0:T(4,128)(2,1)S(1)}, bf16[8,16,4,128]{3,2,1,0:T(4,128)(2,1)}, u32[]{:S(2)}) copy-start(bf16[8,16,4,128]{3,2,1,0:T(4,128)(2,1)} %param.11) | copy-start | bytes 393220
  79.2 11.5 %collective-permute-start.6 = (bf16[4,224,128]{2,1,0:T(8,128)(2,1)S(1)}, bf16[4,224,128]{2,1,0:T(8,128)(2,1)S(1)}, u32[]{:S(2)}, u32[]{:S(2)}) collective-permute-start(bf16[4,224,128]{2,1,0:T(8,128)(2,1)S(1)} %fusion.7), channel_id=1, source_target_pairs={{0,24},{4,28},{8,16},{12,20},{16,8},{20,12},{24,0},{28,4},{1,25},{... | collective-permute-start | bytes 688136 | tf_op jit(solution)/shard_map/ppermute | solution.py:37
  82.3 11.7 %collective-permute-start.8 = (bf16[4,224,128]{2,1,0:T(8,128)(2,1)S(1)}, bf16[4,224,128]{2,1,0:T(8,128)(2,1)S(1)}, u32[]{:S(2)}, u32[]{:S(2)}) collective-permute-start(bf16[4,224,128]{2,1,0:T(8,128)(2,1)S(1)} %fusion.8), channel_id=1, source_target_pairs={{0,8},{4,12},{8,0},{12,4},{16,24},{20,28},{24,16},{28,20},{1,9},{5... | collective-permute-start | bytes 688136 | tf_op jit(solution)/shard_map/ppermute | solution.py:37
  94.1 7.3 %collective-permute-start.9 = (bf16[4,224,128]{2,1,0:T(8,128)(2,1)S(1)}, bf16[4,224,128]{2,1,0:T(8,128)(2,1)S(1)}, u32[]{:S(2)}, u32[]{:S(2)}) collective-permute-start(bf16[4,224,128]{2,1,0:T(8,128)(2,1)S(1)} %fusion.9), channel_id=1, source_target_pairs={{0,4},{4,0},{8,12},{12,8},{16,20},{20,16},{24,28},{28,24},{1,5},{5... | collective-permute-start | bytes 688136 | tf_op jit(solution)/shard_map/ppermute | solution.py:37
  101.5 3.0 %copy-start.1 = (bf16[128,27,128]{2,0,1:T(8,128)(2,1)S(1)}, bf16[128,27,128]{2,0,1:T(8,128)(2,1)}, u32[]{:S(2)}) copy-start(bf16[128,27,128]{2,0,1:T(8,128)(2,1)} %param.12) | copy-start | bytes 2654212
  101.5 3.0 %copy-start.3 = (bf16[8,16,4,128]{3,1,2,0:T(8,128)(2,1)S(1)}, bf16[8,16,4,128]{3,1,2,0:T(8,128)(2,1)}, u32[]{:S(2)}) copy-start(bf16[8,16,4,128]{3,1,2,0:T(8,128)(2,1)} %copy-done.2) | copy-start | bytes 393220
  101.5 3.0 %copy-start.6 = (bf16[128,512]{1,0:T(8,128)(2,1)S(1)}, bf16[128,512]{1,0:T(8,128)(2,1)}, u32[]{:S(2)}) copy-start(bf16[128,512]{1,0:T(8,128)(2,1)} %up_ref.1) | copy-start | bytes 393220
  102.2 16.3 %collective-permute-start.10 = (bf16[2,224,128]{2,1,0:T(8,128)(2,1)}, bf16[2,224,128]{2,1,0:T(8,128)(2,1)}, u32[]{:S(2)}, u32[]{:S(2)}) collective-permute-start(bf16[2,224,128]{2,1,0:T(8,128)(2,1)} %fusion.10), channel_id=1, source_target_pairs={{0,64},{32,96},{64,0},{96,32},{128,192},{160,224},{192,128},{224,1... | collective-permute-start | bytes 344072 | tf_op jit(solution)/shard_map/ppermute | solution.py:37
  106.8 12.6 %all-to-all-start.3 = ((bf16[8,64,128]{2,1,0:T(8,128)(2,1)}), bf16[8,64,128]{2,1,0:T(8,128)(2,1)S(1)}, u32[]{:S(2)}, u32[]{:S(2)}) async-start(bf16[8,64,128]{2,1,0:T(8,128)(2,1)} %bitcast.32), calls=%async_computation.3 | async-start | bytes 262144 | tf_op jit(solution)/shard_map/all_to_all | solution.py:20
  112.5 14.6 %collective-permute-start.12 = (bf16[992,128]{1,0:T(8,128)(2,1)S(1)}, bf16[992,128]{1,0:T(8,128)(2,1)S(1)}, u32[]{:S(2)}, u32[]{:S(2)}) collective-permute-start(bf16[992,128]{1,0:T(8,128)(2,1)S(1)} %get-tuple-element.45), channel_id=1, source_target_pairs={{0,1},{1,0},{2,3},{3,2},{4,5},{5,4},{6,7},{7,6},{8,9},{9,8},{10,11... | collective-permute-start | bytes 761864 | tf_op jit(solution)/shard_map/ppermute | solution.py:37
  116.7 10.5 %collective-permute-start.13 = (bf16[992,128]{1,0:T(8,128)(2,1)S(1)}, bf16[992,128]{1,0:T(8,128)(2,1)S(1)}, u32[]{:S(2)}, u32[]{:S(2)}) collective-permute-start(bf16[992,128]{1,0:T(8,128)(2,1)S(1)} %get-tuple-element.46), channel_id=1, source_target_pairs={{0,2},{1,3},{2,0},{3,1},{4,6},{5,7},{6,4},{7,5},{8,10},{9,11},{10,... | collective-permute-start | bytes 761864 | tf_op jit(solution)/shard_map/ppermute | solution.py:37
  118.4 12.2 %collective-permute-start.14 = (bf16[992,128]{1,0:T(8,128)(2,1)S(1)}, bf16[992,128]{1,0:T(8,128)(2,1)S(1)}, u32[]{:S(2)}, u32[]{:S(2)}) collective-permute-start(bf16[992,128]{1,0:T(8,128)(2,1)S(1)} %get-tuple-element.47), channel_id=1, source_target_pairs={{0,3},{1,2},{2,1},{3,0},{4,7},{5,6},{6,5},{7,4},{8,11},{9,10},{10,... | collective-permute-start | bytes 761864 | tf_op jit(solution)/shard_map/ppermute | solution.py:37
  119.4 7.0 %collective-permute-start.11 = (bf16[224,128]{1,0:T(8,128)(2,1)S(1)}, bf16[224,128]{1,0:T(8,128)(2,1)S(1)}, u32[]{:S(2)}, u32[]{:S(2)}) collective-permute-start(bf16[224,128]{1,0:T(8,128)(2,1)S(1)} %fusion.12), channel_id=1, source_target_pairs={{0,128},{32,160},{64,192},{96,224},{128,0},{160,32},{192,64},{224,... | collective-permute-start | bytes 172040 | tf_op jit(solution)/shard_map/ppermute | solution.py:37

commit v12 on v11

--- a/solution.py
+++ b/solution.py
@@ -268,12 +268,12 @@
 
 
 def bottom_kernel(
-    down_ref, up_ref, before_ref, pre_ref, after_ref, weight_ref, part_ref, shift_ref
+    down_ref, up_ref, before_ref, pre_ref, after_ref, weight_ref, aux_ref, part_ref, shift_ref
 ):
     _, far_d, far_w, height, filters = shift_ref.shape
     depth, width = far_d - 2, far_w - 2
     rows = depth * width * height
-    channels = part_ref.shape[1]
+    channels = part_ref.shape[2]
     back = dot_nt(down_ref[...], up_ref[...])
     saved = jnp.concatenate([before_ref[...], pre_ref[...], after_ref[...]], axis=1)
     saved = saved.reshape(depth * far_w * height, filters)
@@ -297,7 +297,10 @@
             )
             weight = jnp.concatenate([weight_ref[tap + c] for c in range(3)], axis=1)
             total += dot_nt(piece, weight)
-    part_ref[...] = total.astype(jnp.bfloat16)
+    share = rows // part_ref.shape[0]
+    for j in range(part_ref.shape[0]):
+        part_ref[j, :share] = total[j * share : (j + 1) * share].astype(jnp.bfloat16)
+        part_ref[j, share:] = aux_ref[...]
 
 
 def bottom_weight_kernel(down_ref, pre_ref, source_ref, shift_ref, *refs):
@@ -485,10 +488,8 @@
     aux_sum = by_depth[:, nc * cells :].astype(f32).sum(axis=0).astype(bf16)
     line = by_depth[:, : nc * cells].reshape(nx, nc, half_d * half_h, window, inner)[:, :, :, :wide]
     split = nx * nc * half_d * half_h * wide
-    by_height = spread(jnp.concatenate([line.reshape(split, inner), aux_sum]), "gy")
-    aux_weight_grad = by_height[:, split : split + CLASSES].astype(f32).sum(axis=0).T
     down_wide = (
-        by_height[:, :split]
+        spread(line.reshape(split, inner), "gy")
         .reshape(ny, nx, nc, half_d, half_h, wide, inner)
         .transpose(1, 3, 5, 0, 4, 2, 6)
         .reshape(bottom_d * wide * bottom_h, full)
@@ -497,7 +498,8 @@
     even_sum = first_sum(even_sum[0], even_sum[1].astype(bf16), 6)
     odd_sum = first_sum(odd_sum[0], odd_sum[1].astype(bf16), 2)
     down_wide = behind(down_wide, even_sum, odd_sum)
-    level_part = summed_by_pairs(jnp.stack([even_sum, odd_sum]), "gy", [1], [1])
+    kept_sum, sent_sum = mine_and_other(jnp.stack([even_sum, odd_sum]), "gy", 1, 0)
+    got_sum = swap(sent_sum.astype(bf16), "gy", 1)
 
     bottom_rows = bottom_d * block * bottom_h
     channel_width = bottom_weight.shape[0]
@@ -505,7 +507,7 @@
     part, shifts = local_call(
         bottom_kernel,
         (
-            struct((bottom_rows, channel_width), bf16),
+            struct((ny, bottom_rows // ny + CLASS_ROWS, channel_width), bf16),
             struct((3, bottom_d + 2, wide, bottom_h, filters), bf16),
         ),
         [],
@@ -517,6 +519,7 @@
         turned_pre,
         pre_after,
         bottom_weight.transpose(1, 0, 2),
+        aux_sum,
     )
     both = local_call(
         bottom_weight_kernel,
@@ -529,7 +532,10 @@
         bottom_input.transpose(0, 2, 1, 3).reshape(bottom_rows, channel_width),
         shifts,
     )
-    part = exchange(part.reshape(ny, bottom_rows // ny, channel_width), "gy")
+    level_part = kept_sum + behind(got_sum, part).astype(f32)
+    part = exchange(part, "gy")
+    share = bottom_rows // ny
+    aux_weight_grad = part[:, share : share + CLASSES].astype(f32).sum(axis=0).T
     level_part = summed_by_pairs(level_part, "gx", bits_of("gx")[:-1], bits_of("gx")[-2::-1], part)
     if span != chunk:
         odd = lax.rem(at_y + at_x * ny, 2)
@@ -537,17 +543,17 @@
     level_weight_grad = level_part.T
     share = bottom_d // ny
     bottom_input_grad = (
-        part.astype(f32)
+        part[:, : bottom_rows // ny]
+        .astype(f32)
         .sum(axis=0)
         .astype(bf16)
         .reshape(share, block, bottom_h, channel_width)
         .transpose(0, 2, 1, 3)
     )
-    both = sum(
-        (both[k] if k == 0 else swap(both[k], "col", k)).astype(f32) for k in range(nc)
-    )
-    bottom_weight_grad = both[: TAPS * thin].reshape(TAPS, thin, filters).transpose(1, 0, 2)
-    up_weight_grad = both[TAPS * thin :]
+    both = [both[k] if k == 0 else swap(both[k], "col", k) for k in range(nc)]
+    bottom_weight_grad = sum(x[: TAPS * thin].astype(f32) for x in both)
+    bottom_weight_grad = bottom_weight_grad.reshape(TAPS, thin, filters).transpose(1, 0, 2)
+    up_weight_grad = sum(x[TAPS * thin :].astype(f32) for x in both)
     return (
         level_input_grad,
         bottom_input_grad,

time: 134 us -> 135 us (level)
  blocking collectives: 19 us -> 9.83 us
  starting transfers between devices: 48.5 us -> 56.7 us
  other arithmetic: 4.49 us -> 6.81 us
  waiting for transfers between devices: 31.9 us -> 29.8 us
    all_to_all x1 -> x0, blocking collectives: 9.16 us -> none  [exchange(): return lax.all_to_all(x, axis, split_axis=0, concat_axis=0, tiled=False)]
    ppermute x13, waiting for transfers between devices: 27.7 us -> 21.6 us  [swap(): lax.ppermute(x, axis, [(i, i ^ bit) for i in range(lax.axis_size(axis))])]
    all_to_all x3 -> x4, starting transfers between devices: 17.3 us -> 23.2 us  [exchange(): return lax.all_to_all(x, axis, split_axis=0, concat_axis=0, tiled=False)]
    all_to_all x3 -> x4, waiting for transfers between devices: 4.29 us -> 8.17 us  [exchange(): return lax.all_to_all(x, axis, split_axis=0, concat_axis=0, tiled=False)]
    unnamed x26 -> x37, local copies, waits for them, and re-layouts: 4.71 us -> 7.73 us
    slice x3 -> x0, local copies, waits for them, and re-layouts: 2.61 us -> none  [the longest x1 1.19 us: per_device(): by_height[:, :split].reshape(ny, nx, nc, half_d, half_h, wide, inner)]
    add x1 -> x3, other arithmetic: 0.12 us -> 2.54 us  [the longest x1 1.03 us: per_device(): level_part = kept_sum + behind(got_sum, part).astype(f32)]
    ppermute x13, starting transfers between devices: 29.3 us -> 31.4 us  [swap(): lax.ppermute(x, axis, [(i, i ^ bit) for i in range(lax.axis_size(axis))])]
  transfers between devices with their start and end apart: 18 -> 19, of which waited for: 8 -> 8; matrix products, arithmetic and copies ran while one was open for 8% -> 7% of each run, Pallas kernels for 2% -> 7%
where the time goes in v12:
time: 135 us; the launch traced here: 133 us
  starting transfers between devices  56.7 us (42%)
  waiting for transfers between devices  29.8 us (22%)
  Pallas kernels  16.2 us (12%)
  local copies, waits for them, and re-layouts  12.5 us (9%)
  blocking collectives  9.83 us (7%)
  other arithmetic  6.81 us (5%)
    ppermute x13, starting transfers between devices, swap(): lax.ppermute(x, axis, [(i, i ^ bit) for i in range(lax.axis_size(axis))])  31.4 us
    all_to_all x4, starting transfers between devices, exchange(): return lax.all_to_all(x, axis, split_axis=0, concat_axis=0, tiled=False)  23.2 us
    ppermute x13, waiting for transfers between devices, swap(): lax.ppermute(x, axis, [(i, i ^ bit) for i in range(lax.axis_size(axis))])  21.6 us
    pallas_call x6, Pallas kernels, local_call(): pl.pallas_call(body, out_shape=list(out_shapes), in_specs=[pl.BlockSpec(m...  16.2 us
    all_gather x1, blocking collectives, per_device(): gathered = lax.all_gather(payload, 'col')  9.83 us
    all_to_all x4, waiting for transfers between devices, exchange(): return lax.all_to_all(x, axis, split_axis=0, concat_axis=0, tiled=False)  8.17 us
    unnamed x37, local copies, waits for them, and re-layouts  7.73 us
  transfers between devices with their start and end apart: 19, of which 8 were waited for; matrix products, arithmetic and copies ran while one was open for 7% of the time, Pallas kernels for 7%

profile of v12, /device:TPU:1, one launch (start us, length us, event | category | flops | bytes accessed | tf_op | source)
XLA Modules:
  0.0 132.8 jit_solution(817919482930918114)
XLA Ops:
  0.7 1.7 %shard_map.145 = bf16[528,128]{1,0:T(8,128)(2,1)} custom-call(bf16[256,128]{1,0:T(8,128)(2,1)} %bitcast.105, bf16[256,128]{1,0:T(8,128)(2,1)} %bitcast.123, bf16[14,128]{1,0:T(8,128)(2,1)} %bitcast.127, bf16[128,13824]{1,0:T(8,128)(2,1)} %weight_ref.1, bf16[256,128]{1,0:T(8,128)(2,1)} %bitcast.102, bf16[128,512]{1,0:T(8,128)(2,1)} %up_ref.1, ...), custom_call_target="tpu_custom_call" | custom-call | bytes 65536 | tf_op jit(solution)/shard_map/pallas_call | solution.py:87
  2.4 9.8 %all-gather = bf16[2112,128]{1,0:T(8,128)(2,1)S(1)} all-gather(bf16[528,128]{1,0:T(8,128)(2,1)} %shard_map.145), channel_id=2, replica_groups=mesh['gx'=8,'gy'=8,'col'=4] {'col'}, dimensions={0}, use_global_device_ids=true | all-gather | bytes 675840 | tf_op jit(solution)/shard_map/all_gather | solution.py:383
  12.2 1.3 shard_map.146
  13.5 0.7 copy-done.4
  14.8 1.3 collective-permute-start.1
  16.1 0.9 copy.38
  17.1 0.9 slice_bitcast_fusion.5
  17.9 1.5 %collective-permute-done.even_x_ref = bf16[128,512]{1,0:T(8,128)(2,1)} collective-permute-done((bf16[128,512]{1,0:T(8,128)(2,1)}, bf16[128,512]{1,0:T(8,128)(2,1)}, u32[]{:S(2)}, u32[]{:S(2)}) %collective-permute-start) | collective-permute-done | bytes 131104 | tf_op jit(solution)/shard_map/ppermute | solution.py:37
  19.5 0.8 select_bitcast_fusion.5
  20.4 1.9 %collective-permute-start.2 = (bf16[4,32,512]{2,1,0:T(8,128)(2,1)S(1)}, bf16[4,32,512]{2,1,0:T(8,128)(2,1)S(1)}, u32[]{:S(2)}, u32[]{:S(2)}) collective-permute-start(bf16[4,32,512]{2,1,0:T(8,128)(2,1)S(1)} %get-tuple-element.63), channel_id=1, source_target_pairs={{0,4},{4,0},{8,12},{12,8},{16,20},{20,16},{24,28},{28,24},{1,5},{5... | collective-permute-start | bytes 393224 | tf_op jit(solution)/shard_map/ppermute | solution.py:37
  22.2 0.7 collective-permute-start.3
  23.0 2.8 %collective-permute-done.2.even_y_ref = bf16[4,32,512]{2,1,0:T(8,128)(2,1)S(1)} collective-permute-done((bf16[4,32,512]{2,1,0:T(8,128)(2,1)S(1)}, bf16[4,32,512]{2,1,0:T(8,128)(2,1)S(1)}, u32[]{:S(2)}, u32[]{:S(2)}) %collective-permute-start.2) | collective-permute-done | bytes 131104 | tf_op jit(solution)/shard_map/ppermute | solution.py:37
  25.8 0.9 copy-done.5
  26.7 0.8 copy-done.7
  27.6 3.8 %shard_map.147 = (bf16[4,6,32,512]{3,2,1,0:T(8,128)(2,1)S(1)}, bf16[256,128]{1,0:T(8,128)(2,1)}, bf16[4,144,128]{2,1,0:T(8,128)(2,1)S(1)}, bf16[448,512]{1,0:T(8,128)(2,1)}) custom-call(bf16[256,512]{1,0:T(8,128)(2,1)S(1)} %copy-done.5, bf16[128,512]{1,0:T(8,128)(2,1)} %collective-permute-done.even_x_ref, bf16[128,512]{1,0:T(8,128)(2,1)} %collective-permute-done.1.odd_x_ref, ...), custom_call_target="tpu_custom_call" | custom-call | flops 905969664 | bytes 3538944 | tf_op jit(solution)/shard_map/pallas_call | solution.py:87
  31.4 0.7 copy-done.10
  32.0 0.9 copy-done.12
  32.9 4.3 %collective-permute-start.4 = (bf16[448,512]{1,0:T(8,128)(2,1)}, bf16[448,512]{1,0:T(8,128)(2,1)S(1)}, u32[]{:S(2)}, u32[]{:S(2)}) collective-permute-start(bf16[448,512]{1,0:T(8,128)(2,1)} %get-tuple-element.34), channel_id=1, source_target_pairs={{0,32},{32,0},{64,96},{96,64},{128,160},{160,128},{192,224},{224,1... | collective-permute-start | bytes 1376264 | tf_op jit(solution)/shard_map/ppermute | solution.py:37
  37.2 5.7 %all-to-all-start = ((bf16[4,144,128]{2,1,0:T(8,128)(2,1)}), bf16[4,144,128]{2,1,0:T(8,128)(2,1)S(1)}, u32[]{:S(2)}, u32[]{:S(2)}) async-start(bf16[4,144,128]{2,1,0:T(8,128)(2,1)} %copy-done.10), calls=%async_computation | async-start | bytes 294912 | tf_op jit(solution)/shard_map/all_to_all | solution.py:20
  42.9 3.2 %collective-permute-done.4.got_ref = bf16[448,512]{1,0:T(8,128)(2,1)S(1)} collective-permute-done((bf16[448,512]{1,0:T(8,128)(2,1)}, bf16[448,512]{1,0:T(8,128)(2,1)S(1)}, u32[]{:S(2)}, u32[]{:S(2)}) %collective-permute-start.4) | collective-permute-done | bytes 458784 | tf_op jit(solution)/shard_map/ppermute | solution.py:37
  46.1 0.8 copy-done.8
  47.0 1.1 copy-done.13
  48.1 6.1 %shard_map.148 = (bf16[2,4,224,128]{3,2,1,0:T(8,128)(2,1)S(1)}, bf16[2,4,224,128]{3,2,1,0:T(8,128)(2,1)S(1)}, bf16[2,4,224,128]{3,2,1,0:T(8,128)(2,1)S(1)}, bf16[2,4,224,128]{3,2,1,0:T(8,128)(2,1)S(1)}) custom-call(bf16[4,6,32,512]{3,2,1,0:T(8,128)(2,1)S(1)} %copy-done.13, bf16[256,128]{1,0:T(8,128)(2,1)S(1)} %bitcast.104, ...), custom_call_target="tpu_custom_call" | custom-call | flops 905969664 | bytes 3670016 | tf_op jit(solution)/shard_map/pallas_call | solution.py:87
  54.2 7.8 %collective-permute-start.7 = (bf16[2,4,224,128]{3,2,1,0:T(8,128)(2,1)S(1)}, bf16[2,4,224,128]{3,2,1,0:T(8,128)(2,1)S(1)}, u32[]{:S(2)}, u32[]{:S(2)}) collective-permute-start(bf16[2,4,224,128]{3,2,1,0:T(8,128)(2,1)S(1)} %get-tuple-element.40), channel_id=1, source_target_pairs={{0,24},{4,28},{8,16},{12,20},{16,8},{20,12},{24,0},{28,4},{1,25},{... | collective-permute-start | bytes 1376264 | tf_op jit(solution)/shard_map/ppermute | solution.py:37
  62.0 0.7 broadcast_in_dim.6
  62.7 7.2 %all-to-all-start.1 = ((bf16[8,80,128]{2,1,0:T(8,128)(2,1)}), bf16[8,80,128]{2,1,0:T(8,128)(2,1)S(1)}, u32[]{:S(2)}, u32[]{:S(2)}) async-start(bf16[8,80,128]{2,1,0:T(8,128)(2,1)} %broadcast_in_dim.6), calls=%async_computation.1 | async-start | bytes 327680 | tf_op jit(solution)/shard_map/all_to_all | solution.py:20
  70.0 8.2 %all-to-all-done.1 = bf16[8,80,128]{2,1,0:T(8,128)(2,1)S(1)} async-done(((bf16[8,80,128]{2,1,0:T(8,128)(2,1)}), bf16[8,80,128]{2,1,0:T(8,128)(2,1)S(1)}, u32[]{:S(2)}, u32[]{:S(2)}) %all-to-all-start.1) | async-done | bytes 163872 | tf_op jit(solution)/shard_map/all_to_all | solution.py:20
  78.2 1.0 broadcast_in_dim.15
  79.2 4.3 %all-to-all-start.2 = ((bf16[8,384,128]{2,1,0:T(8,128)(2,1)}), bf16[8,384,128]{2,1,0:T(8,128)(2,1)}, u32[]{:S(2)}, u32[]{:S(2)}) async-start(bf16[8,384,128]{2,1,0:T(8,128)(2,1)} %broadcast_in_dim.15), calls=%async_computation.2 | async-start | bytes 1572864 | tf_op jit(solution)/shard_map/all_to_all | solution.py:20
  83.7 1.7 %collective-permute-start.8 = (bf16[4,224,128]{2,1,0:T(8,128)(2,1)S(1)}, bf16[4,224,128]{2,1,0:T(8,128)(2,1)S(1)}, u32[]{:S(2)}, u32[]{:S(2)}) collective-permute-start(bf16[4,224,128]{2,1,0:T(8,128)(2,1)S(1)} %fusion.8), channel_id=1, source_target_pairs={{0,8},{4,12},{8,0},{12,4},{16,24},{20,28},{24,16},{28,20},{1,9},{5... | collective-permute-start | bytes 688136 | tf_op jit(solution)/shard_map/ppermute | solution.py:37
  85.5 1.9 %collective-permute-start.6 = (bf16[4,224,128]{2,1,0:T(8,128)(2,1)S(1)}, bf16[4,224,128]{2,1,0:T(8,128)(2,1)S(1)}, u32[]{:S(2)}, u32[]{:S(2)}) collective-permute-start(bf16[4,224,128]{2,1,0:T(8,128)(2,1)S(1)} %fusion.7), channel_id=1, source_target_pairs={{0,24},{4,28},{8,16},{12,20},{16,8},{20,12},{24,0},{28,4},{1,25},{... | collective-permute-start | bytes 688136 | tf_op jit(solution)/shard_map/ppermute | solution.py:37
  87.4 6.7 %collective-permute-done.8 = bf16[4,224,128]{2,1,0:T(8,128)(2,1)S(1)} collective-permute-done((bf16[4,224,128]{2,1,0:T(8,128)(2,1)S(1)}, bf16[4,224,128]{2,1,0:T(8,128)(2,1)S(1)}, u32[]{:S(2)}, u32[]{:S(2)}) %collective-permute-start.8) | collective-permute-done | bytes 229408 | tf_op jit(solution)/shard_map/ppermute | solution.py:37
  94.3 0.7 collective-permute-done.6
  95.1 0.8 fusion.9
  95.9 5.2 %collective-permute-start.9 = (bf16[4,224,128]{2,1,0:T(8,128)(2,1)}, bf16[4,224,128]{2,1,0:T(8,128)(2,1)}, u32[]{:S(2)}, u32[]{:S(2)}) collective-permute-start(bf16[4,224,128]{2,1,0:T(8,128)(2,1)} %fusion.9), channel_id=1, source_target_pairs={{0,4},{4,0},{8,12},{12,8},{16,20},{20,16},{24,28},{28,24},{1,5},{5... | collective-permute-start | bytes 688136 | tf_op jit(solution)/shard_map/ppermute | solution.py:37
  101.1 1.6 %copy.27 = bf16[8,384,128]{2,0,1:T(8,128)(2,1)S(1)} copy(bf16[8,384,128]{2,1,0:T(8,128)(2,1)} %all-to-all-done.2) | data formatting | bytes 1572864 | tf_op jit(solution)/shard_map/all_to_all | solution.py:20
  103.4 2.3 %shard_map.149 = (bf16[8,80,128]{2,1,0:T(8,128)(2,1)}, bf16[3,10,6,16,128]{4,3,2,1,0:T(8,128)(2,1)S(1)}) custom-call(bf16[768,512]{1,0:T(8,128)(2,1)S(1)} %bitcast.93, bf16[128,512]{1,0:T(8,128)(2,1)S(1)} %copy-done.6, bf16[8,1,16,128]{3,2,1,0:T(8,128)(2,1)S(1)} %get-tuple-element.73.before_ref, bf16[8,4,16,128]{3,2,1,0:T(8,128)(2,1)S(1)} %bitcast.99, ...), custom_call_target="tpu_custom_call" | custom-call | flops 452984832 | bytes 884736 | tf_op jit(solution)/shard_map/pallas_call | solution.py:87
  105.7 1.0 fusion.4
  107.0 6.0 %all-to-all-start.3 = ((bf16[8,80,128]{2,1,0:T(8,128)(2,1)}), bf16[8,80,128]{2,1,0:T(8,128)(2,1)S(1)}, u32[]{:S(2)}, u32[]{:S(2)}) async-start(bf16[8,80,128]{2,1,0:T(8,128)(2,1)} %get-tuple-element.42), calls=%async_computation.3 | async-start | bytes 327680 | tf_op jit(solution)/shard_map/all_to_all | solution.py:20
  113.0 0.9 shard_map.150
  114.0 3.7 %collective-permute-start.12 = (bf16[992,128]{1,0:T(8,128)(2,1)S(1)}, bf16[992,128]{1,0:T(8,128)(2,1)S(1)}, u32[]{:S(2)}, u32[]{:S(2)}) collective-permute-start(bf16[992,128]{1,0:T(8,128)(2,1)S(1)} %get-tuple-element.47), channel_id=1, source_target_pairs={{0,1},{1,0},{2,3},{3,2},{4,5},{5,4},{6,7},{7,6},{8,9},{9,8},{10,11... | collective-permute-start | bytes 761864 | tf_op jit(solution)/shard_map/ppermute | solution.py:37
  117.8 1.7 %collective-permute-start.14 = (bf16[992,128]{1,0:T(8,128)(2,1)S(1)}, bf16[992,128]{1,0:T(8,128)(2,1)S(1)}, u32[]{:S(2)}, u32[]{:S(2)}) collective-permute-start(bf16[992,128]{1,0:T(8,128)(2,1)S(1)} %get-tuple-element.49), channel_id=1, source_target_pairs={{0,3},{1,2},{2,1},{3,0},{4,7},{5,6},{6,5},{7,4},{8,11},{9,10},{10,... | collective-permute-start | bytes 761864 | tf_op jit(solution)/shard_map/ppermute | solution.py:37
  119.4 0.9 bitcast_add_fusion
  120.4 2.5 %collective-permute-start.11 = (bf16[224,128]{1,0:T(8,128)(2,1)S(1)}, bf16[224,128]{1,0:T(8,128)(2,1)S(1)}, u32[]{:S(2)}, u32[]{:S(2)}) collective-permute-start(bf16[224,128]{1,0:T(8,128)(2,1)S(1)} %fusion.12), channel_id=1, source_target_pairs={{0,128},{32,160},{64,192},{96,224},{128,0},{160,32},{192,64},{224,... | collective-permute-start | bytes 172040 | tf_op jit(solution)/shard_map/ppermute | solution.py:37
  124.1 3.3 %collective-permute-done.11 = bf16[224,128]{1,0:T(8,128)(2,1)S(1)} collective-permute-done((bf16[224,128]{1,0:T(8,128)(2,1)S(1)}, bf16[224,128]{1,0:T(8,128)(2,1)S(1)}, u32[]{:S(2)}, u32[]{:S(2)}) %collective-permute-start.11) | collective-permute-done | bytes 57376 | tf_op jit(solution)/shard_map/ppermute | solution.py:37
  127.5 0.7 fusion.11
  128.1 3.2 %collective-permute-done.14 = bf16[992,128]{1,0:T(8,128)(2,1)S(1)} collective-permute-done((bf16[992,128]{1,0:T(8,128)(2,1)S(1)}, bf16[992,128]{1,0:T(8,128)(2,1)S(1)}, u32[]{:S(2)}, u32[]{:S(2)}) %collective-permute-start.14) | collective-permute-done | bytes 253984 | tf_op jit(solution)/shard_map/ppermute | solution.py:37
  132.0 0.9 convert_add_fusion.2
  (68 shorter events, 4.0 us)
Async XLA Ops:
  0.6 11.6 %copy-start.9 = (bf16[2,4,32,128]{3,2,1,0:T(8,128)(2,1)S(1)}, bf16[2,4,32,128]{3,2,1,0:T(8,128)(2,1)}, u32[]{:S(2)}) copy-start(bf16[2,4,32,128]{3,2,1,0:T(8,128)(2,1)} %param.15) | copy-start | bytes 196612
  0.6 11.5 %copy-start.11 = (s32[2,4,32]{2,1,0:T(4,128)S(1)}, s32[2,4,32]{2,1,0:T(4,128)}, u32[]{:S(2)}) copy-start(s32[2,4,32]{2,1,0:T(4,128)} %label_ref.1) | copy-start | bytes 3076
  0.7 25.1 %copy-start = (bf16[128,13824]{1,0:T(8,128)(2,1)S(1)}, bf16[128,13824]{1,0:T(8,128)(2,1)}, u32[]{:S(2)}) copy-start(bf16[128,13824]{1,0:T(8,128)(2,1)} %weight_ref.1) | copy-start | bytes 10616836
  13.5 0.7 copy-start.4
  14.2 5.3 %collective-permute-start = (bf16[128,512]{1,0:T(8,128)(2,1)}, bf16[128,512]{1,0:T(8,128)(2,1)}, u32[]{:S(2)}, u32[]{:S(2)}) collective-permute-start(bf16[128,512]{1,0:T(8,128)(2,1)} %get-tuple-element.29), channel_id=1, source_target_pairs={{0,32},{32,0},{64,96},{96,64},{128,160},{160,128},{192,224},{224,1... | collective-permute-start | bytes 393224 | tf_op jit(solution)/shard_map/ppermute | solution.py:37
  14.8 4.7 %collective-permute-start.1 = (bf16[128,512]{1,0:T(8,128)(2,1)}, bf16[128,512]{1,0:T(8,128)(2,1)}, u32[]{:S(2)}, u32[]{:S(2)}) collective-permute-start(bf16[128,512]{1,0:T(8,128)(2,1)} %get-tuple-element.30), channel_id=1, source_target_pairs={{32,64},{64,32},{96,128},{128,96},{160,192},{192,160},{33,65},{65,... | collective-permute-start | bytes 393224 | tf_op jit(solution)/shard_map/ppermute | solution.py:42
  17.1 5.8 %copy-start.2 = (bf16[8,16,4,128]{3,1,2,0:T(8,128)(2,1)}, bf16[8,16,4,128]{3,1,2,0:T(8,128)(2,1)S(1)}, u32[]{:S(2)}) copy-start(bf16[8,16,4,128]{3,1,2,0:T(8,128)(2,1)S(1)} %copy.38) | copy-start | bytes 393220
  20.4 5.4 %collective-permute-start.2 = (bf16[4,32,512]{2,1,0:T(8,128)(2,1)S(1)}, bf16[4,32,512]{2,1,0:T(8,128)(2,1)S(1)}, u32[]{:S(2)}, u32[]{:S(2)}) collective-permute-start(bf16[4,32,512]{2,1,0:T(8,128)(2,1)S(1)} %get-tuple-element.63), channel_id=1, source_target_pairs={{0,4},{4,0},{8,12},{12,8},{16,20},{20,16},{24,28},{28,24},{1,5},{5... | collective-permute-start | bytes 393224 | tf_op jit(solution)/shard_map/ppermute | solution.py:37
  22.2 3.5 %collective-permute-start.3 = (bf16[4,32,512]{2,1,0:T(8,128)(2,1)S(1)}, bf16[4,32,512]{2,1,0:T(8,128)(2,1)S(1)}, u32[]{:S(2)}, u32[]{:S(2)}) collective-permute-start(bf16[4,32,512]{2,1,0:T(8,128)(2,1)S(1)} %get-tuple-element.62), channel_id=1, source_target_pairs={{4,8},{8,4},{12,16},{16,12},{20,24},{24,20},{5,9},{9,5},{13,17},{1... | collective-permute-start | bytes 393224 | tf_op jit(solution)/shard_map/ppermute | solution.py:42
  25.8 1.0 copy-start.5
  26.7 0.8 copy-start.7
  31.4 0.7 copy-start.10
  32.0 0.9 copy-start.12
  32.9 13.2 %collective-permute-start.4 = (bf16[448,512]{1,0:T(8,128)(2,1)}, bf16[448,512]{1,0:T(8,128)(2,1)S(1)}, u32[]{:S(2)}, u32[]{:S(2)}) collective-permute-start(bf16[448,512]{1,0:T(8,128)(2,1)} %get-tuple-element.34), channel_id=1, source_target_pairs={{0,32},{32,0},{64,96},{96,64},{128,160},{160,128},{192,224},{224,1... | collective-permute-start | bytes 1376264 | tf_op jit(solution)/shard_map/ppermute | solution.py:37
  37.2 24.7 %all-to-all-start = ((bf16[4,144,128]{2,1,0:T(8,128)(2,1)}), bf16[4,144,128]{2,1,0:T(8,128)(2,1)S(1)}, u32[]{:S(2)}, u32[]{:S(2)}) async-start(bf16[4,144,128]{2,1,0:T(8,128)(2,1)} %copy-done.10), calls=%async_computation | async-start | bytes 294912 | tf_op jit(solution)/shard_map/all_to_all | solution.py:20
  46.1 0.8 copy-start.8
  47.0 1.1 copy-start.13
  54.2 29.3 %collective-permute-start.7 = (bf16[2,4,224,128]{3,2,1,0:T(8,128)(2,1)S(1)}, bf16[2,4,224,128]{3,2,1,0:T(8,128)(2,1)S(1)}, u32[]{:S(2)}, u32[]{:S(2)}) collective-permute-start(bf16[2,4,224,128]{3,2,1,0:T(8,128)(2,1)S(1)} %get-tuple-element.40), channel_id=1, source_target_pairs={{0,24},{4,28},{8,16},{12,20},{16,8},{20,12},{24,0},{28,4},{1,25},{... | collective-permute-start | bytes 1376264 | tf_op jit(solution)/shard_map/ppermute | solution.py:37
  62.7 15.5 %all-to-all-start.1 = ((bf16[8,80,128]{2,1,0:T(8,128)(2,1)}), bf16[8,80,128]{2,1,0:T(8,128)(2,1)S(1)}, u32[]{:S(2)}, u32[]{:S(2)}) async-start(bf16[8,80,128]{2,1,0:T(8,128)(2,1)} %broadcast_in_dim.6), calls=%async_computation.1 | async-start | bytes 327680 | tf_op jit(solution)/shard_map/all_to_all | solution.py:20
  69.9 15.5 %collective-permute-start.5 = (bf16[2,4,224,128]{3,2,1,0:T(8,128)(2,1)S(1)}, bf16[2,4,224,128]{3,2,1,0:T(8,128)(2,1)S(1)}, u32[]{:S(2)}, u32[]{:S(2)}) collective-permute-start(bf16[2,4,224,128]{3,2,1,0:T(8,128)(2,1)S(1)} %get-tuple-element.38), channel_id=1, source_target_pairs={{0,8},{4,12},{8,0},{12,4},{16,24},{20,28},{24,16},{28,20},{1,9},{5... | collective-permute-start | bytes 1376264 | tf_op jit(solution)/shard_map/ppermute | solution.py:37
  79.2 21.9 %all-to-all-start.2 = ((bf16[8,384,128]{2,1,0:T(8,128)(2,1)}), bf16[8,384,128]{2,1,0:T(8,128)(2,1)}, u32[]{:S(2)}, u32[]{:S(2)}) async-start(bf16[8,384,128]{2,1,0:T(8,128)(2,1)} %broadcast_in_dim.15), calls=%async_computation.2 | async-start | bytes 1572864 | tf_op jit(solution)/shard_map/all_to_all | solution.py:20
  83.7 10.5 %collective-permute-start.8 = (bf16[4,224,128]{2,1,0:T(8,128)(2,1)S(1)}, bf16[4,224,128]{2,1,0:T(8,128)(2,1)S(1)}, u32[]{:S(2)}, u32[]{:S(2)}) collective-permute-start(bf16[4,224,128]{2,1,0:T(8,128)(2,1)S(1)} %fusion.8), channel_id=1, source_target_pairs={{0,8},{4,12},{8,0},{12,4},{16,24},{20,28},{24,16},{28,20},{1,9},{5... | collective-permute-start | bytes 688136 | tf_op jit(solution)/shard_map/ppermute | solution.py:37
  85.5 9.5 %collective-permute-start.6 = (bf16[4,224,128]{2,1,0:T(8,128)(2,1)S(1)}, bf16[4,224,128]{2,1,0:T(8,128)(2,1)S(1)}, u32[]{:S(2)}, u32[]{:S(2)}) collective-permute-start(bf16[4,224,128]{2,1,0:T(8,128)(2,1)S(1)} %fusion.7), channel_id=1, source_target_pairs={{0,24},{4,28},{8,16},{12,20},{16,8},{20,12},{24,0},{28,4},{1,25},{... | collective-permute-start | bytes 688136 | tf_op jit(solution)/shard_map/ppermute | solution.py:37
  94.2 9.1 %copy-start.1 = (bf16[128,27,128]{2,0,1:T(8,128)(2,1)S(1)}, bf16[128,27,128]{2,0,1:T(8,128)(2,1)}, u32[]{:S(2)}) copy-start(bf16[128,27,128]{2,0,1:T(8,128)(2,1)} %param.12) | copy-start | bytes 2654212
  94.2 9.1 %copy-start.3 = (bf16[8,16,4,128]{3,1,2,0:T(8,128)(2,1)S(1)}, bf16[8,16,4,128]{3,1,2,0:T(8,128)(2,1)}, u32[]{:S(2)}) copy-start(bf16[8,16,4,128]{3,1,2,0:T(8,128)(2,1)} %copy-done.2) | copy-start | bytes 393220
  94.2 9.1 %copy-start.6 = (bf16[128,512]{1,0:T(8,128)(2,1)S(1)}, bf16[128,512]{1,0:T(8,128)(2,1)}, u32[]{:S(2)}) copy-start(bf16[128,512]{1,0:T(8,128)(2,1)} %up_ref.1) | copy-start | bytes 393220
  95.1 8.1 %copy-start.14 = (f32[4,224,128]{2,1,0:T(8,128)}, f32[4,224,128]{2,1,0:T(8,128)S(1)}, u32[]{:S(2)}) copy-start(f32[4,224,128]{2,1,0:T(8,128)S(1)} %fusion.6) | copy-start | bytes 1376260
  95.9 9.8 %collective-permute-start.9 = (bf16[4,224,128]{2,1,0:T(8,128)(2,1)}, bf16[4,224,128]{2,1,0:T(8,128)(2,1)}, u32[]{:S(2)}, u32[]{:S(2)}) collective-permute-start(bf16[4,224,128]{2,1,0:T(8,128)(2,1)} %fusion.9), channel_id=1, source_target_pairs={{0,4},{4,0},{8,12},{12,8},{16,20},{20,16},{24,28},{28,24},{1,5},{5... | collective-permute-start | bytes 688136 | tf_op jit(solution)/shard_map/ppermute | solution.py:37
  102.8 4.2 %copy-start.16 = (bf16[8,16,4,128]{3,2,1,0:T(4,128)(2,1)S(1)}, bf16[8,16,4,128]{3,2,1,0:T(4,128)(2,1)}, u32[]{:S(2)}) copy-start(bf16[8,16,4,128]{3,2,1,0:T(4,128)(2,1)} %param.11) | copy-start | bytes 393220
  103.2 2.5 %copy-start.15 = (f32[4,224,128]{2,1,0:T(8,128)S(1)}, f32[4,224,128]{2,1,0:T(8,128)}, u32[]{:S(2)}) copy-start(f32[4,224,128]{2,1,0:T(8,128)} %copy-done.14) | copy-start | bytes 1376260
  106.8 12.7 %collective-permute-start.10 = (bf16[2,224,128]{2,1,0:T(8,128)(2,1)S(1)}, bf16[2,224,128]{2,1,0:T(8,128)(2,1)}, u32[]{:S(2)}, u32[]{:S(2)}) collective-permute-start(bf16[2,224,128]{2,1,0:T(8,128)(2,1)S(1)} %fusion.10), channel_id=1, source_target_pairs={{0,64},{32,96},{64,0},{96,32},{128,192},{160,224},{192,128},{224,1... | collective-permute-start | bytes 344072 | tf_op jit(solution)/shard_map/ppermute | solution.py:37
  107.0 13.4 %all-to-all-start.3 = ((bf16[8,80,128]{2,1,0:T(8,128)(2,1)}), bf16[8,80,128]{2,1,0:T(8,128)(2,1)S(1)}, u32[]{:S(2)}, u32[]{:S(2)}) async-start(bf16[8,80,128]{2,1,0:T(8,128)(2,1)} %get-tuple-element.42), calls=%async_computation.3 | async-start | bytes 327680 | tf_op jit(solution)/shard_map/all_to_all | solution.py:20
  114.0 14.2 %collective-permute-start.12 = (bf16[992,128]{1,0:T(8,128)(2,1)S(1)}, bf16[992,128]{1,0:T(8,128)(2,1)S(1)}, u32[]{:S(2)}, u32[]{:S(2)}) collective-permute-start(bf16[992,128]{1,0:T(8,128)(2,1)S(1)} %get-tuple-element.47), channel_id=1, source_target_pairs={{0,1},{1,0},{2,3},{3,2},{4,5},{5,4},{6,7},{7,6},{8,9},{9,8},{10,11... | collective-permute-start | bytes 761864 | tf_op jit(solution)/shard_map/ppermute | solution.py:37
  117.7 10.4 %collective-permute-start.13 = (bf16[992,128]{1,0:T(8,128)(2,1)S(1)}, bf16[992,128]{1,0:T(8,128)(2,1)S(1)}, u32[]{:S(2)}, u32[]{:S(2)}) collective-permute-start(bf16[992,128]{1,0:T(8,128)(2,1)S(1)} %get-tuple-element.48), channel_id=1, source_target_pairs={{0,2},{1,3},{2,0},{3,1},{4,6},{5,7},{6,4},{7,5},{8,10},{9,11},{10,... | collective-permute-start | bytes 761864 | tf_op jit(solution)/shard_map/ppermute | solution.py:37
  117.8 13.6 %collective-permute-start.14 = (bf16[992,128]{1,0:T(8,128)(2,1)S(1)}, bf16[992,128]{1,0:T(8,128)(2,1)S(1)}, u32[]{:S(2)}, u32[]{:S(2)}) collective-permute-start(bf16[992,128]{1,0:T(8,128)(2,1)S(1)} %get-tuple-element.49), channel_id=1, source_target_pairs={{0,3},{1,2},{2,1},{3,0},{4,7},{5,6},{6,5},{7,4},{8,11},{9,10},{10,... | collective-permute-start | bytes 761864 | tf_op jit(solution)/shard_map/ppermute | solution.py:37
  120.4 7.0 %collective-permute-start.11 = (bf16[224,128]{1,0:T(8,128)(2,1)S(1)}, bf16[224,128]{1,0:T(8,128)(2,1)S(1)}, u32[]{:S(2)}, u32[]{:S(2)}) collective-permute-start(bf16[224,128]{1,0:T(8,128)(2,1)S(1)} %fusion.12), channel_id=1, source_target_pairs={{0,128},{32,160},{64,192},{96,224},{128,0},{160,32},{192,64},{224,... | collective-permute-start | bytes 172040 | tf_op jit(solution)/shard_map/ppermute | solution.py:37

commit v13 on v12

--- a/solution.py
+++ b/solution.py
@@ -532,8 +532,8 @@
         bottom_input.transpose(0, 2, 1, 3).reshape(bottom_rows, channel_width),
         shifts,
     )
-    level_part = kept_sum + behind(got_sum, part).astype(f32)
-    part = exchange(part, "gy")
+    level_part = kept_sum + behind(got_sum, both[0]).astype(f32)
+    part = exchange(behind(part, both[0]), "gy")
     share = bottom_rows // ny
     aux_weight_grad = part[:, share : share + CLASSES].astype(f32).sum(axis=0).T
     level_part = summed_by_pairs(level_part, "gx", bits_of("gx")[:-1], bits_of("gx")[-2::-1], part)

time: 135 us -> 138 us (1.022)
  waiting for transfers between devices: 29.8 us -> 36.5 us
  other arithmetic: 6.81 us -> 4.24 us
  starting transfers between devices: 56.7 us -> 55.2 us
    all_to_all x4, waiting for transfers between devices: 8.17 us -> 18 us  [exchange(): return lax.all_to_all(x, axis, split_axis=0, concat_axis=0, tiled=False)]
    ppermute x13, waiting for transfers between devices: 21.6 us -> 18.4 us  [swap(): lax.ppermute(x, axis, [(i, i ^ bit) for i in range(lax.axis_size(axis))])]
    all_to_all x4, starting transfers between devices: 23.2 us -> 21.2 us  [exchange(): return lax.all_to_all(x, axis, split_axis=0, concat_axis=0, tiled=False)]
    unnamed x37 -> x31, local copies, waits for them, and re-layouts: 7.73 us -> 7.71 us
where the time goes in v13:
time: 138 us; the launch traced here: 136 us
  starting transfers between devices  55.2 us (40%)
  waiting for transfers between devices  36.5 us (26%)
  Pallas kernels  16.2 us (12%)
  local copies, waits for them, and re-layouts  13.4 us (10%)
  blocking collectives  9.83 us (7%)
  other arithmetic  4.24 us (3%)
    ppermute x13, starting transfers between devices, swap(): lax.ppermute(x, axis, [(i, i ^ bit) for i in range(lax.axis_size(axis))])  32 us
    all_to_all x4, starting transfers between devices, exchange(): return lax.all_to_all(x, axis, split_axis=0, concat_axis=0, tiled=False)  21.2 us
    ppermute x13, waiting for transfers between devices, swap(): lax.ppermute(x, axis, [(i, i ^ bit) for i in range(lax.axis_size(axis))])  18.4 us
    all_to_all x4, waiting for transfers between devices, exchange(): return lax.all_to_all(x, axis, split_axis=0, concat_axis=0, tiled=False)  18 us
    pallas_call x6, Pallas kernels, local_call(): pl.pallas_call(body, out_shape=list(out_shapes), in_specs=[pl.BlockSpec(m...  16.2 us
    all_gather x1, blocking collectives, per_device(): gathered = lax.all_gather(payload, 'col')  9.83 us
    unnamed x31, local copies, waits for them, and re-layouts  7.71 us
  transfers between devices with their start and end apart: 19, of which 8 were waited for; matrix products, arithmetic and copies ran while one was open for 7% of the time, Pallas kernels for 7%

profile of v13, /device:TPU:1, one launch (start us, length us, event | category | flops | bytes accessed | tf_op | source)
XLA Modules:
  0.0 136.4 jit_solution(7794315239954720430)
XLA Ops:
  0.7 1.7 %shard_map.145 = bf16[528,128]{1,0:T(8,128)(2,1)} custom-call(bf16[256,128]{1,0:T(8,128)(2,1)} %bitcast.105, bf16[256,128]{1,0:T(8,128)(2,1)} %bitcast.123, bf16[14,128]{1,0:T(8,128)(2,1)} %bitcast.127, bf16[128,13824]{1,0:T(8,128)(2,1)} %weight_ref.1, bf16[256,128]{1,0:T(8,128)(2,1)} %bitcast.102, bf16[128,512]{1,0:T(8,128)(2,1)} %up_ref.1, ...), custom_call_target="tpu_custom_call" | custom-call | bytes 65536 | tf_op jit(solution)/shard_map/pallas_call | solution.py:87
  2.4 9.8 %all-gather = bf16[2112,128]{1,0:T(8,128)(2,1)S(1)} all-gather(bf16[528,128]{1,0:T(8,128)(2,1)} %shard_map.145), channel_id=2, replica_groups=mesh['gx'=8,'gy'=8,'col'=4] {'col'}, dimensions={0}, use_global_device_ids=true | all-gather | bytes 675840 | tf_op jit(solution)/shard_map/all_gather | solution.py:383
  12.2 1.3 shard_map.146
  13.5 0.7 copy-done.4
  14.8 1.3 collective-permute-start.1
  16.1 0.9 copy.38
  17.1 0.9 slice_bitcast_fusion.5
  17.9 1.5 %collective-permute-done.even_x_ref = bf16[128,512]{1,0:T(8,128)(2,1)} collective-permute-done((bf16[128,512]{1,0:T(8,128)(2,1)}, bf16[128,512]{1,0:T(8,128)(2,1)}, u32[]{:S(2)}, u32[]{:S(2)}) %collective-permute-start) | collective-permute-done | bytes 131104 | tf_op jit(solution)/shard_map/ppermute | solution.py:37
  19.5 0.8 select_bitcast_fusion.5
  20.4 1.9 %collective-permute-start.2 = (bf16[4,32,512]{2,1,0:T(8,128)(2,1)S(1)}, bf16[4,32,512]{2,1,0:T(8,128)(2,1)S(1)}, u32[]{:S(2)}, u32[]{:S(2)}) collective-permute-start(bf16[4,32,512]{2,1,0:T(8,128)(2,1)S(1)} %get-tuple-element.65), channel_id=1, source_target_pairs={{0,4},{4,0},{8,12},{12,8},{16,20},{20,16},{24,28},{28,24},{1,5},{5... | collective-permute-start | bytes 393224 | tf_op jit(solution)/shard_map/ppermute | solution.py:37
  22.2 0.7 collective-permute-start.3
  23.0 2.8 %collective-permute-done.2.even_y_ref = bf16[4,32,512]{2,1,0:T(8,128)(2,1)S(1)} collective-permute-done((bf16[4,32,512]{2,1,0:T(8,128)(2,1)S(1)}, bf16[4,32,512]{2,1,0:T(8,128)(2,1)S(1)}, u32[]{:S(2)}, u32[]{:S(2)}) %collective-permute-start.2) | collective-permute-done | bytes 131104 | tf_op jit(solution)/shard_map/ppermute | solution.py:37
  25.8 0.9 copy-done.5
  26.7 0.8 copy-done.7
  27.6 3.8 %shard_map.147 = (bf16[4,6,32,512]{3,2,1,0:T(8,128)(2,1)S(1)}, bf16[256,128]{1,0:T(8,128)(2,1)}, bf16[4,144,128]{2,1,0:T(8,128)(2,1)S(1)}, bf16[448,512]{1,0:T(8,128)(2,1)}) custom-call(bf16[256,512]{1,0:T(8,128)(2,1)S(1)} %copy-done.5, bf16[128,512]{1,0:T(8,128)(2,1)} %collective-permute-done.even_x_ref, bf16[128,512]{1,0:T(8,128)(2,1)} %collective-permute-done.1.odd_x_ref, ...), custom_call_target="tpu_custom_call" | custom-call | flops 905969664 | bytes 3538944 | tf_op jit(solution)/shard_map/pallas_call | solution.py:87
  31.4 0.7 copy-done.10
  32.1 0.9 copy-done.12
  32.9 4.3 %collective-permute-start.4 = (bf16[448,512]{1,0:T(8,128)(2,1)}, bf16[448,512]{1,0:T(8,128)(2,1)S(1)}, u32[]{:S(2)}, u32[]{:S(2)}) collective-permute-start(bf16[448,512]{1,0:T(8,128)(2,1)} %get-tuple-element.35), channel_id=1, source_target_pairs={{0,32},{32,0},{64,96},{96,64},{128,160},{160,128},{192,224},{224,1... | collective-permute-start | bytes 1376264 | tf_op jit(solution)/shard_map/ppermute | solution.py:37
  37.2 5.7 %all-to-all-start = ((bf16[4,144,128]{2,1,0:T(8,128)(2,1)}), bf16[4,144,128]{2,1,0:T(8,128)(2,1)S(1)}, u32[]{:S(2)}, u32[]{:S(2)}) async-start(bf16[4,144,128]{2,1,0:T(8,128)(2,1)} %copy-done.10), calls=%async_computation | async-start | bytes 294912 | tf_op jit(solution)/shard_map/all_to_all | solution.py:20
  42.9 3.2 %collective-permute-done.4.got_ref = bf16[448,512]{1,0:T(8,128)(2,1)S(1)} collective-permute-done((bf16[448,512]{1,0:T(8,128)(2,1)}, bf16[448,512]{1,0:T(8,128)(2,1)S(1)}, u32[]{:S(2)}, u32[]{:S(2)}) %collective-permute-start.4) | collective-permute-done | bytes 458784 | tf_op jit(solution)/shard_map/ppermute | solution.py:37
  46.2 0.8 copy-done.8
  47.0 1.1 copy-done.13
  48.1 6.1 %shard_map.148 = (bf16[2,4,224,128]{3,2,1,0:T(8,128)(2,1)S(1)}, bf16[2,4,224,128]{3,2,1,0:T(8,128)(2,1)S(1)}, bf16[2,4,224,128]{3,2,1,0:T(8,128)(2,1)S(1)}, bf16[2,4,224,128]{3,2,1,0:T(8,128)(2,1)S(1)}) custom-call(bf16[4,6,32,512]{3,2,1,0:T(8,128)(2,1)S(1)} %copy-done.13, bf16[256,128]{1,0:T(8,128)(2,1)S(1)} %bitcast.104, ...), custom_call_target="tpu_custom_call" | custom-call | flops 905969664 | bytes 3670016 | tf_op jit(solution)/shard_map/pallas_call | solution.py:87
  54.2 7.8 %collective-permute-start.7 = (bf16[2,4,224,128]{3,2,1,0:T(8,128)(2,1)S(1)}, bf16[2,4,224,128]{3,2,1,0:T(8,128)(2,1)S(1)}, u32[]{:S(2)}, u32[]{:S(2)}) collective-permute-start(bf16[2,4,224,128]{3,2,1,0:T(8,128)(2,1)S(1)} %get-tuple-element.41), channel_id=1, source_target_pairs={{0,24},{4,28},{8,16},{12,20},{16,8},{20,12},{24,0},{28,4},{1,25},{... | collective-permute-start | bytes 1376264 | tf_op jit(solution)/shard_map/ppermute | solution.py:37
  62.0 0.7 broadcast_in_dim.6
  62.7 7.2 %all-to-all-start.1 = ((bf16[8,80,128]{2,1,0:T(8,128)(2,1)}), bf16[8,80,128]{2,1,0:T(8,128)(2,1)S(1)}, u32[]{:S(2)}, u32[]{:S(2)}) async-start(bf16[8,80,128]{2,1,0:T(8,128)(2,1)} %broadcast_in_dim.6), calls=%async_computation.1 | async-start | bytes 327680 | tf_op jit(solution)/shard_map/all_to_all | solution.py:20
  69.9 0.9 copy.30
  71.0 7.2 %all-to-all-done.1 = bf16[8,80,128]{2,1,0:T(8,128)(2,1)S(1)} async-done(((bf16[8,80,128]{2,1,0:T(8,128)(2,1)}), bf16[8,80,128]{2,1,0:T(8,128)(2,1)S(1)}, u32[]{:S(2)}, u32[]{:S(2)}) %all-to-all-start.1) | async-done | bytes 163872 | tf_op jit(solution)/shard_map/all_to_all | solution.py:20
  78.3 1.0 broadcast_in_dim.15
  79.3 4.3 %all-to-all-start.2 = ((bf16[8,384,128]{2,1,0:T(8,128)(2,1)}), bf16[8,384,128]{2,1,0:T(8,128)(2,1)}, u32[]{:S(2)}, u32[]{:S(2)}) async-start(bf16[8,384,128]{2,1,0:T(8,128)(2,1)} %broadcast_in_dim.15), calls=%async_computation.2 | async-start | bytes 1572864 | tf_op jit(solution)/shard_map/all_to_all | solution.py:20
  83.7 1.7 %collective-permute-start.8 = (bf16[4,224,128]{2,1,0:T(8,128)(2,1)S(1)}, bf16[4,224,128]{2,1,0:T(8,128)(2,1)S(1)}, u32[]{:S(2)}, u32[]{:S(2)}) collective-permute-start(bf16[4,224,128]{2,1,0:T(8,128)(2,1)S(1)} %fusion.8), channel_id=1, source_target_pairs={{0,8},{4,12},{8,0},{12,4},{16,24},{20,28},{24,16},{28,20},{1,9},{5... | collective-permute-start | bytes 688136 | tf_op jit(solution)/shard_map/ppermute | solution.py:37
  85.6 1.9 %collective-permute-start.6 = (bf16[4,224,128]{2,1,0:T(8,128)(2,1)S(1)}, bf16[4,224,128]{2,1,0:T(8,128)(2,1)S(1)}, u32[]{:S(2)}, u32[]{:S(2)}) collective-permute-start(bf16[4,224,128]{2,1,0:T(8,128)(2,1)S(1)} %fusion.7), channel_id=1, source_target_pairs={{0,24},{4,28},{8,16},{12,20},{16,8},{20,12},{24,0},{28,4},{1,25},{... | collective-permute-start | bytes 688136 | tf_op jit(solution)/shard_map/ppermute | solution.py:37
  87.4 6.7 %collective-permute-done.8 = bf16[4,224,128]{2,1,0:T(8,128)(2,1)S(1)} collective-permute-done((bf16[4,224,128]{2,1,0:T(8,128)(2,1)S(1)}, bf16[4,224,128]{2,1,0:T(8,128)(2,1)S(1)}, u32[]{:S(2)}, u32[]{:S(2)}) %collective-permute-start.8) | collective-permute-done | bytes 229408 | tf_op jit(solution)/shard_map/ppermute | solution.py:37
  94.3 0.8 collective-permute-done.6
  95.2 5.3 %collective-permute-start.9 = (bf16[4,224,128]{2,1,0:T(8,128)(2,1)S(1)}, bf16[4,224,128]{2,1,0:T(8,128)(2,1)S(1)}, u32[]{:S(2)}, u32[]{:S(2)}) collective-permute-start(bf16[4,224,128]{2,1,0:T(8,128)(2,1)S(1)} %fusion.9), channel_id=1, source_target_pairs={{0,4},{4,0},{8,12},{12,8},{16,20},{20,16},{24,28},{28,24},{1,5},{5... | collective-permute-start | bytes 688136 | tf_op jit(solution)/shard_map/ppermute | solution.py:37
  100.5 1.6 %copy.27 = bf16[8,384,128]{2,0,1:T(8,128)(2,1)S(1)} copy(bf16[8,384,128]{2,1,0:T(8,128)(2,1)} %all-to-all-done.2) | data formatting | bytes 1572864 | tf_op jit(solution)/shard_map/all_to_all | solution.py:20
  102.7 2.3 %shard_map.149 = (bf16[8,80,128]{2,1,0:T(8,128)(2,1)}, bf16[3,10,6,16,128]{4,3,2,1,0:T(8,128)(2,1)S(1)}) custom-call(bf16[768,512]{1,0:T(8,128)(2,1)S(1)} %bitcast.93, bf16[128,512]{1,0:T(8,128)(2,1)S(1)} %copy-done.6, bf16[8,1,16,128]{3,2,1,0:T(8,128)(2,1)S(1)} %get-tuple-element.75.before_ref, bf16[8,4,16,128]{3,2,1,0:T(8,128)(2,1)S(1)} %bitcast.99, ...), custom_call_target="tpu_custom_call" | custom-call | flops 452984832 | bytes 884736 | tf_op jit(solution)/shard_map/pallas_call | solution.py:87
  105.0 0.9 shard_map.150
  106.3 4.3 %collective-permute-start.12 = (bf16[992,128]{1,0:T(8,128)(2,1)S(1)}, bf16[992,128]{1,0:T(8,128)(2,1)S(1)}, u32[]{:S(2)}, u32[]{:S(2)}) collective-permute-start(bf16[992,128]{1,0:T(8,128)(2,1)S(1)} %get-tuple-element.49), channel_id=1, source_target_pairs={{0,1},{1,0},{2,3},{3,2},{4,5},{5,4},{6,7},{7,6},{8,9},{9,8},{10,11... | collective-permute-start | bytes 761864 | tf_op jit(solution)/shard_map/ppermute | solution.py:37
  110.7 1.6 %collective-permute-start.14 = (bf16[992,128]{1,0:T(8,128)(2,1)S(1)}, bf16[992,128]{1,0:T(8,128)(2,1)S(1)}, u32[]{:S(2)}, u32[]{:S(2)}) collective-permute-start(bf16[992,128]{1,0:T(8,128)(2,1)S(1)} %get-tuple-element.51), channel_id=1, source_target_pairs={{0,3},{1,2},{2,1},{3,0},{4,7},{5,6},{6,5},{7,4},{8,11},{9,10},{10,... | collective-permute-start | bytes 761864 | tf_op jit(solution)/shard_map/ppermute | solution.py:37
  112.3 4.0 %all-to-all-start.3 = ((bf16[8,80,128]{2,1,0:T(8,128)(2,1)}), bf16[8,80,128]{2,1,0:T(8,128)(2,1)S(1)}, u32[]{:S(2)}, u32[]{:S(2)}) async-start(bf16[8,80,128]{2,1,0:T(8,128)(2,1)} %get-tuple-element.46), calls=%async_computation.3 | async-start | bytes 327680 | tf_op jit(solution)/shard_map/all_to_all | solution.py:20
  116.4 10.8 %all-to-all-done.3 = bf16[8,80,128]{2,1,0:T(8,128)(2,1)S(1)} async-done(((bf16[8,80,128]{2,1,0:T(8,128)(2,1)}), bf16[8,80,128]{2,1,0:T(8,128)(2,1)S(1)}, u32[]{:S(2)}, u32[]{:S(2)}) %all-to-all-start.3) | async-done | bytes 163872 | tf_op jit(solution)/shard_map/all_to_all | solution.py:20
  127.2 2.5 %collective-permute-start.11 = (bf16[224,128]{1,0:T(8,128)(2,1)S(1)}, bf16[224,128]{1,0:T(8,128)(2,1)S(1)}, u32[]{:S(2)}, u32[]{:S(2)}) collective-permute-start(bf16[224,128]{1,0:T(8,128)(2,1)S(1)} %fusion.12), channel_id=1, source_target_pairs={{0,128},{32,160},{64,192},{96,224},{128,0},{160,32},{192,64},{224,... | collective-permute-start | bytes 172040 | tf_op jit(solution)/shard_map/ppermute | solution.py:37
  129.7 0.6 copy.32
  130.9 3.3 %collective-permute-done.11 = bf16[224,128]{1,0:T(8,128)(2,1)S(1)} collective-permute-done((bf16[224,128]{1,0:T(8,128)(2,1)S(1)}, bf16[224,128]{1,0:T(8,128)(2,1)S(1)}, u32[]{:S(2)}, u32[]{:S(2)}) %collective-permute-start.11) | collective-permute-done | bytes 57376 | tf_op jit(solution)/shard_map/ppermute | solution.py:37
  134.2 0.7 fusion.11
  134.9 0.7 convert_add_fusion.3
  135.6 0.9 convert_add_fusion.2
  (62 shorter events, 2.9 us)
Async XLA Ops:
  0.6 11.6 %copy-start.9 = (bf16[2,4,32,128]{3,2,1,0:T(8,128)(2,1)S(1)}, bf16[2,4,32,128]{3,2,1,0:T(8,128)(2,1)}, u32[]{:S(2)}) copy-start(bf16[2,4,32,128]{3,2,1,0:T(8,128)(2,1)} %param.15) | copy-start | bytes 196612
  0.6 11.5 %copy-start.11 = (s32[2,4,32]{2,1,0:T(4,128)S(1)}, s32[2,4,32]{2,1,0:T(4,128)}, u32[]{:S(2)}) copy-start(s32[2,4,32]{2,1,0:T(4,128)} %label_ref.1) | copy-start | bytes 3076
  0.7 25.1 %copy-start = (bf16[128,13824]{1,0:T(8,128)(2,1)S(1)}, bf16[128,13824]{1,0:T(8,128)(2,1)}, u32[]{:S(2)}) copy-start(bf16[128,13824]{1,0:T(8,128)(2,1)} %weight_ref.1) | copy-start | bytes 10616836
  13.5 0.7 copy-start.4
  14.2 5.3 %collective-permute-start = (bf16[128,512]{1,0:T(8,128)(2,1)}, bf16[128,512]{1,0:T(8,128)(2,1)}, u32[]{:S(2)}, u32[]{:S(2)}) collective-permute-start(bf16[128,512]{1,0:T(8,128)(2,1)} %get-tuple-element.30), channel_id=1, source_target_pairs={{0,32},{32,0},{64,96},{96,64},{128,160},{160,128},{192,224},{224,1... | collective-permute-start | bytes 393224 | tf_op jit(solution)/shard_map/ppermute | solution.py:37
  14.8 4.7 %collective-permute-start.1 = (bf16[128,512]{1,0:T(8,128)(2,1)}, bf16[128,512]{1,0:T(8,128)(2,1)}, u32[]{:S(2)}, u32[]{:S(2)}) collective-permute-start(bf16[128,512]{1,0:T(8,128)(2,1)} %get-tuple-element.31), channel_id=1, source_target_pairs={{32,64},{64,32},{96,128},{128,96},{160,192},{192,160},{33,65},{65,... | collective-permute-start | bytes 393224 | tf_op jit(solution)/shard_map/ppermute | solution.py:42
  17.1 5.8 %copy-start.2 = (bf16[8,16,4,128]{3,1,2,0:T(8,128)(2,1)}, bf16[8,16,4,128]{3,1,2,0:T(8,128)(2,1)S(1)}, u32[]{:S(2)}) copy-start(bf16[8,16,4,128]{3,1,2,0:T(8,128)(2,1)S(1)} %copy.38) | copy-start | bytes 393220
  20.4 5.4 %collective-permute-start.2 = (bf16[4,32,512]{2,1,0:T(8,128)(2,1)S(1)}, bf16[4,32,512]{2,1,0:T(8,128)(2,1)S(1)}, u32[]{:S(2)}, u32[]{:S(2)}) collective-permute-start(bf16[4,32,512]{2,1,0:T(8,128)(2,1)S(1)} %get-tuple-element.65), channel_id=1, source_target_pairs={{0,4},{4,0},{8,12},{12,8},{16,20},{20,16},{24,28},{28,24},{1,5},{5... | collective-permute-start | bytes 393224 | tf_op jit(solution)/shard_map/ppermute | solution.py:37
  22.2 3.5 %collective-permute-start.3 = (bf16[4,32,512]{2,1,0:T(8,128)(2,1)S(1)}, bf16[4,32,512]{2,1,0:T(8,128)(2,1)S(1)}, u32[]{:S(2)}, u32[]{:S(2)}) collective-permute-start(bf16[4,32,512]{2,1,0:T(8,128)(2,1)S(1)} %get-tuple-element.64), channel_id=1, source_target_pairs={{4,8},{8,4},{12,16},{16,12},{20,24},{24,20},{5,9},{9,5},{13,17},{1... | collective-permute-start | bytes 393224 | tf_op jit(solution)/shard_map/ppermute | solution.py:42
  25.8 1.0 copy-start.5
  26.7 0.8 copy-start.7
  31.4 0.7 copy-start.10
  32.1 0.9 copy-start.12
  32.9 13.2 %collective-permute-start.4 = (bf16[448,512]{1,0:T(8,128)(2,1)}, bf16[448,512]{1,0:T(8,128)(2,1)S(1)}, u32[]{:S(2)}, u32[]{:S(2)}) collective-permute-start(bf16[448,512]{1,0:T(8,128)(2,1)} %get-tuple-element.35), channel_id=1, source_target_pairs={{0,32},{32,0},{64,96},{96,64},{128,160},{160,128},{192,224},{224,1... | collective-permute-start | bytes 1376264 | tf_op jit(solution)/shard_map/ppermute | solution.py:37
  37.2 24.7 %all-to-all-start = ((bf16[4,144,128]{2,1,0:T(8,128)(2,1)}), bf16[4,144,128]{2,1,0:T(8,128)(2,1)S(1)}, u32[]{:S(2)}, u32[]{:S(2)}) async-start(bf16[4,144,128]{2,1,0:T(8,128)(2,1)} %copy-done.10), calls=%async_computation | async-start | bytes 294912 | tf_op jit(solution)/shard_map/all_to_all | solution.py:20
  46.2 0.8 copy-start.8
  47.0 1.1 copy-start.13
  54.2 29.3 %collective-permute-start.7 = (bf16[2,4,224,128]{3,2,1,0:T(8,128)(2,1)S(1)}, bf16[2,4,224,128]{3,2,1,0:T(8,128)(2,1)S(1)}, u32[]{:S(2)}, u32[]{:S(2)}) collective-permute-start(bf16[2,4,224,128]{3,2,1,0:T(8,128)(2,1)S(1)} %get-tuple-element.41), channel_id=1, source_target_pairs={{0,24},{4,28},{8,16},{12,20},{16,8},{20,12},{24,0},{28,4},{1,25},{... | collective-permute-start | bytes 1376264 | tf_op jit(solution)/shard_map/ppermute | solution.py:37
  62.7 15.5 %all-to-all-start.1 = ((bf16[8,80,128]{2,1,0:T(8,128)(2,1)}), bf16[8,80,128]{2,1,0:T(8,128)(2,1)S(1)}, u32[]{:S(2)}, u32[]{:S(2)}) async-start(bf16[8,80,128]{2,1,0:T(8,128)(2,1)} %broadcast_in_dim.6), calls=%async_computation.1 | async-start | bytes 327680 | tf_op jit(solution)/shard_map/all_to_all | solution.py:20
  70.9 14.5 %collective-permute-start.5 = (bf16[2,4,224,128]{3,2,1,0:T(8,128)(2,1)S(1)}, bf16[2,4,224,128]{3,2,1,0:T(8,128)(2,1)S(1)}, u32[]{:S(2)}, u32[]{:S(2)}) collective-permute-start(bf16[2,4,224,128]{3,2,1,0:T(8,128)(2,1)S(1)} %get-tuple-element.39), channel_id=1, source_target_pairs={{0,8},{4,12},{8,0},{12,4},{16,24},{20,28},{24,16},{28,20},{1,9},{5... | collective-permute-start | bytes 1376264 | tf_op jit(solution)/shard_map/ppermute | solution.py:37
  79.3 21.2 %all-to-all-start.2 = ((bf16[8,384,128]{2,1,0:T(8,128)(2,1)}), bf16[8,384,128]{2,1,0:T(8,128)(2,1)}, u32[]{:S(2)}, u32[]{:S(2)}) async-start(bf16[8,384,128]{2,1,0:T(8,128)(2,1)} %broadcast_in_dim.15), calls=%async_computation.2 | async-start | bytes 1572864 | tf_op jit(solution)/shard_map/all_to_all | solution.py:20
  83.7 10.5 %collective-permute-start.8 = (bf16[4,224,128]{2,1,0:T(8,128)(2,1)S(1)}, bf16[4,224,128]{2,1,0:T(8,128)(2,1)S(1)}, u32[]{:S(2)}, u32[]{:S(2)}) collective-permute-start(bf16[4,224,128]{2,1,0:T(8,128)(2,1)S(1)} %fusion.8), channel_id=1, source_target_pairs={{0,8},{4,12},{8,0},{12,4},{16,24},{20,28},{24,16},{28,20},{1,9},{5... | collective-permute-start | bytes 688136 | tf_op jit(solution)/shard_map/ppermute | solution.py:37
  85.6 9.5 %collective-permute-start.6 = (bf16[4,224,128]{2,1,0:T(8,128)(2,1)S(1)}, bf16[4,224,128]{2,1,0:T(8,128)(2,1)S(1)}, u32[]{:S(2)}, u32[]{:S(2)}) collective-permute-start(bf16[4,224,128]{2,1,0:T(8,128)(2,1)S(1)} %fusion.7), channel_id=1, source_target_pairs={{0,24},{4,28},{8,16},{12,20},{16,8},{20,12},{24,0},{28,4},{1,25},{... | collective-permute-start | bytes 688136 | tf_op jit(solution)/shard_map/ppermute | solution.py:37
  94.2 8.4 %copy-start.1 = (bf16[128,27,128]{2,0,1:T(8,128)(2,1)S(1)}, bf16[128,27,128]{2,0,1:T(8,128)(2,1)}, u32[]{:S(2)}) copy-start(bf16[128,27,128]{2,0,1:T(8,128)(2,1)} %param.12) | copy-start | bytes 2654212
  94.2 8.4 %copy-start.3 = (bf16[8,16,4,128]{3,1,2,0:T(8,128)(2,1)S(1)}, bf16[8,16,4,128]{3,1,2,0:T(8,128)(2,1)}, u32[]{:S(2)}) copy-start(bf16[8,16,4,128]{3,1,2,0:T(8,128)(2,1)} %copy-done.2) | copy-start | bytes 393220
  94.2 8.4 %copy-start.6 = (bf16[128,512]{1,0:T(8,128)(2,1)S(1)}, bf16[128,512]{1,0:T(8,128)(2,1)}, u32[]{:S(2)}) copy-start(bf16[128,512]{1,0:T(8,128)(2,1)} %up_ref.1) | copy-start | bytes 393220
  95.2 10.8 %collective-permute-start.9 = (bf16[4,224,128]{2,1,0:T(8,128)(2,1)S(1)}, bf16[4,224,128]{2,1,0:T(8,128)(2,1)S(1)}, u32[]{:S(2)}, u32[]{:S(2)}) collective-permute-start(bf16[4,224,128]{2,1,0:T(8,128)(2,1)S(1)} %fusion.9), channel_id=1, source_target_pairs={{0,4},{4,0},{8,12},{12,8},{16,20},{20,16},{24,28},{28,24},{1,5},{5... | collective-permute-start | bytes 688136 | tf_op jit(solution)/shard_map/ppermute | solution.py:37
  106.1 10.2 %collective-permute-start.10 = (bf16[2,224,128]{2,1,0:T(8,128)(2,1)S(1)}, bf16[2,224,128]{2,1,0:T(8,128)(2,1)S(1)}, u32[]{:S(2)}, u32[]{:S(2)}) collective-permute-start(bf16[2,224,128]{2,1,0:T(8,128)(2,1)S(1)} %fusion.10), channel_id=1, source_target_pairs={{0,64},{32,96},{64,0},{96,32},{128,192},{160,224},{192,128},{224,1... | collective-permute-start | bytes 344072 | tf_op jit(solution)/shard_map/ppermute | solution.py:37
  106.3 28.6 %collective-permute-start.12 = (bf16[992,128]{1,0:T(8,128)(2,1)S(1)}, bf16[992,128]{1,0:T(8,128)(2,1)S(1)}, u32[]{:S(2)}, u32[]{:S(2)}) collective-permute-start(bf16[992,128]{1,0:T(8,128)(2,1)S(1)} %get-tuple-element.49), channel_id=1, source_target_pairs={{0,1},{1,0},{2,3},{3,2},{4,5},{5,4},{6,7},{7,6},{8,9},{9,8},{10,11... | collective-permute-start | bytes 761864 | tf_op jit(solution)/shard_map/ppermute | solution.py:37
  110.6 24.3 %collective-permute-start.13 = (bf16[992,128]{1,0:T(8,128)(2,1)S(1)}, bf16[992,128]{1,0:T(8,128)(2,1)S(1)}, u32[]{:S(2)}, u32[]{:S(2)}) collective-permute-start(bf16[992,128]{1,0:T(8,128)(2,1)S(1)} %get-tuple-element.50), channel_id=1, source_target_pairs={{0,2},{1,3},{2,0},{3,1},{4,6},{5,7},{6,4},{7,5},{8,10},{9,11},{10,... | collective-permute-start | bytes 761864 | tf_op jit(solution)/shard_map/ppermute | solution.py:37
  110.7 24.3 %collective-permute-start.14 = (bf16[992,128]{1,0:T(8,128)(2,1)S(1)}, bf16[992,128]{1,0:T(8,128)(2,1)S(1)}, u32[]{:S(2)}, u32[]{:S(2)}) collective-permute-start(bf16[992,128]{1,0:T(8,128)(2,1)S(1)} %get-tuple-element.51), channel_id=1, source_target_pairs={{0,3},{1,2},{2,1},{3,0},{4,7},{5,6},{6,5},{7,4},{8,11},{9,10},{10,... | collective-permute-start | bytes 761864 | tf_op jit(solution)/shard_map/ppermute | solution.py:37
  112.3 14.9 %all-to-all-start.3 = ((bf16[8,80,128]{2,1,0:T(8,128)(2,1)}), bf16[8,80,128]{2,1,0:T(8,128)(2,1)S(1)}, u32[]{:S(2)}, u32[]{:S(2)}) async-start(bf16[8,80,128]{2,1,0:T(8,128)(2,1)} %get-tuple-element.46), calls=%async_computation.3 | async-start | bytes 327680 | tf_op jit(solution)/shard_map/all_to_all | solution.py:20
  127.2 7.0 %collective-permute-start.11 = (bf16[224,128]{1,0:T(8,128)(2,1)S(1)}, bf16[224,128]{1,0:T(8,128)(2,1)S(1)}, u32[]{:S(2)}, u32[]{:S(2)}) collective-permute-start(bf16[224,128]{1,0:T(8,128)(2,1)S(1)} %fusion.12), channel_id=1, source_target_pairs={{0,128},{32,160},{64,192},{96,224},{128,0},{160,32},{192,64},{224,... | collective-permute-start | bytes 172040 | tf_op jit(solution)/shard_map/ppermute | solution.py:37
